TPU v7x, 32 devices: a whole 2x2x4 slice. The times are simulated.
32 devices in a mesh: grp: 2 (over x), fsdp: 4 (over z), item: 4 (over y, core).
Axes of the slice: x: 2, y: 2, z: 4, core: 2. Of those that a mesh axis runs over, the one named last changes fastest.
Arguments:
- hidden_states: bfloat16 [2048, 16, 4096], P(('grp', 'fsdp', 'item')), may hold values from -6 to 6
- positives: bfloat16 [2048, 1024], P(('grp', 'fsdp', 'item')), may hold values from -6 to 6
- negatives: int32 [2048, 32], P(('grp', 'fsdp', 'item')), may hold values from 0 to 4095, as said below
- lengths: int32 [2048], P(('grp', 'fsdp', 'item')), may hold values from 1 to 16, as said below
- norm_gain: bfloat16 [4096], replicated, may hold values from 0.25 to 1.75
- proj_weight: bfloat16 [4096, 1024], P('fsdp'), may hold values from -0.09375 to 0.09375
- pool_query: float32 [1024], replicated, may hold values from -6 to 6
- slab: bfloat16 [4096, 1024], P('item'), may hold values from -6 to 6
Outputs:
- grad_proj: float32 [4096, 1024], P('fsdp')
- grad_query: float32 [1024], replicated
- mean_loss: float32 [], replicated
Inputs may be any that keep to these rules, and one draw needn't show every extreme that they name: `negatives`: entries 8 o to 8 (o + 1) - 1 of each query's list are rows of owner block o, the slab rows 1024 o to 1024 (o + 1) - 1; a row may repeat. The first lengths[q] token slots of query q are valid.
All inputs are finite; a program needn't handle non-finite values.
Results may differ from a plain program's by a relative error of at most 0.0043.
Values may be sent and summed in bfloat16 or wider, within the bound.
No kernel may reach another device: no remote copies, remote signals or barrier semaphores. Data moves between devices by JAX's collectives and lax.ppermute only.
A program may use at most 128 MiB of HBM per device.

v0:
```python
import functools
import math

import jax
import jax.numpy as jnp
from jax import lax
from jax.experimental import pallas as pl
from jax.experimental.pallas import tpu as pltpu
from jax.sharding import PartitionSpec as P

sharpness_divisor = 0.05
norm_eps = 1e-05
embed_eps = 1e-06

EVERY = ("fsdp", "grp", "item")
PLANE = ("grp", "item")
F32 = jnp.float32
BF16 = jnp.bfloat16
LANES = 128
MIB = 1024 * 1024
VMEM = pl.BlockSpec(memory_space=pltpu.VMEM)
SMEM = pl.BlockSpec(memory_space=pltpu.SMEM)


def shape(dims, dtype):
    return jax.ShapeDtypeStruct(dims, dtype)


def call(kernel, outs, ins, name, flops=0, scratch=(), smem=0, after=()):
    run = kernel
    if after:
        count = len(ins)

        def run(*refs):
            kernel(*refs[:count], *refs[count + len(after) :])

    moved = sum(math.prod(a.shape) * a.dtype.itemsize for a in list(ins) + list(outs))
    held = sum(math.prod(s.shape) * jnp.dtype(s.dtype).itemsize for s in scratch)
    return pl.pallas_call(
        run,
        out_shape=outs,
        in_specs=[SMEM] * smem
        + [VMEM] * (len(ins) - smem)
        + [pl.BlockSpec(memory_space=pl.ANY)] * len(after),
        out_specs=[VMEM] * len(outs),
        scratch_shapes=scratch,
        cost_estimate=pl.CostEstimate(flops=flops, bytes_accessed=moved, transcendentals=0),
        compiler_params=pltpu.CompilerParams(vmem_limit_bytes=2 * (moved + held) + 6 * MIB),
        name=name,
    )(*ins, *after)


def shift(values, axis, k):
    n = lax.axis_size(axis)
    return lax.ppermute(values, axis, [(i, (i + k) % n) for i in range(n)])


def split_bf16(values):
    high = values.astype(BF16)
    low = (values - high.astype(F32)).astype(BF16)
    return high, low


def nt(left, right):
    return lax.dot_general(left, right, (((1,), (1,)), ((), ())), preferred_element_type=F32)


def tn(left, right):
    return lax.dot_general(left, right, (((0,), (0,)), ((), ())), preferred_element_type=F32)


def norm_kernel(event_ref, states_ref, gain_ref, normed_ref):
    tokens, width = states_ref.shape
    step = 4 * LANES if width % (4 * LANES) == 0 else width
    for top in range(0, tokens, 32):
        rows = slice(top, top + 32)
        squares = jnp.zeros((32, step), F32)
        for at in range(0, width, step):
            part = states_ref[rows, at : at + step].astype(F32)
            squares = squares + part * part
        inv_rms = lax.rsqrt(jnp.sum(squares, axis=1, keepdims=True) / width + norm_eps)
        for at in range(0, width, step):
            part = states_ref[rows, at : at + step].astype(F32)
            part = part * inv_rms * gain_ref[:, at : at + step]
            normed_ref[rows, at : at + step] = part.astype(BF16)


def norm_rows(event, states, gain):
    tokens, width = states.shape
    block = 128 if tokens % 128 == 0 else tokens
    rows = pl.BlockSpec((block, width), lambda i: (i, 0))
    return pl.pallas_call(
        norm_kernel,
        grid=(tokens // block,),
        out_shape=shape((tokens, width), BF16),
        in_specs=[pl.BlockSpec(memory_space=pl.ANY), rows, pl.BlockSpec((1, width), lambda i: (0, 0))],
        out_specs=rows,
        cost_estimate=pl.CostEstimate(
            flops=6 * tokens * width, bytes_accessed=4 * tokens * width, transcendentals=0
        ),
        compiler_params=pltpu.CompilerParams(vmem_limit_bytes=10 * MIB),
        name="norm_rows",
    )(event, states, gain)


def gate_kernel(seq, root, blocks, z_ref, normed_ref, u_ref, len_ref, lists_ref, event_ref, *rest):
    half = blocks // 2
    outs, gated_ref, curve_ref, copy_ref, rows_ref = rest[:half], *rest[half:]
    step = pl.program_id(0)
    tokens, width = normed_ref.shape
    count = tokens // seq
    chunk = 4 * LANES if width % (4 * LANES) == 0 else width
    logits = []
    for top in range(0, tokens, 32):
        total = jnp.zeros((32, chunk), F32)
        for at in range(0, width, chunk):
            part = normed_ref[top : top + 32, at : at + chunk].astype(F32)
            total = total + part * u_ref[:, at : at + chunk]
        logits.append(jnp.sum(total, axis=1, keepdims=True))
    logit = jnp.concatenate(logits, axis=0) / root
    gate = 1.0 / (1.0 + jnp.exp(-logit))
    slot = lax.rem(lax.broadcasted_iota(jnp.int32, (tokens, 1), 0), seq)
    valid = jnp.where(slot < len_ref[...], 1.0, 0.0) / len_ref[...].astype(F32)
    gated = valid * gate
    gated_ref[...] = gated
    curve_ref[...] = gated * (1.0 - gate) / root
    owner = lax.broadcasted_iota(jnp.int32, (tokens, count), 0) // seq
    mine = owner == lax.broadcasted_iota(jnp.int32, (tokens, count), 1)
    high, low = split_bf16(jnp.where(mine, gated, 0.0))
    both = tn(jnp.concatenate([high, low], axis=1), normed_ref[...])
    rows_ref[pl.ds(pl.multiple_of(step * count, count), count), :] = both[:count] + both[count:]

    @pl.when(step == pl.num_programs(0) - 1)
    def _():
        copy_ref[...] = lists_ref[...]
        depth = width // blocks
        place = lax.rem(z_ref[0], half)
        for k in range(half):
            for j in range(2):
                at = (j * half + lax.rem(place + k, half)) * depth
                outs[k][:, j * depth : (j + 1) * depth] = rows_ref[
                    :, pl.ds(pl.multiple_of(at, LANES), depth)
                ].astype(BF16)


def gate_rows(z, normed, u, token_lengths, lists, event, seq, root, blocks):
    tokens, width = normed.shape
    queries = tokens // seq
    group = 16 if queries % 16 == 0 else queries
    step_tokens = group * seq
    half = blocks // 2
    outs = [shape((queries, width // half), BF16)] * half + [shape((tokens, 1), F32)] * 2
    outs.append(shape(lists.shape, lists.dtype))
    column = pl.BlockSpec((step_tokens, 1), lambda i: (i, 0))
    whole = lambda dims: pl.BlockSpec(dims, lambda i: (0, 0))
    return pl.pallas_call(
        functools.partial(gate_kernel, seq, root, blocks),
        grid=(queries // group,),
        out_shape=outs,
        in_specs=[
            SMEM,
            pl.BlockSpec((step_tokens, width), lambda i: (i, 0)),
            whole((1, width)),
            column,
            whole(lists.shape),
            pl.BlockSpec(memory_space=pl.ANY),
        ],
        out_specs=[whole((queries, width // half))] * half + [column] * 2 + [whole(lists.shape)],
        scratch_shapes=[pltpu.VMEM((queries, width), F32)],
        cost_estimate=pl.CostEstimate(
            flops=4 * tokens * width, bytes_accessed=2 * tokens * width, transcendentals=0
        ),
        compiler_params=pltpu.CompilerParams(vmem_limit_bytes=16 * MIB),
        name="gate_rows",
    )(z, normed, u, token_lengths, lists, event)


def pack_kernel(*refs):
    rows = refs[0].shape[0]
    for k, ref in enumerate(refs[:-1]):
        refs[-1][k * rows : (k + 1) * rows, :] = ref[...]


def pack(pieces, name, event):
    rows, width = pieces[0].shape
    out = shape((len(pieces) * rows, width), pieces[0].dtype)
    return call(pack_kernel, [out], pieces, name, after=[event])[0]


def forward_kernel(n, packs, side_ref, places_ref, *refs):
    pieces, weight_ref, shares = refs[:n], refs[n], refs[n + 1 : n + 1 + packs]
    outs = refs[n + 1 + packs : 2 * n + 1 + packs]
    mirror_ref, held_ref, away_ref = refs[2 * n + 1 + packs :]
    rows = pieces[0].shape[0]
    depth = weight_ref.shape[0]
    side = side_ref[0]
    for k in range(n):
        part = slice(k * rows, (k + 1) * rows)
        held_ref[part, :] = pieces[k][:, pl.ds(pl.multiple_of(side * depth, LANES), depth)]
        away_ref[part, :] = pieces[k][:, pl.ds(pl.multiple_of((1 - side) * depth, LANES), depth)]
    count = places_ref.shape[0] // packs
    share = shares[0].shape[0] // count
    for p in range(packs):
        for j in range(count):
            at = pl.multiple_of(places_ref[p * count + j] * share, share)
            mirror_ref[pl.ds(at, share), :] = shares[p][j * share : (j + 1) * share, :]
    product = jnp.dot(held_ref[...], weight_ref[...], preferred_element_type=F32)
    product = product + jnp.dot(away_ref[...], mirror_ref[...], preferred_element_type=F32)
    for k in range(n):
        outs[k][...] = product[k * rows : (k + 1) * rows].astype(outs[k].dtype)


def back_kernel(n, side_ref, *refs):
    pieces, weight_ref, mirror_ref, outs = refs[:n], refs[n], refs[n + 1], refs[n + 2 :]
    rows = pieces[0].shape[0]
    depth = weight_ref.shape[0]
    side = side_ref[0]
    stack = jnp.concatenate([p[...] for p in pieces], axis=0)
    own = nt(stack, weight_ref[...]).astype(BF16)
    mirror = nt(stack, mirror_ref[...]).astype(BF16)
    for k in range(n):
        part = slice(k * rows, (k + 1) * rows)
        outs[k][:, pl.ds(pl.multiple_of(side * depth, LANES), depth)] = own[part]
        outs[k][:, pl.ds(pl.multiple_of((1 - side) * depth, LANES), depth)] = mirror[part]


def embed_kernel(root, n, *refs):
    parts, packed = refs[:n], refs[n:-4]
    pooled_ref, unit_ref, embedded_ref, pack_ref = refs[-4:]
    pooled = parts[0][...]
    for part in parts[1:]:
        pooled = pooled + part[...].astype(F32)
    unit = lax.rsqrt(jnp.mean(pooled * pooled, axis=1, keepdims=True) + embed_eps) / root
    pooled_ref[...] = pooled
    unit_ref[...] = unit
    embedded_ref[...] = (pooled * unit).astype(BF16)
    pack_kernel(*packed, pack_ref)


def count_kernel(n, root, base_ref, slab_ref, *refs):
    lists, counts_ref, scale_ref = refs[:n], refs[n], refs[n + 1]
    queries = lists[0].shape[0]
    rows, width = slab_ref.shape
    slab = slab_ref[...].astype(F32)
    high, low = split_bf16(slab * slab)
    ones = jnp.ones((8, width), BF16)
    row_sq = (nt(ones, high) + nt(ones, low))[0:1]
    scale_ref[...] = lax.rsqrt(row_sq / width + embed_eps) / root / sharpness_divisor
    ids = lax.broadcasted_iota(jnp.int32, (queries, LANES), 1)
    for k in range(n):
        own = lists[k][...] - base_ref[0]
        columns = [
            jnp.broadcast_to(own[:, entry : entry + 1], (queries, LANES)) for entry in range(own.shape[1])
        ]
        for at in range(0, rows, LANES):
            total = jnp.zeros(ids.shape, F32)
            for column in columns:
                total = total + jnp.where(column == ids + at, 1.0, 0.0)
            counts_ref[k * queries : (k + 1) * queries, at : at + LANES] = total


def contrast_kernel(n, *refs):
    pieces, (slab_ref, scale_ref, counts_ref), outs = refs[:n], refs[n : n + 3], refs[n + 3 :]
    queries, width = pieces[0].shape
    embedded = jnp.concatenate([p[...] for p in pieces], axis=0)
    slab = slab_ref[...]
    scale = scale_ref[...]
    heavy = counts_ref[...] * jnp.exp(nt(embedded, slab) * scale)
    denom = jnp.sum(heavy, axis=1, keepdims=True)
    grad = jnp.dot((heavy * scale).astype(BF16), slab, preferred_element_type=F32)
    high, low = split_bf16(denom)
    lane = lax.broadcasted_iota(jnp.int32, (queries, LANES), 1)
    for k in range(n):
        part = slice(k * queries, (k + 1) * queries)
        outs[k][:, :width] = grad[part].astype(outs[k].dtype)
        if k == 0:
            tail = jnp.where(lane == 0, denom[part], 0.0)
        else:
            tail = jnp.where(lane == 0, high[part].astype(F32), jnp.where(lane == 1, low[part].astype(F32), 0.0))
        outs[k][:, width:] = tail.astype(outs[k].dtype)


def grad_kernel(n, packed_count, root, *refs):
    parts = refs[:n]
    pos_ref, pooled_ref, unit_ref, embedded_ref = refs[n : n + 4]
    packed = refs[n + 4 : n + 4 + packed_count]
    grad_ref, columns_ref, loss_ref, pack_ref = refs[n + 4 + packed_count :]
    queries, width = pos_ref.shape
    total = parts[0][:, :width]
    denom = jnp.sum(parts[0][:, width:], axis=1, keepdims=True)
    for part in parts[1:]:
        total = total + part[:, :width].astype(F32)
        denom = denom + jnp.sum(part[:, width:].astype(F32), axis=1, keepdims=True)
    positive = pos_ref[...].astype(F32)
    scale = (
        lax.rsqrt(jnp.mean(positive * positive, axis=1, keepdims=True) + embed_eps)
        / root
        / sharpness_divisor
    )
    score = jnp.sum(embedded_ref[...].astype(F32) * positive, axis=1, keepdims=True) * scale
    pos_exp = jnp.exp(score)
    denom = denom + pos_exp
    loss_ref[...] = jnp.broadcast_to(jnp.sum(jnp.log(denom) - score), loss_ref.shape)
    grad_embed = total / denom + (pos_exp / denom - 1.0) * scale * positive
    pooled, unit = pooled_ref[...], unit_ref[...]
    mean_sq = jnp.mean(pooled * pooled, axis=1, keepdims=True)
    radial = jnp.sum(pooled * grad_embed, axis=1, keepdims=True)
    grad = unit * grad_embed - pooled * (radial * unit / (width * (mean_sq + embed_eps)))
    grad = grad.astype(BF16)
    grad_ref[...] = grad
    cols = columns_ref.shape[2]
    places = width // cols
    for j in range(columns_ref.shape[0]):
        at = (j % places) * cols
        columns_ref[j] = grad[:, at : at + cols]
    pack_kernel(*packed, pack_ref)


def slope_kernel(seq, blocks, z_ref, normed_ref, curve_ref, loss_ref, *rest):
    half = blocks // 2
    backs, out_ref, all_ref, sum_ref = rest[:half], rest[-3], rest[-2], rest[-1]
    step = pl.program_id(0)
    tokens, width = normed_ref.shape
    count = tokens // seq
    depth = width // blocks
    place = lax.rem(z_ref[0], half)

    def block_at(j, k):
        return pl.ds(pl.multiple_of((j * half + lax.rem(place + k, half)) * depth, LANES), depth)

    @pl.when(step == 0)
    def _():
        sum_ref[...] = jnp.zeros_like(sum_ref)
        for k in range(half):
            for j in range(2):
                all_ref[:, block_at(j, k)] = backs[k][:, j * depth : (j + 1) * depth].astype(F32)

    back = all_ref[pl.ds(pl.multiple_of(step * count, count), count), :]
    normed = normed_ref[...].astype(F32).reshape(count, seq, width)
    dots = jnp.sum(normed * back[:, None, :], axis=2, keepdims=True)
    slope = curve_ref[...].reshape(count, seq, 1) * dots
    heavy = (slope * normed).reshape(tokens // 8, 8, width)
    sum_ref[...] += jnp.sum(heavy, axis=0)

    @pl.when(step == pl.num_programs(0) - 1)
    def _():
        total = jnp.sum(sum_ref[...], axis=0, keepdims=True)
        loss = jnp.broadcast_to(loss_ref[...], (7, LANES))
        share = width // out_ref.shape[0]
        for to in range(out_ref.shape[0]):
            out_ref[to, 1:8, :] = loss
            out_ref[to, 0:1, :share] = total[:, to * share : (to + 1) * share]


def slope_rows(z, normed, curve, loss, backs, seq, blocks, devices, after):
    tokens, width = normed.shape
    half = blocks // 2
    queries = tokens // seq
    group = 8 if queries % 8 == 0 else queries
    step_tokens = group * seq
    whole = lambda dims: pl.BlockSpec(dims, lambda i: (0, 0))
    return pl.pallas_call(
        functools.partial(slope_kernel, seq, blocks),
        grid=(queries // group,),
        out_shape=shape((devices, 8, LANES), F32),
        in_specs=[
            SMEM,
            pl.BlockSpec((step_tokens, width), lambda i: (i, 0)),
            pl.BlockSpec((step_tokens, 1), lambda i: (i, 0)),
            whole((1, LANES)),
        ]
        + [whole((queries, width // half))] * half
        + [pl.BlockSpec(memory_space=pl.ANY)],
        out_specs=pl.BlockSpec((devices, 8, LANES), lambda i: (0, 0, 0)),
        scratch_shapes=[pltpu.VMEM((queries, width), F32), pltpu.VMEM((8, width), F32)],
        cost_estimate=pl.CostEstimate(
            flops=4 * tokens * width, bytes_accessed=2 * tokens * width, transcendentals=0
        ),
        compiler_params=pltpu.CompilerParams(vmem_limit_bytes=20 * MIB),
        name="slope_rows",
    )(z, normed, curve, loss, *backs, after)


def columns_kernel(n, order_ref, grads_ref, *refs):
    pieces, out_ref, sorted_ref = refs[:n], refs[n], refs[n + 1]
    chunk = grads_ref.shape[1]
    for j in range(sorted_ref.shape[0] // chunk):
        sorted_ref[j * chunk : (j + 1) * chunk, :] = grads_ref[order_ref[j]]
    at = pieces[0].shape[0]
    total = tn(sorted_ref[0:at, :], pieces[0][...])
    for piece in pieces[1:]:
        rows = piece.shape[0]
        total = total + tn(sorted_ref[at : at + rows, :], piece[...])
        at += rows
    out_ref[...] = total.T.astype(BF16)


def query_kernel(share, place_ref, parts_ref, weight_ref, out_ref, loss_ref):
    total = jnp.sum(parts_ref[...], axis=0)
    loss_ref[...] = total[1:2]
    line = total[0:1]
    high, low = split_bf16(jnp.broadcast_to(line[:, :share], (8, share)))
    weight = weight_ref[pl.ds(pl.multiple_of(place_ref[0] * share, share), share), :]
    part = (
        jnp.dot(high, weight, preferred_element_type=F32)
        + jnp.dot(low, weight, preferred_element_type=F32)
    )[0:1]
    lines = part.shape[1] // LANES
    rows = [part[:, k * LANES : (k + 1) * LANES] for k in range(lines)] + [line]
    rows.append(jnp.zeros((out_ref.shape[1] - lines - 1, LANES), F32))
    out_ref[...] = jnp.broadcast_to(jnp.concatenate(rows, axis=0)[None], out_ref.shape)


def finish_kernel(n, *refs):
    z_ref, place_ref, sums_ref, pool_ref = refs[:4]
    pieces, out_ref, query_ref = refs[4 : 4 + n], refs[-2], refs[-1]
    rows, cols = pieces[0].shape[0] // (place_ref.shape[0] // n), pieces[0].shape[1]
    places = place_ref.shape[0]
    share = rows // places
    lines = query_ref.shape[0]
    query_ref[...] = jnp.sum(sums_ref[:, :lines, :], axis=0)
    for p in range(places):
        line = sums_ref[z_ref[0] * places + p, lines : lines + 1, :share]
        slope = jnp.broadcast_to(line, (LANES, share)).T
        part = slice(p * share, (p + 1) * share)
        for k in range(places):
            piece = pieces[k // (places // n)]
            base = k % (places // n) * rows
            at = pl.ds(pl.multiple_of(place_ref[k] * cols, LANES), cols)
            mine = piece[base + p * share : base + (p + 1) * share, :].astype(F32)
            out_ref[part, at] = mine + slope * pool_ref[:, at]


def body(hidden_states, positives, negatives, lengths, norm_gain, proj_weight, pool_query, slab):
    queries, seq, width = hidden_states.shape
    depth, proj_width = proj_weight.shape
    n_z, n_g, n_i = lax.axis_size("fsdp"), lax.axis_size("grp"), lax.axis_size("item")
    assert n_z % 2 == 0
    half = n_z // 2
    n_c = 2 if n_i % 2 == 0 else 1
    n_h = n_i // n_c
    n_plane = n_g * n_i
    n_all = n_z * n_plane
    z, g, i = lax.axis_index("fsdp"), lax.axis_index("grp"), lax.axis_index("item")
    h, c = i // n_c, lax.rem(i, n_c)
    side, member = z // half, lax.rem(z, half)
    root = math.sqrt(proj_width)
    steps_z, steps_i = range(1, n_z), range(1, n_i)

    def ints(*values):
        return jnp.stack([jnp.asarray(v, jnp.int32) for v in values])

    z_arr, side_arr = ints(z), ints(side)

    def plane_shift(values, dg, dh, dc):
        pairs = []
        for pg in range(n_g):
            for ph in range(n_h):
                for pc in range(n_c):
                    to = ((pg + dg) % n_g) * n_i + ((ph + dh) % n_h) * n_c + (pc + dc) % n_c
                    pairs.append((pg * n_i + ph * n_c + pc, to))
        return lax.ppermute(values, PLANE, pairs)

    def half_shift(values, k):
        pairs = [(a, a // half * half + (a % half + k) % half) for a in range(n_z)]
        return lax.ppermute(values, "fsdp", pairs)

    def mirror_shift(values):
        return lax.ppermute(values, "fsdp", [(a, (a + half) % n_z) for a in range(n_z)])

    def source(dg, dh, dc):
        return (
            lax.rem(g - dg + n_g, n_g),
            lax.rem(h - dh + n_h, n_h) * n_c + lax.rem(c - dc + n_c, n_c),
        )

    chips = [(dg, dh) for dg in range(n_g) for dh in range(n_h)]

    share = depth // n_plane
    place = g * n_i + i
    weight_share = lax.dynamic_slice_in_dim(proj_weight, place * share, share, 0)
    far_share = mirror_shift(weight_share)

    block_u = jnp.sum(proj_weight.astype(F32) * pool_query[None, :], axis=1).reshape(1, depth)
    u_parts = [block_u] + [shift(block_u, "fsdp", k) for k in steps_z]
    u = jnp.zeros((1, width), F32)
    for k in range(n_z):
        u = lax.dynamic_update_slice(u, u_parts[k], (0, lax.rem(z - k + n_z, n_z) * depth))

    normed = norm_rows(u, hidden_states.reshape(-1, width), norm_gain.astype(F32).reshape(1, width))

    far_share = pack([far_share], "far_share", normed)
    chip_shares = [far_share if dg == dh == 0 else plane_shift(far_share, dg, dh, 0) for dg, dh in chips]
    share_places = []
    for dc in range(n_c):
        for dg, dh in chips:
            from_g, from_i = source(dg, dh, dc)
            share_places.append(from_g * n_i + from_i)

    token_lengths = jnp.broadcast_to(lengths[:, None], (queries, seq)).reshape(-1, 1)
    *sends, gated, curve, own_lists = gate_rows(
        z_arr, normed, u, token_lengths, negatives, far_share, seq, root, n_z
    )

    packs = [pack(chip_shares, "pack_shares", gated)]
    packs += [plane_shift(packs[0], 0, 0, dc) for dc in range(1, n_c)]

    pieces = [sends[0]] + [half_shift(sends[k], k) for k in range(1, half)]
    lists = [own_lists] + [shift(own_lists, "item", k) for k in steps_i]
    counts, slab_scale = call(
        functools.partial(count_kernel, n_i, root),
        [shape((n_i * queries, slab.shape[0]), F32), shape((1, slab.shape[0]), F32)],
        [ints(i * slab.shape[0]), slab] + lists, "list_counts", smem=1,
    )
    block = shape((half * queries, depth), BF16)
    *parts, mirror, held, away = call(
        functools.partial(forward_kernel, half, n_c),
        [shape((queries, proj_width), F32)]
        + [shape((queries, proj_width), BF16)] * (half - 1)
        + [shape((depth, proj_width), BF16), block, block],
        [side_arr, ints(*share_places)] + pieces + [proj_weight] + packs, "forward",
        flops=4 * half * queries * depth * proj_width, smem=2, after=[counts],
    )
    parts = [parts[0]] + [half_shift(parts[k], -k) for k in range(1, half)]
    near = [held] + [plane_shift(held, 0, dh, 0) for dh in range(1, n_h)]
    other = mirror_shift(away)
    row = shape((queries, proj_width), F32)
    row16 = shape((queries, proj_width), BF16)
    pooled, unit, embedded, near = call(
        functools.partial(embed_kernel, root, half),
        [row, shape((queries, 1), F32), row16, shape((n_h * half * queries, depth), BF16)],
        parts + near, "embed",
    )

    pieces = [embedded] + [shift(embedded, "item", k) for k in steps_i]
    near_far = [plane_shift(near, dg, 0, 0) for dg in range(1, n_g)]
    wide = (queries, proj_width + LANES)
    parts = call(
        functools.partial(contrast_kernel, n_i),
        [shape(wide, F32)] + [shape(wide, BF16)] * (n_i - 1),
        pieces + [slab, slab_scale, counts], "contrast",
        flops=4 * n_i * queries * slab.shape[0] * proj_width, after=[other],
    )
    parts = [parts[0]] + [shift(parts[k], "item", -k) for k in steps_i]
    near_cores = [plane_shift(near, 0, 0, dc) for dc in range(1, n_c)]
    others = [other] + [plane_shift(other, dg, 0, 0) for dg in range(1, n_g)]
    cols = proj_width // n_plane
    grad, grad_columns, loss, others = call(
        functools.partial(grad_kernel, n_i, n_g, root),
        [
            row16, shape((n_all, queries, cols), BF16), shape((1, LANES), F32),
            shape((n_g * half * queries, depth), BF16),
        ],
        parts + [positives, pooled, unit, embedded] + others, "grad_pooled", after=near_far + near_cores,
    )

    all_columns = lax.all_to_all(grad_columns, EVERY, 0, 0, tiled=True)
    pieces = [grad] + [half_shift(grad, k) for k in range(1, half)]
    backs = call(
        functools.partial(back_kernel, half), [shape((queries, 2 * depth), BF16)] * half,
        [side_arr] + pieces + [proj_weight, mirror], "backward",
        flops=4 * half * queries * depth * proj_width, smem=1,
    )
    own_back = backs[0]
    backs = [backs[0]] + [half_shift(backs[k], -k) for k in range(1, half)]
    near_sets = [(near, 0)] + [(near_far[dg - 1], dg) for dg in range(1, n_g)]
    other_sets = [(others, 0)] + [(plane_shift(others, 0, dh, 0), dh) for dh in range(1, n_h)]
    spread, order = [], []
    for dc in range(n_c):
        for array, dg in near_sets:
            if dc and dg == 0:
                spread.append(near_cores[dc - 1])
            else:
                spread.append(array if dc == 0 else plane_shift(array, 0, 0, dc))
            order += [(side, k, dg, dh, dc) for dh in range(n_h) for k in range(half)]
        for array, dh in other_sets:
            spread.append(array if dc == 0 else plane_shift(array, 0, 0, dc))
            order += [(1 - side, k, dg, dh, dc) for dg in range(n_g) for k in range(half)]
    ranks = []
    for from_side, k, dg, dh, dc in order:
        from_g, from_i = source(dg, dh, dc)
        from_z = from_side * half + lax.rem(member - k + half, half)
        ranks.append((from_z * n_g + from_g) * n_i + from_i)
    block_columns = call(
        functools.partial(columns_kernel, len(spread)), [shape((depth, cols), BF16)],
        [ints(*ranks), all_columns] + spread, "grad_columns",
        flops=2 * n_all * queries * depth * cols, scratch=[pltpu.VMEM((n_all * queries, cols), BF16)], smem=1,
        after=[own_back],
    )[0]
    on_chips = [block_columns if dg == dh == 0 else plane_shift(block_columns, dg, dh, 0) for dg, dh in chips]
    slopes = slope_rows(z_arr, normed, curve, loss, backs, seq, n_z, n_all, block_columns)
    slopes = lax.all_to_all(slopes, EVERY, 0, 0, tiled=True)
    finished = [pack(on_chips, "pack_columns", slopes)]
    finished += [plane_shift(finished[0], 0, 0, dc) for dc in range(1, n_c)]
    lines = proj_width // LANES
    sums, loss_total = call(
        functools.partial(query_kernel, share),
        [shape((n_all, lines // 8 * 8 + 8, LANES), F32), shape((1, LANES), F32)],
        [ints(place), slopes, proj_weight], "slope_sum", smem=1,
    )
    sums = lax.all_to_all(sums, EVERY, 0, 0, tiled=True)
    grad_proj, grad_query = call(
        functools.partial(finish_kernel, len(finished)),
        [shape((depth, proj_width), F32), shape((lines, LANES), F32)],
        [z_arr, ints(*share_places), sums, pool_query.reshape(1, -1)] + finished, "finish", smem=2,
    )
    mean_loss = loss_total[0, 0] / (queries * n_all)
    return (grad_proj, grad_query.reshape(proj_width), mean_loss)


def solution(mesh):
    return jax.shard_map(
        body,
        mesh=mesh,
        in_specs=(
            P(("grp", "fsdp", "item"), None, None),
            P(("grp", "fsdp", "item"), None),
            P(("grp", "fsdp", "item"), None),
            P(("grp", "fsdp", "item")),
            P(),
            P("fsdp", None),
            P(),
            P("item", None),
        ),
        out_specs=(P("fsdp", None), P(), P()),
        check_vma=False,
    )
```

profile of v0, /device:TPU:0, one launch (start us, length us, event | category | flops | bytes accessed | tf_op | source)
XLA Modules:
  0.0 176.2 jit_solution(10695539445045355208)
XLA Ops:
  0.6 2.1 %multiply_reduce_fusion = f32[1024]{0:T(1024)S(1)} fusion(bf16[1024,1024]{1,0:T(8,128)(2,1)} %weight_ref.1, f32[1024]{0:T(1024)} %param.14), kind=kLoop, calls=%fused_computation | loop fusion | flops 3144704 | bytes 2105344 | tf_op jit(solution)/shard_map/reduce_sum | solution.py:484
  2.7 5.1 %collective-permute-start.2 = (f32[1,1024]{1,0:T(1,128)S(1)}, f32[1,1024]{1,0:T(1,128)S(1)}, u32[]{:S(2)}, u32[]{:S(2)}) collective-permute-start(f32[1,1024]{1,0:T(1,128)S(1)} %bitcast.55), channel_id=1, source_target_pairs={{0,12},{4,0},{8,4},{12,8},{1,13},{5,1},{9,5},{13,9},{2,14},{6,2},{... | collective-permute-start | bytes 12296 | tf_op jit(solution)/shard_map/ppermute | solution.py:55
  7.8 1.0 collective-permute-start
  8.8 1.0 constant_dynamic-slice_fusion
  9.8 2.0 %collective-permute-start.3 = (bf16[128,1024]{1,0:T(8,128)(2,1)S(1)}, bf16[128,1024]{1,0:T(8,128)(2,1)S(1)}, u32[]{:S(2)}, u32[]{:S(2)}) collective-permute-start(bf16[128,1024]{1,0:T(8,128)(2,1)S(1)} %constant_dynamic-slice_fusion), channel_id=1, source_target_pairs={{0,8},{4,12},{8,0},{12,4},{1,9},{5,13},{9,1},{13,5},{2,10},{6,14},... | collective-permute-start | bytes 786440 | tf_op jit(solution)/shard_map/ppermute | solution.py:469
  11.8 0.7 reshape.34
  12.5 0.8 collective-permute-done
  13.4 3.4 %copy-done.4 = bf16[64,16,4096]{2,1,0:T(8,128)(2,1)S(1)} copy-done((bf16[64,16,4096]{2,1,0:T(8,128)(2,1)S(1)}, bf16[64,16,4096]{2,1,0:T(8,128)(2,1)}, u32[]{:S(2)}) %copy-start.4) | copy-done | bytes 8388632
  16.7 3.4 %norm_rows.1.refs_1_.normed_ref = bf16[1024,4096]{1,0:T(8,128)(2,1)S(1)} custom-call(f32[1,4096]{1,0:T(1,128)S(1)} %constant_dynamic-update-slice_fusion.event_ref.u_ref, bf16[1024,4096]{1,0:T(8,128)(2,1)S(1)} %bitcast.51, f32[1,4096]{1,0:T(1,128)S(1)} %bitcast.52), custom_call_target="tpu_custom_call" | custom-call | flops 25165824 | bytes 16777216 | tf_op jit(solution)/shard_map/norm_rows/pallas_call | solution.py:92
  20.2 3.4 %collective-permute-done.3.refs_0_ = bf16[128,1024]{1,0:T(8,128)(2,1)S(1)} collective-permute-done((bf16[128,1024]{1,0:T(8,128)(2,1)S(1)}, bf16[128,1024]{1,0:T(8,128)(2,1)S(1)}, u32[]{:S(2)}, u32[]{:S(2)}) %collective-permute-start.3) | collective-permute-done | bytes 262176 | tf_op jit(solution)/shard_map/ppermute | solution.py:469
  23.7 2.5 %collective-permute-start.7 = (bf16[128,1024]{1,0:T(8,128)(2,1)S(1)}, bf16[128,1024]{1,0:T(8,128)(2,1)S(1)}, u32[]{:S(2)}, u32[]{:S(2)}) collective-permute-start(bf16[128,1024]{1,0:T(8,128)(2,1)S(1)} %far_share.1.event_ref.refs_0_), channel_id=1, source_target_pairs={{0,18},{1,19},{2,16},{3,17},{16,2},{17,3},{18,0},{19,1},{4,22},{5,... | collective-permute-start | bytes 786440 | tf_op jit(solution)/shard_map/ppermute | solution.py:462
  27.7 3.4 %copy-done.1 = bf16[1024,4096]{1,0:T(8,128)(2,1)S(1)} copy-done((bf16[1024,4096]{1,0:T(8,128)(2,1)S(1)}, bf16[1024,4096]{1,0:T(8,128)(2,1)}, u32[]{:S(2)}) %copy-start.1) | copy-done | bytes 8388632
  31.1 5.2 %gate_rows.1 = (bf16[64,2048]{1,0:T(8,128)(2,1)S(1)}, bf16[64,2048]{1,0:T(8,128)(2,1)}, f32[1024,1]{1,0:T(8,128)S(1)}, f32[1024,1]{1,0:T(8,128)S(1)}, s32[64,32]{1,0:T(8,128)S(1)}) custom-call(s32[1]{0:T(128)} %bitcast.z_ref.refs_0_, bf16[1024,4096]{1,0:T(8,128)(2,1)S(1)} %copy-done.1, f32[1,4096]{1,0:T(1,128)S(1)} %constant_dynamic-update-slice_fusion.event_ref.u_ref, ...), custom_call_target="tpu_custom_call" | custom-call | flops 16777216 | bytes 8388608 | tf_op jit(solution)/shard_map/gate_rows/pallas_call | solution.py:156
  36.3 0.8 copy-done.11
  37.1 0.7 copy-done.16
  37.8 0.7 copy-done.18
  38.5 0.7 copy-done.20
  39.2 0.7 copy-done.22
  39.9 0.9 copy-done.19
  40.9 0.9 copy-done.21
  41.8 0.9 copy-done.23
  43.5 1.3 collective-permute-start.11
  45.4 1.0 collective-permute-done.11.refs_3_
  46.4 2.6 %collective-permute-done.10.refs_2_ = s32[64,32]{1,0:T(8,128)S(1)} collective-permute-done((s32[64,32]{1,0:T(8,128)S(1)}, s32[64,32]{1,0:T(8,128)S(1)}, u32[]{:S(2)}, u32[]{:S(2)}) %collective-permute-start.10) | collective-permute-done | bytes 8224 | tf_op jit(solution)/shard_map/ppermute | solution.py:55
  49.0 1.6 copy-done.5
  50.6 4.9 %list_counts.1 = (f32[256,1024]{1,0:T(8,128)S(1)}, f32[1,1024]{1,0:T(1,128)S(1)}) custom-call(s32[1]{0:T(128)} %bitcast.14.base_ref, bf16[1024,1024]{1,0:T(8,128)(2,1)S(1)} %copy-done.5, s32[64,32]{1,0:T(8,128)S(1)} %get-tuple-element.37.refs_0_, s32[64,32]{1,0:T(8,128)S(1)} %collective-permute-done.9.refs_1_, s32[64,32]{1,0:T(8,128)S(1)} %collective-permute-done.10.refs_2_, ...), custom_call_target="tpu_custom_call" | custom-call | bytes 3182596 | tf_op jit(solution)/shard_map/list_counts/pallas_call | solution.py:39
  55.6 0.9 copy-done.17
  56.5 2.1 %forward.1 = (f32[64,1024]{1,0:T(8,128)S(1)}, bf16[64,1024]{1,0:T(8,128)(2,1)S(1)}, bf16[1024,1024]{1,0:T(8,128)(2,1)S(1)}, bf16[128,1024]{1,0:T(8,128)(2,1)S(1)}, bf16[128,1024]{1,0:T(8,128)(2,1)S(1)}) custom-call(s32[1]{0:T(128)} %bitcast.13.refs_0_.side_ref, s32[8]{0:T(128)S(1)} %stack.156.refs_1_, bf16[64,2048]{1,0:T(8,128)(2,1)S(1)} %copy-done.17, ...), custom_call_target="tpu_custom_call" | custom-call | flops 536870912 | bytes 7733284 | tf_op jit(solution)/shard_map/forward/pallas_call | solution.py:39
  58.6 1.2 collective-permute-start.13
  59.9 3.1 %collective-permute-start.17 = (bf16[128,1024]{1,0:T(8,128)(2,1)S(1)}, bf16[128,1024]{1,0:T(8,128)(2,1)S(1)}, u32[]{:S(2)}, u32[]{:S(2)}) collective-permute-start(bf16[128,1024]{1,0:T(8,128)(2,1)S(1)} %get-tuple-element.44), channel_id=1, source_target_pairs={{0,8},{4,12},{8,0},{12,4},{1,9},{5,13},{9,1},{13,5},{2,10},{6,14},... | collective-permute-start | bytes 786440 | tf_op jit(solution)/shard_map/ppermute | solution.py:469
  63.3 6.8 %collective-permute-done.12.refs_1_ = bf16[64,1024]{1,0:T(8,128)(2,1)S(1)} collective-permute-done((bf16[64,1024]{1,0:T(8,128)(2,1)S(1)}, bf16[64,1024]{1,0:T(8,128)(2,1)S(1)}, u32[]{:S(2)}, u32[]{:S(2)}) %collective-permute-start.12) | collective-permute-done | bytes 131104 | tf_op jit(solution)/shard_map/ppermute | solution.py:466
  70.3 1.6 collective-permute-start.22
  71.9 0.8 collective-permute-start.16
  72.7 0.9 collective-permute-done.17.refs_7_.refs_8_
  73.6 1.5 collective-permute-start.21
  75.1 1.0 collective-permute-start.15
  76.8 4.3 %collective-permute-done.15.refs_2_ = bf16[64,1024]{1,0:T(8,128)(2,1)S(1)} collective-permute-done((bf16[64,1024]{1,0:T(8,128)(2,1)S(1)}, bf16[64,1024]{1,0:T(8,128)(2,1)S(1)}, u32[]{:S(2)}, u32[]{:S(2)}) %collective-permute-start.15) | collective-permute-done | bytes 131104 | tf_op jit(solution)/shard_map/ppermute | solution.py:55
  81.5 1.4 contrast.1
  83.0 1.1 collective-permute-start.19
  84.1 6.2 %collective-permute-done.21.refs_9_ = bf16[128,1024]{1,0:T(8,128)(2,1)S(1)} collective-permute-done((bf16[128,1024]{1,0:T(8,128)(2,1)S(1)}, bf16[128,1024]{1,0:T(8,128)(2,1)S(1)}, u32[]{:S(2)}, u32[]{:S(2)}) %collective-permute-start.21) | collective-permute-done | bytes 262176 | tf_op jit(solution)/shard_map/ppermute | solution.py:462
  90.3 4.6 %collective-permute-done.20.refs_3_ = bf16[64,1152]{1,0:T(8,128)(2,1)S(1)} collective-permute-done((bf16[64,1152]{1,0:T(8,128)(2,1)S(1)}, bf16[64,1152]{1,0:T(8,128)(2,1)S(1)}, u32[]{:S(2)}, u32[]{:S(2)}) %collective-permute-start.20) | collective-permute-done | bytes 147488 | tf_op jit(solution)/shard_map/ppermute | solution.py:55
  94.9 1.2 grad_pooled.1
  96.1 0.8 copy-done.9
  96.9 0.8 copy-done.13
  97.7 1.0 collective-permute-start.26
  98.7 4.2 %all-to-all-start = ((bf16[32,64,128]{2,1,0:T(8,128)(2,1)}), bf16[32,64,128]{2,1,0:T(8,128)(2,1)S(1)}, u32[]{:S(2)}, u32[]{:S(2)}) async-start(bf16[32,64,128]{2,1,0:T(8,128)(2,1)} %copy-done.13), calls=%async_computation | async-start | bytes 1048576 | tf_op jit(solution)/shard_map/all_to_all | solution.py:557
  103.5 11.3 %collective-permute-done.26.refs_5_ = bf16[256,1024]{1,0:T(8,128)(2,1)} collective-permute-done((bf16[256,1024]{1,0:T(8,128)(2,1)}, bf16[256,1024]{1,0:T(8,128)(2,1)}, u32[]{:S(2)}, u32[]{:S(2)}) %collective-permute-start.26) | collective-permute-done | bytes 524320 | tf_op jit(solution)/shard_map/ppermute | solution.py:462
  114.8 2.7 %collective-permute-start.24 = (bf16[64,1024]{1,0:T(8,128)(2,1)S(1)}, bf16[64,1024]{1,0:T(8,128)(2,1)S(1)}, u32[]{:S(2)}, u32[]{:S(2)}) collective-permute-start(bf16[64,1024]{1,0:T(8,128)(2,1)S(1)} %get-tuple-element.53.refs_0_), channel_id=1, source_target_pairs={{0,4},{4,0},{8,12},{12,8},{1,5},{5,1},{9,13},{13,9},{2,6},{6,2},{1... | collective-permute-start | bytes 393224 | tf_op jit(solution)/shard_map/ppermute | solution.py:466
  117.6 4.2 %collective-permute-done.24.refs_1_ = bf16[64,1024]{1,0:T(8,128)(2,1)S(1)} collective-permute-done((bf16[64,1024]{1,0:T(8,128)(2,1)S(1)}, bf16[64,1024]{1,0:T(8,128)(2,1)S(1)}, u32[]{:S(2)}, u32[]{:S(2)}) %collective-permute-start.24) | collective-permute-done | bytes 131104 | tf_op jit(solution)/shard_map/ppermute | solution.py:466
  121.7 1.6 copy-done.8
  123.3 2.2 %backward.1 = (bf16[64,2048]{1,0:T(8,128)(2,1)S(1)}, bf16[64,2048]{1,0:T(8,128)(2,1)}) custom-call(s32[1]{0:T(128)} %bitcast.13.refs_0_.side_ref, bf16[64,1024]{1,0:T(8,128)(2,1)S(1)} %get-tuple-element.53.refs_0_, bf16[64,1024]{1,0:T(8,128)(2,1)S(1)} %collective-permute-done.24.refs_1_, bf16[1024,1024]{1,0:T(8,128)(2,1)S(1)} %copy-done.3, ...), custom_call_target="tpu_custom_call" | custom-call | flops 536870912 | bytes 4980740 | tf_op jit(solution)/shard_map/backward/pallas_call | solution.py:39
  125.5 1.7 collective-permute-start.25
  127.4 1.0 copy-done.10
  128.5 1.0 copy-done.15
  129.5 2.6 %grad_columns.1.rest_2_.refs_0_ = bf16[1024,128]{1,0:T(8,128)(2,1)S(1)} custom-call(s32[32]{0:T(128)S(1)} %stack.192.refs_0_, bf16[32,64,128]{2,1,0:T(8,128)(2,1)S(1)} %all-to-all-done.refs_1_, bf16[256,1024]{1,0:T(8,128)(2,1)S(1)} %copy-done.15, bf16[256,1024]{1,0:T(8,128)(2,1)S(1)} %copy-done.10, bf16[256,1024]{1,0:T(8,128)(2,1)} %get-tuple-element.58.refs_4_, ...), custom_call_target="tpu_custom_call" | custom-call | flops 536870912 | bytes 4980864 | tf_op jit(solution)/shard_map/grad_columns/pallas_call | solution.py:39
  132.1 2.3 %collective-permute-start.32 = (bf16[1024,128]{1,0:T(8,128)(2,1)S(1)}, bf16[1024,128]{1,0:T(8,128)(2,1)S(1)}, u32[]{:S(2)}, u32[]{:S(2)}) collective-permute-start(bf16[1024,128]{1,0:T(8,128)(2,1)S(1)} %grad_columns.1.rest_2_.refs_0_), channel_id=1, source_target_pairs={{0,18},{1,19},{2,16},{3,17},{16,2},{17,3},{18,0},{19,1},{4,22},{5,... | collective-permute-start | bytes 786440 | tf_op jit(solution)/shard_map/ppermute | solution.py:462
  134.6 1.0 collective-permute-start.30
  135.7 3.4 %copy-done.2 = bf16[1024,4096]{1,0:T(8,128)(2,1)S(1)} copy-done((bf16[1024,4096]{1,0:T(8,128)(2,1)S(1)}, bf16[1024,4096]{1,0:T(8,128)(2,1)}, u32[]{:S(2)}) %copy-start.2) | copy-done | bytes 8388632
  139.1 6.2 %slope_rows.1 = f32[32,8,128]{2,1,0:T(8,128)S(1)} custom-call(s32[1]{0:T(128)} %bitcast.z_ref.refs_0_, bf16[1024,4096]{1,0:T(8,128)(2,1)S(1)} %copy-done.2, f32[1024,1]{1,0:T(8,128)S(1)} %copy-done.12, f32[1,128]{1,0:T(1,128)S(1)} %get-tuple-element.52.loss_ref, bf16[64,2048]{1,0:T(8,128)(2,1)S(1)} %get-tuple-element.55.refs_10_.rest_0_, ...), custom_call_target="tpu_custom_call" | custom-call | flops 16777216 | bytes 8388608 | tf_op jit(solution)/shard_map/slope_rows/pallas_call | solution.py:362
  145.3 11.2 %all_to_all.15.parts_ref.refs_4_ = f32[32,8,128]{2,1,0:T(8,128)S(1)} all-to-all(f32[32,8,128]{2,1,0:T(8,128)S(1)} %slope_rows.1), channel_id=1, replica_groups=mesh['grp'=2,'fsdp'=4,'item'=4] {'fsdp','grp','item'}, dimensions={0} | all-to-all | bytes 262144 | tf_op jit(solution)/shard_map/all_to_all | solution.py:592
  156.9 0.9 slope_sum.1
  157.8 2.6 %all-to-all-start.2 = ((f32[32,16,128]{2,1,0:T(8,128)}), f32[32,16,128]{2,1,0:T(8,128)S(1)}, u32[]{:S(2)}, u32[]{:S(2)}) async-start(f32[32,16,128]{2,1,0:T(8,128)} %get-tuple-element.59), calls=%async_computation.2 | async-start | bytes 524288 | tf_op jit(solution)/shard_map/all_to_all | solution.py:601
  160.4 10.6 %all-to-all-done.2.refs_2_ = f32[32,16,128]{2,1,0:T(8,128)S(1)} async-done(((f32[32,16,128]{2,1,0:T(8,128)}), f32[32,16,128]{2,1,0:T(8,128)S(1)}, u32[]{:S(2)}, u32[]{:S(2)}) %all-to-all-start.2) | async-done | bytes 262176 | tf_op jit(solution)/shard_map/all_to_all | solution.py:601
  171.0 4.1 %finish.1 = (f32[1024,1024]{1,0:T(8,128)}, f32[8,128]{1,0:T(8,128)}) custom-call(s32[1]{0:T(128)} %bitcast.z_ref.refs_0_, s32[8]{0:T(128)S(1)} %stack.156.refs_1_, f32[32,16,128]{2,1,0:T(8,128)S(1)} %all-to-all-done.2.refs_2_, f32[1,1024]{1,0:T(1,128)S(1)} %bitcast.53, bf16[4096,128]{1,0:T(8,128)(2,1)S(1)} %pack_columns.1.refs_4_, ...), custom_call_target="tpu_custom_call" | custom-call | bytes 6561828 | tf_op jit(solution)/shard_map/finish/pallas_call | solution.py:39
  (93 shorter events, 5.7 us)
Async XLA Ops:
  2.7 10.6 %collective-permute-start.2 = (f32[1,1024]{1,0:T(1,128)S(1)}, f32[1,1024]{1,0:T(1,128)S(1)}, u32[]{:S(2)}, u32[]{:S(2)}) collective-permute-start(f32[1,1024]{1,0:T(1,128)S(1)} %bitcast.55), channel_id=1, source_target_pairs={{0,12},{4,0},{8,4},{12,8},{1,13},{5,1},{9,5},{13,9},{2,14},{6,2},{... | collective-permute-start | bytes 12296 | tf_op jit(solution)/shard_map/ppermute | solution.py:55
  7.8 5.5 %collective-permute-start.1 = (f32[1,1024]{1,0:T(1,128)S(1)}, f32[1,1024]{1,0:T(1,128)S(1)}, u32[]{:S(2)}, u32[]{:S(2)}) collective-permute-start(f32[1,1024]{1,0:T(1,128)S(1)} %bitcast.56), channel_id=1, source_target_pairs={{0,8},{4,12},{8,0},{12,4},{1,9},{5,13},{9,1},{13,5},{2,10},{6,14},... | collective-permute-start | bytes 12296 | tf_op jit(solution)/shard_map/ppermute | solution.py:55
  7.8 5.5 %collective-permute-start = (f32[1,1024]{1,0:T(1,128)S(1)}, f32[1,1024]{1,0:T(1,128)S(1)}, u32[]{:S(2)}, u32[]{:S(2)}) collective-permute-start(f32[1,1024]{1,0:T(1,128)S(1)} %bitcast.57), channel_id=1, source_target_pairs={{0,4},{4,8},{8,12},{12,0},{1,5},{5,9},{9,13},{13,1},{2,6},{6,10},{... | collective-permute-start | bytes 12296 | tf_op jit(solution)/shard_map/ppermute | solution.py:55
  9.8 13.8 %collective-permute-start.3 = (bf16[128,1024]{1,0:T(8,128)(2,1)S(1)}, bf16[128,1024]{1,0:T(8,128)(2,1)S(1)}, u32[]{:S(2)}, u32[]{:S(2)}) collective-permute-start(bf16[128,1024]{1,0:T(8,128)(2,1)S(1)} %constant_dynamic-slice_fusion), channel_id=1, source_target_pairs={{0,8},{4,12},{8,0},{12,4},{1,9},{5,13},{9,1},{13,5},{2,10},{6,14},... | collective-permute-start | bytes 786440 | tf_op jit(solution)/shard_map/ppermute | solution.py:469
  13.4 3.4 %copy-start.4 = (bf16[64,16,4096]{2,1,0:T(8,128)(2,1)S(1)}, bf16[64,16,4096]{2,1,0:T(8,128)(2,1)}, u32[]{:S(2)}) copy-start(bf16[64,16,4096]{2,1,0:T(8,128)(2,1)} %param.8) | copy-start | bytes 25165828
  20.2 3.5 %copy-start = (bf16[1024,4096]{1,0:T(8,128)(2,1)}, bf16[1024,4096]{1,0:T(8,128)(2,1)S(1)}, u32[]{:S(2)}) copy-start(bf16[1024,4096]{1,0:T(8,128)(2,1)S(1)} %norm_rows.1.refs_1_.normed_ref) | copy-start | bytes 25165828
  20.2 7.0 %copy-start.26 = (s32[64,32]{0,1:T(8,128)S(1)}, s32[64,32]{0,1:T(8,128)}, u32[]{:S(2)}) copy-start(s32[64,32]{0,1:T(8,128)} %param.10) | copy-start | bytes 24580
  20.2 7.1 %copy-start.27 = (s32[64]{0:T(128)S(1)}, s32[64]{0:T(128)}, u32[]{:S(2)}) copy-start(s32[64]{0:T(128)} %param.11) | copy-start | bytes 772
  23.7 14.2 %collective-permute-start.7 = (bf16[128,1024]{1,0:T(8,128)(2,1)S(1)}, bf16[128,1024]{1,0:T(8,128)(2,1)S(1)}, u32[]{:S(2)}, u32[]{:S(2)}) collective-permute-start(bf16[128,1024]{1,0:T(8,128)(2,1)S(1)} %far_share.1.event_ref.refs_0_), channel_id=1, source_target_pairs={{0,18},{1,19},{2,16},{3,17},{16,2},{17,3},{18,0},{19,1},{4,22},{5,... | collective-permute-start | bytes 786440 | tf_op jit(solution)/shard_map/ppermute | solution.py:462
  26.2 12.4 %collective-permute-start.6 = (bf16[128,1024]{1,0:T(8,128)(2,1)S(1)}, bf16[128,1024]{1,0:T(8,128)(2,1)S(1)}, u32[]{:S(2)}, u32[]{:S(2)}) collective-permute-start(bf16[128,1024]{1,0:T(8,128)(2,1)S(1)} %far_share.1.event_ref.refs_0_), channel_id=1, source_target_pairs={{0,16},{1,17},{2,18},{3,19},{16,0},{17,1},{18,2},{19,3},{4,20},{5,... | collective-permute-start | bytes 786440 | tf_op jit(solution)/shard_map/ppermute | solution.py:462
  26.7 12.5 %collective-permute-start.5 = (bf16[128,1024]{1,0:T(8,128)(2,1)S(1)}, bf16[128,1024]{1,0:T(8,128)(2,1)S(1)}, u32[]{:S(2)}, u32[]{:S(2)}) collective-permute-start(bf16[128,1024]{1,0:T(8,128)(2,1)S(1)} %far_share.1.event_ref.refs_0_), channel_id=1, source_target_pairs={{0,2},{1,3},{2,0},{3,1},{16,18},{17,19},{18,16},{19,17},{4,6},{5,7... | collective-permute-start | bytes 786440 | tf_op jit(solution)/shard_map/ppermute | solution.py:462
  27.7 3.4 %copy-start.1 = (bf16[1024,4096]{1,0:T(8,128)(2,1)S(1)}, bf16[1024,4096]{1,0:T(8,128)(2,1)}, u32[]{:S(2)}) copy-start(bf16[1024,4096]{1,0:T(8,128)(2,1)} %copy-done) | copy-start | bytes 25165828
  36.3 0.8 copy-start.11
  37.1 0.7 copy-start.16
  37.8 17.7 %copy-start.3 = (bf16[1024,1024]{1,0:T(8,128)(2,1)S(1)}, bf16[1024,1024]{1,0:T(8,128)(2,1)}, u32[]{:S(2)}) copy-start(bf16[1024,1024]{1,0:T(8,128)(2,1)} %weight_ref.1) | copy-start | bytes 6291460
  37.8 0.7 copy-start.18
  38.5 0.7 copy-start.20
  39.2 0.7 copy-start.22
  39.9 0.9 copy-start.19
  40.9 0.9 copy-start.21
  41.8 0.9 copy-start.23
  42.9 12.7 %collective-permute-start.8 = (bf16[512,1024]{1,0:T(8,128)(2,1)S(1)}, bf16[512,1024]{1,0:T(8,128)(2,1)}, u32[]{:S(2)}, u32[]{:S(2)}) collective-permute-start(bf16[512,1024]{1,0:T(8,128)(2,1)S(1)} %pack_shares.1.refs_5_), channel_id=1, source_target_pairs={{0,1},{1,0},{2,3},{3,2},{16,17},{17,16},{18,19},{19,18},{4,5},{5,4... | collective-permute-start | bytes 3145736 | tf_op jit(solution)/shard_map/ppermute | solution.py:462
  42.9 12.6 %collective-permute-start.4 = (bf16[64,2048]{1,0:T(8,128)(2,1)}, bf16[64,2048]{1,0:T(8,128)(2,1)S(1)}, u32[]{:S(2)}, u32[]{:S(2)}) collective-permute-start(bf16[64,2048]{1,0:T(8,128)(2,1)} %get-tuple-element.35), channel_id=1, source_target_pairs={{0,4},{4,0},{8,12},{12,8},{1,5},{5,1},{9,13},{13,9},{2,6},{6,2},{1... | collective-permute-start | bytes 786440 | tf_op jit(solution)/shard_map/ppermute | solution.py:466
  43.5 2.9 %collective-permute-start.11 = (s32[64,32]{1,0:T(8,128)S(1)}, s32[64,32]{1,0:T(8,128)S(1)}, u32[]{:S(2)}, u32[]{:S(2)}) collective-permute-start(s32[64,32]{1,0:T(8,128)S(1)} %get-tuple-element.37.refs_0_), channel_id=1, source_target_pairs={{0,3},{1,0},{2,1},{3,2},{4,7},{5,4},{6,5},{7,6},{8,11},{9,8},{10,9... | collective-permute-start | bytes 24584 | tf_op jit(solution)/shard_map/ppermute | solution.py:55
  44.8 4.2 %collective-permute-start.10 = (s32[64,32]{1,0:T(8,128)S(1)}, s32[64,32]{1,0:T(8,128)S(1)}, u32[]{:S(2)}, u32[]{:S(2)}) collective-permute-start(s32[64,32]{1,0:T(8,128)S(1)} %get-tuple-element.37.refs_0_), channel_id=1, source_target_pairs={{0,2},{1,3},{2,0},{3,1},{4,6},{5,7},{6,4},{7,5},{8,10},{9,11},{10,... | collective-permute-start | bytes 24584 | tf_op jit(solution)/shard_map/ppermute | solution.py:55
  45.3 3.7 %collective-permute-start.9 = (s32[64,32]{1,0:T(8,128)S(1)}, s32[64,32]{1,0:T(8,128)S(1)}, u32[]{:S(2)}, u32[]{:S(2)}) collective-permute-start(s32[64,32]{1,0:T(8,128)S(1)} %get-tuple-element.37.refs_0_), channel_id=1, source_target_pairs={{0,1},{1,2},{2,3},{3,0},{4,5},{5,6},{6,7},{7,4},{8,9},{9,10},{10,1... | collective-permute-start | bytes 24584 | tf_op jit(solution)/shard_map/ppermute | solution.py:55
  49.0 1.6 copy-start.5
  50.6 30.9 %copy-start.6 = (bf16[1024,1024]{1,0:T(8,128)(2,1)S(1)}, bf16[1024,1024]{1,0:T(8,128)(2,1)}, u32[]{:S(2)}) copy-start(bf16[1024,1024]{1,0:T(8,128)(2,1)} %refs_4_.4) | copy-start | bytes 6291460
  55.5 1.0 copy-start.17
  56.5 38.4 %copy-start.24 = (bf16[64,1024]{1,0:T(8,128)(2,1)S(1)}, bf16[64,1024]{1,0:T(8,128)(2,1)}, u32[]{:S(2)}) copy-start(bf16[64,1024]{1,0:T(8,128)(2,1)} %refs_4_.5) | copy-start | bytes 393220
  58.6 24.3 %copy-start.7 = (bf16[1024,1024]{1,0:T(8,128)(2,1)}, bf16[1024,1024]{1,0:T(8,128)(2,1)S(1)}, u32[]{:S(2)}) copy-start(bf16[1024,1024]{1,0:T(8,128)(2,1)S(1)} %get-tuple-element.54.refs_3_) | copy-start | bytes 6291460
  58.6 11.5 %collective-permute-start.13 = (bf16[128,1024]{1,0:T(8,128)(2,1)S(1)}, bf16[128,1024]{1,0:T(8,128)(2,1)S(1)}, u32[]{:S(2)}, u32[]{:S(2)}) collective-permute-start(bf16[128,1024]{1,0:T(8,128)(2,1)S(1)} %get-tuple-element.41.refs_2_), channel_id=1, source_target_pairs={{0,2},{1,3},{2,0},{3,1},{16,18},{17,19},{18,16},{19,17},{4,6},{5,7... | collective-permute-start | bytes 786440 | tf_op jit(solution)/shard_map/ppermute | solution.py:462
  59.9 13.7 %collective-permute-start.17 = (bf16[128,1024]{1,0:T(8,128)(2,1)S(1)}, bf16[128,1024]{1,0:T(8,128)(2,1)S(1)}, u32[]{:S(2)}, u32[]{:S(2)}) collective-permute-start(bf16[128,1024]{1,0:T(8,128)(2,1)S(1)} %get-tuple-element.44), channel_id=1, source_target_pairs={{0,8},{4,12},{8,0},{12,4},{1,9},{5,13},{9,1},{13,5},{2,10},{6,14},... | collective-permute-start | bytes 786440 | tf_op jit(solution)/shard_map/ppermute | solution.py:469
  63.0 7.1 %collective-permute-start.12 = (bf16[64,1024]{1,0:T(8,128)(2,1)S(1)}, bf16[64,1024]{1,0:T(8,128)(2,1)S(1)}, u32[]{:S(2)}, u32[]{:S(2)}) collective-permute-start(bf16[64,1024]{1,0:T(8,128)(2,1)S(1)} %get-tuple-element.40), channel_id=1, source_target_pairs={{0,4},{4,0},{8,12},{12,8},{1,5},{5,1},{9,13},{13,9},{2,6},{6,2},{1... | collective-permute-start | bytes 393224 | tf_op jit(solution)/shard_map/ppermute | solution.py:466
  70.2 25.8 %copy-start.14 = (bf16[256,1024]{1,0:T(8,128)(2,1)}, bf16[256,1024]{1,0:T(8,128)(2,1)S(1)}, u32[]{:S(2)}) copy-start(bf16[256,1024]{1,0:T(8,128)(2,1)S(1)} %get-tuple-element.51.refs_2_) | copy-start | bytes 1572868
  70.3 24.6 %collective-permute-start.23 = (bf16[256,1024]{1,0:T(8,128)(2,1)S(1)}, bf16[256,1024]{1,0:T(8,128)(2,1)S(1)}, u32[]{:S(2)}, u32[]{:S(2)}) collective-permute-start(bf16[256,1024]{1,0:T(8,128)(2,1)S(1)} %get-tuple-element.51.refs_2_), channel_id=1, source_target_pairs={{0,1},{1,0},{2,3},{3,2},{16,17},{17,16},{18,19},{19,18},{4,5},{5,4... | collective-permute-start | bytes 1572872 | tf_op jit(solution)/shard_map/ppermute | solution.py:462
  70.3 24.5 %collective-permute-start.22 = (bf16[256,1024]{1,0:T(8,128)(2,1)S(1)}, bf16[256,1024]{1,0:T(8,128)(2,1)S(1)}, u32[]{:S(2)}, u32[]{:S(2)}) collective-permute-start(bf16[256,1024]{1,0:T(8,128)(2,1)S(1)} %get-tuple-element.51.refs_2_), channel_id=1, source_target_pairs={{0,16},{1,17},{2,18},{3,19},{16,0},{17,1},{18,2},{19,3},{4,20},{5,... | collective-permute-start | bytes 1572872 | tf_op jit(solution)/shard_map/ppermute | solution.py:462
  71.9 4.2 %collective-permute-start.16 = (bf16[64,1024]{1,0:T(8,128)(2,1)S(1)}, bf16[64,1024]{1,0:T(8,128)(2,1)S(1)}, u32[]{:S(2)}, u32[]{:S(2)}) collective-permute-start(bf16[64,1024]{1,0:T(8,128)(2,1)S(1)} %get-tuple-element.42.refs_0_.refs_7_), channel_id=1, source_target_pairs={{0,3},{1,0},{2,1},{3,2},{4,7},{5,4},{6,5},{7,6},{8,11},{9,8},{10,9... | collective-permute-start | bytes 393224 | tf_op jit(solution)/shard_map/ppermute | solution.py:55
  73.6 16.7 %collective-permute-start.21 = (bf16[128,1024]{1,0:T(8,128)(2,1)S(1)}, bf16[128,1024]{1,0:T(8,128)(2,1)S(1)}, u32[]{:S(2)}, u32[]{:S(2)}) collective-permute-start(bf16[128,1024]{1,0:T(8,128)(2,1)S(1)} %collective-permute-done.17.refs_7_.refs_8_), channel_id=1, source_target_pairs={{0,16},{1,17},{2,18},{3,19},{16,0},{17,1},{18,2},{19,3},{4,20},{5,... | collective-permute-start | bytes 786440 | tf_op jit(solution)/shard_map/ppermute | solution.py:462
  75.1 6.0 %collective-permute-start.15 = (bf16[64,1024]{1,0:T(8,128)(2,1)S(1)}, bf16[64,1024]{1,0:T(8,128)(2,1)S(1)}, u32[]{:S(2)}, u32[]{:S(2)}) collective-permute-start(bf16[64,1024]{1,0:T(8,128)(2,1)S(1)} %get-tuple-element.42.refs_0_.refs_7_), channel_id=1, source_target_pairs={{0,2},{1,3},{2,0},{3,1},{4,6},{5,7},{6,4},{7,5},{8,10},{9,11},{10,... | collective-permute-start | bytes 393224 | tf_op jit(solution)/shard_map/ppermute | solution.py:55
  76.1 5.3 %collective-permute-start.14 = (bf16[64,1024]{1,0:T(8,128)(2,1)S(1)}, bf16[64,1024]{1,0:T(8,128)(2,1)S(1)}, u32[]{:S(2)}, u32[]{:S(2)}) collective-permute-start(bf16[64,1024]{1,0:T(8,128)(2,1)S(1)} %get-tuple-element.42.refs_0_.refs_7_), channel_id=1, source_target_pairs={{0,1},{1,2},{2,3},{3,0},{4,5},{5,6},{6,7},{7,4},{8,9},{9,10},{10,1... | collective-permute-start | bytes 393224 | tf_op jit(solution)/shard_map/ppermute | solution.py:55
  82.9 7.4 %collective-permute-start.18 = (bf16[64,1152]{1,0:T(8,128)(2,1)S(1)}, bf16[64,1152]{1,0:T(8,128)(2,1)S(1)}, u32[]{:S(2)}, u32[]{:S(2)}) collective-permute-start(bf16[64,1152]{1,0:T(8,128)(2,1)S(1)} %get-tuple-element.46), channel_id=1, source_target_pairs={{0,3},{1,0},{2,1},{3,2},{4,7},{5,4},{6,5},{7,6},{8,11},{9,8},{10,9... | collective-permute-start | bytes 442376 | tf_op jit(solution)/shard_map/ppermute | solution.py:55
  83.0 7.3 %collective-permute-start.19 = (bf16[64,1152]{1,0:T(8,128)(2,1)S(1)}, bf16[64,1152]{1,0:T(8,128)(2,1)S(1)}, u32[]{:S(2)}, u32[]{:S(2)}) collective-permute-start(bf16[64,1152]{1,0:T(8,128)(2,1)S(1)} %get-tuple-element.47), channel_id=1, source_target_pairs={{0,2},{1,3},{2,0},{3,1},{4,6},{5,7},{6,4},{7,5},{8,10},{9,11},{10,... | collective-permute-start | bytes 442376 | tf_op jit(solution)/shard_map/ppermute | solution.py:55
  90.3 4.6 %collective-permute-start.20 = (bf16[64,1152]{1,0:T(8,128)(2,1)S(1)}, bf16[64,1152]{1,0:T(8,128)(2,1)S(1)}, u32[]{:S(2)}, u32[]{:S(2)}) collective-permute-start(bf16[64,1152]{1,0:T(8,128)(2,1)S(1)} %get-tuple-element.48), channel_id=1, source_target_pairs={{0,1},{1,2},{2,3},{3,0},{4,5},{5,6},{6,7},{7,4},{8,9},{9,10},{10,1... | collective-permute-start | bytes 442376 | tf_op jit(solution)/shard_map/ppermute | solution.py:55
  96.1 0.8 copy-start.9
  96.9 0.8 copy-start.13
  97.7 17.1 %collective-permute-start.26 = (bf16[256,1024]{1,0:T(8,128)(2,1)}, bf16[256,1024]{1,0:T(8,128)(2,1)}, u32[]{:S(2)}, u32[]{:S(2)}) collective-permute-start(bf16[256,1024]{1,0:T(8,128)(2,1)} %get-tuple-element.58.refs_4_), channel_id=1, source_target_pairs={{0,2},{1,3},{2,0},{3,1},{16,18},{17,19},{18,16},{19,17},{4,6},{5,7... | collective-permute-start | bytes 1572872 | tf_op jit(solution)/shard_map/ppermute | solution.py:462
  98.7 28.7 %all-to-all-start = ((bf16[32,64,128]{2,1,0:T(8,128)(2,1)}), bf16[32,64,128]{2,1,0:T(8,128)(2,1)S(1)}, u32[]{:S(2)}, u32[]{:S(2)}) async-start(bf16[32,64,128]{2,1,0:T(8,128)(2,1)} %copy-done.13), calls=%async_computation | async-start | bytes 1048576 | tf_op jit(solution)/shard_map/all_to_all | solution.py:557
  102.9 24.4 %collective-permute-start.28 = (bf16[256,1024]{1,0:T(8,128)(2,1)}, bf16[256,1024]{1,0:T(8,128)(2,1)}, u32[]{:S(2)}, u32[]{:S(2)}) collective-permute-start(bf16[256,1024]{1,0:T(8,128)(2,1)} %get-tuple-element.58.refs_4_), channel_id=1, source_target_pairs={{0,1},{1,0},{2,3},{3,2},{16,17},{17,16},{18,19},{19,18},{4,5},{5,4... | collective-permute-start | bytes 1572872 | tf_op jit(solution)/shard_map/ppermute | solution.py:462
  103.2 24.1 %collective-permute-start.27 = (bf16[256,1024]{1,0:T(8,128)(2,1)}, bf16[256,1024]{1,0:T(8,128)(2,1)}, u32[]{:S(2)}, u32[]{:S(2)}) collective-permute-start(bf16[256,1024]{1,0:T(8,128)(2,1)} %copy-done.9), channel_id=1, source_target_pairs={{0,1},{1,0},{2,3},{3,2},{16,17},{17,16},{18,19},{19,18},{4,5},{5,4... | collective-permute-start | bytes 1572872 | tf_op jit(solution)/shard_map/ppermute | solution.py:462
  114.8 12.6 %collective-permute-start.29 = (bf16[256,1024]{1,0:T(8,128)(2,1)}, bf16[256,1024]{1,0:T(8,128)(2,1)}, u32[]{:S(2)}, u32[]{:S(2)}) collective-permute-start(bf16[256,1024]{1,0:T(8,128)(2,1)} %collective-permute-done.26.refs_5_), channel_id=1, source_target_pairs={{0,1},{1,0},{2,3},{3,2},{16,17},{17,16},{18,19},{19,18},{4,5},{5,4... | collective-permute-start | bytes 1572872 | tf_op jit(solution)/shard_map/ppermute | solution.py:462
  114.8 6.9 %collective-permute-start.24 = (bf16[64,1024]{1,0:T(8,128)(2,1)S(1)}, bf16[64,1024]{1,0:T(8,128)(2,1)S(1)}, u32[]{:S(2)}, u32[]{:S(2)}) collective-permute-start(bf16[64,1024]{1,0:T(8,128)(2,1)S(1)} %get-tuple-element.53.refs_0_), channel_id=1, source_target_pairs={{0,4},{4,0},{8,12},{12,8},{1,5},{5,1},{9,13},{13,9},{2,6},{6,2},{1... | collective-permute-start | bytes 393224 | tf_op jit(solution)/shard_map/ppermute | solution.py:466
  121.7 1.6 copy-start.8
  125.5 10.1 %collective-permute-start.25 = (bf16[64,2048]{1,0:T(8,128)(2,1)}, bf16[64,2048]{1,0:T(8,128)(2,1)}, u32[]{:S(2)}, u32[]{:S(2)}) collective-permute-start(bf16[64,2048]{1,0:T(8,128)(2,1)} %get-tuple-element.56), channel_id=1, source_target_pairs={{0,4},{4,0},{8,12},{12,8},{1,5},{5,1},{9,13},{13,9},{2,6},{6,2},{1... | collective-permute-start | bytes 786440 | tf_op jit(solution)/shard_map/ppermute | solution.py:466
  127.4 1.0 copy-start.10
  128.5 1.0 copy-start.15
  129.5 6.2 %copy-start.12 = (f32[1024,1]{1,0:T(8,128)S(1)}, f32[1024,1]{1,0:T(8,128)}, u32[]{:S(2)}) copy-start(f32[1024,1]{1,0:T(8,128)} %copy-done.11) | copy-start | bytes 12292
  132.1 24.4 %collective-permute-start.32 = (bf16[1024,128]{1,0:T(8,128)(2,1)S(1)}, bf16[1024,128]{1,0:T(8,128)(2,1)S(1)}, u32[]{:S(2)}, u32[]{:S(2)}) collective-permute-start(bf16[1024,128]{1,0:T(8,128)(2,1)S(1)} %grad_columns.1.rest_2_.refs_0_), channel_id=1, source_target_pairs={{0,18},{1,19},{2,16},{3,17},{16,2},{17,3},{18,0},{19,1},{4,22},{5,... | collective-permute-start | bytes 786440 | tf_op jit(solution)/shard_map/ppermute | solution.py:462
  134.4 22.1 %collective-permute-start.31 = (bf16[1024,128]{1,0:T(8,128)(2,1)S(1)}, bf16[1024,128]{1,0:T(8,128)(2,1)S(1)}, u32[]{:S(2)}, u32[]{:S(2)}) collective-permute-start(bf16[1024,128]{1,0:T(8,128)(2,1)S(1)} %grad_columns.1.rest_2_.refs_0_), channel_id=1, source_target_pairs={{0,16},{1,17},{2,18},{3,19},{16,0},{17,1},{18,2},{19,3},{4,20},{5,... | collective-permute-start | bytes 786440 | tf_op jit(solution)/shard_map/ppermute | solution.py:462
  134.6 21.9 %collective-permute-start.30 = (bf16[1024,128]{1,0:T(8,128)(2,1)S(1)}, bf16[1024,128]{1,0:T(8,128)(2,1)S(1)}, u32[]{:S(2)}, u32[]{:S(2)}) collective-permute-start(bf16[1024,128]{1,0:T(8,128)(2,1)S(1)} %grad_columns.1.rest_2_.refs_0_), channel_id=1, source_target_pairs={{0,2},{1,3},{2,0},{3,1},{16,18},{17,19},{18,16},{19,17},{4,6},{5,7... | collective-permute-start | bytes 786440 | tf_op jit(solution)/shard_map/ppermute | solution.py:462
  135.7 3.4 %copy-start.2 = (bf16[1024,4096]{1,0:T(8,128)(2,1)S(1)}, bf16[1024,4096]{1,0:T(8,128)(2,1)}, u32[]{:S(2)}) copy-start(bf16[1024,4096]{1,0:T(8,128)(2,1)} %copy-done) | copy-start | bytes 25165828
  145.3 25.7 %copy-start.25 = (f32[1024]{0:T(1024)S(1)}, f32[1024]{0:T(1024)}, u32[]{:S(2)}) copy-start(f32[1024]{0:T(1024)} %param.14) | copy-start | bytes 12292
  156.6 14.4 %collective-permute-start.33 = (bf16[4096,128]{1,0:T(8,128)(2,1)S(1)}, bf16[4096,128]{1,0:T(8,128)(2,1)}, u32[]{:S(2)}, u32[]{:S(2)}) collective-permute-start(bf16[4096,128]{1,0:T(8,128)(2,1)S(1)} %pack_columns.1.refs_4_), channel_id=1, source_target_pairs={{0,1},{1,0},{2,3},{3,2},{16,17},{17,16},{18,19},{19,18},{4,5},{5,4... | collective-permute-start | bytes 3145736 | tf_op jit(solution)/shard_map/ppermute | solution.py:462
  157.8 13.2 %all-to-all-start.2 = ((f32[32,16,128]{2,1,0:T(8,128)}), f32[32,16,128]{2,1,0:T(8,128)S(1)}, u32[]{:S(2)}, u32[]{:S(2)}) async-start(f32[32,16,128]{2,1,0:T(8,128)} %get-tuple-element.59), calls=%async_computation.2 | async-start | bytes 524288 | tf_op jit(solution)/shard_map/all_to_all | solution.py:601
where the time goes:
time: 177 us; the launch traced here: 176 us
  waiting for transfers between devices  57.1 us (32%)
  starting transfers between devices  42.1 us (24%)
  Pallas kernels  34.6 us (20%)
  local copies, waits for them, and re-layouts  26.1 us (15%)
  blocking collectives  11.2 us (6%)
  other arithmetic  2.77 us (2%)
  between operations  2.17 us (1%)
    unnamed x57, local copies, waits for them, and re-layouts  24.6 us
    pallas_call x12, Pallas kernels, call(): pl.pallas_call(run, out_shape=outs, in_specs=[SMEM] * smem + [VMEM] * (le...  19.8 us
    ppermute x16, waiting for transfers between devices, plane_shift(): return lax.ppermute(values, PLANE, pairs)  17.6 us
    ppermute x12, waiting for transfers between devices, shift(): return lax.ppermute(values, axis, [(i, (i + k) % n) for i in range(n)])  13.7 us
    ppermute x16, starting transfers between devices, plane_shift(): return lax.ppermute(values, PLANE, pairs)  13.4 us
    ppermute x12, starting transfers between devices, shift(): return lax.ppermute(values, axis, [(i, (i + k) % n) for i in range(n)])  11.5 us
    all_to_all x1, blocking collectives, body(): slopes = lax.all_to_all(slopes, EVERY, 0, 0, tiled=True)  11.2 us
    ppermute x4, waiting for transfers between devices, half_shift(): return lax.ppermute(values, 'fsdp', pairs)  11 us
  transfers between devices with their start and end apart: 36, of which 13 were waited for; matrix products, arithmetic and copies ran while one was open for 1% of the time, Pallas kernels for 15%

commit v1 on v0

--- a/solution.py
+++ b/solution.py
@@ -26,24 +26,35 @@
     return jax.ShapeDtypeStruct(dims, dtype)
 
 
-def call(kernel, outs, ins, name, flops=0, scratch=(), smem=0, after=()):
-    run = kernel
-    if after:
-        count = len(ins)
-
-        def run(*refs):
-            kernel(*refs[:count], *refs[count + len(after) :])
-
+def call(kernel, outs, ins, name, flops=0, scratch=(), smem=0, kept=0, after=()):
+    count, first = len(ins), smem + kept
+    copied = ins[first:]
     moved = sum(math.prod(a.shape) * a.dtype.itemsize for a in list(ins) + list(outs))
     held = sum(math.prod(s.shape) * jnp.dtype(s.dtype).itemsize for s in scratch)
+
+    def run(*refs):
+        rest = refs[count + len(after) :]
+        results, buffers = rest[: len(outs)], rest[len(outs) : len(outs) + len(copied)]
+        own, sems = rest[len(outs) + len(copied) : -1], rest[-1]
+        copies = [
+            pltpu.make_async_copy(src, dst, sems.at[k])
+            for k, (src, dst) in enumerate(zip(refs[first:count], buffers))
+        ]
+        for copy in copies:
+            copy.start()
+        for copy in copies:
+            copy.wait()
+        kernel(*refs[:first], *buffers, *results, *own)
+
+    anywhere = pl.BlockSpec(memory_space=pl.ANY)
     return pl.pallas_call(
         run,
         out_shape=outs,
-        in_specs=[SMEM] * smem
-        + [VMEM] * (len(ins) - smem)
-        + [pl.BlockSpec(memory_space=pl.ANY)] * len(after),
+        in_specs=[SMEM] * smem + [VMEM] * kept + [anywhere] * (len(copied) + len(after)),
         out_specs=[VMEM] * len(outs),
-        scratch_shapes=scratch,
+        scratch_shapes=[pltpu.VMEM(a.shape, a.dtype) for a in copied]
+        + list(scratch)
+        + [pltpu.SemaphoreType.DMA((max(len(copied), 1),))],
         cost_estimate=pl.CostEstimate(flops=flops, bytes_accessed=moved, transcendentals=0),
         compiler_params=pltpu.CompilerParams(vmem_limit_bytes=2 * (moved + held) + 6 * MIB),
         name=name,
@@ -98,14 +109,16 @@
         cost_estimate=pl.CostEstimate(
             flops=6 * tokens * width, bytes_accessed=4 * tokens * width, transcendentals=0
         ),
-        compiler_params=pltpu.CompilerParams(vmem_limit_bytes=10 * MIB),
+        compiler_params=pltpu.CompilerParams(vmem_limit_bytes=60 * MIB),
         name="norm_rows",
     )(event, states, gain)
 
 
 def gate_kernel(seq, root, blocks, z_ref, normed_ref, u_ref, len_ref, lists_ref, event_ref, *rest):
     half = blocks // 2
-    outs, gated_ref, curve_ref, copy_ref, rows_ref = rest[:half], *rest[half:]
+    outs, gated_ref, curve_ref, copies, rows_ref = (
+        rest[:half], rest[half], rest[half + 1], rest[half + 2 : -1], rest[-1]
+    )
     step = pl.program_id(0)
     tokens, width = normed_ref.shape
     count = tokens // seq
@@ -132,7 +145,15 @@
 
     @pl.when(step == pl.num_programs(0) - 1)
     def _():
-        copy_ref[...] = lists_ref[...]
+        owners = len(copies)
+        own = lists_ref.shape[1] // owners
+        for k in range(owners):
+            picked = jnp.zeros(copies[k].shape, jnp.int32)
+            for j in range(owners):
+                picked = jnp.where(
+                    lax.rem(z_ref[1] + k, owners) == j, lists_ref[:, j * own : (j + 1) * own], picked
+                )
+            copies[k][...] = picked
         depth = width // blocks
         place = lax.rem(z_ref[0], half)
         for k in range(half):
@@ -143,14 +164,14 @@
                 ].astype(BF16)
 
 
-def gate_rows(z, normed, u, token_lengths, lists, event, seq, root, blocks):
+def gate_rows(z, normed, u, token_lengths, lists, event, seq, root, blocks, owners):
     tokens, width = normed.shape
     queries = tokens // seq
     group = 16 if queries % 16 == 0 else queries
     step_tokens = group * seq
     half = blocks // 2
     outs = [shape((queries, width // half), BF16)] * half + [shape((tokens, 1), F32)] * 2
-    outs.append(shape(lists.shape, lists.dtype))
+    outs += [shape((queries, lists.shape[1] // owners), lists.dtype)] * owners
     column = pl.BlockSpec((step_tokens, 1), lambda i: (i, 0))
     whole = lambda dims: pl.BlockSpec(dims, lambda i: (0, 0))
     return pl.pallas_call(
@@ -165,12 +186,13 @@
             whole(lists.shape),
             pl.BlockSpec(memory_space=pl.ANY),
         ],
-        out_specs=[whole((queries, width // half))] * half + [column] * 2 + [whole(lists.shape)],
+        out_specs=[whole((queries, width // half))] * half + [column] * 2
+        + [whole((queries, lists.shape[1] // owners))] * owners,
         scratch_shapes=[pltpu.VMEM((queries, width), F32)],
         cost_estimate=pl.CostEstimate(
             flops=4 * tokens * width, bytes_accessed=2 * tokens * width, transcendentals=0
         ),
-        compiler_params=pltpu.CompilerParams(vmem_limit_bytes=16 * MIB),
+        compiler_params=pltpu.CompilerParams(vmem_limit_bytes=60 * MIB),
         name="gate_rows",
     )(z, normed, u, token_lengths, lists, event)
 
@@ -183,12 +205,35 @@
 
 def pack(pieces, name, event):
     rows, width = pieces[0].shape
-    out = shape((len(pieces) * rows, width), pieces[0].dtype)
-    return call(pack_kernel, [out], pieces, name, after=[event])[0]
-
-
-def forward_kernel(n, packs, side_ref, places_ref, *refs):
-    pieces, weight_ref, shares = refs[:n], refs[n], refs[n + 1 : n + 1 + packs]
+    n = len(pieces)
+
+    def run(*refs):
+        out_ref, sems = refs[-2], refs[-1]
+        copies = [
+            pltpu.make_async_copy(refs[k], out_ref.at[pl.ds(k * rows, rows), :], sems.at[k])
+            for k in range(n)
+        ]
+        for copy in copies:
+            copy.start()
+        for copy in copies:
+            copy.wait()
+
+    anywhere = pl.BlockSpec(memory_space=pl.ANY)
+    return pl.pallas_call(
+        run,
+        out_shape=shape((n * rows, width), pieces[0].dtype),
+        in_specs=[anywhere] * (n + 1),
+        out_specs=anywhere,
+        scratch_shapes=[pltpu.SemaphoreType.DMA((n,))],
+        cost_estimate=pl.CostEstimate(flops=0, bytes_accessed=4 * n * rows * width, transcendentals=0),
+        compiler_params=pltpu.CompilerParams(vmem_limit_bytes=4 * MIB),
+        name=name,
+    )(*pieces, event)
+
+
+def forward_kernel(n, packs, side_ref, places_ref, weight_ref, *refs):
+    refs = refs[:n] + (weight_ref,) + refs[n:]
+    pieces, shares = refs[:n], refs[n + 1 : n + 1 + packs]
     outs = refs[n + 1 + packs : 2 * n + 1 + packs]
     mirror_ref, held_ref, away_ref = refs[2 * n + 1 + packs :]
     rows = pieces[0].shape[0]
@@ -210,8 +255,9 @@
         outs[k][...] = product[k * rows : (k + 1) * rows].astype(outs[k].dtype)
 
 
-def back_kernel(n, side_ref, *refs):
-    pieces, weight_ref, mirror_ref, outs = refs[:n], refs[n], refs[n + 1], refs[n + 2 :]
+def back_kernel(n, packed, side_ref, weight_ref, mirror_ref, *refs):
+    pieces, outs = refs[:n], refs[n + packed : -1]
+    pack_kernel(*refs[n : n + packed], refs[-1])
     rows = pieces[0].shape[0]
     depth = weight_ref.shape[0]
     side = side_ref[0]
@@ -225,8 +271,9 @@
 
 
 def embed_kernel(root, n, *refs):
-    parts, packed = refs[:n], refs[n:-4]
-    pooled_ref, unit_ref, embedded_ref, pack_ref = refs[-4:]
+    parts, away_ref, packed = refs[:n], refs[n], refs[n + 1 : -5]
+    pooled_ref, unit_ref, embedded_ref, pack_ref, pass_ref = refs[-5:]
+    pass_ref[...] = away_ref[...]
     pooled = parts[0][...]
     for part in parts[1:]:
         pooled = pooled + part[...].astype(F32)
@@ -260,7 +307,7 @@
 
 
 def contrast_kernel(n, *refs):
-    pieces, (slab_ref, scale_ref, counts_ref), outs = refs[:n], refs[n : n + 3], refs[n + 3 :]
+    (slab_ref, scale_ref, counts_ref), pieces, outs = refs[:3], refs[3 : n + 3], refs[n + 3 :]
     queries, width = pieces[0].shape
     embedded = jnp.concatenate([p[...] for p in pieces], axis=0)
     slab = slab_ref[...]
@@ -280,11 +327,10 @@
         outs[k][:, width:] = tail.astype(outs[k].dtype)
 
 
-def grad_kernel(n, packed_count, root, *refs):
-    parts = refs[:n]
-    pos_ref, pooled_ref, unit_ref, embedded_ref = refs[n : n + 4]
-    packed = refs[n + 4 : n + 4 + packed_count]
-    grad_ref, columns_ref, loss_ref, pack_ref = refs[n + 4 + packed_count :]
+def grad_kernel(n, root, *refs):
+    pos_ref, pooled_ref, unit_ref, embedded_ref = refs[:4]
+    parts = refs[4 : n + 4]
+    grad_ref, columns_ref, loss_ref = refs[n + 4 :]
     queries, width = pos_ref.shape
     total = parts[0][:, :width]
     denom = jnp.sum(parts[0][:, width:], axis=1, keepdims=True)
@@ -313,12 +359,11 @@
     for j in range(columns_ref.shape[0]):
         at = (j % places) * cols
         columns_ref[j] = grad[:, at : at + cols]
-    pack_kernel(*packed, pack_ref)
-
-
-def slope_kernel(seq, blocks, z_ref, normed_ref, curve_ref, loss_ref, *rest):
+
+
+def slope_kernel(seq, blocks, plane, z_ref, normed_ref, curve_ref, loss_ref, *rest):
     half = blocks // 2
-    backs, out_ref, all_ref, sum_ref = rest[:half], rest[-3], rest[-2], rest[-1]
+    backs, (out_ref, all_ref, sum_ref) = rest[:half], rest[-3:]
     step = pl.program_id(0)
     tokens, width = normed_ref.shape
     count = tokens // seq
@@ -345,40 +390,48 @@
     @pl.when(step == pl.num_programs(0) - 1)
     def _():
         total = jnp.sum(sum_ref[...], axis=0, keepdims=True)
-        loss = jnp.broadcast_to(loss_ref[...], (7, LANES))
-        share = width // out_ref.shape[0]
-        for to in range(out_ref.shape[0]):
-            out_ref[to, 1:8, :] = loss
-            out_ref[to, 0:1, :share] = total[:, to * share : (to + 1) * share]
-
-
-def slope_rows(z, normed, curve, loss, backs, seq, blocks, devices, after):
+        lines = depth // LANES
+        devices, height = out_ref.shape[0], out_ref.shape[1]
+        loss = jnp.broadcast_to(loss_ref[...], (height - 2 * lines, LANES))
+        for member in range(half):
+            rows = []
+            for j in range(2):
+                for line in range(lines):
+                    at = (j * half + member) * depth + line * LANES
+                    rows.append(total[:, at : at + LANES])
+            message = jnp.concatenate(rows + [loss], axis=0)
+            for to in range(devices):
+                if to // plane % half == member:
+                    out_ref[to] = message
+
+
+def slope_rows(z, normed, curve, loss, backs, seq, blocks, devices, plane):
     tokens, width = normed.shape
     half = blocks // 2
+    height = 2 * (width // blocks // LANES) // 8 * 8 + 8
     queries = tokens // seq
     group = 8 if queries % 8 == 0 else queries
     step_tokens = group * seq
     whole = lambda dims: pl.BlockSpec(dims, lambda i: (0, 0))
     return pl.pallas_call(
-        functools.partial(slope_kernel, seq, blocks),
+        functools.partial(slope_kernel, seq, blocks, plane),
         grid=(queries // group,),
-        out_shape=shape((devices, 8, LANES), F32),
+        out_shape=shape((devices, height, LANES), F32),
         in_specs=[
             SMEM,
             pl.BlockSpec((step_tokens, width), lambda i: (i, 0)),
             pl.BlockSpec((step_tokens, 1), lambda i: (i, 0)),
             whole((1, LANES)),
         ]
-        + [whole((queries, width // half))] * half
-        + [pl.BlockSpec(memory_space=pl.ANY)],
-        out_specs=pl.BlockSpec((devices, 8, LANES), lambda i: (0, 0, 0)),
+        + [whole((queries, width // half))] * half,
+        out_specs=pl.BlockSpec((devices, height, LANES), lambda i: (0, 0, 0)),
         scratch_shapes=[pltpu.VMEM((queries, width), F32), pltpu.VMEM((8, width), F32)],
         cost_estimate=pl.CostEstimate(
             flops=4 * tokens * width, bytes_accessed=2 * tokens * width, transcendentals=0
         ),
-        compiler_params=pltpu.CompilerParams(vmem_limit_bytes=20 * MIB),
+        compiler_params=pltpu.CompilerParams(vmem_limit_bytes=60 * MIB),
         name="slope_rows",
-    )(z, normed, curve, loss, *backs, after)
+    )(z, normed, curve, loss, *backs)
 
 
 def columns_kernel(n, order_ref, grads_ref, *refs):
@@ -395,39 +448,39 @@
     out_ref[...] = total.T.astype(BF16)
 
 
-def query_kernel(share, place_ref, parts_ref, weight_ref, out_ref, loss_ref):
+def query_kernel(side_ref, weight_ref, mirror_ref, parts_ref, part_ref, slope_ref, loss_ref):
+    depth = weight_ref.shape[0]
+    lines = depth // LANES
     total = jnp.sum(parts_ref[...], axis=0)
-    loss_ref[...] = total[1:2]
-    line = total[0:1]
-    high, low = split_bf16(jnp.broadcast_to(line[:, :share], (8, share)))
-    weight = weight_ref[pl.ds(pl.multiple_of(place_ref[0] * share, share), share), :]
-    part = (
-        jnp.dot(high, weight, preferred_element_type=F32)
-        + jnp.dot(low, weight, preferred_element_type=F32)
-    )[0:1]
-    lines = part.shape[1] // LANES
-    rows = [part[:, k * LANES : (k + 1) * LANES] for k in range(lines)] + [line]
-    rows.append(jnp.zeros((out_ref.shape[1] - lines - 1, LANES), F32))
-    out_ref[...] = jnp.broadcast_to(jnp.concatenate(rows, axis=0)[None], out_ref.shape)
-
-
-def finish_kernel(n, *refs):
-    z_ref, place_ref, sums_ref, pool_ref = refs[:4]
-    pieces, out_ref, query_ref = refs[4 : 4 + n], refs[-2], refs[-1]
-    rows, cols = pieces[0].shape[0] // (place_ref.shape[0] // n), pieces[0].shape[1]
+    loss_ref[...] = total[2 * lines : 2 * lines + 1]
+    side = side_ref[0]
+    part = jnp.zeros(part_ref.shape, F32)
+    for j in range(2):
+        rows = total[j * lines : (j + 1) * lines]
+        row = jnp.concatenate([rows[k : k + 1] for k in range(lines)], axis=1)
+        high, low = split_bf16(jnp.broadcast_to(row, (8, depth)))
+
+        @pl.when(side == j)
+        def _():
+            slope_ref[...] = rows
+
+        weight = jnp.where(side == j, weight_ref[...], mirror_ref[...])
+        part = part + jnp.dot(high, weight, preferred_element_type=F32)[0:1]
+        part = part + jnp.dot(low, weight, preferred_element_type=F32)[0:1]
+    part_ref[...] = part
+
+
+def finish_kernel(n, place_ref, pool_ref, slope_ref, *refs):
+    pieces, out_ref = refs[:n], refs[-1]
     places = place_ref.shape[0]
-    share = rows // places
-    lines = query_ref.shape[0]
-    query_ref[...] = jnp.sum(sums_ref[:, :lines, :], axis=0)
-    for p in range(places):
-        line = sums_ref[z_ref[0] * places + p, lines : lines + 1, :share]
-        slope = jnp.broadcast_to(line, (LANES, share)).T
-        part = slice(p * share, (p + 1) * share)
+    rows, cols = out_ref.shape[0], pieces[0].shape[1]
+    for line in range(rows // LANES):
+        part = slice(line * LANES, (line + 1) * LANES)
+        slope = jnp.broadcast_to(slope_ref[line : line + 1, :], (LANES, LANES)).T
         for k in range(places):
-            piece = pieces[k // (places // n)]
-            base = k % (places // n) * rows
+            base = k % (places // n) * rows + line * LANES
+            mine = pieces[k // (places // n)][base : base + LANES, :].astype(F32)
             at = pl.ds(pl.multiple_of(place_ref[k] * cols, LANES), cols)
-            mine = piece[base + p * share : base + (p + 1) * share, :].astype(F32)
             out_ref[part, at] = mine + slope * pool_ref[:, at]
 
 
@@ -498,19 +551,20 @@
             share_places.append(from_g * n_i + from_i)
 
     token_lengths = jnp.broadcast_to(lengths[:, None], (queries, seq)).reshape(-1, 1)
-    *sends, gated, curve, own_lists = gate_rows(
-        z_arr, normed, u, token_lengths, negatives, far_share, seq, root, n_z
-    )
+    gate_outs = gate_rows(
+        ints(z, i), normed, u, token_lengths, negatives, far_share, seq, root, n_z, n_i
+    )
+    sends, (gated, curve), lists = gate_outs[:half], gate_outs[half : half + 2], gate_outs[half + 2 :]
 
     packs = [pack(chip_shares, "pack_shares", gated)]
     packs += [plane_shift(packs[0], 0, 0, dc) for dc in range(1, n_c)]
 
     pieces = [sends[0]] + [half_shift(sends[k], k) for k in range(1, half)]
-    lists = [own_lists] + [shift(own_lists, "item", k) for k in steps_i]
+    lists = [lists[0]] + [shift(lists[k], "item", k) for k in steps_i]
     counts, slab_scale = call(
         functools.partial(count_kernel, n_i, root),
         [shape((n_i * queries, slab.shape[0]), F32), shape((1, slab.shape[0]), F32)],
-        [ints(i * slab.shape[0]), slab] + lists, "list_counts", smem=1,
+        [ints(i * slab.shape[0]), slab] + lists, "list_counts", smem=1, kept=1,
     )
     block = shape((half * queries, depth), BF16)
     *parts, mirror, held, away = call(
@@ -518,19 +572,19 @@
         [shape((queries, proj_width), F32)]
         + [shape((queries, proj_width), BF16)] * (half - 1)
         + [shape((depth, proj_width), BF16), block, block],
-        [side_arr, ints(*share_places)] + pieces + [proj_weight] + packs, "forward",
-        flops=4 * half * queries * depth * proj_width, smem=2, after=[counts],
+        [side_arr, ints(*share_places), proj_weight] + pieces + packs, "forward",
+        flops=4 * half * queries * depth * proj_width, smem=2, kept=1, after=[counts],
     )
     parts = [parts[0]] + [half_shift(parts[k], -k) for k in range(1, half)]
     near = [held] + [plane_shift(held, 0, dh, 0) for dh in range(1, n_h)]
-    other = mirror_shift(away)
     row = shape((queries, proj_width), F32)
     row16 = shape((queries, proj_width), BF16)
-    pooled, unit, embedded, near = call(
+    pooled, unit, embedded, near, away = call(
         functools.partial(embed_kernel, root, half),
-        [row, shape((queries, 1), F32), row16, shape((n_h * half * queries, depth), BF16)],
-        parts + near, "embed",
-    )
+        [row, shape((queries, 1), F32), row16, shape((n_h * half * queries, depth), BF16), block],
+        parts + [away] + near, "embed",
+    )
+    other = mirror_shift(away)
 
     pieces = [embedded] + [shift(embedded, "item", k) for k in steps_i]
     near_far = [plane_shift(near, dg, 0, 0) for dg in range(1, n_g)]
@@ -538,40 +592,37 @@
     parts = call(
         functools.partial(contrast_kernel, n_i),
         [shape(wide, F32)] + [shape(wide, BF16)] * (n_i - 1),
-        pieces + [slab, slab_scale, counts], "contrast",
-        flops=4 * n_i * queries * slab.shape[0] * proj_width, after=[other],
+        [slab, slab_scale, counts] + pieces, "contrast",
+        flops=4 * n_i * queries * slab.shape[0] * proj_width, kept=3,
     )
     parts = [parts[0]] + [shift(parts[k], "item", -k) for k in steps_i]
     near_cores = [plane_shift(near, 0, 0, dc) for dc in range(1, n_c)]
+    near_far_cores = [[plane_shift(array, 0, 0, dc) for array in near_far] for dc in range(1, n_c)]
     others = [other] + [plane_shift(other, dg, 0, 0) for dg in range(1, n_g)]
     cols = proj_width // n_plane
-    grad, grad_columns, loss, others = call(
-        functools.partial(grad_kernel, n_i, n_g, root),
-        [
-            row16, shape((n_all, queries, cols), BF16), shape((1, LANES), F32),
-            shape((n_g * half * queries, depth), BF16),
-        ],
-        parts + [positives, pooled, unit, embedded] + others, "grad_pooled", after=near_far + near_cores,
+    grad, grad_columns, loss = call(
+        functools.partial(grad_kernel, n_i, root),
+        [row16, shape((n_all, queries, cols), BF16), shape((1, LANES), F32)],
+        [positives, pooled, unit, embedded] + parts, "grad_pooled", kept=4,
+        after=near_far + near_cores + sum(near_far_cores, []) + others,
     )
 
     all_columns = lax.all_to_all(grad_columns, EVERY, 0, 0, tiled=True)
     pieces = [grad] + [half_shift(grad, k) for k in range(1, half)]
-    backs = call(
-        functools.partial(back_kernel, half), [shape((queries, 2 * depth), BF16)] * half,
-        [side_arr] + pieces + [proj_weight, mirror], "backward",
-        flops=4 * half * queries * depth * proj_width, smem=1,
-    )
-    own_back = backs[0]
+    *backs, others = call(
+        functools.partial(back_kernel, half, n_g),
+        [shape((queries, 2 * depth), BF16)] * half + [shape((n_g * half * queries, depth), BF16)],
+        [side_arr, proj_weight, mirror] + pieces + others, "backward",
+        flops=4 * half * queries * depth * proj_width, smem=1, kept=2,
+    )
     backs = [backs[0]] + [half_shift(backs[k], -k) for k in range(1, half)]
+    slopes = slope_rows(ints(z, 0), normed, curve, loss, backs, seq, n_z, n_all, n_plane)
     near_sets = [(near, 0)] + [(near_far[dg - 1], dg) for dg in range(1, n_g)]
     other_sets = [(others, 0)] + [(plane_shift(others, 0, dh, 0), dh) for dh in range(1, n_h)]
     spread, order = [], []
     for dc in range(n_c):
         for array, dg in near_sets:
-            if dc and dg == 0:
-                spread.append(near_cores[dc - 1])
-            else:
-                spread.append(array if dc == 0 else plane_shift(array, 0, 0, dc))
+            spread.append(array if dc == 0 else ([near_cores[dc - 1]] + near_far_cores[dc - 1])[dg])
             order += [(side, k, dg, dh, dc) for dh in range(n_h) for k in range(half)]
         for array, dh in other_sets:
             spread.append(array if dc == 0 else plane_shift(array, 0, 0, dc))
@@ -585,25 +636,22 @@
         functools.partial(columns_kernel, len(spread)), [shape((depth, cols), BF16)],
         [ints(*ranks), all_columns] + spread, "grad_columns",
         flops=2 * n_all * queries * depth * cols, scratch=[pltpu.VMEM((n_all * queries, cols), BF16)], smem=1,
-        after=[own_back],
+        after=[slopes],
     )[0]
     on_chips = [block_columns if dg == dh == 0 else plane_shift(block_columns, dg, dh, 0) for dg, dh in chips]
-    slopes = slope_rows(z_arr, normed, curve, loss, backs, seq, n_z, n_all, block_columns)
-    slopes = lax.all_to_all(slopes, EVERY, 0, 0, tiled=True)
+    all_slopes = lax.all_to_all(slopes, EVERY, 0, 0, tiled=True)
+    query_part, my_slope, loss_total = call(
+        query_kernel,
+        [shape((1, proj_width), F32), shape((depth // LANES, LANES), F32), shape((1, LANES), F32)],
+        [side_arr, proj_weight, mirror, all_slopes], "slope_sum", smem=1, kept=2,
+    )
     finished = [pack(on_chips, "pack_columns", slopes)]
     finished += [plane_shift(finished[0], 0, 0, dc) for dc in range(1, n_c)]
-    lines = proj_width // LANES
-    sums, loss_total = call(
-        functools.partial(query_kernel, share),
-        [shape((n_all, lines // 8 * 8 + 8, LANES), F32), shape((1, LANES), F32)],
-        [ints(place), slopes, proj_weight], "slope_sum", smem=1,
-    )
-    sums = lax.all_to_all(sums, EVERY, 0, 0, tiled=True)
-    grad_proj, grad_query = call(
-        functools.partial(finish_kernel, len(finished)),
-        [shape((depth, proj_width), F32), shape((lines, LANES), F32)],
-        [z_arr, ints(*share_places), sums, pool_query.reshape(1, -1)] + finished, "finish", smem=2,
-    )
+    grad_query = query_part + sum(half_shift(query_part, k) for k in range(1, half))
+    grad_proj = call(
+        functools.partial(finish_kernel, len(finished)), [shape((depth, proj_width), F32)],
+        [ints(*share_places), pool_query.reshape(1, -1), my_slope] + finished, "finish", smem=1, kept=2,
+    )[0]
     mean_loss = loss_total[0, 0] / (queries * n_all)
     return (grad_proj, grad_query.reshape(proj_width), mean_loss)
 

time: 177 us -> 193 us (1.090)
  Pallas kernels: 34.6 us -> 47.3 us
  waiting for transfers between devices: 57.1 us -> 62.5 us
  local copies, waits for them, and re-layouts: 26.1 us -> 21.1 us
  starting transfers between devices: 42.1 us -> 37.3 us
  blocking collectives: 11.2 us -> 15.9 us
  other arithmetic: 2.77 us -> 5.15 us
    ppermute x16, waiting for transfers between devices: 17.6 us -> 32.4 us  [plane_shift(): return lax.ppermute(values, PLANE, pairs)]
    all_to_all x1 -> x0, waiting for transfers between devices: 10.6 us -> none  [body(): sums = lax.all_to_all(sums, EVERY, 0, 0, tiled=True)]
    ppermute x4 -> x5, waiting for transfers between devices: 11 us -> 20.9 us  [half_shift(): return lax.ppermute(values, 'fsdp', pairs)]
    pallas_call x1, Pallas kernels: 3.44 us -> 10.2 us  [norm_rows(): pl.pallas_call(norm_kernel, grid=(tokens // block,), out_shape=shape((tok...]
    ppermute x12, waiting for transfers between devices: 13.7 us -> 7.57 us  [shift(): return lax.ppermute(values, axis, [(i, (i + k) % n) for i in range(n)])]
    unnamed x57 -> x61, local copies, waits for them, and re-layouts: 24.6 us -> 18.7 us
    all_to_all x1, blocking collectives: 11.2 us -> 15.9 us  [body(): all_slopes = lax.all_to_all(slopes, EVERY, 0, 0, tiled=True)]
    pallas_call x13, Pallas kernels: 26 us -> 29 us  [the longest x9 19.3 us: call(): pl.pallas_call(run, out_shape=outs, in_specs=[SMEM] * smem + [VMEM] * kep...]
  transfers between devices with their start and end apart: 36 -> 36, of which waited for: 13 -> 19; matrix products, arithmetic and copies ran while one was open for 1% -> 3% of each run, Pallas kernels for 15% -> 17%
where the time goes in v1:
time: 193 us; the launch traced here: 191 us
  waiting for transfers between devices  62.5 us (32%)
  Pallas kernels  47.3 us (25%)
  starting transfers between devices  37.3 us (19%)
  local copies, waits for them, and re-layouts  21.1 us (11%)
  blocking collectives  15.9 us (8%)
  other arithmetic  5.15 us (3%)
  between operations  2.21 us (1%)
    ppermute x16, waiting for transfers between devices, plane_shift(): return lax.ppermute(values, PLANE, pairs)  32.4 us
    ppermute x5, waiting for transfers between devices, half_shift(): return lax.ppermute(values, 'fsdp', pairs)  20.9 us
    pallas_call x9, Pallas kernels, call(): pl.pallas_call(run, out_shape=outs, in_specs=[SMEM] * smem + [VMEM] * kep...  19.3 us
    unnamed x61, local copies, waits for them, and re-layouts  18.7 us
    all_to_all x1, blocking collectives, body(): all_slopes = lax.all_to_all(slopes, EVERY, 0, 0, tiled=True)  15.9 us
    ppermute x12, starting transfers between devices, shift(): return lax.ppermute(values, axis, [(i, (i + k) % n) for i in range(n)])  13.5 us
    ppermute x16, starting transfers between devices, plane_shift(): return lax.ppermute(values, PLANE, pairs)  13 us
    pallas_call x1, Pallas kernels, norm_rows(): pl.pallas_call(norm_kernel, grid=(tokens // block,), out_shape=shape((tok...  10.2 us
  transfers between devices with their start and end apart: 36, of which 19 were waited for; matrix products, arithmetic and copies ran while one was open for 3% of the time, Pallas kernels for 17%

profile of v1, /device:TPU:0, one launch (start us, length us, event | category | flops | bytes accessed | tf_op | source)
XLA Modules:
  0.0 191.4 jit_solution(4188974985418924794)
XLA Ops:
  0.6 2.1 %multiply_reduce_fusion = f32[1024]{0:T(1024)S(1)} fusion(bf16[1024,1024]{1,0:T(8,128)(2,1)} %refs_1_.5, f32[1024]{0:T(1024)} %param.14), kind=kLoop, calls=%fused_computation | loop fusion | flops 3144704 | bytes 2105344 | tf_op jit(solution)/shard_map/reduce_sum | solution.py:537
  2.7 5.1 %collective-permute-start.2 = (f32[1,1024]{1,0:T(1,128)S(1)}, f32[1,1024]{1,0:T(1,128)S(1)}, u32[]{:S(2)}, u32[]{:S(2)}) collective-permute-start(f32[1,1024]{1,0:T(1,128)S(1)} %bitcast.55), channel_id=1, source_target_pairs={{0,12},{4,0},{8,4},{12,8},{1,13},{5,1},{9,5},{13,9},{2,14},{6,2},{... | collective-permute-start | bytes 12296 | tf_op jit(solution)/shard_map/ppermute | solution.py:66
  7.8 1.0 collective-permute-start
  8.8 1.0 constant_dynamic-slice_fusion
  9.8 2.0 %collective-permute-start.3 = (bf16[128,1024]{1,0:T(8,128)(2,1)S(1)}, bf16[128,1024]{1,0:T(8,128)(2,1)S(1)}, u32[]{:S(2)}, u32[]{:S(2)}) collective-permute-start(bf16[128,1024]{1,0:T(8,128)(2,1)S(1)} %constant_dynamic-slice_fusion), channel_id=1, source_target_pairs={{0,8},{4,12},{8,0},{12,4},{1,9},{5,13},{9,1},{13,5},{2,10},{6,14},... | collective-permute-start | bytes 786440 | tf_op jit(solution)/shard_map/ppermute | solution.py:522
  11.8 1.3 reshape.37
  14.0 10.2 %norm_rows.1.refs_1_.normed_ref = bf16[1024,4096]{1,0:T(8,128)(2,1)} custom-call(f32[1,4096]{1,0:T(1,128)} %copy-done.27, bf16[1024,4096]{1,0:T(8,128)(2,1)} %bitcast.53, f32[1,4096]{1,0:T(1,128)} %bitcast.54), custom_call_target="tpu_custom_call" | custom-call | flops 25165824 | bytes 16777216 | tf_op jit(solution)/shard_map/norm_rows/pallas_call | solution.py:103
  24.1 3.4 %copy-done = bf16[1024,4096]{1,0:T(8,128)(2,1)S(1)} copy-done((bf16[1024,4096]{1,0:T(8,128)(2,1)S(1)}, bf16[1024,4096]{1,0:T(8,128)(2,1)}, u32[]{:S(2)}) %copy-start) | copy-done | bytes 8388632
  27.6 2.5 %collective-permute-start.7 = (bf16[128,1024]{1,0:T(8,128)(2,1)S(1)}, bf16[128,1024]{1,0:T(8,128)(2,1)S(1)}, u32[]{:S(2)}, u32[]{:S(2)}) collective-permute-start(bf16[128,1024]{1,0:T(8,128)(2,1)S(1)} %far_share.1.event_ref.refs_0_), channel_id=1, source_target_pairs={{0,18},{1,19},{2,16},{3,17},{16,2},{17,3},{18,0},{19,1},{4,22},{5,... | collective-permute-start | bytes 786440 | tf_op jit(solution)/shard_map/ppermute | solution.py:515
  31.1 0.7 copy.13.lists_ref
  31.9 1.1 reshape.39.len_ref
  33.6 8.1 %gate_rows.1 = (bf16[64,2048]{1,0:T(8,128)(2,1)}, bf16[64,2048]{1,0:T(8,128)(2,1)}, f32[1024,1]{1,0:T(8,128)}, f32[1024,1]{1,0:T(8,128)}, s32[64,8]{1,0:T(8,128)...) custom-call(s32[2]{0:T(128)} %pad_add_fusion.z_ref, bf16[1024,4096]{1,0:T(8,128)(2,1)} %norm_rows.1.refs_1_.normed_ref, ...), custom_call_target="tpu_custom_call" | custom-call | flops 16777216 | bytes 8388608 | tf_op jit(solution)/shard_map/gate_rows/pallas_call | solution.py:177
  42.4 0.7 copy-done.19
  43.1 0.7 copy-done.21
  43.8 0.9 copy-done.6
  44.8 1.0 copy-done.11
  45.8 0.9 copy-done.18
  46.8 0.9 copy-done.20
  47.7 0.9 copy-done.22
  48.9 1.4 collective-permute-start.4
  50.4 1.5 collective-permute-start.10
  51.9 1.3 collective-permute-start.11
  53.8 0.7 collective-permute-done.10.refs_4_
  55.1 1.6 copy-done.7
  56.7 0.8 copy-done.24
  57.5 2.0 %list_counts.1 = (f32[256,1024]{1,0:T(8,128)S(1)}, f32[1,1024]{1,0:T(1,128)S(1)}) custom-call(s32[1]{0:T(128)} %bitcast.15.refs_0_, bf16[1024,1024]{1,0:T(8,128)(2,1)S(1)} %copy-done.7, s32[64,8]{1,0:T(8,128)S(1)} %copy-done.24, s32[64,8]{1,0:T(8,128)S(1)} %collective-permute-done.9.refs_3_, s32[64,8]{1,0:T(8,128)S(1)} %collective-permute-done.10.refs_4_, ...), custom_call_target="tpu_custom_call" | custom-call | bytes 3158020 | tf_op jit(solution)/shard_map/list_counts/pallas_call | solution.py:50
  59.6 2.8 %forward.1 = (f32[64,1024]{1,0:T(8,128)S(1)}, bf16[64,1024]{1,0:T(8,128)(2,1)S(1)}, bf16[1024,1024]{1,0:T(8,128)(2,1)S(1)}, bf16[128,1024]{1,0:T(8,128)(2,1)S(1)}, bf16[128,1024]{1,0:T(8,128)(2,1)S(1)}) custom-call(s32[1]{0:T(128)} %bitcast.9.refs_0_, s32[8]{0:T(128)S(1)} %stack.162.refs_1_.refs_0_, bf16[1024,1024]{1,0:T(8,128)(2,1)S(1)} %copy-done.1, ...), custom_call_target="tpu_custom_call" | custom-call | flops 536870912 | bytes 7733284 | tf_op jit(solution)/shard_map/forward/pallas_call | solution.py:50
  62.4 1.0 collective-permute-start.13
  63.4 0.7 collective-permute-start.12
  64.1 5.4 %collective-permute-done.12.refs_1_ = bf16[64,1024]{1,0:T(8,128)(2,1)S(1)} collective-permute-done((bf16[64,1024]{1,0:T(8,128)(2,1)S(1)}, bf16[64,1024]{1,0:T(8,128)(2,1)S(1)}, u32[]{:S(2)}, u32[]{:S(2)}) %collective-permute-start.12) | collective-permute-done | bytes 131104 | tf_op jit(solution)/shard_map/ppermute | solution.py:519
  69.5 2.1 %collective-permute-done.13.refs_4_ = bf16[128,1024]{1,0:T(8,128)(2,1)S(1)} collective-permute-done((bf16[128,1024]{1,0:T(8,128)(2,1)S(1)}, bf16[128,1024]{1,0:T(8,128)(2,1)S(1)}, u32[]{:S(2)}, u32[]{:S(2)}) %collective-permute-start.13) | collective-permute-done | bytes 262176 | tf_op jit(solution)/shard_map/ppermute | solution.py:515
  72.1 1.6 collective-permute-start.20
  73.7 1.3 collective-permute-start.15
  75.0 2.0 %collective-permute-start.23 = (bf16[128,1024]{1,0:T(8,128)(2,1)S(1)}, bf16[128,1024]{1,0:T(8,128)(2,1)S(1)}, u32[]{:S(2)}, u32[]{:S(2)}) collective-permute-start(bf16[128,1024]{1,0:T(8,128)(2,1)S(1)} %get-tuple-element.59), channel_id=1, source_target_pairs={{0,8},{4,12},{8,0},{12,4},{1,9},{5,13},{9,1},{13,5},{2,10},{6,14},... | collective-permute-start | bytes 786440 | tf_op jit(solution)/shard_map/ppermute | solution.py:522
  77.6 1.7 collective-permute-start.21
  79.3 6.7 %collective-permute-done.20.refs_8_.refs_3_ = bf16[256,1024]{1,0:T(8,128)(2,1)S(1)} collective-permute-done((bf16[256,1024]{1,0:T(8,128)(2,1)S(1)}, bf16[256,1024]{1,0:T(8,128)(2,1)S(1)}, u32[]{:S(2)}, u32[]{:S(2)}) %collective-permute-start.20) | collective-permute-done | bytes 524320 | tf_op jit(solution)/shard_map/ppermute | solution.py:515
  86.0 2.1 %contrast.1 = (f32[64,1152]{1,0:T(8,128)S(1)}, bf16[64,1152]{1,0:T(8,128)(2,1)S(1)}, bf16[64,1152]{1,0:T(8,128)(2,1)S(1)}, bf16[64,1152]{1,0:T(8,128)(2,1)S(1)}) custom-call(bf16[1024,1024]{1,0:T(8,128)(2,1)S(1)} %copy-done.8, f32[1,1024]{1,0:T(1,128)S(1)} %get-tuple-element.53.refs_1_, f32[256,1024]{1,0:T(8,128)S(1)} %get-tuple-element.43.refs_7_.refs_2_, ...), custom_call_target="tpu_custom_call" | custom-call | flops 1073741824 | bytes 4411392 | tf_op jit(solution)/shard_map/contrast/pallas_call | solution.py:50
  88.1 0.9 collective-permute-start.17
  89.0 1.6 collective-permute-done.23.refs_11_.refs_5_
  91.9 1.4 collective-permute-start.19
  93.3 4.7 %collective-permute-done.18.refs_6_ = bf16[64,1152]{1,0:T(8,128)(2,1)S(1)} collective-permute-done((bf16[64,1152]{1,0:T(8,128)(2,1)S(1)}, bf16[64,1152]{1,0:T(8,128)(2,1)S(1)}, u32[]{:S(2)}, u32[]{:S(2)}) %collective-permute-start.18) | collective-permute-done | bytes 147488 | tf_op jit(solution)/shard_map/ppermute | solution.py:66
  98.8 1.1 grad_pooled.1
  100.0 0.8 copy-done.12
  100.9 4.9 %collective-permute-done.25.refs_4_ = bf16[64,1024]{1,0:T(8,128)(2,1)S(1)} collective-permute-done((bf16[64,1024]{1,0:T(8,128)(2,1)S(1)}, bf16[64,1024]{1,0:T(8,128)(2,1)S(1)}, u32[]{:S(2)}, u32[]{:S(2)}) %collective-permute-start.25) | collective-permute-done | bytes 131104 | tf_op jit(solution)/shard_map/ppermute | solution.py:519
  105.7 2.6 %backward.1 = (bf16[64,2048]{1,0:T(8,128)(2,1)S(1)}, bf16[64,2048]{1,0:T(8,128)(2,1)S(1)}, bf16[256,1024]{1,0:T(8,128)(2,1)}) custom-call(s32[1]{0:T(128)} %bitcast.9.refs_0_, bf16[1024,1024]{1,0:T(8,128)(2,1)S(1)} %copy-done.1, bf16[1024,1024]{1,0:T(8,128)(2,1)S(1)} %get-tuple-element.44.refs_2_, bf16[64,1024]{1,0:T(8,128)(2,1)S(1)} %get-tuple-element.61.refs_3_, ...), custom_call_target="tpu_custom_call" | custom-call | flops 536870912 | bytes 6029316 | tf_op jit(solution)/shard_map/backward/pallas_call | solution.py:50
  109.0 0.9 collective-permute-start.27
  109.9 3.5 %all-to-all-start.1 = ((bf16[32,64,128]{2,1,0:T(8,128)(2,1)}), bf16[32,64,128]{2,1,0:T(8,128)(2,1)}, u32[]{:S(2)}, u32[]{:S(2)}) async-start(bf16[32,64,128]{2,1,0:T(8,128)(2,1)} %copy-done.12), calls=%async_computation.1 | async-start | bytes 1048576 | tf_op jit(solution)/shard_map/all_to_all | solution.py:610
  113.5 12.0 %collective-permute-done.27.refs_5_ = bf16[256,1024]{1,0:T(8,128)(2,1)} collective-permute-done((bf16[256,1024]{1,0:T(8,128)(2,1)}, bf16[256,1024]{1,0:T(8,128)(2,1)}, u32[]{:S(2)}, u32[]{:S(2)}) %collective-permute-start.27) | collective-permute-done | bytes 524320 | tf_op jit(solution)/shard_map/ppermute | solution.py:515
  126.3 8.1 %collective-permute-done.26.rest_1_ = bf16[64,2048]{1,0:T(8,128)(2,1)} collective-permute-done((bf16[64,2048]{1,0:T(8,128)(2,1)S(1)}, bf16[64,2048]{1,0:T(8,128)(2,1)}, u32[]{:S(2)}, u32[]{:S(2)}) %collective-permute-start.26) | collective-permute-done | bytes 262176 | tf_op jit(solution)/shard_map/ppermute | solution.py:519
  134.4 9.5 %slope_rows.1.refs_10_.refs_4_ = f32[32,24,128]{2,1,0:T(8,128)} custom-call(s32[2]{0:T(128)} %pad_add_fusion.1.z_ref, bf16[1024,4096]{1,0:T(8,128)(2,1)} %norm_rows.1.refs_1_.normed_ref, f32[1024,1]{1,0:T(8,128)} %get-tuple-element.45.curve_ref, f32[1,128]{1,0:T(1,128)} %copy-done.26, bf16[64,2048]{1,0:T(8,128)(2,1)} %copy-done.16, ...), custom_call_target="tpu_custom_call" | custom-call | flops 16777216 | bytes 8388608 | tf_op jit(solution)/shard_map/slope_rows/pallas_call | solution.py:416
  143.9 1.1 copy-done.4
  145.0 1.0 copy-done.10
  146.0 1.0 copy-done.14
  147.1 3.2 %grad_columns.1.refs_0_ = bf16[1024,128]{1,0:T(8,128)(2,1)S(1)} custom-call(s32[32]{0:T(128)S(1)} %stack.201.refs_0_, bf16[32,64,128]{2,1,0:T(8,128)(2,1)} %all-to-all-done.1.refs_1_, bf16[256,1024]{1,0:T(8,128)(2,1)S(1)} %copy-done.14, bf16[256,1024]{1,0:T(8,128)(2,1)S(1)} %collective-permute-done.20.refs_8_.refs_3_, ...), custom_call_target="tpu_custom_call" | custom-call | flops 536870912 | bytes 4980864 | tf_op jit(solution)/shard_map/grad_columns/pallas_call | solution.py:50
  150.3 1.6 collective-permute-start.32
  151.9 1.1 collective-permute-start.31
  153.0 0.8 collective-permute-start.30
  153.8 6.7 %collective-permute-done.32.refs_3_ = bf16[1024,128]{1,0:T(8,128)(2,1)S(1)} collective-permute-done((bf16[1024,128]{1,0:T(8,128)(2,1)S(1)}, bf16[1024,128]{1,0:T(8,128)(2,1)S(1)}, u32[]{:S(2)}, u32[]{:S(2)}) %collective-permute-start.32) | collective-permute-done | bytes 262176 | tf_op jit(solution)/shard_map/ppermute | solution.py:515
  160.5 4.1 %collective-permute-done.31.refs_2_ = bf16[1024,128]{1,0:T(8,128)(2,1)S(1)} collective-permute-done((bf16[1024,128]{1,0:T(8,128)(2,1)S(1)}, bf16[1024,128]{1,0:T(8,128)(2,1)S(1)}, u32[]{:S(2)}, u32[]{:S(2)}) %collective-permute-start.31) | collective-permute-done | bytes 262176 | tf_op jit(solution)/shard_map/ppermute | solution.py:515
  165.0 15.9 %all_to_all.10.refs_3_ = f32[32,24,128]{2,1,0:T(8,128)S(1)} all-to-all(f32[32,24,128]{2,1,0:T(8,128)S(1)} %copy-done.4), channel_id=1, replica_groups=mesh['grp'=2,'fsdp'=4,'item'=4] {'fsdp','grp','item'}, dimensions={0} | all-to-all | bytes 786432 | tf_op jit(solution)/shard_map/all_to_all | solution.py:642
  180.9 1.5 slope_sum.1
  182.5 1.1 collective-permute-start.34
  183.6 2.6 %collective-permute-done.34 = f32[1,1024]{1,0:T(1,128)S(1)} collective-permute-done((f32[1,1024]{1,0:T(1,128)S(1)}, f32[1,1024]{1,0:T(1,128)S(1)}, u32[]{:S(2)}, u32[]{:S(2)}) %collective-permute-start.34) | collective-permute-done | bytes 4128 | tf_op jit(solution)/shard_map/ppermute | solution.py:519
  186.7 3.6 %finish.1 = f32[1024,1024]{1,0:T(8,128)} custom-call(s32[8]{0:T(128)S(1)} %stack.162.refs_1_.refs_0_, f32[1,1024]{1,0:T(1,128)S(1)} %bitcast.51, f32[8,128]{1,0:T(8,128)S(1)} %get-tuple-element.64.refs_2_, bf16[4096,128]{1,0:T(8,128)(2,1)S(1)} %pack_columns.1.refs_3_, bf16[4096,128]{1,0:T(8,128)(2,1)S(1)} %collective-permute-done.33.refs_4_), custom_call_target="tpu_custom_call" | custom-call | bytes 6299680 | tf_op jit(solution)/shard_map/finish/pallas_call | solution.py:50
  (100 shorter events, 10.8 us)
Async XLA Ops:
  2.7 10.6 %collective-permute-start.2 = (f32[1,1024]{1,0:T(1,128)S(1)}, f32[1,1024]{1,0:T(1,128)S(1)}, u32[]{:S(2)}, u32[]{:S(2)}) collective-permute-start(f32[1,1024]{1,0:T(1,128)S(1)} %bitcast.55), channel_id=1, source_target_pairs={{0,12},{4,0},{8,4},{12,8},{1,13},{5,1},{9,5},{13,9},{2,14},{6,2},{... | collective-permute-start | bytes 12296 | tf_op jit(solution)/shard_map/ppermute | solution.py:66
  7.8 5.5 %collective-permute-start.1 = (f32[1,1024]{1,0:T(1,128)S(1)}, f32[1,1024]{1,0:T(1,128)S(1)}, u32[]{:S(2)}, u32[]{:S(2)}) collective-permute-start(f32[1,1024]{1,0:T(1,128)S(1)} %bitcast.56), channel_id=1, source_target_pairs={{0,8},{4,12},{8,0},{12,4},{1,9},{5,13},{9,1},{13,5},{2,10},{6,14},... | collective-permute-start | bytes 12296 | tf_op jit(solution)/shard_map/ppermute | solution.py:66
  7.8 5.5 %collective-permute-start = (f32[1,1024]{1,0:T(1,128)S(1)}, f32[1,1024]{1,0:T(1,128)S(1)}, u32[]{:S(2)}, u32[]{:S(2)}) collective-permute-start(f32[1,1024]{1,0:T(1,128)S(1)} %bitcast.57), channel_id=1, source_target_pairs={{0,4},{4,8},{8,12},{12,0},{1,5},{5,9},{9,13},{13,1},{2,6},{6,10},{... | collective-permute-start | bytes 12296 | tf_op jit(solution)/shard_map/ppermute | solution.py:66
  9.8 14.3 %collective-permute-start.3 = (bf16[128,1024]{1,0:T(8,128)(2,1)S(1)}, bf16[128,1024]{1,0:T(8,128)(2,1)S(1)}, u32[]{:S(2)}, u32[]{:S(2)}) collective-permute-start(bf16[128,1024]{1,0:T(8,128)(2,1)S(1)} %constant_dynamic-slice_fusion), channel_id=1, source_target_pairs={{0,8},{4,12},{8,0},{12,4},{1,9},{5,13},{9,1},{13,5},{2,10},{6,14},... | collective-permute-start | bytes 786440 | tf_op jit(solution)/shard_map/ppermute | solution.py:522
  24.1 3.4 %copy-start = (bf16[1024,4096]{1,0:T(8,128)(2,1)S(1)}, bf16[1024,4096]{1,0:T(8,128)(2,1)}, u32[]{:S(2)}) copy-start(bf16[1024,4096]{1,0:T(8,128)(2,1)} %norm_rows.1.refs_1_.normed_ref) | copy-start | bytes 25165828
  27.5 3.6 %copy-start.28 = (s32[64,32]{0,1:T(8,128)S(1)}, s32[64,32]{0,1:T(8,128)}, u32[]{:S(2)}) copy-start(s32[64,32]{0,1:T(8,128)} %param.10) | copy-start | bytes 24580
  27.5 4.3 %copy-start.29 = (s32[64]{0:T(128)S(1)}, s32[64]{0:T(128)}, u32[]{:S(2)}) copy-start(s32[64]{0:T(128)} %param.11) | copy-start | bytes 772
  27.6 6.0 %copy-start.5 = (bf16[128,1024]{1,0:T(8,128)(2,1)}, bf16[128,1024]{1,0:T(8,128)(2,1)S(1)}, u32[]{:S(2)}) copy-start(bf16[128,1024]{1,0:T(8,128)(2,1)S(1)} %far_share.1.event_ref.refs_0_) | copy-start | bytes 786436
  27.6 14.1 %collective-permute-start.7 = (bf16[128,1024]{1,0:T(8,128)(2,1)S(1)}, bf16[128,1024]{1,0:T(8,128)(2,1)S(1)}, u32[]{:S(2)}, u32[]{:S(2)}) collective-permute-start(bf16[128,1024]{1,0:T(8,128)(2,1)S(1)} %far_share.1.event_ref.refs_0_), channel_id=1, source_target_pairs={{0,18},{1,19},{2,16},{3,17},{16,2},{17,3},{18,0},{19,1},{4,22},{5,... | collective-permute-start | bytes 786440 | tf_op jit(solution)/shard_map/ppermute | solution.py:515
  30.1 12.3 %collective-permute-start.6 = (bf16[128,1024]{1,0:T(8,128)(2,1)S(1)}, bf16[128,1024]{1,0:T(8,128)(2,1)S(1)}, u32[]{:S(2)}, u32[]{:S(2)}) collective-permute-start(bf16[128,1024]{1,0:T(8,128)(2,1)S(1)} %far_share.1.event_ref.refs_0_), channel_id=1, source_target_pairs={{0,16},{1,17},{2,18},{3,19},{16,0},{17,1},{18,2},{19,3},{4,20},{5,... | collective-permute-start | bytes 786440 | tf_op jit(solution)/shard_map/ppermute | solution.py:515
  30.6 12.5 %collective-permute-start.5 = (bf16[128,1024]{1,0:T(8,128)(2,1)S(1)}, bf16[128,1024]{1,0:T(8,128)(2,1)S(1)}, u32[]{:S(2)}, u32[]{:S(2)}) collective-permute-start(bf16[128,1024]{1,0:T(8,128)(2,1)S(1)} %far_share.1.event_ref.refs_0_), channel_id=1, source_target_pairs={{0,2},{1,3},{2,0},{3,1},{16,18},{17,19},{18,16},{19,17},{4,6},{5,7... | collective-permute-start | bytes 786440 | tf_op jit(solution)/shard_map/ppermute | solution.py:515
  41.7 17.9 %copy-start.1 = (bf16[1024,1024]{1,0:T(8,128)(2,1)S(1)}, bf16[1024,1024]{1,0:T(8,128)(2,1)}, u32[]{:S(2)}) copy-start(bf16[1024,1024]{1,0:T(8,128)(2,1)} %refs_1_.5) | copy-start | bytes 6291460
  41.7 0.7 copy-start.17
  42.4 0.7 copy-start.19
  43.8 0.9 copy-start.6
  44.8 1.0 copy-start.11
  45.8 0.9 copy-start.18
  46.8 0.9 copy-start.20
  47.7 0.9 copy-start.22
  48.7 10.9 %copy-start.15 = (bf16[64,2048]{1,0:T(8,128)(2,1)S(1)}, bf16[64,2048]{1,0:T(8,128)(2,1)}, u32[]{:S(2)}) copy-start(bf16[64,2048]{1,0:T(8,128)(2,1)} %get-tuple-element.36.refs_3_) | copy-start | bytes 786436
  48.8 10.7 %collective-permute-start.8 = (bf16[512,1024]{1,0:T(8,128)(2,1)S(1)}, bf16[512,1024]{1,0:T(8,128)(2,1)}, u32[]{:S(2)}, u32[]{:S(2)}) collective-permute-start(bf16[512,1024]{1,0:T(8,128)(2,1)S(1)} %pack_shares.1.refs_5_), channel_id=1, source_target_pairs={{0,1},{1,0},{2,3},{3,2},{16,17},{17,16},{18,19},{19,18},{4,5},{5,4... | collective-permute-start | bytes 3145736 | tf_op jit(solution)/shard_map/ppermute | solution.py:515
  48.9 10.6 %collective-permute-start.4 = (bf16[64,2048]{1,0:T(8,128)(2,1)}, bf16[64,2048]{1,0:T(8,128)(2,1)}, u32[]{:S(2)}, u32[]{:S(2)}) collective-permute-start(bf16[64,2048]{1,0:T(8,128)(2,1)} %get-tuple-element.37), channel_id=1, source_target_pairs={{0,4},{4,0},{8,12},{12,8},{1,5},{5,1},{9,13},{13,9},{2,6},{6,2},{1... | collective-permute-start | bytes 786440 | tf_op jit(solution)/shard_map/ppermute | solution.py:519
  50.2 3.6 %collective-permute-start.9 = (s32[64,8]{1,0:T(8,128)}, s32[64,8]{1,0:T(8,128)S(1)}, u32[]{:S(2)}, u32[]{:S(2)}) collective-permute-start(s32[64,8]{1,0:T(8,128)} %get-tuple-element.40), channel_id=1, source_target_pairs={{0,1},{1,2},{2,3},{3,0},{4,5},{5,6},{6,7},{7,4},{8,9},{9,10},{10,1... | collective-permute-start | bytes 6152 | tf_op jit(solution)/shard_map/ppermute | solution.py:66
  50.4 4.1 %collective-permute-start.10 = (s32[64,8]{1,0:T(8,128)}, s32[64,8]{1,0:T(8,128)S(1)}, u32[]{:S(2)}, u32[]{:S(2)}) collective-permute-start(s32[64,8]{1,0:T(8,128)} %get-tuple-element.41), channel_id=1, source_target_pairs={{0,2},{1,3},{2,0},{3,1},{4,6},{5,7},{6,4},{7,5},{8,10},{9,11},{10,... | collective-permute-start | bytes 6152 | tf_op jit(solution)/shard_map/ppermute | solution.py:66
  51.9 3.2 %collective-permute-start.11 = (s32[64,8]{1,0:T(8,128)}, s32[64,8]{1,0:T(8,128)S(1)}, u32[]{:S(2)}, u32[]{:S(2)}) collective-permute-start(s32[64,8]{1,0:T(8,128)} %get-tuple-element.42), channel_id=1, source_target_pairs={{0,3},{1,0},{2,1},{3,2},{4,7},{5,4},{6,5},{7,6},{8,11},{9,8},{10,9... | collective-permute-start | bytes 6152 | tf_op jit(solution)/shard_map/ppermute | solution.py:66
  55.1 1.6 copy-start.7
  56.7 0.8 copy-start.24
  57.5 28.5 %copy-start.8 = (bf16[1024,1024]{1,0:T(8,128)(2,1)S(1)}, bf16[1024,1024]{1,0:T(8,128)(2,1)}, u32[]{:S(2)}) copy-start(bf16[1024,1024]{1,0:T(8,128)(2,1)} %refs_0_.2) | copy-start | bytes 6291460
  59.6 39.3 %copy-start.23 = (bf16[64,1024]{1,0:T(8,128)(2,1)S(1)}, bf16[64,1024]{1,0:T(8,128)(2,1)}, u32[]{:S(2)}) copy-start(bf16[64,1024]{1,0:T(8,128)(2,1)} %refs_0_.3) | copy-start | bytes 393220
  62.4 43.4 %copy-start.2 = (bf16[1024,1024]{1,0:T(8,128)(2,1)}, bf16[1024,1024]{1,0:T(8,128)(2,1)S(1)}, u32[]{:S(2)}) copy-start(bf16[1024,1024]{1,0:T(8,128)(2,1)S(1)} %get-tuple-element.44.refs_2_) | copy-start | bytes 6291460
  62.4 9.2 %collective-permute-start.13 = (bf16[128,1024]{1,0:T(8,128)(2,1)S(1)}, bf16[128,1024]{1,0:T(8,128)(2,1)S(1)}, u32[]{:S(2)}, u32[]{:S(2)}) collective-permute-start(bf16[128,1024]{1,0:T(8,128)(2,1)S(1)} %get-tuple-element.49.refs_3_), channel_id=1, source_target_pairs={{0,2},{1,3},{2,0},{3,1},{16,18},{17,19},{18,16},{19,17},{4,6},{5,7... | collective-permute-start | bytes 786440 | tf_op jit(solution)/shard_map/ppermute | solution.py:515
  63.4 6.1 %collective-permute-start.12 = (bf16[64,1024]{1,0:T(8,128)(2,1)S(1)}, bf16[64,1024]{1,0:T(8,128)(2,1)S(1)}, u32[]{:S(2)}, u32[]{:S(2)}) collective-permute-start(bf16[64,1024]{1,0:T(8,128)(2,1)S(1)} %get-tuple-element.47), channel_id=1, source_target_pairs={{0,4},{4,0},{8,12},{12,8},{1,5},{5,1},{9,13},{13,9},{2,6},{6,2},{1... | collective-permute-start | bytes 393224 | tf_op jit(solution)/shard_map/ppermute | solution.py:519
  72.1 26.8 %copy-start.13 = (bf16[256,1024]{1,0:T(8,128)(2,1)}, bf16[256,1024]{1,0:T(8,128)(2,1)S(1)}, u32[]{:S(2)}) copy-start(bf16[256,1024]{1,0:T(8,128)(2,1)S(1)} %get-tuple-element.58.refs_2_) | copy-start | bytes 1572868
  72.1 14.0 %collective-permute-start.20 = (bf16[256,1024]{1,0:T(8,128)(2,1)S(1)}, bf16[256,1024]{1,0:T(8,128)(2,1)S(1)}, u32[]{:S(2)}, u32[]{:S(2)}) collective-permute-start(bf16[256,1024]{1,0:T(8,128)(2,1)S(1)} %get-tuple-element.58.refs_2_), channel_id=1, source_target_pairs={{0,16},{1,17},{2,18},{3,19},{16,0},{17,1},{18,2},{19,3},{4,20},{5,... | collective-permute-start | bytes 1572872 | tf_op jit(solution)/shard_map/ppermute | solution.py:515
  73.6 4.0 %collective-permute-start.16 = (bf16[64,1024]{1,0:T(8,128)(2,1)S(1)}, bf16[64,1024]{1,0:T(8,128)(2,1)S(1)}, u32[]{:S(2)}, u32[]{:S(2)}) collective-permute-start(bf16[64,1024]{1,0:T(8,128)(2,1)S(1)} %get-tuple-element.52.refs_3_), channel_id=1, source_target_pairs={{0,3},{1,0},{2,1},{3,2},{4,7},{5,4},{6,5},{7,6},{8,11},{9,8},{10,9... | collective-permute-start | bytes 393224 | tf_op jit(solution)/shard_map/ppermute | solution.py:66
  73.7 12.3 %collective-permute-start.15 = (bf16[64,1024]{1,0:T(8,128)(2,1)S(1)}, bf16[64,1024]{1,0:T(8,128)(2,1)S(1)}, u32[]{:S(2)}, u32[]{:S(2)}) collective-permute-start(bf16[64,1024]{1,0:T(8,128)(2,1)S(1)} %get-tuple-element.52.refs_3_), channel_id=1, source_target_pairs={{0,2},{1,3},{2,0},{3,1},{4,6},{5,7},{6,4},{7,5},{8,10},{9,11},{10,... | collective-permute-start | bytes 393224 | tf_op jit(solution)/shard_map/ppermute | solution.py:66
  75.0 11.0 %collective-permute-start.14 = (bf16[64,1024]{1,0:T(8,128)(2,1)S(1)}, bf16[64,1024]{1,0:T(8,128)(2,1)S(1)}, u32[]{:S(2)}, u32[]{:S(2)}) collective-permute-start(bf16[64,1024]{1,0:T(8,128)(2,1)S(1)} %get-tuple-element.52.refs_3_), channel_id=1, source_target_pairs={{0,1},{1,2},{2,3},{3,0},{4,5},{5,6},{6,7},{7,4},{8,9},{9,10},{10,1... | collective-permute-start | bytes 393224 | tf_op jit(solution)/shard_map/ppermute | solution.py:66
  75.0 15.6 %collective-permute-start.23 = (bf16[128,1024]{1,0:T(8,128)(2,1)S(1)}, bf16[128,1024]{1,0:T(8,128)(2,1)S(1)}, u32[]{:S(2)}, u32[]{:S(2)}) collective-permute-start(bf16[128,1024]{1,0:T(8,128)(2,1)S(1)} %get-tuple-element.59), channel_id=1, source_target_pairs={{0,8},{4,12},{8,0},{12,4},{1,9},{5,13},{9,1},{13,5},{2,10},{6,14},... | collective-permute-start | bytes 786440 | tf_op jit(solution)/shard_map/ppermute | solution.py:522
  77.6 21.2 %collective-permute-start.21 = (bf16[256,1024]{1,0:T(8,128)(2,1)S(1)}, bf16[256,1024]{1,0:T(8,128)(2,1)S(1)}, u32[]{:S(2)}, u32[]{:S(2)}) collective-permute-start(bf16[256,1024]{1,0:T(8,128)(2,1)S(1)} %get-tuple-element.58.refs_2_), channel_id=1, source_target_pairs={{0,1},{1,0},{2,3},{3,2},{16,17},{17,16},{18,19},{19,18},{4,5},{5,4... | collective-permute-start | bytes 1572872 | tf_op jit(solution)/shard_map/ppermute | solution.py:515
  86.0 12.8 %collective-permute-start.22 = (bf16[256,1024]{1,0:T(8,128)(2,1)S(1)}, bf16[256,1024]{1,0:T(8,128)(2,1)S(1)}, u32[]{:S(2)}, u32[]{:S(2)}) collective-permute-start(bf16[256,1024]{1,0:T(8,128)(2,1)S(1)} %collective-permute-done.20.refs_8_.refs_3_), channel_id=1, source_target_pairs={{0,1},{1,0},{2,3},{3,2},{16,17},{17,16},{18,19},{19,18},{4,5},{5,4... | collective-permute-start | bytes 1572872 | tf_op jit(solution)/shard_map/ppermute | solution.py:515
  88.1 3.7 %collective-permute-start.17 = (bf16[64,1152]{1,0:T(8,128)(2,1)S(1)}, bf16[64,1152]{1,0:T(8,128)(2,1)S(1)}, u32[]{:S(2)}, u32[]{:S(2)}) collective-permute-start(bf16[64,1152]{1,0:T(8,128)(2,1)S(1)} %get-tuple-element.55), channel_id=1, source_target_pairs={{0,3},{1,0},{2,1},{3,2},{4,7},{5,4},{6,5},{7,6},{8,11},{9,8},{10,9... | collective-permute-start | bytes 442376 | tf_op jit(solution)/shard_map/ppermute | solution.py:66
  90.6 8.2 %collective-permute-start.24 = (bf16[128,1024]{1,0:T(8,128)(2,1)S(1)}, bf16[128,1024]{1,0:T(8,128)(2,1)S(1)}, u32[]{:S(2)}, u32[]{:S(2)}) collective-permute-start(bf16[128,1024]{1,0:T(8,128)(2,1)S(1)} %collective-permute-done.23.refs_11_.refs_5_), channel_id=1, source_target_pairs={{0,16},{1,17},{2,18},{3,19},{16,0},{17,1},{18,2},{19,3},{4,20},{5,... | collective-permute-start | bytes 786440 | tf_op jit(solution)/shard_map/ppermute | solution.py:515
  91.2 6.8 %collective-permute-start.18 = (bf16[64,1152]{1,0:T(8,128)(2,1)S(1)}, bf16[64,1152]{1,0:T(8,128)(2,1)S(1)}, u32[]{:S(2)}, u32[]{:S(2)}) collective-permute-start(bf16[64,1152]{1,0:T(8,128)(2,1)S(1)} %get-tuple-element.56), channel_id=1, source_target_pairs={{0,2},{1,3},{2,0},{3,1},{4,6},{5,7},{6,4},{7,5},{8,10},{9,11},{10,... | collective-permute-start | bytes 442376 | tf_op jit(solution)/shard_map/ppermute | solution.py:66
  91.9 6.4 %collective-permute-start.19 = (bf16[64,1152]{1,0:T(8,128)(2,1)S(1)}, bf16[64,1152]{1,0:T(8,128)(2,1)S(1)}, u32[]{:S(2)}, u32[]{:S(2)}) collective-permute-start(bf16[64,1152]{1,0:T(8,128)(2,1)S(1)} %get-tuple-element.57), channel_id=1, source_target_pairs={{0,1},{1,2},{2,3},{3,0},{4,5},{5,6},{6,7},{7,4},{8,9},{9,10},{10,1... | collective-permute-start | bytes 442376 | tf_op jit(solution)/shard_map/ppermute | solution.py:66
  98.8 9.5 %copy-start.9 = (bf16[256,1024]{1,0:T(8,128)(2,1)}, bf16[256,1024]{1,0:T(8,128)(2,1)S(1)}, u32[]{:S(2)}) copy-start(bf16[256,1024]{1,0:T(8,128)(2,1)S(1)} %collective-permute-done.22.refs_10_.refs_7_) | copy-start | bytes 1572868
  100.0 0.8 copy-start.12
  100.8 8.3 %copy-start.26 = (f32[1,128]{1,0:T(1,128)}, f32[1,128]{1,0:T(1,128)S(1)}, u32[]{:S(2)}) copy-start(f32[1,128]{1,0:T(1,128)S(1)} %get-tuple-element.60.loss_ref) | copy-start | bytes 1540
  100.8 5.0 %collective-permute-start.25 = (bf16[64,1024]{1,0:T(8,128)(2,1)S(1)}, bf16[64,1024]{1,0:T(8,128)(2,1)S(1)}, u32[]{:S(2)}, u32[]{:S(2)}) collective-permute-start(bf16[64,1024]{1,0:T(8,128)(2,1)S(1)} %get-tuple-element.61.refs_3_), channel_id=1, source_target_pairs={{0,4},{4,0},{8,12},{12,8},{1,5},{5,1},{9,13},{13,9},{2,6},{6,2},{1... | collective-permute-start | bytes 393224 | tf_op jit(solution)/shard_map/ppermute | solution.py:519
  108.3 0.7 copy-start.16
  109.0 16.5 %collective-permute-start.27 = (bf16[256,1024]{1,0:T(8,128)(2,1)}, bf16[256,1024]{1,0:T(8,128)(2,1)}, u32[]{:S(2)}, u32[]{:S(2)}) collective-permute-start(bf16[256,1024]{1,0:T(8,128)(2,1)} %get-tuple-element.66.refs_4_), channel_id=1, source_target_pairs={{0,2},{1,3},{2,0},{3,1},{16,18},{17,19},{18,16},{19,17},{4,6},{5,7... | collective-permute-start | bytes 1572872 | tf_op jit(solution)/shard_map/ppermute | solution.py:515
  109.9 33.9 %all-to-all-start.1 = ((bf16[32,64,128]{2,1,0:T(8,128)(2,1)}), bf16[32,64,128]{2,1,0:T(8,128)(2,1)}, u32[]{:S(2)}, u32[]{:S(2)}) async-start(bf16[32,64,128]{2,1,0:T(8,128)(2,1)} %copy-done.12), calls=%async_computation.1 | async-start | bytes 1048576 | tf_op jit(solution)/shard_map/all_to_all | solution.py:610
  113.4 30.4 %collective-permute-start.28 = (bf16[256,1024]{1,0:T(8,128)(2,1)}, bf16[256,1024]{1,0:T(8,128)(2,1)}, u32[]{:S(2)}, u32[]{:S(2)}) collective-permute-start(bf16[256,1024]{1,0:T(8,128)(2,1)} %get-tuple-element.66.refs_4_), channel_id=1, source_target_pairs={{0,1},{1,0},{2,3},{3,2},{16,17},{17,16},{18,19},{19,18},{4,5},{5,4... | collective-permute-start | bytes 1572872 | tf_op jit(solution)/shard_map/ppermute | solution.py:515
  125.5 18.3 %collective-permute-start.29 = (bf16[256,1024]{1,0:T(8,128)(2,1)}, bf16[256,1024]{1,0:T(8,128)(2,1)}, u32[]{:S(2)}, u32[]{:S(2)}) collective-permute-start(bf16[256,1024]{1,0:T(8,128)(2,1)} %collective-permute-done.27.refs_5_), channel_id=1, source_target_pairs={{0,1},{1,0},{2,3},{3,2},{16,17},{17,16},{18,19},{19,18},{4,5},{5,4... | collective-permute-start | bytes 1572872 | tf_op jit(solution)/shard_map/ppermute | solution.py:515
  125.5 8.8 %collective-permute-start.26 = (bf16[64,2048]{1,0:T(8,128)(2,1)S(1)}, bf16[64,2048]{1,0:T(8,128)(2,1)}, u32[]{:S(2)}, u32[]{:S(2)}) collective-permute-start(bf16[64,2048]{1,0:T(8,128)(2,1)S(1)} %get-tuple-element.63), channel_id=1, source_target_pairs={{0,4},{4,0},{8,12},{12,8},{1,5},{5,1},{9,13},{13,9},{2,6},{6,2},{1... | collective-permute-start | bytes 786440 | tf_op jit(solution)/shard_map/ppermute | solution.py:519
  143.8 37.1 %copy-start.3 = (bf16[1024,1024]{1,0:T(8,128)(2,1)S(1)}, bf16[1024,1024]{1,0:T(8,128)(2,1)}, u32[]{:S(2)}) copy-start(bf16[1024,1024]{1,0:T(8,128)(2,1)} %copy-done.2) | copy-start | bytes 6291460
  143.9 1.1 copy-start.4
  145.0 1.0 copy-start.10
  146.0 1.0 copy-start.14
  150.3 36.5 %copy-start.25 = (f32[1024]{0:T(1024)S(1)}, f32[1024]{0:T(1024)}, u32[]{:S(2)}) copy-start(f32[1024]{0:T(1024)} %param.14) | copy-start | bytes 12292
  150.3 10.2 %collective-permute-start.32 = (bf16[1024,128]{1,0:T(8,128)(2,1)S(1)}, bf16[1024,128]{1,0:T(8,128)(2,1)S(1)}, u32[]{:S(2)}, u32[]{:S(2)}) collective-permute-start(bf16[1024,128]{1,0:T(8,128)(2,1)S(1)} %grad_columns.1.refs_0_), channel_id=1, source_target_pairs={{0,18},{1,19},{2,16},{3,17},{16,2},{17,3},{18,0},{19,1},{4,22},{5,... | collective-permute-start | bytes 786440 | tf_op jit(solution)/shard_map/ppermute | solution.py:515
  151.9 12.7 %collective-permute-start.31 = (bf16[1024,128]{1,0:T(8,128)(2,1)S(1)}, bf16[1024,128]{1,0:T(8,128)(2,1)S(1)}, u32[]{:S(2)}, u32[]{:S(2)}) collective-permute-start(bf16[1024,128]{1,0:T(8,128)(2,1)S(1)} %grad_columns.1.refs_0_), channel_id=1, source_target_pairs={{0,16},{1,17},{2,18},{3,19},{16,0},{17,1},{18,2},{19,3},{4,20},{5,... | collective-permute-start | bytes 786440 | tf_op jit(solution)/shard_map/ppermute | solution.py:515
  153.0 11.8 %collective-permute-start.30 = (bf16[1024,128]{1,0:T(8,128)(2,1)S(1)}, bf16[1024,128]{1,0:T(8,128)(2,1)S(1)}, u32[]{:S(2)}, u32[]{:S(2)}) collective-permute-start(bf16[1024,128]{1,0:T(8,128)(2,1)S(1)} %grad_columns.1.refs_0_), channel_id=1, source_target_pairs={{0,2},{1,3},{2,0},{3,1},{16,18},{17,19},{18,16},{19,17},{4,6},{5,7... | collective-permute-start | bytes 786440 | tf_op jit(solution)/shard_map/ppermute | solution.py:515
  164.9 21.8 %collective-permute-start.33 = (bf16[4096,128]{1,0:T(8,128)(2,1)S(1)}, bf16[4096,128]{1,0:T(8,128)(2,1)S(1)}, u32[]{:S(2)}, u32[]{:S(2)}) collective-permute-start(bf16[4096,128]{1,0:T(8,128)(2,1)S(1)} %pack_columns.1.refs_3_), channel_id=1, source_target_pairs={{0,1},{1,0},{2,3},{3,2},{16,17},{17,16},{18,19},{19,18},{4,5},{5,4... | collective-permute-start | bytes 3145736 | tf_op jit(solution)/shard_map/ppermute | solution.py:515
  182.5 3.7 %collective-permute-start.34 = (f32[1,1024]{1,0:T(1,128)S(1)}, f32[1,1024]{1,0:T(1,128)S(1)}, u32[]{:S(2)}, u32[]{:S(2)}) collective-permute-start(f32[1,1024]{1,0:T(1,128)S(1)} %get-tuple-element.67), channel_id=1, source_target_pairs={{0,4},{4,0},{8,12},{12,8},{1,5},{5,1},{9,13},{13,9},{2,6},{6,2},{1... | collective-permute-start | bytes 12296 | tf_op jit(solution)/shard_map/ppermute | solution.py:519
  (2 other events, 1.3 us)

commit v2 on v1

--- a/solution.py
+++ b/solution.py
@@ -26,35 +26,22 @@
     return jax.ShapeDtypeStruct(dims, dtype)
 
 
-def call(kernel, outs, ins, name, flops=0, scratch=(), smem=0, kept=0, after=()):
-    count, first = len(ins), smem + kept
-    copied = ins[first:]
+def call(kernel, outs, ins, name, flops=0, scratch=(), smem=0, after=()):
+    count = len(ins)
     moved = sum(math.prod(a.shape) * a.dtype.itemsize for a in list(ins) + list(outs))
     held = sum(math.prod(s.shape) * jnp.dtype(s.dtype).itemsize for s in scratch)
 
     def run(*refs):
-        rest = refs[count + len(after) :]
-        results, buffers = rest[: len(outs)], rest[len(outs) : len(outs) + len(copied)]
-        own, sems = rest[len(outs) + len(copied) : -1], rest[-1]
-        copies = [
-            pltpu.make_async_copy(src, dst, sems.at[k])
-            for k, (src, dst) in enumerate(zip(refs[first:count], buffers))
-        ]
-        for copy in copies:
-            copy.start()
-        for copy in copies:
-            copy.wait()
-        kernel(*refs[:first], *buffers, *results, *own)
-
-    anywhere = pl.BlockSpec(memory_space=pl.ANY)
+        kernel(*refs[:count], *refs[count + len(after) :])
+
     return pl.pallas_call(
         run,
         out_shape=outs,
-        in_specs=[SMEM] * smem + [VMEM] * kept + [anywhere] * (len(copied) + len(after)),
+        in_specs=[SMEM] * smem
+        + [VMEM] * (count - smem)
+        + [pl.BlockSpec(memory_space=pl.ANY)] * len(after),
         out_specs=[VMEM] * len(outs),
-        scratch_shapes=[pltpu.VMEM(a.shape, a.dtype) for a in copied]
-        + list(scratch)
-        + [pltpu.SemaphoreType.DMA((max(len(copied), 1),))],
+        scratch_shapes=list(scratch),
         cost_estimate=pl.CostEstimate(flops=flops, bytes_accessed=moved, transcendentals=0),
         compiler_params=pltpu.CompilerParams(vmem_limit_bytes=2 * (moved + held) + 6 * MIB),
         name=name,
@@ -80,7 +67,7 @@
     return lax.dot_general(left, right, (((0,), (0,)), ((), ())), preferred_element_type=F32)
 
 
-def norm_kernel(event_ref, states_ref, gain_ref, normed_ref):
+def norm_kernel(states_ref, gain_ref, normed_ref):
     tokens, width = states_ref.shape
     step = 4 * LANES if width % (4 * LANES) == 0 else width
     for top in range(0, tokens, 32):
@@ -96,22 +83,23 @@
             normed_ref[rows, at : at + step] = part.astype(BF16)
 
 
-def norm_rows(event, states, gain):
+def norm_rows(events, states, gain):
     tokens, width = states.shape
     block = 128 if tokens % 128 == 0 else tokens
     rows = pl.BlockSpec((block, width), lambda i: (i, 0))
     return pl.pallas_call(
-        norm_kernel,
+        lambda *refs: norm_kernel(*refs[len(events) :]),
         grid=(tokens // block,),
         out_shape=shape((tokens, width), BF16),
-        in_specs=[pl.BlockSpec(memory_space=pl.ANY), rows, pl.BlockSpec((1, width), lambda i: (0, 0))],
+        in_specs=[pl.BlockSpec(memory_space=pl.ANY)] * len(events)
+        + [rows, pl.BlockSpec((1, width), lambda i: (0, 0))],
         out_specs=rows,
         cost_estimate=pl.CostEstimate(
             flops=6 * tokens * width, bytes_accessed=4 * tokens * width, transcendentals=0
         ),
-        compiler_params=pltpu.CompilerParams(vmem_limit_bytes=60 * MIB),
+        compiler_params=pltpu.CompilerParams(vmem_limit_bytes=10 * MIB),
         name="norm_rows",
-    )(event, states, gain)
+    )(*events, states, gain)
 
 
 def gate_kernel(seq, root, blocks, z_ref, normed_ref, u_ref, len_ref, lists_ref, event_ref, *rest):
@@ -192,7 +180,7 @@
         cost_estimate=pl.CostEstimate(
             flops=4 * tokens * width, bytes_accessed=2 * tokens * width, transcendentals=0
         ),
-        compiler_params=pltpu.CompilerParams(vmem_limit_bytes=60 * MIB),
+        compiler_params=pltpu.CompilerParams(vmem_limit_bytes=16 * MIB),
         name="gate_rows",
     )(z, normed, u, token_lengths, lists, event)
 
@@ -205,30 +193,8 @@
 
 def pack(pieces, name, event):
     rows, width = pieces[0].shape
-    n = len(pieces)
-
-    def run(*refs):
-        out_ref, sems = refs[-2], refs[-1]
-        copies = [
-            pltpu.make_async_copy(refs[k], out_ref.at[pl.ds(k * rows, rows), :], sems.at[k])
-            for k in range(n)
-        ]
-        for copy in copies:
-            copy.start()
-        for copy in copies:
-            copy.wait()
-
-    anywhere = pl.BlockSpec(memory_space=pl.ANY)
-    return pl.pallas_call(
-        run,
-        out_shape=shape((n * rows, width), pieces[0].dtype),
-        in_specs=[anywhere] * (n + 1),
-        out_specs=anywhere,
-        scratch_shapes=[pltpu.SemaphoreType.DMA((n,))],
-        cost_estimate=pl.CostEstimate(flops=0, bytes_accessed=4 * n * rows * width, transcendentals=0),
-        compiler_params=pltpu.CompilerParams(vmem_limit_bytes=4 * MIB),
-        name=name,
-    )(*pieces, event)
+    out = shape((len(pieces) * rows, width), pieces[0].dtype)
+    return call(pack_kernel, [out], pieces, name, after=[event])[0]
 
 
 def forward_kernel(n, packs, side_ref, places_ref, weight_ref, *refs):
@@ -429,13 +395,14 @@
         cost_estimate=pl.CostEstimate(
             flops=4 * tokens * width, bytes_accessed=2 * tokens * width, transcendentals=0
         ),
-        compiler_params=pltpu.CompilerParams(vmem_limit_bytes=60 * MIB),
+        compiler_params=pltpu.CompilerParams(vmem_limit_bytes=20 * MIB),
         name="slope_rows",
     )(z, normed, curve, loss, *backs)
 
 
-def columns_kernel(n, order_ref, grads_ref, *refs):
-    pieces, out_ref, sorted_ref = refs[:n], refs[n], refs[n + 1]
+def columns_kernel(n, order_ref, slopes_ref, grads_ref, *refs):
+    pieces, (out_ref, pass_ref, sorted_ref) = refs[:n], refs[n:]
+    pass_ref[...] = slopes_ref[...]
     chunk = grads_ref.shape[1]
     for j in range(sorted_ref.shape[0] // chunk):
         sorted_ref[j * chunk : (j + 1) * chunk, :] = grads_ref[order_ref[j]]
@@ -540,19 +507,36 @@
     for k in range(n_z):
         u = lax.dynamic_update_slice(u, u_parts[k], (0, lax.rem(z - k + n_z, n_z) * depth))
 
-    normed = norm_rows(u, hidden_states.reshape(-1, width), norm_gain.astype(F32).reshape(1, width))
-
-    far_share = pack([far_share], "far_share", normed)
-    chip_shares = [far_share if dg == dh == 0 else plane_shift(far_share, dg, dh, 0) for dg, dh in chips]
     share_places = []
     for dc in range(n_c):
         for dg, dh in chips:
             from_g, from_i = source(dg, dh, dc)
             share_places.append(from_g * n_i + from_i)
-
+    share_places = ints(*share_places)
+    order = []
+    for dc in range(n_c):
+        for dg in range(n_g):
+            order += [(side, k, dg, dh, dc) for dh in range(n_h) for k in range(half)]
+        for dh in range(n_h):
+            order += [(1 - side, k, dg, dh, dc) for dg in range(n_g) for k in range(half)]
+    ranks = []
+    for from_side, k, dg, dh, dc in order:
+        from_g, from_i = source(dg, dh, dc)
+        from_z = from_side * half + lax.rem(member - k + half, half)
+        ranks.append((from_z * n_g + from_g) * n_i + from_i)
+    ranks = ints(*ranks)
+    both_arr, base_arr = ints(z, i), ints(i * slab.shape[0])
     token_lengths = jnp.broadcast_to(lengths[:, None], (queries, seq)).reshape(-1, 1)
+    events = [u, token_lengths, share_places, ranks, both_arr, base_arr, side_arr]
+    normed = norm_rows(
+        events, hidden_states.reshape(-1, width),
+        norm_gain.astype(F32).reshape(1, width)
+    )
+
+    far_share = pack([far_share], "far_share", normed)
+    chip_shares = [far_share if dg == dh == 0 else plane_shift(far_share, dg, dh, 0) for dg, dh in chips]
     gate_outs = gate_rows(
-        ints(z, i), normed, u, token_lengths, negatives, far_share, seq, root, n_z, n_i
+        both_arr, normed, u, token_lengths, negatives, far_share, seq, root, n_z, n_i
     )
     sends, (gated, curve), lists = gate_outs[:half], gate_outs[half : half + 2], gate_outs[half + 2 :]
 
@@ -564,7 +548,7 @@
     counts, slab_scale = call(
         functools.partial(count_kernel, n_i, root),
         [shape((n_i * queries, slab.shape[0]), F32), shape((1, slab.shape[0]), F32)],
-        [ints(i * slab.shape[0]), slab] + lists, "list_counts", smem=1, kept=1,
+        [base_arr, slab] + lists, "list_counts", smem=1,
     )
     block = shape((half * queries, depth), BF16)
     *parts, mirror, held, away = call(
@@ -572,8 +556,8 @@
         [shape((queries, proj_width), F32)]
         + [shape((queries, proj_width), BF16)] * (half - 1)
         + [shape((depth, proj_width), BF16), block, block],
-        [side_arr, ints(*share_places), proj_weight] + pieces + packs, "forward",
-        flops=4 * half * queries * depth * proj_width, smem=2, kept=1, after=[counts],
+        [side_arr, share_places, proj_weight] + pieces + packs, "forward",
+        flops=4 * half * queries * depth * proj_width, smem=2, after=[counts],
     )
     parts = [parts[0]] + [half_shift(parts[k], -k) for k in range(1, half)]
     near = [held] + [plane_shift(held, 0, dh, 0) for dh in range(1, n_h)]
@@ -593,7 +577,7 @@
         functools.partial(contrast_kernel, n_i),
         [shape(wide, F32)] + [shape(wide, BF16)] * (n_i - 1),
         [slab, slab_scale, counts] + pieces, "contrast",
-        flops=4 * n_i * queries * slab.shape[0] * proj_width, kept=3,
+        flops=4 * n_i * queries * slab.shape[0] * proj_width,
     )
     parts = [parts[0]] + [shift(parts[k], "item", -k) for k in steps_i]
     near_cores = [plane_shift(near, 0, 0, dc) for dc in range(1, n_c)]
@@ -603,7 +587,7 @@
     grad, grad_columns, loss = call(
         functools.partial(grad_kernel, n_i, root),
         [row16, shape((n_all, queries, cols), BF16), shape((1, LANES), F32)],
-        [positives, pooled, unit, embedded] + parts, "grad_pooled", kept=4,
+        [positives, pooled, unit, embedded] + parts, "grad_pooled",
         after=near_far + near_cores + sum(near_far_cores, []) + others,
     )
 
@@ -613,44 +597,37 @@
         functools.partial(back_kernel, half, n_g),
         [shape((queries, 2 * depth), BF16)] * half + [shape((n_g * half * queries, depth), BF16)],
         [side_arr, proj_weight, mirror] + pieces + others, "backward",
-        flops=4 * half * queries * depth * proj_width, smem=1, kept=2,
+        flops=4 * half * queries * depth * proj_width, smem=1,
     )
     backs = [backs[0]] + [half_shift(backs[k], -k) for k in range(1, half)]
-    slopes = slope_rows(ints(z, 0), normed, curve, loss, backs, seq, n_z, n_all, n_plane)
-    near_sets = [(near, 0)] + [(near_far[dg - 1], dg) for dg in range(1, n_g)]
-    other_sets = [(others, 0)] + [(plane_shift(others, 0, dh, 0), dh) for dh in range(1, n_h)]
-    spread, order = [], []
+    slopes = slope_rows(both_arr, normed, curve, loss, backs, seq, n_z, n_all, n_plane)
+    across = [plane_shift(others, 0, dh, 0) for dh in range(1, n_h)]
+    late = [pack([array], "late", slopes) for array in across]
+    spread = []
     for dc in range(n_c):
-        for array, dg in near_sets:
-            spread.append(array if dc == 0 else ([near_cores[dc - 1]] + near_far_cores[dc - 1])[dg])
-            order += [(side, k, dg, dh, dc) for dh in range(n_h) for k in range(half)]
-        for array, dh in other_sets:
-            spread.append(array if dc == 0 else plane_shift(array, 0, 0, dc))
-            order += [(1 - side, k, dg, dh, dc) for dg in range(n_g) for k in range(half)]
-    ranks = []
-    for from_side, k, dg, dh, dc in order:
-        from_g, from_i = source(dg, dh, dc)
-        from_z = from_side * half + lax.rem(member - k + half, half)
-        ranks.append((from_z * n_g + from_g) * n_i + from_i)
-    block_columns = call(
-        functools.partial(columns_kernel, len(spread)), [shape((depth, cols), BF16)],
-        [ints(*ranks), all_columns] + spread, "grad_columns",
+        if dc == 0:
+            spread += [near, *near_far, others, *across]
+        else:
+            spread += [near_cores[dc - 1], *near_far_cores[dc - 1]]
+            spread += [plane_shift(array, 0, 0, dc) for array in [others, *late]]
+    block_columns, slopes = call(
+        functools.partial(columns_kernel, len(spread)), [shape((depth, cols), BF16), shape(slopes.shape, F32)],
+        [ranks, slopes, all_columns] + spread, "grad_columns",
         flops=2 * n_all * queries * depth * cols, scratch=[pltpu.VMEM((n_all * queries, cols), BF16)], smem=1,
-        after=[slopes],
-    )[0]
+    )
     on_chips = [block_columns if dg == dh == 0 else plane_shift(block_columns, dg, dh, 0) for dg, dh in chips]
     all_slopes = lax.all_to_all(slopes, EVERY, 0, 0, tiled=True)
     query_part, my_slope, loss_total = call(
         query_kernel,
         [shape((1, proj_width), F32), shape((depth // LANES, LANES), F32), shape((1, LANES), F32)],
-        [side_arr, proj_weight, mirror, all_slopes], "slope_sum", smem=1, kept=2,
-    )
-    finished = [pack(on_chips, "pack_columns", slopes)]
+        [side_arr, proj_weight, mirror, all_slopes], "slope_sum", smem=1,
+    )
+    finished = [pack(on_chips, "pack_columns", all_slopes)]
     finished += [plane_shift(finished[0], 0, 0, dc) for dc in range(1, n_c)]
     grad_query = query_part + sum(half_shift(query_part, k) for k in range(1, half))
     grad_proj = call(
         functools.partial(finish_kernel, len(finished)), [shape((depth, proj_width), F32)],
-        [ints(*share_places), pool_query.reshape(1, -1), my_slope] + finished, "finish", smem=1, kept=2,
+        [share_places, pool_query.reshape(1, -1), my_slope] + finished, "finish", smem=1,
     )[0]
     mean_loss = loss_total[0, 0] / (queries * n_all)
     return (grad_proj, grad_query.reshape(proj_width), mean_loss)

time: 193 us -> 174 us (0.902)
  Pallas kernels: 47.3 us -> 31.2 us
  blocking collectives: 15.9 us -> 0 us
  starting transfers between devices: 37.3 us -> 44.8 us
  waiting for transfers between devices: 62.5 us -> 67.5 us
  local copies, waits for them, and re-layouts: 21.1 us -> 24.4 us
    all_to_all x1 -> x0, blocking collectives: 15.9 us -> none  [body(): all_slopes = lax.all_to_all(slopes, EVERY, 0, 0, tiled=True)]
    pallas_call x13 -> x14, Pallas kernels: 29.8 us -> 20 us  [the longest x13 16.5 us: call(): pl.pallas_call(run, out_shape=outs, in_specs=[SMEM] * smem + [VMEM] * (co...]
    ppermute x5, waiting for transfers between devices: 20.9 us -> 27 us  [half_shift(): return lax.ppermute(values, 'fsdp', pairs)]
    ppermute x16, waiting for transfers between devices: 32.4 us -> 26.8 us  [plane_shift(): return lax.ppermute(values, PLANE, pairs)]
    all_to_all x0 -> x1, starting transfers between devices: none -> 4.62 us  [body(): all_slopes = lax.all_to_all(slopes, EVERY, 0, 0, tiled=True)]
    ppermute x2, waiting for transfers between devices: 1.58 us -> 5.43 us  [mirror_shift(): lax.ppermute(values, 'fsdp', [(a, (a + half) % n_z) for a in range(n_z)])]
    pallas_call x1, Pallas kernels: 9.45 us -> 5.84 us  [slope_rows(): pl.pallas_call(functools.partial(slope_kernel, seq, blocks, plane), grid=...]
    unnamed x61 -> x51, local copies, waits for them, and re-layouts: 18.7 us -> 22.2 us
  transfers between devices with their start and end apart: 36 -> 37, of which waited for: 19 -> 20; matrix products, arithmetic and copies ran while one was open for 3% -> 2% of each run, Pallas kernels for 17% -> 12%
where the time goes in v2:
time: 174 us
  waiting for transfers between devices  67.5 us (39%)
  starting transfers between devices  44.8 us (26%)
  Pallas kernels  31.2 us (18%)
  local copies, waits for them, and re-layouts  24.4 us (14%)
  other arithmetic  3.45 us (2%)
  between operations  2.19 us (1%)
    ppermute x5, waiting for transfers between devices, half_shift(): return lax.ppermute(values, 'fsdp', pairs)  27 us
    ppermute x16, waiting for transfers between devices, plane_shift(): return lax.ppermute(values, PLANE, pairs)  26.8 us
    unnamed x51, local copies, waits for them, and re-layouts  22.2 us
    pallas_call x13, Pallas kernels, call(): pl.pallas_call(run, out_shape=outs, in_specs=[SMEM] * smem + [VMEM] * (co...  16.5 us
    ppermute x12, starting transfers between devices, shift(): return lax.ppermute(values, axis, [(i, (i + k) % n) for i in range(n)])  12.6 us
    ppermute x16, starting transfers between devices, plane_shift(): return lax.ppermute(values, PLANE, pairs)  12.5 us
    ppermute x12, waiting for transfers between devices, shift(): return lax.ppermute(values, axis, [(i, (i + k) % n) for i in range(n)])  8.35 us
    ppermute x5, starting transfers between devices, half_shift(): return lax.ppermute(values, 'fsdp', pairs)  5.87 us
  transfers between devices with their start and end apart: 37, of which 20 were waited for; matrix products, arithmetic and copies ran while one was open for 2% of the time, Pallas kernels for 12%

profile of v2, /device:TPU:0, one launch (start us, length us, event | category | flops | bytes accessed | tf_op | source)
XLA Modules:
  0.0 173.6 jit_solution(6330747705302834871)
XLA Ops:
  0.6 2.1 %multiply_reduce_fusion = f32[1024]{0:T(1024)S(1)} fusion(bf16[1024,1024]{1,0:T(8,128)(2,1)} %refs_1_.5, f32[1024]{0:T(1024)} %param.14), kind=kLoop, calls=%fused_computation | loop fusion | flops 3144704 | bytes 2105344 | tf_op jit(solution)/shard_map/reduce_sum | solution.py:504
  2.7 5.1 %collective-permute-start.2 = (f32[1,1024]{1,0:T(1,128)S(1)}, f32[1,1024]{1,0:T(1,128)S(1)}, u32[]{:S(2)}, u32[]{:S(2)}) collective-permute-start(f32[1,1024]{1,0:T(1,128)S(1)} %bitcast.55), channel_id=1, source_target_pairs={{0,12},{4,0},{8,4},{12,8},{1,13},{5,1},{9,5},{13,9},{2,14},{6,2},{... | collective-permute-start | bytes 12296 | tf_op jit(solution)/shard_map/ppermute | solution.py:53
  7.8 1.0 collective-permute-start
  8.8 1.0 constant_dynamic-slice_fusion
  9.8 2.0 %collective-permute-start.3 = (bf16[128,1024]{1,0:T(8,128)(2,1)S(1)}, bf16[128,1024]{1,0:T(8,128)(2,1)S(1)}, u32[]{:S(2)}, u32[]{:S(2)}) collective-permute-start(bf16[128,1024]{1,0:T(8,128)(2,1)S(1)} %constant_dynamic-slice_fusion), channel_id=1, source_target_pairs={{0,8},{4,12},{8,0},{12,4},{1,9},{5,13},{9,1},{13,5},{2,10},{6,14},... | collective-permute-start | bytes 786440 | tf_op jit(solution)/shard_map/ppermute | solution.py:489
  11.9 0.7 reshape.37
  12.6 0.7 broadcast_in_dim.5
  14.0 3.4 %copy-done.6 = bf16[64,16,4096]{2,1,0:T(8,128)(2,1)S(1)} copy-done((bf16[64,16,4096]{2,1,0:T(8,128)(2,1)S(1)}, bf16[64,16,4096]{2,1,0:T(8,128)(2,1)}, u32[]{:S(2)}) %copy-start.6) | copy-done | bytes 8388632
  17.3 3.4 %norm_rows.1.refs_1_.normed_ref = bf16[1024,4096]{1,0:T(8,128)(2,1)S(1)} custom-call(f32[1,4096]{1,0:T(1,128)S(1)} %constant_dynamic-update-slice_fusion.refs_0_.u_ref, s32[1024,1]{1,0:T(8,128)S(1)} %reshape.39.refs_1_.len_ref, s32[8]{0:T(128)S(1)} %stack.149.refs_2_.refs_1_.refs_0_, s32[32]{0:T(128)S(1)} %stack.186.refs_3_.refs_0_, ...), custom_call_target="tpu_custom_call" | custom-call | flops 25165824 | bytes 16777216 | tf_op jit(solution)/shard_map/norm_rows/pallas_call | solution.py:90
  20.8 2.8 %collective-permute-done.3.refs_0_ = bf16[128,1024]{1,0:T(8,128)(2,1)S(1)} collective-permute-done((bf16[128,1024]{1,0:T(8,128)(2,1)S(1)}, bf16[128,1024]{1,0:T(8,128)(2,1)S(1)}, u32[]{:S(2)}, u32[]{:S(2)}) %collective-permute-start.3) | collective-permute-done | bytes 262176 | tf_op jit(solution)/shard_map/ppermute | solution.py:489
  24.1 2.4 %collective-permute-start.7 = (bf16[128,1024]{1,0:T(8,128)(2,1)S(1)}, bf16[128,1024]{1,0:T(8,128)(2,1)S(1)}, u32[]{:S(2)}, u32[]{:S(2)}) collective-permute-start(bf16[128,1024]{1,0:T(8,128)(2,1)S(1)} %far_share.1.event_ref.refs_0_), channel_id=1, source_target_pairs={{0,18},{1,19},{2,16},{3,17},{16,2},{17,3},{18,0},{19,1},{4,22},{5,... | collective-permute-start | bytes 786440 | tf_op jit(solution)/shard_map/ppermute | solution.py:482
  27.7 3.4 %copy-done.1 = bf16[1024,4096]{1,0:T(8,128)(2,1)S(1)} copy-done((bf16[1024,4096]{1,0:T(8,128)(2,1)S(1)}, bf16[1024,4096]{1,0:T(8,128)(2,1)}, u32[]{:S(2)}) %copy-start.1) | copy-done | bytes 8388632
  31.1 5.4 %gate_rows.1 = (bf16[64,2048]{1,0:T(8,128)(2,1)S(1)}, bf16[64,2048]{1,0:T(8,128)(2,1)S(1)}, f32[1024,1]{1,0:T(8,128)S(1)}, f32[1024,1]{1,0:T(8,128)S(1)}, s32[64...) custom-call(s32[2]{0:T(128)S(1)} %pad_add_fusion.refs_4_.z_ref, ...), custom_call_target="tpu_custom_call" | custom-call | flops 16777216 | bytes 8388608 | tf_op jit(solution)/shard_map/gate_rows/pallas_call | solution.py:165
  36.5 1.4 collective-permute-done.6.refs_2_
  38.1 1.5 collective-permute-start.4
  39.8 1.4 collective-permute-start.10
  41.2 1.3 collective-permute-start.11
  42.9 0.7 collective-permute-done.10.refs_4_
  44.1 1.8 %list_counts.1 = (f32[256,1024]{1,0:T(8,128)S(1)}, f32[1,1024]{1,0:T(1,128)S(1)}) custom-call(s32[1]{0:T(128)} %bitcast.45.refs_5_.refs_0_, bf16[1024,1024]{1,0:T(8,128)(2,1)S(1)} %copy-done.7, s32[64,8]{1,0:T(8,128)S(1)} %get-tuple-element.41.refs_2_, s32[64,8]{1,0:T(8,128)S(1)} %collective-permute-done.9.refs_3_, ...), custom_call_target="tpu_custom_call" | custom-call | bytes 3158020 | tf_op jit(solution)/shard_map/list_counts/pallas_call | solution.py:37
  45.9 0.9 collective-permute-done.4.refs_4_
  46.8 1.4 forward.1
  48.3 1.5 collective-permute-start.13
  49.7 1.5 collective-permute-start.12
  51.2 3.8 %collective-permute-done.12.refs_1_ = bf16[64,1024]{1,0:T(8,128)(2,1)S(1)} collective-permute-done((bf16[64,1024]{1,0:T(8,128)(2,1)S(1)}, bf16[64,1024]{1,0:T(8,128)(2,1)S(1)}, u32[]{:S(2)}, u32[]{:S(2)}) %collective-permute-start.12) | collective-permute-done | bytes 131104 | tf_op jit(solution)/shard_map/ppermute | solution.py:486
  55.0 1.7 collective-permute-done.13.refs_4_
  56.8 1.6 collective-permute-start.20
  58.5 1.3 collective-permute-start.15
  60.0 2.8 %collective-permute-start.23 = (bf16[128,1024]{1,0:T(8,128)(2,1)S(1)}, bf16[128,1024]{1,0:T(8,128)(2,1)S(1)}, u32[]{:S(2)}, u32[]{:S(2)}) collective-permute-start(bf16[128,1024]{1,0:T(8,128)(2,1)S(1)} %get-tuple-element.61), channel_id=1, source_target_pairs={{0,8},{4,12},{8,0},{12,4},{1,9},{5,13},{9,1},{13,5},{2,10},{6,14},... | collective-permute-start | bytes 786440 | tf_op jit(solution)/shard_map/ppermute | solution.py:489
  62.8 1.3 collective-permute-start.21
  64.1 6.0 %collective-permute-done.20.refs_8_.refs_4_ = bf16[256,1024]{1,0:T(8,128)(2,1)S(1)} collective-permute-done((bf16[256,1024]{1,0:T(8,128)(2,1)S(1)}, bf16[256,1024]{1,0:T(8,128)(2,1)S(1)}, u32[]{:S(2)}, u32[]{:S(2)}) %collective-permute-start.20) | collective-permute-done | bytes 524320 | tf_op jit(solution)/shard_map/ppermute | solution.py:482
  70.1 1.4 contrast.1
  71.5 1.6 collective-permute-start.17
  73.1 2.6 %collective-permute-done.23.refs_11_.refs_5_ = bf16[128,1024]{1,0:T(8,128)(2,1)S(1)} collective-permute-done((bf16[128,1024]{1,0:T(8,128)(2,1)S(1)}, bf16[128,1024]{1,0:T(8,128)(2,1)S(1)}, u32[]{:S(2)}, u32[]{:S(2)}) %collective-permute-start.23) | collective-permute-done | bytes 262176 | tf_op jit(solution)/shard_map/ppermute | solution.py:489
  76.6 6.3 %collective-permute-done.18.refs_6_ = bf16[64,1152]{1,0:T(8,128)(2,1)S(1)} collective-permute-done((bf16[64,1152]{1,0:T(8,128)(2,1)S(1)}, bf16[64,1152]{1,0:T(8,128)(2,1)S(1)}, u32[]{:S(2)}, u32[]{:S(2)}) %collective-permute-start.18) | collective-permute-done | bytes 147488 | tf_op jit(solution)/shard_map/ppermute | solution.py:53
  84.5 0.8 copy-done.12
  85.3 5.0 %collective-permute-done.25.refs_4_ = bf16[64,1024]{1,0:T(8,128)(2,1)S(1)} collective-permute-done((bf16[64,1024]{1,0:T(8,128)(2,1)S(1)}, bf16[64,1024]{1,0:T(8,128)(2,1)S(1)}, u32[]{:S(2)}, u32[]{:S(2)}) %collective-permute-start.25) | collective-permute-done | bytes 131104 | tf_op jit(solution)/shard_map/ppermute | solution.py:486
  90.3 2.2 %backward.1 = (bf16[64,2048]{1,0:T(8,128)(2,1)S(1)}, bf16[64,2048]{1,0:T(8,128)(2,1)S(1)}, bf16[256,1024]{1,0:T(8,128)(2,1)}) custom-call(s32[1]{0:T(128)} %bitcast.9.refs_6_.refs_0_, bf16[1024,1024]{1,0:T(8,128)(2,1)S(1)} %copy-done.3, bf16[1024,1024]{1,0:T(8,128)(2,1)S(1)} %get-tuple-element.46.refs_2_, bf16[64,1024]{1,0:T(8,128)(2,1)S(1)} %get-tuple-element.63.refs_3_, ...), custom_call_target="tpu_custom_call" | custom-call | flops 536870912 | bytes 6029316 | tf_op jit(solution)/shard_map/backward/pallas_call | solution.py:37
  92.4 0.7 copy-done.20
  93.6 4.4 %all-to-all-start = ((bf16[32,64,128]{2,1,0:T(8,128)(2,1)}), bf16[32,64,128]{2,1,0:T(8,128)(2,1)}, u32[]{:S(2)}, u32[]{:S(2)}) async-start(bf16[32,64,128]{2,1,0:T(8,128)(2,1)} %copy-done.12), calls=%async_computation | async-start | bytes 1048576 | tf_op jit(solution)/shard_map/all_to_all | solution.py:594
  98.0 1.6 collective-permute-start.26
  99.6 15.0 %collective-permute-done.26.rest_1_ = bf16[64,2048]{1,0:T(8,128)(2,1)S(1)} collective-permute-done((bf16[64,2048]{1,0:T(8,128)(2,1)S(1)}, bf16[64,2048]{1,0:T(8,128)(2,1)S(1)}, u32[]{:S(2)}, u32[]{:S(2)}) %collective-permute-start.26) | collective-permute-done | bytes 262176 | tf_op jit(solution)/shard_map/ppermute | solution.py:486
  114.6 3.4 %copy-done.2 = bf16[1024,4096]{1,0:T(8,128)(2,1)S(1)} copy-done((bf16[1024,4096]{1,0:T(8,128)(2,1)S(1)}, bf16[1024,4096]{1,0:T(8,128)(2,1)}, u32[]{:S(2)}) %copy-start.2) | copy-done | bytes 8388632
  118.0 1.0 copy-done.11
  119.0 0.9 copy-done.21
  120.0 5.8 %slope_rows.1.refs_1_ = f32[32,24,128]{2,1,0:T(8,128)S(1)} custom-call(s32[2]{0:T(128)S(1)} %pad_add_fusion.refs_4_.z_ref, bf16[1024,4096]{1,0:T(8,128)(2,1)S(1)} %copy-done.2, f32[1024,1]{1,0:T(8,128)S(1)} %copy-done.11, f32[1,128]{1,0:T(1,128)S(1)} %get-tuple-element.62.loss_ref, bf16[64,2048]{1,0:T(8,128)(2,1)S(1)} %copy-done.21, ...), custom_call_target="tpu_custom_call" | custom-call | flops 16777216 | bytes 8388608 | tf_op jit(solution)/shard_map/slope_rows/pallas_call | solution.py:382
  125.9 1.9 %late.1 = bf16[256,1024]{1,0:T(8,128)(2,1)} custom-call(bf16[256,1024]{1,0:T(8,128)(2,1)} %collective-permute-done.27.refs_0_.refs_6_, f32[32,24,128]{2,1,0:T(8,128)S(1)} %slope_rows.1.refs_1_), custom_call_target="tpu_custom_call" | custom-call | bytes 1048576 | tf_op jit(solution)/shard_map/late/pallas_call | solution.py:37
  127.7 0.8 copy-done.15
  128.5 1.4 collective-permute-done.29.refs_10_
  130.0 1.0 copy-done.9
  131.0 1.0 copy-done.14
  132.1 1.0 copy-done.16
  133.1 2.4 %grad_columns.1 = (bf16[1024,128]{1,0:T(8,128)(2,1)S(1)}, f32[32,24,128]{2,1,0:T(8,128)S(1)}) custom-call(s32[32]{0:T(128)S(1)} %stack.186.refs_3_.refs_0_, f32[32,24,128]{2,1,0:T(8,128)S(1)} %slope_rows.1.refs_1_, bf16[32,64,128]{2,1,0:T(8,128)(2,1)} %all-to-all-done.refs_2_, bf16[256,1024]{1,0:T(8,128)(2,1)S(1)} %copy-done.14, ...), custom_call_target="tpu_custom_call" | custom-call | flops 536870912 | bytes 5767296 | tf_op jit(solution)/shard_map/grad_columns/pallas_call | solution.py:37
  135.5 0.8 copy-done.17
  136.3 0.7 copy-done.18
  137.0 4.6 %all-to-all-start.1 = ((f32[32,24,128]{2,1,0:T(8,128)}), f32[32,24,128]{2,1,0:T(8,128)S(1)}, u32[]{:S(2)}, u32[]{:S(2)}) async-start(f32[32,24,128]{2,1,0:T(8,128)} %copy-done.17), calls=%async_computation.1 | async-start | bytes 786432 | tf_op jit(solution)/shard_map/all_to_all | solution.py:619
  141.6 2.7 %collective-permute-start.32 = (bf16[1024,128]{1,0:T(8,128)(2,1)}, bf16[1024,128]{1,0:T(8,128)(2,1)S(1)}, u32[]{:S(2)}, u32[]{:S(2)}) collective-permute-start(bf16[1024,128]{1,0:T(8,128)(2,1)} %copy-done.18), channel_id=1, source_target_pairs={{0,18},{1,19},{2,16},{3,17},{16,2},{17,3},{18,0},{19,1},{4,22},{5,... | collective-permute-start | bytes 786440 | tf_op jit(solution)/shard_map/ppermute | solution.py:482
  145.2 10.7 %collective-permute-done.32.refs_3_ = bf16[1024,128]{1,0:T(8,128)(2,1)S(1)} collective-permute-done((bf16[1024,128]{1,0:T(8,128)(2,1)}, bf16[1024,128]{1,0:T(8,128)(2,1)S(1)}, u32[]{:S(2)}, u32[]{:S(2)}) %collective-permute-start.32) | collective-permute-done | bytes 262176 | tf_op jit(solution)/shard_map/ppermute | solution.py:482
  155.9 4.3 %collective-permute-done.31.refs_2_ = bf16[1024,128]{1,0:T(8,128)(2,1)S(1)} collective-permute-done((bf16[1024,128]{1,0:T(8,128)(2,1)}, bf16[1024,128]{1,0:T(8,128)(2,1)S(1)}, u32[]{:S(2)}, u32[]{:S(2)}) %collective-permute-start.31) | collective-permute-done | bytes 262176 | tf_op jit(solution)/shard_map/ppermute | solution.py:482
  160.8 0.9 copy-done.19
  161.9 1.6 copy-done.5
  163.5 1.3 slope_sum.1
  164.8 1.3 collective-permute-start.34
  166.1 2.3 %collective-permute-done.34 = f32[1,1024]{1,0:T(1,128)S(1)} collective-permute-done((f32[1,1024]{1,0:T(1,128)S(1)}, f32[1,1024]{1,0:T(1,128)S(1)}, u32[]{:S(2)}, u32[]{:S(2)}) %collective-permute-start.34) | collective-permute-done | bytes 4128 | tf_op jit(solution)/shard_map/ppermute | solution.py:486
  169.0 3.4 %finish.1 = f32[1024,1024]{1,0:T(8,128)} custom-call(s32[8]{0:T(128)S(1)} %stack.149.refs_2_.refs_1_.refs_0_, f32[1,1024]{1,0:T(1,128)S(1)} %bitcast.53, f32[8,128]{1,0:T(8,128)S(1)} %get-tuple-element.69.refs_2_, bf16[4096,128]{1,0:T(8,128)(2,1)S(1)} %pack_columns.1.refs_3_, bf16[4096,128]{1,0:T(8,128)(2,1)S(1)} %collective-permute-done.33.refs_4_), custom_call_target="tpu_custom_call" | custom-call | bytes 6299680 | tf_op jit(solution)/shard_map/finish/pallas_call | solution.py:37
  (91 shorter events, 9.0 us)
Async XLA Ops:
  2.7 11.2 %collective-permute-start.2 = (f32[1,1024]{1,0:T(1,128)S(1)}, f32[1,1024]{1,0:T(1,128)S(1)}, u32[]{:S(2)}, u32[]{:S(2)}) collective-permute-start(f32[1,1024]{1,0:T(1,128)S(1)} %bitcast.55), channel_id=1, source_target_pairs={{0,12},{4,0},{8,4},{12,8},{1,13},{5,1},{9,5},{13,9},{2,14},{6,2},{... | collective-permute-start | bytes 12296 | tf_op jit(solution)/shard_map/ppermute | solution.py:53
  7.8 6.1 %collective-permute-start.1 = (f32[1,1024]{1,0:T(1,128)S(1)}, f32[1,1024]{1,0:T(1,128)S(1)}, u32[]{:S(2)}, u32[]{:S(2)}) collective-permute-start(f32[1,1024]{1,0:T(1,128)S(1)} %bitcast.56), channel_id=1, source_target_pairs={{0,8},{4,12},{8,0},{12,4},{1,9},{5,13},{9,1},{13,5},{2,10},{6,14},... | collective-permute-start | bytes 12296 | tf_op jit(solution)/shard_map/ppermute | solution.py:53
  7.8 6.1 %collective-permute-start = (f32[1,1024]{1,0:T(1,128)S(1)}, f32[1,1024]{1,0:T(1,128)S(1)}, u32[]{:S(2)}, u32[]{:S(2)}) collective-permute-start(f32[1,1024]{1,0:T(1,128)S(1)} %bitcast.57), channel_id=1, source_target_pairs={{0,4},{4,8},{8,12},{12,0},{1,5},{5,9},{9,13},{13,1},{2,6},{6,10},{... | collective-permute-start | bytes 12296 | tf_op jit(solution)/shard_map/ppermute | solution.py:53
  9.8 13.8 %collective-permute-start.3 = (bf16[128,1024]{1,0:T(8,128)(2,1)S(1)}, bf16[128,1024]{1,0:T(8,128)(2,1)S(1)}, u32[]{:S(2)}, u32[]{:S(2)}) collective-permute-start(bf16[128,1024]{1,0:T(8,128)(2,1)S(1)} %constant_dynamic-slice_fusion), channel_id=1, source_target_pairs={{0,8},{4,12},{8,0},{12,4},{1,9},{5,13},{9,1},{13,5},{2,10},{6,14},... | collective-permute-start | bytes 786440 | tf_op jit(solution)/shard_map/ppermute | solution.py:489
  13.9 3.4 %copy-start.6 = (bf16[64,16,4096]{2,1,0:T(8,128)(2,1)S(1)}, bf16[64,16,4096]{2,1,0:T(8,128)(2,1)}, u32[]{:S(2)}) copy-start(bf16[64,16,4096]{2,1,0:T(8,128)(2,1)} %param.8) | copy-start | bytes 25165828
  20.8 3.3 %copy-start = (bf16[1024,4096]{1,0:T(8,128)(2,1)}, bf16[1024,4096]{1,0:T(8,128)(2,1)S(1)}, u32[]{:S(2)}) copy-start(bf16[1024,4096]{1,0:T(8,128)(2,1)S(1)} %norm_rows.1.refs_1_.normed_ref) | copy-start | bytes 25165828
  20.8 6.8 %copy-start.24 = (s32[64,32]{0,1:T(8,128)S(1)}, s32[64,32]{0,1:T(8,128)}, u32[]{:S(2)}) copy-start(s32[64,32]{0,1:T(8,128)} %param.10) | copy-start | bytes 24580
  24.1 12.4 %collective-permute-start.7 = (bf16[128,1024]{1,0:T(8,128)(2,1)S(1)}, bf16[128,1024]{1,0:T(8,128)(2,1)S(1)}, u32[]{:S(2)}, u32[]{:S(2)}) collective-permute-start(bf16[128,1024]{1,0:T(8,128)(2,1)S(1)} %far_share.1.event_ref.refs_0_), channel_id=1, source_target_pairs={{0,18},{1,19},{2,16},{3,17},{16,2},{17,3},{18,0},{19,1},{4,22},{5,... | collective-permute-start | bytes 786440 | tf_op jit(solution)/shard_map/ppermute | solution.py:482
  26.5 11.4 %collective-permute-start.6 = (bf16[128,1024]{1,0:T(8,128)(2,1)S(1)}, bf16[128,1024]{1,0:T(8,128)(2,1)S(1)}, u32[]{:S(2)}, u32[]{:S(2)}) collective-permute-start(bf16[128,1024]{1,0:T(8,128)(2,1)S(1)} %far_share.1.event_ref.refs_0_), channel_id=1, source_target_pairs={{0,16},{1,17},{2,18},{3,19},{16,0},{17,1},{18,2},{19,3},{4,20},{5,... | collective-permute-start | bytes 786440 | tf_op jit(solution)/shard_map/ppermute | solution.py:482
  27.1 10.8 %collective-permute-start.5 = (bf16[128,1024]{1,0:T(8,128)(2,1)S(1)}, bf16[128,1024]{1,0:T(8,128)(2,1)S(1)}, u32[]{:S(2)}, u32[]{:S(2)}) collective-permute-start(bf16[128,1024]{1,0:T(8,128)(2,1)S(1)} %far_share.1.event_ref.refs_0_), channel_id=1, source_target_pairs={{0,2},{1,3},{2,0},{3,1},{16,18},{17,19},{18,16},{19,17},{4,6},{5,7... | collective-permute-start | bytes 786440 | tf_op jit(solution)/shard_map/ppermute | solution.py:482
  27.7 3.4 %copy-start.1 = (bf16[1024,4096]{1,0:T(8,128)(2,1)S(1)}, bf16[1024,4096]{1,0:T(8,128)(2,1)}, u32[]{:S(2)}) copy-start(bf16[1024,4096]{1,0:T(8,128)(2,1)} %copy-done) | copy-start | bytes 25165828
  31.1 13.0 %copy-start.7 = (bf16[1024,1024]{1,0:T(8,128)(2,1)S(1)}, bf16[1024,1024]{1,0:T(8,128)(2,1)}, u32[]{:S(2)}) copy-start(bf16[1024,1024]{1,0:T(8,128)(2,1)} %refs_0_.2) | copy-start | bytes 6291460
  36.4 10.4 %copy-start.10 = (f32[1024,1]{1,0:T(8,128)}, f32[1024,1]{1,0:T(8,128)S(1)}, u32[]{:S(2)}) copy-start(f32[1024,1]{1,0:T(8,128)S(1)} %get-tuple-element.47.curve_ref) | copy-start | bytes 12292
  36.5 10.4 %copy-start.3 = (bf16[1024,1024]{1,0:T(8,128)(2,1)S(1)}, bf16[1024,1024]{1,0:T(8,128)(2,1)}, u32[]{:S(2)}) copy-start(bf16[1024,1024]{1,0:T(8,128)(2,1)} %refs_1_.5) | copy-start | bytes 6291460
  38.0 8.8 %collective-permute-start.8 = (bf16[512,1024]{1,0:T(8,128)(2,1)S(1)}, bf16[512,1024]{1,0:T(8,128)(2,1)S(1)}, u32[]{:S(2)}, u32[]{:S(2)}) collective-permute-start(bf16[512,1024]{1,0:T(8,128)(2,1)S(1)} %pack_shares.1.refs_5_), channel_id=1, source_target_pairs={{0,1},{1,0},{2,3},{3,2},{16,17},{17,16},{18,19},{19,18},{4,5},{5,4... | collective-permute-start | bytes 3145736 | tf_op jit(solution)/shard_map/ppermute | solution.py:482
  38.1 8.7 %collective-permute-start.4 = (bf16[64,2048]{1,0:T(8,128)(2,1)S(1)}, bf16[64,2048]{1,0:T(8,128)(2,1)S(1)}, u32[]{:S(2)}, u32[]{:S(2)}) collective-permute-start(bf16[64,2048]{1,0:T(8,128)(2,1)S(1)} %get-tuple-element.39), channel_id=1, source_target_pairs={{0,4},{4,0},{8,12},{12,8},{1,5},{5,1},{9,13},{13,9},{2,6},{6,2},{1... | collective-permute-start | bytes 786440 | tf_op jit(solution)/shard_map/ppermute | solution.py:486
  39.6 3.3 %collective-permute-start.9 = (s32[64,8]{1,0:T(8,128)S(1)}, s32[64,8]{1,0:T(8,128)S(1)}, u32[]{:S(2)}, u32[]{:S(2)}) collective-permute-start(s32[64,8]{1,0:T(8,128)S(1)} %get-tuple-element.42), channel_id=1, source_target_pairs={{0,1},{1,2},{2,3},{3,0},{4,5},{5,6},{6,7},{7,4},{8,9},{9,10},{10,1... | collective-permute-start | bytes 6152 | tf_op jit(solution)/shard_map/ppermute | solution.py:53
  39.8 3.9 %collective-permute-start.10 = (s32[64,8]{1,0:T(8,128)S(1)}, s32[64,8]{1,0:T(8,128)S(1)}, u32[]{:S(2)}, u32[]{:S(2)}) collective-permute-start(s32[64,8]{1,0:T(8,128)S(1)} %get-tuple-element.43), channel_id=1, source_target_pairs={{0,2},{1,3},{2,0},{3,1},{4,6},{5,7},{6,4},{7,5},{8,10},{9,11},{10,... | collective-permute-start | bytes 6152 | tf_op jit(solution)/shard_map/ppermute | solution.py:53
  41.2 2.9 %collective-permute-start.11 = (s32[64,8]{1,0:T(8,128)S(1)}, s32[64,8]{1,0:T(8,128)S(1)}, u32[]{:S(2)}, u32[]{:S(2)}) collective-permute-start(s32[64,8]{1,0:T(8,128)S(1)} %get-tuple-element.44), channel_id=1, source_target_pairs={{0,3},{1,0},{2,1},{3,2},{4,7},{5,4},{6,5},{7,6},{8,11},{9,8},{10,9... | collective-permute-start | bytes 6152 | tf_op jit(solution)/shard_map/ppermute | solution.py:53
  46.8 37.2 %copy-start.22 = (bf16[64,1024]{1,0:T(8,128)(2,1)S(1)}, bf16[64,1024]{1,0:T(8,128)(2,1)}, u32[]{:S(2)}) copy-start(bf16[64,1024]{1,0:T(8,128)(2,1)} %refs_0_.3) | copy-start | bytes 393220
  48.2 42.0 %copy-start.4 = (bf16[1024,1024]{1,0:T(8,128)(2,1)}, bf16[1024,1024]{1,0:T(8,128)(2,1)S(1)}, u32[]{:S(2)}) copy-start(bf16[1024,1024]{1,0:T(8,128)(2,1)S(1)} %get-tuple-element.46.refs_2_) | copy-start | bytes 6291460
  48.3 8.4 %collective-permute-start.13 = (bf16[128,1024]{1,0:T(8,128)(2,1)S(1)}, bf16[128,1024]{1,0:T(8,128)(2,1)S(1)}, u32[]{:S(2)}, u32[]{:S(2)}) collective-permute-start(bf16[128,1024]{1,0:T(8,128)(2,1)S(1)} %get-tuple-element.51.refs_3_), channel_id=1, source_target_pairs={{0,2},{1,3},{2,0},{3,1},{16,18},{17,19},{18,16},{19,17},{4,6},{5,7... | collective-permute-start | bytes 786440 | tf_op jit(solution)/shard_map/ppermute | solution.py:482
  49.7 5.3 %collective-permute-start.12 = (bf16[64,1024]{1,0:T(8,128)(2,1)S(1)}, bf16[64,1024]{1,0:T(8,128)(2,1)S(1)}, u32[]{:S(2)}, u32[]{:S(2)}) collective-permute-start(bf16[64,1024]{1,0:T(8,128)(2,1)S(1)} %get-tuple-element.49), channel_id=1, source_target_pairs={{0,4},{4,0},{8,12},{12,8},{1,5},{5,1},{9,13},{13,9},{2,6},{6,2},{1... | collective-permute-start | bytes 393224 | tf_op jit(solution)/shard_map/ppermute | solution.py:486
  56.8 27.2 %copy-start.13 = (bf16[256,1024]{1,0:T(8,128)(2,1)}, bf16[256,1024]{1,0:T(8,128)(2,1)S(1)}, u32[]{:S(2)}) copy-start(bf16[256,1024]{1,0:T(8,128)(2,1)S(1)} %get-tuple-element.60.refs_3_) | copy-start | bytes 1572868
  56.8 13.2 %collective-permute-start.20 = (bf16[256,1024]{1,0:T(8,128)(2,1)S(1)}, bf16[256,1024]{1,0:T(8,128)(2,1)S(1)}, u32[]{:S(2)}, u32[]{:S(2)}) collective-permute-start(bf16[256,1024]{1,0:T(8,128)(2,1)S(1)} %get-tuple-element.60.refs_3_), channel_id=1, source_target_pairs={{0,16},{1,17},{2,18},{3,19},{16,0},{17,1},{18,2},{19,3},{4,20},{5,... | collective-permute-start | bytes 1572872 | tf_op jit(solution)/shard_map/ppermute | solution.py:482
  58.4 4.4 %collective-permute-start.16 = (bf16[64,1024]{1,0:T(8,128)(2,1)S(1)}, bf16[64,1024]{1,0:T(8,128)(2,1)S(1)}, u32[]{:S(2)}, u32[]{:S(2)}) collective-permute-start(bf16[64,1024]{1,0:T(8,128)(2,1)S(1)} %get-tuple-element.54.refs_3_), channel_id=1, source_target_pairs={{0,3},{1,0},{2,1},{3,2},{4,7},{5,4},{6,5},{7,6},{8,11},{9,8},{10,9... | collective-permute-start | bytes 393224 | tf_op jit(solution)/shard_map/ppermute | solution.py:53
  58.5 11.6 %collective-permute-start.15 = (bf16[64,1024]{1,0:T(8,128)(2,1)S(1)}, bf16[64,1024]{1,0:T(8,128)(2,1)S(1)}, u32[]{:S(2)}, u32[]{:S(2)}) collective-permute-start(bf16[64,1024]{1,0:T(8,128)(2,1)S(1)} %get-tuple-element.54.refs_3_), channel_id=1, source_target_pairs={{0,2},{1,3},{2,0},{3,1},{4,6},{5,7},{6,4},{7,5},{8,10},{9,11},{10,... | collective-permute-start | bytes 393224 | tf_op jit(solution)/shard_map/ppermute | solution.py:53
  59.8 10.3 %collective-permute-start.14 = (bf16[64,1024]{1,0:T(8,128)(2,1)S(1)}, bf16[64,1024]{1,0:T(8,128)(2,1)S(1)}, u32[]{:S(2)}, u32[]{:S(2)}) collective-permute-start(bf16[64,1024]{1,0:T(8,128)(2,1)S(1)} %get-tuple-element.54.refs_3_), channel_id=1, source_target_pairs={{0,1},{1,2},{2,3},{3,0},{4,5},{5,6},{6,7},{7,4},{8,9},{9,10},{10,1... | collective-permute-start | bytes 393224 | tf_op jit(solution)/shard_map/ppermute | solution.py:53
  60.0 15.6 %collective-permute-start.23 = (bf16[128,1024]{1,0:T(8,128)(2,1)S(1)}, bf16[128,1024]{1,0:T(8,128)(2,1)S(1)}, u32[]{:S(2)}, u32[]{:S(2)}) collective-permute-start(bf16[128,1024]{1,0:T(8,128)(2,1)S(1)} %get-tuple-element.61), channel_id=1, source_target_pairs={{0,8},{4,12},{8,0},{12,4},{1,9},{5,13},{9,1},{13,5},{2,10},{6,14},... | collective-permute-start | bytes 786440 | tf_op jit(solution)/shard_map/ppermute | solution.py:489
  62.8 21.2 %collective-permute-start.21 = (bf16[256,1024]{1,0:T(8,128)(2,1)S(1)}, bf16[256,1024]{1,0:T(8,128)(2,1)S(1)}, u32[]{:S(2)}, u32[]{:S(2)}) collective-permute-start(bf16[256,1024]{1,0:T(8,128)(2,1)S(1)} %get-tuple-element.60.refs_3_), channel_id=1, source_target_pairs={{0,1},{1,0},{2,3},{3,2},{16,17},{17,16},{18,19},{19,18},{4,5},{5,4... | collective-permute-start | bytes 1572872 | tf_op jit(solution)/shard_map/ppermute | solution.py:482
  70.1 13.9 %collective-permute-start.22 = (bf16[256,1024]{1,0:T(8,128)(2,1)S(1)}, bf16[256,1024]{1,0:T(8,128)(2,1)S(1)}, u32[]{:S(2)}, u32[]{:S(2)}) collective-permute-start(bf16[256,1024]{1,0:T(8,128)(2,1)S(1)} %collective-permute-done.20.refs_8_.refs_4_), channel_id=1, source_target_pairs={{0,1},{1,0},{2,3},{3,2},{16,17},{17,16},{18,19},{19,18},{4,5},{5,4... | collective-permute-start | bytes 1572872 | tf_op jit(solution)/shard_map/ppermute | solution.py:482
  71.5 5.1 %collective-permute-start.17 = (bf16[64,1152]{1,0:T(8,128)(2,1)S(1)}, bf16[64,1152]{1,0:T(8,128)(2,1)S(1)}, u32[]{:S(2)}, u32[]{:S(2)}) collective-permute-start(bf16[64,1152]{1,0:T(8,128)(2,1)S(1)} %get-tuple-element.57), channel_id=1, source_target_pairs={{0,3},{1,0},{2,1},{3,2},{4,7},{5,4},{6,5},{7,6},{8,11},{9,8},{10,9... | collective-permute-start | bytes 442376 | tf_op jit(solution)/shard_map/ppermute | solution.py:53
  75.7 8.3 %collective-permute-start.24 = (bf16[128,1024]{1,0:T(8,128)(2,1)S(1)}, bf16[128,1024]{1,0:T(8,128)(2,1)S(1)}, u32[]{:S(2)}, u32[]{:S(2)}) collective-permute-start(bf16[128,1024]{1,0:T(8,128)(2,1)S(1)} %collective-permute-done.23.refs_11_.refs_5_), channel_id=1, source_target_pairs={{0,16},{1,17},{2,18},{3,19},{16,0},{17,1},{18,2},{19,3},{4,20},{5,... | collective-permute-start | bytes 786440 | tf_op jit(solution)/shard_map/ppermute | solution.py:482
  76.2 6.7 %collective-permute-start.18 = (bf16[64,1152]{1,0:T(8,128)(2,1)S(1)}, bf16[64,1152]{1,0:T(8,128)(2,1)S(1)}, u32[]{:S(2)}, u32[]{:S(2)}) collective-permute-start(bf16[64,1152]{1,0:T(8,128)(2,1)S(1)} %get-tuple-element.58), channel_id=1, source_target_pairs={{0,2},{1,3},{2,0},{3,1},{4,6},{5,7},{6,4},{7,5},{8,10},{9,11},{10,... | collective-permute-start | bytes 442376 | tf_op jit(solution)/shard_map/ppermute | solution.py:53
  76.6 6.7 %collective-permute-start.19 = (bf16[64,1152]{1,0:T(8,128)(2,1)S(1)}, bf16[64,1152]{1,0:T(8,128)(2,1)S(1)}, u32[]{:S(2)}, u32[]{:S(2)}) collective-permute-start(bf16[64,1152]{1,0:T(8,128)(2,1)S(1)} %get-tuple-element.59), channel_id=1, source_target_pairs={{0,1},{1,2},{2,3},{3,0},{4,5},{5,6},{6,7},{7,4},{8,9},{9,10},{10,1... | collective-permute-start | bytes 442376 | tf_op jit(solution)/shard_map/ppermute | solution.py:53
  84.0 8.4 %copy-start.8 = (bf16[256,1024]{1,0:T(8,128)(2,1)}, bf16[256,1024]{1,0:T(8,128)(2,1)S(1)}, u32[]{:S(2)}) copy-start(bf16[256,1024]{1,0:T(8,128)(2,1)S(1)} %collective-permute-done.22.refs_10_.refs_8_) | copy-start | bytes 1572868
  84.5 0.8 copy-start.12
  85.3 5.0 %collective-permute-start.25 = (bf16[64,1024]{1,0:T(8,128)(2,1)S(1)}, bf16[64,1024]{1,0:T(8,128)(2,1)S(1)}, u32[]{:S(2)}, u32[]{:S(2)}) collective-permute-start(bf16[64,1024]{1,0:T(8,128)(2,1)S(1)} %get-tuple-element.63.refs_3_), channel_id=1, source_target_pairs={{0,4},{4,0},{8,12},{12,8},{1,5},{5,1},{9,13},{13,9},{2,6},{6,2},{1... | collective-permute-start | bytes 393224 | tf_op jit(solution)/shard_map/ppermute | solution.py:486
  92.4 0.7 copy-start.20
  93.2 32.7 %collective-permute-start.27 = (bf16[256,1024]{1,0:T(8,128)(2,1)}, bf16[256,1024]{1,0:T(8,128)(2,1)}, u32[]{:S(2)}, u32[]{:S(2)}) collective-permute-start(bf16[256,1024]{1,0:T(8,128)(2,1)} %get-tuple-element.67.refs_5_), channel_id=1, source_target_pairs={{0,2},{1,3},{2,0},{3,1},{16,18},{17,19},{18,16},{19,17},{4,6},{5,7... | collective-permute-start | bytes 1572872 | tf_op jit(solution)/shard_map/ppermute | solution.py:482
  93.6 34.9 %all-to-all-start = ((bf16[32,64,128]{2,1,0:T(8,128)(2,1)}), bf16[32,64,128]{2,1,0:T(8,128)(2,1)}, u32[]{:S(2)}, u32[]{:S(2)}) async-start(bf16[32,64,128]{2,1,0:T(8,128)(2,1)} %copy-done.12), calls=%async_computation | async-start | bytes 1048576 | tf_op jit(solution)/shard_map/all_to_all | solution.py:594
  98.0 16.6 %collective-permute-start.26 = (bf16[64,2048]{1,0:T(8,128)(2,1)S(1)}, bf16[64,2048]{1,0:T(8,128)(2,1)S(1)}, u32[]{:S(2)}, u32[]{:S(2)}) collective-permute-start(bf16[64,2048]{1,0:T(8,128)(2,1)S(1)} %get-tuple-element.65), channel_id=1, source_target_pairs={{0,4},{4,0},{8,12},{12,8},{1,5},{5,1},{9,13},{13,9},{2,6},{6,2},{1... | collective-permute-start | bytes 786440 | tf_op jit(solution)/shard_map/ppermute | solution.py:486
  99.6 28.1 %collective-permute-start.28 = (bf16[256,1024]{1,0:T(8,128)(2,1)}, bf16[256,1024]{1,0:T(8,128)(2,1)S(1)}, u32[]{:S(2)}, u32[]{:S(2)}) collective-permute-start(bf16[256,1024]{1,0:T(8,128)(2,1)} %get-tuple-element.67.refs_5_), channel_id=1, source_target_pairs={{0,1},{1,0},{2,3},{3,2},{16,17},{17,16},{18,19},{19,18},{4,5},{5,4... | collective-permute-start | bytes 1572872 | tf_op jit(solution)/shard_map/ppermute | solution.py:482
  114.6 3.4 %copy-start.2 = (bf16[1024,4096]{1,0:T(8,128)(2,1)S(1)}, bf16[1024,4096]{1,0:T(8,128)(2,1)}, u32[]{:S(2)}) copy-start(bf16[1024,4096]{1,0:T(8,128)(2,1)} %copy-done) | copy-start | bytes 25165828
  118.0 1.0 copy-start.11
  119.0 0.9 copy-start.21
  127.7 2.3 %collective-permute-start.29 = (bf16[256,1024]{1,0:T(8,128)(2,1)}, bf16[256,1024]{1,0:T(8,128)(2,1)}, u32[]{:S(2)}, u32[]{:S(2)}) collective-permute-start(bf16[256,1024]{1,0:T(8,128)(2,1)} %late.1), channel_id=1, source_target_pairs={{0,1},{1,0},{2,3},{3,2},{16,17},{17,16},{18,19},{19,18},{4,5},{5,4... | collective-permute-start | bytes 1572872 | tf_op jit(solution)/shard_map/ppermute | solution.py:482
  127.7 0.8 copy-start.15
  130.0 1.0 copy-start.9
  131.0 1.0 copy-start.14
  132.1 1.0 copy-start.16
  135.5 0.8 copy-start.17
  136.3 0.7 copy-start.18
  137.0 32.0 %copy-start.23 = (f32[1024]{0:T(1024)S(1)}, f32[1024]{0:T(1024)}, u32[]{:S(2)}) copy-start(f32[1024]{0:T(1024)} %param.14) | copy-start | bytes 12292
  137.0 23.8 %all-to-all-start.1 = ((f32[32,24,128]{2,1,0:T(8,128)}), f32[32,24,128]{2,1,0:T(8,128)S(1)}, u32[]{:S(2)}, u32[]{:S(2)}) async-start(f32[32,24,128]{2,1,0:T(8,128)} %copy-done.17), calls=%async_computation.1 | async-start | bytes 786432 | tf_op jit(solution)/shard_map/all_to_all | solution.py:619
  141.6 14.3 %collective-permute-start.32 = (bf16[1024,128]{1,0:T(8,128)(2,1)}, bf16[1024,128]{1,0:T(8,128)(2,1)S(1)}, u32[]{:S(2)}, u32[]{:S(2)}) collective-permute-start(bf16[1024,128]{1,0:T(8,128)(2,1)} %copy-done.18), channel_id=1, source_target_pairs={{0,18},{1,19},{2,16},{3,17},{16,2},{17,3},{18,0},{19,1},{4,22},{5,... | collective-permute-start | bytes 786440 | tf_op jit(solution)/shard_map/ppermute | solution.py:482
  144.4 15.8 %collective-permute-start.31 = (bf16[1024,128]{1,0:T(8,128)(2,1)}, bf16[1024,128]{1,0:T(8,128)(2,1)S(1)}, u32[]{:S(2)}, u32[]{:S(2)}) collective-permute-start(bf16[1024,128]{1,0:T(8,128)(2,1)} %copy-done.18), channel_id=1, source_target_pairs={{0,16},{1,17},{2,18},{3,19},{16,0},{17,1},{18,2},{19,3},{4,20},{5,... | collective-permute-start | bytes 786440 | tf_op jit(solution)/shard_map/ppermute | solution.py:482
  144.9 15.9 %collective-permute-start.30 = (bf16[1024,128]{1,0:T(8,128)(2,1)}, bf16[1024,128]{1,0:T(8,128)(2,1)S(1)}, u32[]{:S(2)}, u32[]{:S(2)}) collective-permute-start(bf16[1024,128]{1,0:T(8,128)(2,1)} %copy-done.18), channel_id=1, source_target_pairs={{0,2},{1,3},{2,0},{3,1},{16,18},{17,19},{18,16},{19,17},{4,6},{5,7... | collective-permute-start | bytes 786440 | tf_op jit(solution)/shard_map/ppermute | solution.py:482
  160.8 1.0 copy-start.19
  161.8 7.2 %collective-permute-start.33 = (bf16[4096,128]{1,0:T(8,128)(2,1)S(1)}, bf16[4096,128]{1,0:T(8,128)(2,1)S(1)}, u32[]{:S(2)}, u32[]{:S(2)}) collective-permute-start(bf16[4096,128]{1,0:T(8,128)(2,1)S(1)} %pack_columns.1.refs_3_), channel_id=1, source_target_pairs={{0,1},{1,0},{2,3},{3,2},{16,17},{17,16},{18,19},{19,18},{4,5},{5,4... | collective-permute-start | bytes 3145736 | tf_op jit(solution)/shard_map/ppermute | solution.py:482
  161.9 1.6 copy-start.5
  164.8 3.6 %collective-permute-start.34 = (f32[1,1024]{1,0:T(1,128)S(1)}, f32[1,1024]{1,0:T(1,128)S(1)}, u32[]{:S(2)}, u32[]{:S(2)}) collective-permute-start(f32[1,1024]{1,0:T(1,128)S(1)} %get-tuple-element.71), channel_id=1, source_target_pairs={{0,4},{4,0},{8,12},{12,8},{1,5},{5,1},{9,13},{13,9},{2,6},{6,2},{1... | collective-permute-start | bytes 12296 | tf_op jit(solution)/shard_map/ppermute | solution.py:486

commit v3 on v2

--- a/solution.py
+++ b/solution.py
@@ -67,7 +67,8 @@
     return lax.dot_general(left, right, (((0,), (0,)), ((), ())), preferred_element_type=F32)
 
 
-def norm_kernel(states_ref, gain_ref, normed_ref):
+def norm_kernel(states_ref, gain_ref, normed_ref, token_ref):
+    token_ref[...] = jnp.zeros_like(token_ref)
     tokens, width = states_ref.shape
     step = 4 * LANES if width % (4 * LANES) == 0 else width
     for top in range(0, tokens, 32):
@@ -90,10 +91,10 @@
     return pl.pallas_call(
         lambda *refs: norm_kernel(*refs[len(events) :]),
         grid=(tokens // block,),
-        out_shape=shape((tokens, width), BF16),
+        out_shape=[shape((tokens, width), BF16), shape((8, LANES), F32)],
         in_specs=[pl.BlockSpec(memory_space=pl.ANY)] * len(events)
         + [rows, pl.BlockSpec((1, width), lambda i: (0, 0))],
-        out_specs=rows,
+        out_specs=[rows, pl.BlockSpec((8, LANES), lambda i: (0, 0))],
         cost_estimate=pl.CostEstimate(
             flops=6 * tokens * width, bytes_accessed=4 * tokens * width, transcendentals=0
         ),
@@ -197,6 +198,21 @@
     return call(pack_kernel, [out], pieces, name, after=[event])[0]
 
 
+def pass_kernel(from_ref, to_ref):
+    to_ref[...] = from_ref[...]
+
+
+def passed(values, name, event):
+    return call(pass_kernel, [shape(values.shape, values.dtype)], [values], name, after=[event])[0]
+
+
+def add_kernel(*refs):
+    total = refs[0][...]
+    for ref in refs[1:-1]:
+        total = total + ref[...]
+    refs[-1][...] = total
+
+
 def forward_kernel(n, packs, side_ref, places_ref, weight_ref, *refs):
     refs = refs[:n] + (weight_ref,) + refs[n:]
     pieces, shares = refs[:n], refs[n + 1 : n + 1 + packs]
@@ -400,9 +416,8 @@
     )(z, normed, curve, loss, *backs)
 
 
-def columns_kernel(n, order_ref, slopes_ref, grads_ref, *refs):
-    pieces, (out_ref, pass_ref, sorted_ref) = refs[:n], refs[n:]
-    pass_ref[...] = slopes_ref[...]
+def columns_kernel(n, order_ref, grads_ref, *refs):
+    pieces, (out_ref, sorted_ref) = refs[:n], refs[n:]
     chunk = grads_ref.shape[1]
     for j in range(sorted_ref.shape[0] // chunk):
         sorted_ref[j * chunk : (j + 1) * chunk, :] = grads_ref[order_ref[j]]
@@ -438,7 +453,8 @@
 
 
 def finish_kernel(n, place_ref, pool_ref, slope_ref, *refs):
-    pieces, out_ref = refs[:n], refs[-1]
+    pieces, out_ref, token_ref = refs[:n], refs[-2], refs[-1]
+    token_ref[...] = jnp.zeros_like(token_ref)
     places = place_ref.shape[0]
     rows, cols = out_ref.shape[0], pieces[0].shape[1]
     for line in range(rows // LANES):
@@ -528,12 +544,12 @@
     both_arr, base_arr = ints(z, i), ints(i * slab.shape[0])
     token_lengths = jnp.broadcast_to(lengths[:, None], (queries, seq)).reshape(-1, 1)
     events = [u, token_lengths, share_places, ranks, both_arr, base_arr, side_arr]
-    normed = norm_rows(
+    normed, normed_token = norm_rows(
         events, hidden_states.reshape(-1, width),
         norm_gain.astype(F32).reshape(1, width)
     )
 
-    far_share = pack([far_share], "far_share", normed)
+    far_share = pack([far_share], "far_share", normed_token)
     chip_shares = [far_share if dg == dh == 0 else plane_shift(far_share, dg, dh, 0) for dg, dh in chips]
     gate_outs = gate_rows(
         both_arr, normed, u, token_lengths, negatives, far_share, seq, root, n_z, n_i
@@ -591,7 +607,6 @@
         after=near_far + near_cores + sum(near_far_cores, []) + others,
     )
 
-    all_columns = lax.all_to_all(grad_columns, EVERY, 0, 0, tiled=True)
     pieces = [grad] + [half_shift(grad, k) for k in range(1, half)]
     *backs, others = call(
         functools.partial(back_kernel, half, n_g),
@@ -600,6 +615,9 @@
         flops=4 * half * queries * depth * proj_width, smem=1,
     )
     backs = [backs[0]] + [half_shift(backs[k], -k) for k in range(1, half)]
+    all_columns = lax.all_to_all(
+        passed(grad_columns, "columns_out", backs[-1]), EVERY, 0, 0, tiled=True
+    )
     slopes = slope_rows(both_arr, normed, curve, loss, backs, seq, n_z, n_all, n_plane)
     across = [plane_shift(others, 0, dh, 0) for dh in range(1, n_h)]
     late = [pack([array], "late", slopes) for array in across]
@@ -610,24 +628,29 @@
         else:
             spread += [near_cores[dc - 1], *near_far_cores[dc - 1]]
             spread += [plane_shift(array, 0, 0, dc) for array in [others, *late]]
-    block_columns, slopes = call(
-        functools.partial(columns_kernel, len(spread)), [shape((depth, cols), BF16), shape(slopes.shape, F32)],
-        [ranks, slopes, all_columns] + spread, "grad_columns",
+    block_columns = call(
+        functools.partial(columns_kernel, len(spread)), [shape((depth, cols), BF16)],
+        [ranks, all_columns] + spread, "grad_columns",
         flops=2 * n_all * queries * depth * cols, scratch=[pltpu.VMEM((n_all * queries, cols), BF16)], smem=1,
-    )
+    )[0]
     on_chips = [block_columns if dg == dh == 0 else plane_shift(block_columns, dg, dh, 0) for dg, dh in chips]
+    slopes = passed(slopes, "slopes_out", on_chips[1 % len(on_chips)])
     all_slopes = lax.all_to_all(slopes, EVERY, 0, 0, tiled=True)
     query_part, my_slope, loss_total = call(
         query_kernel,
         [shape((1, proj_width), F32), shape((depth // LANES, LANES), F32), shape((1, LANES), F32)],
         [side_arr, proj_weight, mirror, all_slopes], "slope_sum", smem=1,
     )
-    finished = [pack(on_chips, "pack_columns", all_slopes)]
+    finished = [pack(on_chips, "pack_columns", slopes)]
     finished += [plane_shift(finished[0], 0, 0, dc) for dc in range(1, n_c)]
-    grad_query = query_part + sum(half_shift(query_part, k) for k in range(1, half))
-    grad_proj = call(
-        functools.partial(finish_kernel, len(finished)), [shape((depth, proj_width), F32)],
+    query_parts = [query_part] + [half_shift(query_part, k) for k in range(1, half)]
+    grad_proj, finish_token = call(
+        functools.partial(finish_kernel, len(finished)),
+        [shape((depth, proj_width), F32), shape((8, LANES), F32)],
         [share_places, pool_query.reshape(1, -1), my_slope] + finished, "finish", smem=1,
+    )
+    grad_query = call(
+        add_kernel, [shape((1, proj_width), F32)], query_parts, "query_sum", after=[finish_token]
     )[0]
     mean_loss = loss_total[0, 0] / (queries * n_all)
     return (grad_proj, grad_query.reshape(proj_width), mean_loss)

time: 174 us -> 170 us (0.977)
  waiting for transfers between devices: 67.5 us -> 47.6 us
  blocking collectives: 0 us -> 18.7 us
  starting transfers between devices: 44.8 us -> 39.1 us
  local copies, waits for them, and re-layouts: 24.4 us -> 27.6 us
    all_to_all x0 -> x1, blocking collectives: none -> 18.7 us  [body(): all_slopes = lax.all_to_all(slopes, EVERY, 0, 0, tiled=True)]
    ppermute x5, waiting for transfers between devices: 27 us -> 15 us  [half_shift(): return lax.ppermute(values, 'fsdp', pairs)]
    ppermute x16, waiting for transfers between devices: 26.8 us -> 21.5 us  [plane_shift(): return lax.ppermute(values, PLANE, pairs)]
    all_to_all x2 -> x1, starting transfers between devices: 9.02 us -> 3.86 us  [body(): lax.all_to_all(passed(grad_columns, 'columns_out', backs[-1]), EVERY, 0,...]
    unnamed x51 -> x53, local copies, waits for them, and re-layouts: 22.2 us -> 25.3 us
    ppermute x2, waiting for transfers between devices: 5.43 us -> 2.66 us  [mirror_shift(): lax.ppermute(values, 'fsdp', [(a, (a + half) % n_z) for a in range(n_z)])]
    ppermute x5, starting transfers between devices: 5.87 us -> 4.1 us  [half_shift(): return lax.ppermute(values, 'fsdp', pairs)]
    pallas_call x13 -> x16, Pallas kernels: 16.5 us -> 16.4 us  [call(): pl.pallas_call(run, out_shape=outs, in_specs=[SMEM] * smem + [VMEM] * (co...]
  transfers between devices with their start and end apart: 37 -> 36, of which waited for: 20 -> 17; matrix products, arithmetic and copies ran while one was open for 2% -> 2% of each run, Pallas kernels for 12% -> 14%
where the time goes in v3:
time: 170 us; the launch traced here: 169 us
  waiting for transfers between devices  47.6 us (28%)
  starting transfers between devices  39.1 us (23%)
  Pallas kernels  31 us (18%)
  local copies, waits for them, and re-layouts  27.6 us (16%)
  blocking collectives  18.7 us (11%)
  other arithmetic  2.85 us (2%)
  between operations  2.2 us (1%)
    unnamed x53, local copies, waits for them, and re-layouts  25.3 us
    ppermute x16, waiting for transfers between devices, plane_shift(): return lax.ppermute(values, PLANE, pairs)  21.5 us
    all_to_all x1, blocking collectives, body(): all_slopes = lax.all_to_all(slopes, EVERY, 0, 0, tiled=True)  18.7 us
    pallas_call x16, Pallas kernels, call(): pl.pallas_call(run, out_shape=outs, in_specs=[SMEM] * smem + [VMEM] * (co...  16.4 us
    ppermute x5, waiting for transfers between devices, half_shift(): return lax.ppermute(values, 'fsdp', pairs)  15 us
    ppermute x16, starting transfers between devices, plane_shift(): return lax.ppermute(values, PLANE, pairs)  13.9 us
    ppermute x12, starting transfers between devices, shift(): return lax.ppermute(values, axis, [(i, (i + k) % n) for i in range(n)])  12.6 us
    ppermute x12, waiting for transfers between devices, shift(): return lax.ppermute(values, axis, [(i, (i + k) % n) for i in range(n)])  8.42 us
  transfers between devices with their start and end apart: 36, of which 17 were waited for; matrix products, arithmetic and copies ran while one was open for 2% of the time, Pallas kernels for 14%

profile of v3, /device:TPU:0, one launch (start us, length us, event | category | flops | bytes accessed | tf_op | source)
XLA Modules:
  0.0 169.0 jit_solution(13051939294774807892)
XLA Ops:
  0.6 2.1 %multiply_reduce_fusion = f32[1024]{0:T(1024)S(1)} fusion(bf16[1024,1024]{1,0:T(8,128)(2,1)} %refs_1_.5, f32[1024]{0:T(1024)} %param.14), kind=kLoop, calls=%fused_computation | loop fusion | flops 3144704 | bytes 2105344 | tf_op jit(solution)/shard_map/reduce_sum | solution.py:520
  2.7 5.1 %collective-permute-start.2 = (f32[1,1024]{1,0:T(1,128)S(1)}, f32[1,1024]{1,0:T(1,128)S(1)}, u32[]{:S(2)}, u32[]{:S(2)}) collective-permute-start(f32[1,1024]{1,0:T(1,128)S(1)} %bitcast.55), channel_id=1, source_target_pairs={{0,12},{4,0},{8,4},{12,8},{1,13},{5,1},{9,5},{13,9},{2,14},{6,2},{... | collective-permute-start | bytes 12296 | tf_op jit(solution)/shard_map/ppermute | solution.py:53
  7.8 1.0 collective-permute-start
  8.8 1.0 constant_dynamic-slice_fusion
  9.8 2.0 %collective-permute-start.3 = (bf16[128,1024]{1,0:T(8,128)(2,1)S(1)}, bf16[128,1024]{1,0:T(8,128)(2,1)S(1)}, u32[]{:S(2)}, u32[]{:S(2)}) collective-permute-start(bf16[128,1024]{1,0:T(8,128)(2,1)S(1)} %constant_dynamic-slice_fusion), channel_id=1, source_target_pairs={{0,8},{4,12},{8,0},{12,4},{1,9},{5,13},{9,1},{13,5},{2,10},{6,14},... | collective-permute-start | bytes 786440 | tf_op jit(solution)/shard_map/ppermute | solution.py:505
  11.9 0.7 reshape.37
  12.6 0.7 broadcast_in_dim.5
  14.0 3.4 %copy-done.4 = bf16[64,16,4096]{2,1,0:T(8,128)(2,1)S(1)} copy-done((bf16[64,16,4096]{2,1,0:T(8,128)(2,1)S(1)}, bf16[64,16,4096]{2,1,0:T(8,128)(2,1)}, u32[]{:S(2)}) %copy-start.4) | copy-done | bytes 8388632
  17.3 3.4 %norm_rows.1 = (bf16[1024,4096]{1,0:T(8,128)(2,1)S(1)}, f32[8,128]{1,0:T(8,128)S(1)}) custom-call(f32[1,4096]{1,0:T(1,128)S(1)} %constant_dynamic-update-slice_fusion.refs_0_.u_ref, s32[1024,1]{1,0:T(8,128)S(1)} %reshape.39.refs_1_.len_ref, s32[8]{0:T(128)S(1)} %stack.149.refs_2_.refs_1_.refs_0_, s32[32]{0:T(128)S(1)} %stack.186.refs_3_.refs_0_, ...), custom_call_target="tpu_custom_call" | custom-call | flops 25165824 | bytes 16777216 | tf_op jit(solution)/shard_map/norm_rows/pallas_call | solution.py:91
  20.8 3.3 %copy-done.1 = bf16[1024,4096]{1,0:T(8,128)(2,1)} copy-done((bf16[1024,4096]{1,0:T(8,128)(2,1)}, bf16[1024,4096]{1,0:T(8,128)(2,1)S(1)}, u32[]{:S(2)}) %copy-start.1) | copy-done | bytes 8388632
  24.1 2.5 %collective-permute-start.7 = (bf16[128,1024]{1,0:T(8,128)(2,1)S(1)}, bf16[128,1024]{1,0:T(8,128)(2,1)S(1)}, u32[]{:S(2)}, u32[]{:S(2)}) collective-permute-start(bf16[128,1024]{1,0:T(8,128)(2,1)S(1)} %far_share.1.event_ref.refs_0_), channel_id=1, source_target_pairs={{0,18},{1,19},{2,16},{3,17},{16,2},{17,3},{18,0},{19,1},{4,22},{5,... | collective-permute-start | bytes 786440 | tf_op jit(solution)/shard_map/ppermute | solution.py:498
  27.8 3.4 %copy-done.2 = bf16[1024,4096]{1,0:T(8,128)(2,1)S(1)} copy-done((bf16[1024,4096]{1,0:T(8,128)(2,1)S(1)}, bf16[1024,4096]{1,0:T(8,128)(2,1)}, u32[]{:S(2)}) %copy-start.2) | copy-done | bytes 8388632
  31.1 5.4 %gate_rows.1 = (bf16[64,2048]{1,0:T(8,128)(2,1)S(1)}, bf16[64,2048]{1,0:T(8,128)(2,1)S(1)}, f32[1024,1]{1,0:T(8,128)S(1)}, f32[1024,1]{1,0:T(8,128)S(1)}, s32[64...) custom-call(s32[2]{0:T(128)S(1)} %pad_add_fusion.refs_4_.z_ref, ...), custom_call_target="tpu_custom_call" | custom-call | flops 16777216 | bytes 8388608 | tf_op jit(solution)/shard_map/gate_rows/pallas_call | solution.py:166
  36.5 0.8 copy-done.13
  38.2 1.5 collective-permute-start.4
  39.9 1.4 collective-permute-start.10
  41.3 1.3 collective-permute-start.11
  43.0 0.7 collective-permute-done.10.refs_4_
  44.2 1.8 %list_counts.1 = (f32[256,1024]{1,0:T(8,128)S(1)}, f32[1,1024]{1,0:T(1,128)S(1)}) custom-call(s32[1]{0:T(128)} %bitcast.45.refs_5_.refs_0_, bf16[1024,1024]{1,0:T(8,128)(2,1)S(1)} %copy-done.9, s32[64,8]{1,0:T(8,128)S(1)} %get-tuple-element.45.refs_2_, s32[64,8]{1,0:T(8,128)S(1)} %collective-permute-done.9.refs_3_, ...), custom_call_target="tpu_custom_call" | custom-call | bytes 3158020 | tf_op jit(solution)/shard_map/list_counts/pallas_call | solution.py:37
  46.0 0.9 collective-permute-done.4.refs_4_
  46.9 1.4 forward.1
  48.3 1.5 collective-permute-start.13
  49.8 1.5 collective-permute-start.12
  51.3 3.8 %collective-permute-done.12.refs_1_ = bf16[64,1024]{1,0:T(8,128)(2,1)S(1)} collective-permute-done((bf16[64,1024]{1,0:T(8,128)(2,1)S(1)}, bf16[64,1024]{1,0:T(8,128)(2,1)S(1)}, u32[]{:S(2)}, u32[]{:S(2)}) %collective-permute-start.12) | collective-permute-done | bytes 131104 | tf_op jit(solution)/shard_map/ppermute | solution.py:502
  55.1 1.7 collective-permute-done.13.refs_4_
  56.9 1.6 collective-permute-start.20
  58.6 1.3 collective-permute-start.15
  60.1 2.7 %collective-permute-start.23 = (bf16[128,1024]{1,0:T(8,128)(2,1)S(1)}, bf16[128,1024]{1,0:T(8,128)(2,1)S(1)}, u32[]{:S(2)}, u32[]{:S(2)}) collective-permute-start(bf16[128,1024]{1,0:T(8,128)(2,1)S(1)} %get-tuple-element.65), channel_id=1, source_target_pairs={{0,8},{4,12},{8,0},{12,4},{1,9},{5,13},{9,1},{13,5},{2,10},{6,14},... | collective-permute-start | bytes 786440 | tf_op jit(solution)/shard_map/ppermute | solution.py:505
  62.8 1.4 collective-permute-start.21
  64.2 6.0 %collective-permute-done.20.refs_8_.refs_3_ = bf16[256,1024]{1,0:T(8,128)(2,1)S(1)} collective-permute-done((bf16[256,1024]{1,0:T(8,128)(2,1)S(1)}, bf16[256,1024]{1,0:T(8,128)(2,1)S(1)}, u32[]{:S(2)}, u32[]{:S(2)}) %collective-permute-start.20) | collective-permute-done | bytes 524320 | tf_op jit(solution)/shard_map/ppermute | solution.py:498
  70.2 1.4 contrast.1
  71.6 1.6 collective-permute-start.17
  73.1 2.7 %collective-permute-done.23.refs_11_.refs_5_ = bf16[128,1024]{1,0:T(8,128)(2,1)S(1)} collective-permute-done((bf16[128,1024]{1,0:T(8,128)(2,1)S(1)}, bf16[128,1024]{1,0:T(8,128)(2,1)S(1)}, u32[]{:S(2)}, u32[]{:S(2)}) %collective-permute-start.23) | collective-permute-done | bytes 262176 | tf_op jit(solution)/shard_map/ppermute | solution.py:505
  76.7 6.4 %collective-permute-done.18.refs_6_ = bf16[64,1152]{1,0:T(8,128)(2,1)S(1)} collective-permute-done((bf16[64,1152]{1,0:T(8,128)(2,1)S(1)}, bf16[64,1152]{1,0:T(8,128)(2,1)S(1)}, u32[]{:S(2)}, u32[]{:S(2)}) %collective-permute-start.18) | collective-permute-done | bytes 147488 | tf_op jit(solution)/shard_map/ppermute | solution.py:53
  84.7 5.0 %collective-permute-done.25.refs_4_ = bf16[64,1024]{1,0:T(8,128)(2,1)S(1)} collective-permute-done((bf16[64,1024]{1,0:T(8,128)(2,1)S(1)}, bf16[64,1024]{1,0:T(8,128)(2,1)S(1)}, u32[]{:S(2)}, u32[]{:S(2)}) %collective-permute-start.25) | collective-permute-done | bytes 131104 | tf_op jit(solution)/shard_map/ppermute | solution.py:502
  89.6 2.2 %backward.1 = (bf16[64,2048]{1,0:T(8,128)(2,1)S(1)}, bf16[64,2048]{1,0:T(8,128)(2,1)S(1)}, bf16[256,1024]{1,0:T(8,128)(2,1)}) custom-call(s32[1]{0:T(128)} %bitcast.9.refs_6_.refs_0_, bf16[1024,1024]{1,0:T(8,128)(2,1)S(1)} %copy-done, bf16[1024,1024]{1,0:T(8,128)(2,1)S(1)} %get-tuple-element.50.refs_2_, bf16[64,1024]{1,0:T(8,128)(2,1)S(1)} %get-tuple-element.67.refs_3_, ...), custom_call_target="tpu_custom_call" | custom-call | flops 536870912 | bytes 6029316 | tf_op jit(solution)/shard_map/backward/pallas_call | solution.py:37
  91.8 0.7 copy-done.21
  92.5 1.0 collective-permute-start.27
  93.6 5.4 %collective-permute-done.26.rest_1_.refs_1_ = bf16[64,2048]{1,0:T(8,128)(2,1)S(1)} collective-permute-done((bf16[64,2048]{1,0:T(8,128)(2,1)S(1)}, bf16[64,2048]{1,0:T(8,128)(2,1)S(1)}, u32[]{:S(2)}, u32[]{:S(2)}) %collective-permute-start.26) | collective-permute-done | bytes 262176 | tf_op jit(solution)/shard_map/ppermute | solution.py:502
  99.0 0.8 copy-done.10
  99.8 0.7 copy-done.11
  100.5 3.9 %all-to-all-start = ((bf16[32,64,128]{2,1,0:T(8,128)(2,1)}), bf16[32,64,128]{2,1,0:T(8,128)(2,1)}, u32[]{:S(2)}, u32[]{:S(2)}) async-start(bf16[32,64,128]{2,1,0:T(8,128)(2,1)} %copy-done.10), calls=%async_computation | async-start | bytes 1048576 | tf_op jit(solution)/shard_map/all_to_all | solution.py:618
  104.4 3.4 %copy-done.3 = bf16[1024,4096]{1,0:T(8,128)(2,1)S(1)} copy-done((bf16[1024,4096]{1,0:T(8,128)(2,1)S(1)}, bf16[1024,4096]{1,0:T(8,128)(2,1)}, u32[]{:S(2)}) %copy-start.3) | copy-done | bytes 8388632
  107.8 0.9 copy-done.12
  108.8 1.0 copy-done.14
  109.8 0.9 copy-done.22
  110.8 5.8 %slope_rows.1.refs_1_.refs_0_ = f32[32,24,128]{2,1,0:T(8,128)S(1)} custom-call(s32[2]{0:T(128)S(1)} %pad_add_fusion.refs_4_.z_ref, bf16[1024,4096]{1,0:T(8,128)(2,1)S(1)} %copy-done.3, f32[1024,1]{1,0:T(8,128)S(1)} %copy-done.14, f32[1,128]{1,0:T(1,128)S(1)} %get-tuple-element.66.loss_ref, bf16[64,2048]{1,0:T(8,128)(2,1)S(1)} %copy-done.22, ...), custom_call_target="tpu_custom_call" | custom-call | flops 16777216 | bytes 8388608 | tf_op jit(solution)/shard_map/slope_rows/pallas_call | solution.py:398
  116.6 1.1 late.1
  118.3 0.8 copy-done.17
  119.1 0.7 collective-permute-done.29.refs_9_
  119.8 0.8 copy-done.19
  120.6 1.0 copy-done.8
  121.6 1.0 copy-done.16
  122.7 1.0 copy-done.18
  123.7 1.0 copy-done.20
  124.8 2.4 %grad_columns.1.refs_0_ = bf16[1024,128]{1,0:T(8,128)(2,1)S(1)} custom-call(s32[32]{0:T(128)S(1)} %stack.186.refs_3_.refs_0_, bf16[32,64,128]{2,1,0:T(8,128)(2,1)} %all-to-all-done.refs_1_, bf16[256,1024]{1,0:T(8,128)(2,1)S(1)} %copy-done.16, bf16[256,1024]{1,0:T(8,128)(2,1)S(1)} %collective-permute-done.20.refs_8_.refs_3_, ...), custom_call_target="tpu_custom_call" | custom-call | flops 536870912 | bytes 4980864 | tf_op jit(solution)/shard_map/grad_columns/pallas_call | solution.py:37
  127.2 1.6 collective-permute-start.30
  128.8 1.5 collective-permute-start.32
  130.7 10.7 %collective-permute-done.30.refs_1_ = bf16[1024,128]{1,0:T(8,128)(2,1)S(1)} collective-permute-done((bf16[1024,128]{1,0:T(8,128)(2,1)S(1)}, bf16[1024,128]{1,0:T(8,128)(2,1)S(1)}, u32[]{:S(2)}, u32[]{:S(2)}) %collective-permute-start.30) | collective-permute-done | bytes 262176 | tf_op jit(solution)/shard_map/ppermute | solution.py:498
  141.5 1.2 collective-permute-done.31.refs_2_
  142.8 18.7 %all_to_all.10.refs_3_ = f32[32,24,128]{2,1,0:T(8,128)S(1)} all-to-all(f32[32,24,128]{2,1,0:T(8,128)S(1)} %slopes_out.1.refs_4_), channel_id=1, replica_groups=mesh['grp'=2,'fsdp'=4,'item'=4] {'fsdp','grp','item'}, dimensions={0} | all-to-all | bytes 786432 | tf_op jit(solution)/shard_map/all_to_all | solution.py:638
  161.5 1.3 slope_sum.1
  162.8 1.0 collective-permute-start.34
  163.9 3.4 %finish.1 = (f32[1024,1024]{1,0:T(8,128)}, f32[8,128]{1,0:T(8,128)S(1)}) custom-call(s32[8]{0:T(128)S(1)} %stack.149.refs_2_.refs_1_.refs_0_, f32[1,1024]{1,0:T(1,128)S(1)} %bitcast.53, f32[8,128]{1,0:T(8,128)S(1)} %get-tuple-element.72.refs_2_, bf16[4096,128]{1,0:T(8,128)(2,1)S(1)} %pack_columns.1.refs_3_, bf16[4096,128]{1,0:T(8,128)(2,1)S(1)} %collective-permute-done.33.refs_4_), custom_call_target="tpu_custom_call" | custom-call | bytes 6303776 | tf_op jit(solution)/shard_map/finish/pallas_call | solution.py:37
  (94 shorter events, 8.5 us)
Async XLA Ops:
  2.7 11.2 %collective-permute-start.2 = (f32[1,1024]{1,0:T(1,128)S(1)}, f32[1,1024]{1,0:T(1,128)S(1)}, u32[]{:S(2)}, u32[]{:S(2)}) collective-permute-start(f32[1,1024]{1,0:T(1,128)S(1)} %bitcast.55), channel_id=1, source_target_pairs={{0,12},{4,0},{8,4},{12,8},{1,13},{5,1},{9,5},{13,9},{2,14},{6,2},{... | collective-permute-start | bytes 12296 | tf_op jit(solution)/shard_map/ppermute | solution.py:53
  7.8 6.1 %collective-permute-start.1 = (f32[1,1024]{1,0:T(1,128)S(1)}, f32[1,1024]{1,0:T(1,128)S(1)}, u32[]{:S(2)}, u32[]{:S(2)}) collective-permute-start(f32[1,1024]{1,0:T(1,128)S(1)} %bitcast.56), channel_id=1, source_target_pairs={{0,8},{4,12},{8,0},{12,4},{1,9},{5,13},{9,1},{13,5},{2,10},{6,14},... | collective-permute-start | bytes 12296 | tf_op jit(solution)/shard_map/ppermute | solution.py:53
  7.8 6.1 %collective-permute-start = (f32[1,1024]{1,0:T(1,128)S(1)}, f32[1,1024]{1,0:T(1,128)S(1)}, u32[]{:S(2)}, u32[]{:S(2)}) collective-permute-start(f32[1,1024]{1,0:T(1,128)S(1)} %bitcast.57), channel_id=1, source_target_pairs={{0,4},{4,8},{8,12},{12,0},{1,5},{5,9},{9,13},{13,1},{2,6},{6,10},{... | collective-permute-start | bytes 12296 | tf_op jit(solution)/shard_map/ppermute | solution.py:53
  9.8 14.3 %collective-permute-start.3 = (bf16[128,1024]{1,0:T(8,128)(2,1)S(1)}, bf16[128,1024]{1,0:T(8,128)(2,1)S(1)}, u32[]{:S(2)}, u32[]{:S(2)}) collective-permute-start(bf16[128,1024]{1,0:T(8,128)(2,1)S(1)} %constant_dynamic-slice_fusion), channel_id=1, source_target_pairs={{0,8},{4,12},{8,0},{12,4},{1,9},{5,13},{9,1},{13,5},{2,10},{6,14},... | collective-permute-start | bytes 786440 | tf_op jit(solution)/shard_map/ppermute | solution.py:505
  13.9 3.4 %copy-start.4 = (bf16[64,16,4096]{2,1,0:T(8,128)(2,1)S(1)}, bf16[64,16,4096]{2,1,0:T(8,128)(2,1)}, u32[]{:S(2)}) copy-start(bf16[64,16,4096]{2,1,0:T(8,128)(2,1)} %param.8) | copy-start | bytes 25165828
  17.3 10.3 %copy-start.25 = (s32[64,32]{0,1:T(8,128)S(1)}, s32[64,32]{0,1:T(8,128)}, u32[]{:S(2)}) copy-start(s32[64,32]{0,1:T(8,128)} %param.10) | copy-start | bytes 24580
  20.8 3.3 %copy-start.1 = (bf16[1024,4096]{1,0:T(8,128)(2,1)}, bf16[1024,4096]{1,0:T(8,128)(2,1)S(1)}, u32[]{:S(2)}) copy-start(bf16[1024,4096]{1,0:T(8,128)(2,1)S(1)} %get-tuple-element.40.normed_ref) | copy-start | bytes 25165828
  24.1 13.2 %collective-permute-start.7 = (bf16[128,1024]{1,0:T(8,128)(2,1)S(1)}, bf16[128,1024]{1,0:T(8,128)(2,1)S(1)}, u32[]{:S(2)}, u32[]{:S(2)}) collective-permute-start(bf16[128,1024]{1,0:T(8,128)(2,1)S(1)} %far_share.1.event_ref.refs_0_), channel_id=1, source_target_pairs={{0,18},{1,19},{2,16},{3,17},{16,2},{17,3},{18,0},{19,1},{4,22},{5,... | collective-permute-start | bytes 786440 | tf_op jit(solution)/shard_map/ppermute | solution.py:498
  26.6 11.4 %collective-permute-start.6 = (bf16[128,1024]{1,0:T(8,128)(2,1)S(1)}, bf16[128,1024]{1,0:T(8,128)(2,1)S(1)}, u32[]{:S(2)}, u32[]{:S(2)}) collective-permute-start(bf16[128,1024]{1,0:T(8,128)(2,1)S(1)} %far_share.1.event_ref.refs_0_), channel_id=1, source_target_pairs={{0,16},{1,17},{2,18},{3,19},{16,0},{17,1},{18,2},{19,3},{4,20},{5,... | collective-permute-start | bytes 786440 | tf_op jit(solution)/shard_map/ppermute | solution.py:498
  27.2 10.8 %collective-permute-start.5 = (bf16[128,1024]{1,0:T(8,128)(2,1)S(1)}, bf16[128,1024]{1,0:T(8,128)(2,1)S(1)}, u32[]{:S(2)}, u32[]{:S(2)}) collective-permute-start(bf16[128,1024]{1,0:T(8,128)(2,1)S(1)} %far_share.1.event_ref.refs_0_), channel_id=1, source_target_pairs={{0,2},{1,3},{2,0},{3,1},{16,18},{17,19},{18,16},{19,17},{4,6},{5,7... | collective-permute-start | bytes 786440 | tf_op jit(solution)/shard_map/ppermute | solution.py:498
  27.8 3.4 %copy-start.2 = (bf16[1024,4096]{1,0:T(8,128)(2,1)S(1)}, bf16[1024,4096]{1,0:T(8,128)(2,1)}, u32[]{:S(2)}) copy-start(bf16[1024,4096]{1,0:T(8,128)(2,1)} %copy-done.1) | copy-start | bytes 25165828
  31.1 13.0 %copy-start.9 = (bf16[1024,1024]{1,0:T(8,128)(2,1)S(1)}, bf16[1024,1024]{1,0:T(8,128)(2,1)}, u32[]{:S(2)}) copy-start(bf16[1024,1024]{1,0:T(8,128)(2,1)} %refs_0_.2) | copy-start | bytes 6291460
  36.5 0.8 copy-start.13
  37.3 9.5 %copy-start = (bf16[1024,1024]{1,0:T(8,128)(2,1)S(1)}, bf16[1024,1024]{1,0:T(8,128)(2,1)}, u32[]{:S(2)}) copy-start(bf16[1024,1024]{1,0:T(8,128)(2,1)} %refs_1_.5) | copy-start | bytes 6291460
  38.1 8.8 %collective-permute-start.8 = (bf16[512,1024]{1,0:T(8,128)(2,1)S(1)}, bf16[512,1024]{1,0:T(8,128)(2,1)S(1)}, u32[]{:S(2)}, u32[]{:S(2)}) collective-permute-start(bf16[512,1024]{1,0:T(8,128)(2,1)S(1)} %pack_shares.1.refs_5_), channel_id=1, source_target_pairs={{0,1},{1,0},{2,3},{3,2},{16,17},{17,16},{18,19},{19,18},{4,5},{5,4... | collective-permute-start | bytes 3145736 | tf_op jit(solution)/shard_map/ppermute | solution.py:498
  38.2 8.7 %collective-permute-start.4 = (bf16[64,2048]{1,0:T(8,128)(2,1)S(1)}, bf16[64,2048]{1,0:T(8,128)(2,1)S(1)}, u32[]{:S(2)}, u32[]{:S(2)}) collective-permute-start(bf16[64,2048]{1,0:T(8,128)(2,1)S(1)} %get-tuple-element.43), channel_id=1, source_target_pairs={{0,4},{4,0},{8,12},{12,8},{1,5},{5,1},{9,13},{13,9},{2,6},{6,2},{1... | collective-permute-start | bytes 786440 | tf_op jit(solution)/shard_map/ppermute | solution.py:502
  39.7 3.3 %collective-permute-start.9 = (s32[64,8]{1,0:T(8,128)S(1)}, s32[64,8]{1,0:T(8,128)S(1)}, u32[]{:S(2)}, u32[]{:S(2)}) collective-permute-start(s32[64,8]{1,0:T(8,128)S(1)} %get-tuple-element.46), channel_id=1, source_target_pairs={{0,1},{1,2},{2,3},{3,0},{4,5},{5,6},{6,7},{7,4},{8,9},{9,10},{10,1... | collective-permute-start | bytes 6152 | tf_op jit(solution)/shard_map/ppermute | solution.py:53
  39.9 3.9 %collective-permute-start.10 = (s32[64,8]{1,0:T(8,128)S(1)}, s32[64,8]{1,0:T(8,128)S(1)}, u32[]{:S(2)}, u32[]{:S(2)}) collective-permute-start(s32[64,8]{1,0:T(8,128)S(1)} %get-tuple-element.47), channel_id=1, source_target_pairs={{0,2},{1,3},{2,0},{3,1},{4,6},{5,7},{6,4},{7,5},{8,10},{9,11},{10,... | collective-permute-start | bytes 6152 | tf_op jit(solution)/shard_map/ppermute | solution.py:53
  41.3 2.9 %collective-permute-start.11 = (s32[64,8]{1,0:T(8,128)S(1)}, s32[64,8]{1,0:T(8,128)S(1)}, u32[]{:S(2)}, u32[]{:S(2)}) collective-permute-start(s32[64,8]{1,0:T(8,128)S(1)} %get-tuple-element.48), channel_id=1, source_target_pairs={{0,3},{1,0},{2,1},{3,2},{4,7},{5,4},{6,5},{7,6},{8,11},{9,8},{10,9... | collective-permute-start | bytes 6152 | tf_op jit(solution)/shard_map/ppermute | solution.py:53
  46.9 37.2 %copy-start.23 = (bf16[64,1024]{1,0:T(8,128)(2,1)S(1)}, bf16[64,1024]{1,0:T(8,128)(2,1)}, u32[]{:S(2)}) copy-start(bf16[64,1024]{1,0:T(8,128)(2,1)} %refs_0_.3) | copy-start | bytes 393220
  48.3 41.3 %copy-start.5 = (bf16[1024,1024]{1,0:T(8,128)(2,1)}, bf16[1024,1024]{1,0:T(8,128)(2,1)S(1)}, u32[]{:S(2)}) copy-start(bf16[1024,1024]{1,0:T(8,128)(2,1)S(1)} %get-tuple-element.50.refs_2_) | copy-start | bytes 6291460
  48.3 8.4 %collective-permute-start.13 = (bf16[128,1024]{1,0:T(8,128)(2,1)S(1)}, bf16[128,1024]{1,0:T(8,128)(2,1)S(1)}, u32[]{:S(2)}, u32[]{:S(2)}) collective-permute-start(bf16[128,1024]{1,0:T(8,128)(2,1)S(1)} %get-tuple-element.55.refs_3_), channel_id=1, source_target_pairs={{0,2},{1,3},{2,0},{3,1},{16,18},{17,19},{18,16},{19,17},{4,6},{5,7... | collective-permute-start | bytes 786440 | tf_op jit(solution)/shard_map/ppermute | solution.py:498
  49.8 5.3 %collective-permute-start.12 = (bf16[64,1024]{1,0:T(8,128)(2,1)S(1)}, bf16[64,1024]{1,0:T(8,128)(2,1)S(1)}, u32[]{:S(2)}, u32[]{:S(2)}) collective-permute-start(bf16[64,1024]{1,0:T(8,128)(2,1)S(1)} %get-tuple-element.53), channel_id=1, source_target_pairs={{0,4},{4,0},{8,12},{12,8},{1,5},{5,1},{9,13},{13,9},{2,6},{6,2},{1... | collective-permute-start | bytes 393224 | tf_op jit(solution)/shard_map/ppermute | solution.py:502
  56.9 27.2 %copy-start.15 = (bf16[256,1024]{1,0:T(8,128)(2,1)}, bf16[256,1024]{1,0:T(8,128)(2,1)S(1)}, u32[]{:S(2)}) copy-start(bf16[256,1024]{1,0:T(8,128)(2,1)S(1)} %get-tuple-element.64.refs_2_) | copy-start | bytes 1572868
  56.9 13.2 %collective-permute-start.20 = (bf16[256,1024]{1,0:T(8,128)(2,1)S(1)}, bf16[256,1024]{1,0:T(8,128)(2,1)S(1)}, u32[]{:S(2)}, u32[]{:S(2)}) collective-permute-start(bf16[256,1024]{1,0:T(8,128)(2,1)S(1)} %get-tuple-element.64.refs_2_), channel_id=1, source_target_pairs={{0,16},{1,17},{2,18},{3,19},{16,0},{17,1},{18,2},{19,3},{4,20},{5,... | collective-permute-start | bytes 1572872 | tf_op jit(solution)/shard_map/ppermute | solution.py:498
  58.5 4.3 %collective-permute-start.16 = (bf16[64,1024]{1,0:T(8,128)(2,1)S(1)}, bf16[64,1024]{1,0:T(8,128)(2,1)S(1)}, u32[]{:S(2)}, u32[]{:S(2)}) collective-permute-start(bf16[64,1024]{1,0:T(8,128)(2,1)S(1)} %get-tuple-element.58.refs_3_), channel_id=1, source_target_pairs={{0,3},{1,0},{2,1},{3,2},{4,7},{5,4},{6,5},{7,6},{8,11},{9,8},{10,9... | collective-permute-start | bytes 393224 | tf_op jit(solution)/shard_map/ppermute | solution.py:53
  58.6 11.6 %collective-permute-start.15 = (bf16[64,1024]{1,0:T(8,128)(2,1)S(1)}, bf16[64,1024]{1,0:T(8,128)(2,1)S(1)}, u32[]{:S(2)}, u32[]{:S(2)}) collective-permute-start(bf16[64,1024]{1,0:T(8,128)(2,1)S(1)} %get-tuple-element.58.refs_3_), channel_id=1, source_target_pairs={{0,2},{1,3},{2,0},{3,1},{4,6},{5,7},{6,4},{7,5},{8,10},{9,11},{10,... | collective-permute-start | bytes 393224 | tf_op jit(solution)/shard_map/ppermute | solution.py:53
  59.9 10.3 %collective-permute-start.14 = (bf16[64,1024]{1,0:T(8,128)(2,1)S(1)}, bf16[64,1024]{1,0:T(8,128)(2,1)S(1)}, u32[]{:S(2)}, u32[]{:S(2)}) collective-permute-start(bf16[64,1024]{1,0:T(8,128)(2,1)S(1)} %get-tuple-element.58.refs_3_), channel_id=1, source_target_pairs={{0,1},{1,2},{2,3},{3,0},{4,5},{5,6},{6,7},{7,4},{8,9},{9,10},{10,1... | collective-permute-start | bytes 393224 | tf_op jit(solution)/shard_map/ppermute | solution.py:53
  60.1 15.7 %collective-permute-start.23 = (bf16[128,1024]{1,0:T(8,128)(2,1)S(1)}, bf16[128,1024]{1,0:T(8,128)(2,1)S(1)}, u32[]{:S(2)}, u32[]{:S(2)}) collective-permute-start(bf16[128,1024]{1,0:T(8,128)(2,1)S(1)} %get-tuple-element.65), channel_id=1, source_target_pairs={{0,8},{4,12},{8,0},{12,4},{1,9},{5,13},{9,1},{13,5},{2,10},{6,14},... | collective-permute-start | bytes 786440 | tf_op jit(solution)/shard_map/ppermute | solution.py:505
  62.8 21.3 %collective-permute-start.21 = (bf16[256,1024]{1,0:T(8,128)(2,1)S(1)}, bf16[256,1024]{1,0:T(8,128)(2,1)S(1)}, u32[]{:S(2)}, u32[]{:S(2)}) collective-permute-start(bf16[256,1024]{1,0:T(8,128)(2,1)S(1)} %get-tuple-element.64.refs_2_), channel_id=1, source_target_pairs={{0,1},{1,0},{2,3},{3,2},{16,17},{17,16},{18,19},{19,18},{4,5},{5,4... | collective-permute-start | bytes 1572872 | tf_op jit(solution)/shard_map/ppermute | solution.py:498
  70.2 14.0 %collective-permute-start.22 = (bf16[256,1024]{1,0:T(8,128)(2,1)S(1)}, bf16[256,1024]{1,0:T(8,128)(2,1)S(1)}, u32[]{:S(2)}, u32[]{:S(2)}) collective-permute-start(bf16[256,1024]{1,0:T(8,128)(2,1)S(1)} %collective-permute-done.20.refs_8_.refs_3_), channel_id=1, source_target_pairs={{0,1},{1,0},{2,3},{3,2},{16,17},{17,16},{18,19},{19,18},{4,5},{5,4... | collective-permute-start | bytes 1572872 | tf_op jit(solution)/shard_map/ppermute | solution.py:498
  71.6 5.1 %collective-permute-start.17 = (bf16[64,1152]{1,0:T(8,128)(2,1)S(1)}, bf16[64,1152]{1,0:T(8,128)(2,1)S(1)}, u32[]{:S(2)}, u32[]{:S(2)}) collective-permute-start(bf16[64,1152]{1,0:T(8,128)(2,1)S(1)} %get-tuple-element.61), channel_id=1, source_target_pairs={{0,3},{1,0},{2,1},{3,2},{4,7},{5,4},{6,5},{7,6},{8,11},{9,8},{10,9... | collective-permute-start | bytes 442376 | tf_op jit(solution)/shard_map/ppermute | solution.py:53
  75.8 8.3 %collective-permute-start.24 = (bf16[128,1024]{1,0:T(8,128)(2,1)S(1)}, bf16[128,1024]{1,0:T(8,128)(2,1)S(1)}, u32[]{:S(2)}, u32[]{:S(2)}) collective-permute-start(bf16[128,1024]{1,0:T(8,128)(2,1)S(1)} %collective-permute-done.23.refs_11_.refs_5_), channel_id=1, source_target_pairs={{0,16},{1,17},{2,18},{3,19},{16,0},{17,1},{18,2},{19,3},{4,20},{5,... | collective-permute-start | bytes 786440 | tf_op jit(solution)/shard_map/ppermute | solution.py:498
  76.3 6.7 %collective-permute-start.18 = (bf16[64,1152]{1,0:T(8,128)(2,1)S(1)}, bf16[64,1152]{1,0:T(8,128)(2,1)S(1)}, u32[]{:S(2)}, u32[]{:S(2)}) collective-permute-start(bf16[64,1152]{1,0:T(8,128)(2,1)S(1)} %get-tuple-element.62), channel_id=1, source_target_pairs={{0,2},{1,3},{2,0},{3,1},{4,6},{5,7},{6,4},{7,5},{8,10},{9,11},{10,... | collective-permute-start | bytes 442376 | tf_op jit(solution)/shard_map/ppermute | solution.py:53
  76.7 6.8 %collective-permute-start.19 = (bf16[64,1152]{1,0:T(8,128)(2,1)S(1)}, bf16[64,1152]{1,0:T(8,128)(2,1)S(1)}, u32[]{:S(2)}, u32[]{:S(2)}) collective-permute-start(bf16[64,1152]{1,0:T(8,128)(2,1)S(1)} %get-tuple-element.63), channel_id=1, source_target_pairs={{0,1},{1,2},{2,3},{3,0},{4,5},{5,6},{6,7},{7,4},{8,9},{9,10},{10,1... | collective-permute-start | bytes 442376 | tf_op jit(solution)/shard_map/ppermute | solution.py:53
  84.1 7.7 %copy-start.7 = (bf16[256,1024]{1,0:T(8,128)(2,1)}, bf16[256,1024]{1,0:T(8,128)(2,1)S(1)}, u32[]{:S(2)}) copy-start(bf16[256,1024]{1,0:T(8,128)(2,1)S(1)} %collective-permute-done.22.refs_10_.refs_7_) | copy-start | bytes 1572868
  84.6 5.0 %collective-permute-start.25 = (bf16[64,1024]{1,0:T(8,128)(2,1)S(1)}, bf16[64,1024]{1,0:T(8,128)(2,1)S(1)}, u32[]{:S(2)}, u32[]{:S(2)}) collective-permute-start(bf16[64,1024]{1,0:T(8,128)(2,1)S(1)} %get-tuple-element.67.refs_3_), channel_id=1, source_target_pairs={{0,4},{4,0},{8,12},{12,8},{1,5},{5,1},{9,13},{13,9},{2,6},{6,2},{1... | collective-permute-start | bytes 393224 | tf_op jit(solution)/shard_map/ppermute | solution.py:502
  91.8 0.7 copy-start.21
  92.5 6.4 %collective-permute-start.26 = (bf16[64,2048]{1,0:T(8,128)(2,1)S(1)}, bf16[64,2048]{1,0:T(8,128)(2,1)S(1)}, u32[]{:S(2)}, u32[]{:S(2)}) collective-permute-start(bf16[64,2048]{1,0:T(8,128)(2,1)S(1)} %get-tuple-element.69), channel_id=1, source_target_pairs={{0,4},{4,0},{8,12},{12,8},{1,5},{5,1},{9,13},{13,9},{2,6},{6,2},{1... | collective-permute-start | bytes 786440 | tf_op jit(solution)/shard_map/ppermute | solution.py:502
  92.5 24.1 %collective-permute-start.27 = (bf16[256,1024]{1,0:T(8,128)(2,1)}, bf16[256,1024]{1,0:T(8,128)(2,1)}, u32[]{:S(2)}, u32[]{:S(2)}) collective-permute-start(bf16[256,1024]{1,0:T(8,128)(2,1)} %get-tuple-element.71.refs_4_), channel_id=1, source_target_pairs={{0,2},{1,3},{2,0},{3,1},{16,18},{17,19},{18,16},{19,17},{4,6},{5,7... | collective-permute-start | bytes 1572872 | tf_op jit(solution)/shard_map/ppermute | solution.py:498
  99.0 0.8 copy-start.10
  99.8 0.7 copy-start.11
  100.5 20.1 %all-to-all-start = ((bf16[32,64,128]{2,1,0:T(8,128)(2,1)}), bf16[32,64,128]{2,1,0:T(8,128)(2,1)}, u32[]{:S(2)}, u32[]{:S(2)}) async-start(bf16[32,64,128]{2,1,0:T(8,128)(2,1)} %copy-done.10), calls=%async_computation | async-start | bytes 1048576 | tf_op jit(solution)/shard_map/all_to_all | solution.py:618
  104.3 13.9 %collective-permute-start.28 = (bf16[256,1024]{1,0:T(8,128)(2,1)}, bf16[256,1024]{1,0:T(8,128)(2,1)S(1)}, u32[]{:S(2)}, u32[]{:S(2)}) collective-permute-start(bf16[256,1024]{1,0:T(8,128)(2,1)} %get-tuple-element.71.refs_4_), channel_id=1, source_target_pairs={{0,1},{1,0},{2,3},{3,2},{16,17},{17,16},{18,19},{19,18},{4,5},{5,4... | collective-permute-start | bytes 1572872 | tf_op jit(solution)/shard_map/ppermute | solution.py:498
  104.4 3.4 %copy-start.3 = (bf16[1024,4096]{1,0:T(8,128)(2,1)S(1)}, bf16[1024,4096]{1,0:T(8,128)(2,1)}, u32[]{:S(2)}) copy-start(bf16[1024,4096]{1,0:T(8,128)(2,1)} %copy-done.1) | copy-start | bytes 25165828
  107.8 0.9 copy-start.12
  108.8 1.0 copy-start.14
  109.8 0.9 copy-start.22
  117.7 2.1 %collective-permute-start.29 = (bf16[256,1024]{1,0:T(8,128)(2,1)S(1)}, bf16[256,1024]{1,0:T(8,128)(2,1)S(1)}, u32[]{:S(2)}, u32[]{:S(2)}) collective-permute-start(bf16[256,1024]{1,0:T(8,128)(2,1)S(1)} %late.1), channel_id=1, source_target_pairs={{0,1},{1,0},{2,3},{3,2},{16,17},{17,16},{18,19},{19,18},{4,5},{5,4... | collective-permute-start | bytes 1572872 | tf_op jit(solution)/shard_map/ppermute | solution.py:498
  118.3 0.8 copy-start.17
  119.8 0.8 copy-start.19
  120.6 1.0 copy-start.8
  121.6 1.0 copy-start.16
  122.7 1.0 copy-start.18
  123.7 1.0 copy-start.20
  124.8 36.7 %copy-start.6 = (bf16[1024,1024]{1,0:T(8,128)(2,1)S(1)}, bf16[1024,1024]{1,0:T(8,128)(2,1)}, u32[]{:S(2)}) copy-start(bf16[1024,1024]{1,0:T(8,128)(2,1)} %copy-done.5) | copy-start | bytes 6291460
  127.2 14.3 %collective-permute-start.30 = (bf16[1024,128]{1,0:T(8,128)(2,1)S(1)}, bf16[1024,128]{1,0:T(8,128)(2,1)S(1)}, u32[]{:S(2)}, u32[]{:S(2)}) collective-permute-start(bf16[1024,128]{1,0:T(8,128)(2,1)S(1)} %grad_columns.1.refs_0_), channel_id=1, source_target_pairs={{0,2},{1,3},{2,0},{3,1},{16,18},{17,19},{18,16},{19,17},{4,6},{5,7... | collective-permute-start | bytes 786440 | tf_op jit(solution)/shard_map/ppermute | solution.py:498
  128.8 12.7 %collective-permute-start.32 = (bf16[1024,128]{1,0:T(8,128)(2,1)S(1)}, bf16[1024,128]{1,0:T(8,128)(2,1)S(1)}, u32[]{:S(2)}, u32[]{:S(2)}) collective-permute-start(bf16[1024,128]{1,0:T(8,128)(2,1)S(1)} %grad_columns.1.refs_0_), channel_id=1, source_target_pairs={{0,18},{1,19},{2,16},{3,17},{16,2},{17,3},{18,0},{19,1},{4,22},{5,... | collective-permute-start | bytes 786440 | tf_op jit(solution)/shard_map/ppermute | solution.py:498
  130.2 12.4 %collective-permute-start.31 = (bf16[1024,128]{1,0:T(8,128)(2,1)S(1)}, bf16[1024,128]{1,0:T(8,128)(2,1)S(1)}, u32[]{:S(2)}, u32[]{:S(2)}) collective-permute-start(bf16[1024,128]{1,0:T(8,128)(2,1)S(1)} %grad_columns.1.refs_0_), channel_id=1, source_target_pairs={{0,16},{1,17},{2,18},{3,19},{16,0},{17,1},{18,2},{19,3},{4,20},{5,... | collective-permute-start | bytes 786440 | tf_op jit(solution)/shard_map/ppermute | solution.py:498
  141.5 22.4 %copy-start.24 = (f32[1024]{0:T(1024)S(1)}, f32[1024]{0:T(1024)}, u32[]{:S(2)}) copy-start(f32[1024]{0:T(1024)} %param.14) | copy-start | bytes 12292
  142.7 21.1 %collective-permute-start.33 = (bf16[4096,128]{1,0:T(8,128)(2,1)S(1)}, bf16[4096,128]{1,0:T(8,128)(2,1)S(1)}, u32[]{:S(2)}, u32[]{:S(2)}) collective-permute-start(bf16[4096,128]{1,0:T(8,128)(2,1)S(1)} %pack_columns.1.refs_3_), channel_id=1, source_target_pairs={{0,1},{1,0},{2,3},{3,2},{16,17},{17,16},{18,19},{19,18},{4,5},{5,4... | collective-permute-start | bytes 3145736 | tf_op jit(solution)/shard_map/ppermute | solution.py:498
  162.8 4.5 %collective-permute-start.34 = (f32[1,1024]{1,0:T(1,128)S(1)}, f32[1,1024]{1,0:T(1,128)S(1)}, u32[]{:S(2)}, u32[]{:S(2)}) collective-permute-start(f32[1,1024]{1,0:T(1,128)S(1)} %get-tuple-element.74.refs_0_), channel_id=1, source_target_pairs={{0,4},{4,0},{8,12},{12,8},{1,5},{5,1},{9,13},{13,9},{2,6},{6,2},{1... | collective-permute-start | bytes 12296 | tf_op jit(solution)/shard_map/ppermute | solution.py:502

commit v4 on v3

--- a/solution.py
+++ b/solution.py
@@ -26,10 +26,31 @@
     return jax.ShapeDtypeStruct(dims, dtype)
 
 
-def call(kernel, outs, ins, name, flops=0, scratch=(), smem=0, after=()):
+def copying(kernel, smem, shapes):
+    n = len(shapes)
+
+    def run(*refs):
+        sources, buffers, sems = refs[smem : smem + n], refs[-n - 1 : -1], refs[-1]
+        copies = [
+            pltpu.make_async_copy(sources[k], buffers[k], sems.at[k]) for k in range(n)
+        ]
+        for copy in copies:
+            copy.start()
+        for copy in copies:
+            copy.wait()
+        kernel(*refs[:smem], *buffers, *refs[smem + n : -n - 1])
+
+    return run
+
+
+def call(kernel, outs, ins, name, flops=0, scratch=(), smem=0, after=(), copy=False):
     count = len(ins)
+    if copy:
+        shapes = [pltpu.VMEM(a.shape, a.dtype) for a in ins[smem:]]
+        kernel = copying(kernel, smem, shapes)
+        scratch = [*scratch, *shapes, pltpu.SemaphoreType.DMA((len(shapes),))]
     moved = sum(math.prod(a.shape) * a.dtype.itemsize for a in list(ins) + list(outs))
-    held = sum(math.prod(s.shape) * jnp.dtype(s.dtype).itemsize for s in scratch)
+    held = 0 if copy else sum(math.prod(s.shape) * jnp.dtype(s.dtype).itemsize for s in scratch)
 
     def run(*refs):
         kernel(*refs[:count], *refs[count + len(after) :])
@@ -38,7 +59,7 @@
         run,
         out_shape=outs,
         in_specs=[SMEM] * smem
-        + [VMEM] * (count - smem)
+        + [pl.BlockSpec(memory_space=pl.ANY) if copy else VMEM] * (count - smem)
         + [pl.BlockSpec(memory_space=pl.ANY)] * len(after),
         out_specs=[VMEM] * len(outs),
         scratch_shapes=list(scratch),
@@ -67,57 +88,37 @@
     return lax.dot_general(left, right, (((0,), (0,)), ((), ())), preferred_element_type=F32)
 
 
-def norm_kernel(states_ref, gain_ref, normed_ref, token_ref):
-    token_ref[...] = jnp.zeros_like(token_ref)
+def u_kernel(weight_ref, pool_ref, u_ref):
+    pool = jnp.broadcast_to(pool_ref[...], (8, pool_ref.shape[1]))
+    high = pool.astype(BF16)
+    low, last = split_bf16(pool - high.astype(F32))
+    weight = weight_ref[...]
+    u_ref[...] = (nt(high, weight) + nt(low, weight) + nt(last, weight))[0:1]
+
+
+def gate_kernel(seq, root, blocks, z_ref, states_ref, gain_ref, u_ref, len_ref, lists_ref, *rest):
+    half = blocks // 2
+    outs, normed_ref, gated_ref, curve_ref, copies, rows_ref = (
+        rest[:half], rest[half], rest[half + 1], rest[half + 2], rest[half + 3 : -1], rest[-1]
+    )
+    step = pl.program_id(0)
     tokens, width = states_ref.shape
-    step = 4 * LANES if width % (4 * LANES) == 0 else width
-    for top in range(0, tokens, 32):
-        rows = slice(top, top + 32)
-        squares = jnp.zeros((32, step), F32)
-        for at in range(0, width, step):
-            part = states_ref[rows, at : at + step].astype(F32)
-            squares = squares + part * part
-        inv_rms = lax.rsqrt(jnp.sum(squares, axis=1, keepdims=True) / width + norm_eps)
-        for at in range(0, width, step):
-            part = states_ref[rows, at : at + step].astype(F32)
-            part = part * inv_rms * gain_ref[:, at : at + step]
-            normed_ref[rows, at : at + step] = part.astype(BF16)
-
-
-def norm_rows(events, states, gain):
-    tokens, width = states.shape
-    block = 128 if tokens % 128 == 0 else tokens
-    rows = pl.BlockSpec((block, width), lambda i: (i, 0))
-    return pl.pallas_call(
-        lambda *refs: norm_kernel(*refs[len(events) :]),
-        grid=(tokens // block,),
-        out_shape=[shape((tokens, width), BF16), shape((8, LANES), F32)],
-        in_specs=[pl.BlockSpec(memory_space=pl.ANY)] * len(events)
-        + [rows, pl.BlockSpec((1, width), lambda i: (0, 0))],
-        out_specs=[rows, pl.BlockSpec((8, LANES), lambda i: (0, 0))],
-        cost_estimate=pl.CostEstimate(
-            flops=6 * tokens * width, bytes_accessed=4 * tokens * width, transcendentals=0
-        ),
-        compiler_params=pltpu.CompilerParams(vmem_limit_bytes=10 * MIB),
-        name="norm_rows",
-    )(*events, states, gain)
-
-
-def gate_kernel(seq, root, blocks, z_ref, normed_ref, u_ref, len_ref, lists_ref, event_ref, *rest):
-    half = blocks // 2
-    outs, gated_ref, curve_ref, copies, rows_ref = (
-        rest[:half], rest[half], rest[half + 1], rest[half + 2 : -1], rest[-1]
-    )
-    step = pl.program_id(0)
-    tokens, width = normed_ref.shape
     count = tokens // seq
     chunk = 4 * LANES if width % (4 * LANES) == 0 else width
     logits = []
     for top in range(0, tokens, 32):
+        rows = slice(top, top + 32)
+        squares = jnp.zeros((32, chunk), F32)
+        for at in range(0, width, chunk):
+            part = states_ref[rows, at : at + chunk].astype(F32)
+            squares = squares + part * part
+        inv_rms = lax.rsqrt(jnp.sum(squares, axis=1, keepdims=True) / width + norm_eps)
         total = jnp.zeros((32, chunk), F32)
         for at in range(0, width, chunk):
-            part = normed_ref[top : top + 32, at : at + chunk].astype(F32)
-            total = total + part * u_ref[:, at : at + chunk]
+            part = states_ref[rows, at : at + chunk].astype(F32)
+            part = (part * inv_rms * gain_ref[:, at : at + chunk]).astype(BF16)
+            normed_ref[rows, at : at + chunk] = part
+            total = total + part.astype(F32) * u_ref[:, at : at + chunk]
         logits.append(jnp.sum(total, axis=1, keepdims=True))
     logit = jnp.concatenate(logits, axis=0) / root
     gate = 1.0 / (1.0 + jnp.exp(-logit))
@@ -153,37 +154,45 @@
                 ].astype(BF16)
 
 
-def gate_rows(z, normed, u, token_lengths, lists, event, seq, root, blocks, owners):
-    tokens, width = normed.shape
+def gate_rows(z, states, gain, u, token_lengths, lists, events, seq, root, blocks, owners):
+    tokens, width = states.shape
     queries = tokens // seq
     group = 16 if queries % 16 == 0 else queries
     step_tokens = group * seq
     half = blocks // 2
-    outs = [shape((queries, width // half), BF16)] * half + [shape((tokens, 1), F32)] * 2
+    outs = [shape((queries, width // half), BF16)] * half
+    outs += [shape((tokens, width), BF16)] + [shape((tokens, 1), F32)] * 2
     outs += [shape((queries, lists.shape[1] // owners), lists.dtype)] * owners
     column = pl.BlockSpec((step_tokens, 1), lambda i: (i, 0))
+    rows = pl.BlockSpec((step_tokens, width), lambda i: (i, 0))
+    inputs = [z, states, gain, u, token_lengths, lists]
+
+    def run(*refs):
+        gate_kernel(seq, root, blocks, *refs[: len(inputs)], *refs[len(inputs) + len(events) :])
+
     whole = lambda dims: pl.BlockSpec(dims, lambda i: (0, 0))
     return pl.pallas_call(
-        functools.partial(gate_kernel, seq, root, blocks),
+        run,
         grid=(queries // group,),
         out_shape=outs,
         in_specs=[
             SMEM,
-            pl.BlockSpec((step_tokens, width), lambda i: (i, 0)),
+            rows,
+            whole((1, width)),
             whole((1, width)),
             column,
             whole(lists.shape),
-            pl.BlockSpec(memory_space=pl.ANY),
-        ],
-        out_specs=[whole((queries, width // half))] * half + [column] * 2
+        ]
+        + [pl.BlockSpec(memory_space=pl.ANY)] * len(events),
+        out_specs=[whole((queries, width // half))] * half + [rows] + [column] * 2
         + [whole((queries, lists.shape[1] // owners))] * owners,
         scratch_shapes=[pltpu.VMEM((queries, width), F32)],
         cost_estimate=pl.CostEstimate(
-            flops=4 * tokens * width, bytes_accessed=2 * tokens * width, transcendentals=0
+            flops=10 * tokens * width, bytes_accessed=4 * tokens * width, transcendentals=0
         ),
-        compiler_params=pltpu.CompilerParams(vmem_limit_bytes=16 * MIB),
+        compiler_params=pltpu.CompilerParams(vmem_limit_bytes=20 * MIB),
         name="gate_rows",
-    )(z, normed, u, token_lengths, lists, event)
+    )(*inputs, *events)
 
 
 def pack_kernel(*refs):
@@ -343,9 +352,9 @@
         columns_ref[j] = grad[:, at : at + cols]
 
 
-def slope_kernel(seq, blocks, plane, z_ref, normed_ref, curve_ref, loss_ref, *rest):
+def slope_kernel(seq, blocks, z_ref, normed_ref, curve_ref, loss_ref, *rest):
     half = blocks // 2
-    backs, (out_ref, all_ref, sum_ref) = rest[:half], rest[-3:]
+    backs, outs, (all_ref, sum_ref) = rest[:half], rest[half : 2 * half], rest[-2:]
     step = pl.program_id(0)
     tokens, width = normed_ref.shape
     count = tokens // seq
@@ -373,21 +382,20 @@
     def _():
         total = jnp.sum(sum_ref[...], axis=0, keepdims=True)
         lines = depth // LANES
-        devices, height = out_ref.shape[0], out_ref.shape[1]
+        height = outs[0].shape[0]
         loss = jnp.broadcast_to(loss_ref[...], (height - 2 * lines, LANES))
-        for member in range(half):
-            rows = []
+        all_ref[0:1, :] = total
+        for k in range(half):
             for j in range(2):
+                row = all_ref[0:1, block_at(j, k)]
                 for line in range(lines):
-                    at = (j * half + member) * depth + line * LANES
-                    rows.append(total[:, at : at + LANES])
-            message = jnp.concatenate(rows + [loss], axis=0)
-            for to in range(devices):
-                if to // plane % half == member:
-                    out_ref[to] = message
-
-
-def slope_rows(z, normed, curve, loss, backs, seq, blocks, devices, plane):
+                    outs[k][j * lines + line : j * lines + line + 1, :] = row[
+                        :, line * LANES : (line + 1) * LANES
+                    ]
+            outs[k][2 * lines :, :] = loss
+
+
+def slope_rows(z, normed, curve, loss, backs, seq, blocks):
     tokens, width = normed.shape
     half = blocks // 2
     height = 2 * (width // blocks // LANES) // 8 * 8 + 8
@@ -396,9 +404,9 @@
     step_tokens = group * seq
     whole = lambda dims: pl.BlockSpec(dims, lambda i: (0, 0))
     return pl.pallas_call(
-        functools.partial(slope_kernel, seq, blocks, plane),
+        functools.partial(slope_kernel, seq, blocks),
         grid=(queries // group,),
-        out_shape=shape((devices, height, LANES), F32),
+        out_shape=[shape((height, LANES), F32)] * half,
         in_specs=[
             SMEM,
             pl.BlockSpec((step_tokens, width), lambda i: (i, 0)),
@@ -406,7 +414,7 @@
             whole((1, LANES)),
         ]
         + [whole((queries, width // half))] * half,
-        out_specs=pl.BlockSpec((devices, height, LANES), lambda i: (0, 0, 0)),
+        out_specs=[whole((height, LANES))] * half,
         scratch_shapes=[pltpu.VMEM((queries, width), F32), pltpu.VMEM((8, width), F32)],
         cost_estimate=pl.CostEstimate(
             flops=4 * tokens * width, bytes_accessed=2 * tokens * width, transcendentals=0
@@ -433,7 +441,7 @@
 def query_kernel(side_ref, weight_ref, mirror_ref, parts_ref, part_ref, slope_ref, loss_ref):
     depth = weight_ref.shape[0]
     lines = depth // LANES
-    total = jnp.sum(parts_ref[...], axis=0)
+    total = parts_ref[...]
     loss_ref[...] = total[2 * lines : 2 * lines + 1]
     side = side_ref[0]
     part = jnp.zeros(part_ref.shape, F32)
@@ -517,7 +525,10 @@
     weight_share = lax.dynamic_slice_in_dim(proj_weight, place * share, share, 0)
     far_share = mirror_shift(weight_share)
 
-    block_u = jnp.sum(proj_weight.astype(F32) * pool_query[None, :], axis=1).reshape(1, depth)
+    block_u = call(
+        u_kernel, [shape((1, depth), F32)], [proj_weight, pool_query.reshape(1, -1)], "block_u",
+        after=[weight_share],
+    )[0]
     u_parts = [block_u] + [shift(block_u, "fsdp", k) for k in steps_z]
     u = jnp.zeros((1, width), F32)
     for k in range(n_z):
@@ -543,19 +554,13 @@
     ranks = ints(*ranks)
     both_arr, base_arr = ints(z, i), ints(i * slab.shape[0])
     token_lengths = jnp.broadcast_to(lengths[:, None], (queries, seq)).reshape(-1, 1)
-    events = [u, token_lengths, share_places, ranks, both_arr, base_arr, side_arr]
-    normed, normed_token = norm_rows(
-        events, hidden_states.reshape(-1, width),
-        norm_gain.astype(F32).reshape(1, width)
-    )
-
-    far_share = pack([far_share], "far_share", normed_token)
+    events = [far_share, share_places, ranks, base_arr, side_arr]
     chip_shares = [far_share if dg == dh == 0 else plane_shift(far_share, dg, dh, 0) for dg, dh in chips]
     gate_outs = gate_rows(
-        both_arr, normed, u, token_lengths, negatives, far_share, seq, root, n_z, n_i
-    )
-    sends, (gated, curve), lists = gate_outs[:half], gate_outs[half : half + 2], gate_outs[half + 2 :]
-
+        both_arr, hidden_states.reshape(-1, width), norm_gain.astype(F32).reshape(1, width), u,
+        token_lengths, negatives, events, seq, root, n_z, n_i,
+    )
+    sends, (normed, gated, curve), lists = gate_outs[:half], gate_outs[half : half + 3], gate_outs[half + 3 :]
     packs = [pack(chip_shares, "pack_shares", gated)]
     packs += [plane_shift(packs[0], 0, 0, dc) for dc in range(1, n_c)]
 
@@ -618,9 +623,9 @@
     all_columns = lax.all_to_all(
         passed(grad_columns, "columns_out", backs[-1]), EVERY, 0, 0, tiled=True
     )
-    slopes = slope_rows(both_arr, normed, curve, loss, backs, seq, n_z, n_all, n_plane)
+    slopes = slope_rows(both_arr, normed, curve, loss, backs, seq, n_z)
     across = [plane_shift(others, 0, dh, 0) for dh in range(1, n_h)]
-    late = [pack([array], "late", slopes) for array in across]
+    late = [pack([array], "late", slopes[0]) for array in across]
     spread = []
     for dc in range(n_c):
         if dc == 0:
@@ -631,17 +636,25 @@
     block_columns = call(
         functools.partial(columns_kernel, len(spread)), [shape((depth, cols), BF16)],
         [ranks, all_columns] + spread, "grad_columns",
-        flops=2 * n_all * queries * depth * cols, scratch=[pltpu.VMEM((n_all * queries, cols), BF16)], smem=1,
+        flops=2 * n_all * queries * depth * cols, scratch=[pltpu.VMEM((n_all * queries, cols), BF16)], smem=1, copy=True,
     )[0]
     on_chips = [block_columns if dg == dh == 0 else plane_shift(block_columns, dg, dh, 0) for dg, dh in chips]
-    slopes = passed(slopes, "slopes_out", on_chips[1 % len(on_chips)])
-    all_slopes = lax.all_to_all(slopes, EVERY, 0, 0, tiled=True)
+    def total(parts, name):
+        return call(add_kernel, [shape(parts[0].shape, F32)], parts, name)[0]
+
+    slopes = [passed(array, "slopes_out", block_columns) for array in slopes]
+    slope = total([slopes[0]] + [half_shift(slopes[k], k) for k in range(1, half)], "sum_half")
+    slope = total([slope, mirror_shift(slope)], "sum_mirror")
+    for axis, size in ((0, n_g), (1, n_h), (2, n_c)):
+        if size > 1:
+            moves = [[k if a == axis else 0 for a in range(3)] for k in range(1, size)]
+            slope = total([slope] + [plane_shift(slope, *move) for move in moves], "sum_plane")
     query_part, my_slope, loss_total = call(
         query_kernel,
         [shape((1, proj_width), F32), shape((depth // LANES, LANES), F32), shape((1, LANES), F32)],
-        [side_arr, proj_weight, mirror, all_slopes], "slope_sum", smem=1,
-    )
-    finished = [pack(on_chips, "pack_columns", slopes)]
+        [side_arr, proj_weight, mirror, slope], "slope_sum", smem=1,
+    )
+    finished = [pack(on_chips, "pack_columns", slope)]
     finished += [plane_shift(finished[0], 0, 0, dc) for dc in range(1, n_c)]
     query_parts = [query_part] + [half_shift(query_part, k) for k in range(1, half)]
     grad_proj, finish_token = call(

time: 170 us -> 154 us (0.906)
  blocking collectives: 18.7 us -> 0 us
  starting transfers between devices: 39.1 us -> 46.1 us
  local copies, waits for them, and re-layouts: 27.6 us -> 23.4 us
  other arithmetic: 2.85 us -> 0.08 us
  Pallas kernels: 31 us -> 33 us
    all_to_all x1 -> x0, blocking collectives: 18.7 us -> none  [body(): all_slopes = lax.all_to_all(slopes, EVERY, 0, 0, tiled=True)]
    ppermute x16 -> x19, waiting for transfers between devices: 21.5 us -> 13.3 us  [plane_shift(): return lax.ppermute(values, PLANE, pairs)]
    ppermute x2 -> x3, waiting for transfers between devices: 2.66 us -> 9.68 us  [mirror_shift(): lax.ppermute(values, 'fsdp', [(a, (a + half) % n_z) for a in range(n_z)])]
    ppermute x2 -> x3, starting transfers between devices: 4.67 us -> 9.69 us  [mirror_shift(): lax.ppermute(values, 'fsdp', [(a, (a + half) % n_z) for a in range(n_z)])]
    unnamed x53 -> x55, local copies, waits for them, and re-layouts: 25.3 us -> 21.8 us
    ppermute x16 -> x19, starting transfers between devices: 13.9 us -> 17.2 us  [plane_shift(): return lax.ppermute(values, PLANE, pairs)]
    ppermute x5 -> x6, waiting for transfers between devices: 15 us -> 17.9 us  [half_shift(): return lax.ppermute(values, 'fsdp', pairs)]
    ppermute x12, starting transfers between devices: 12.6 us -> 10.3 us  [shift(): return lax.ppermute(values, axis, [(i, (i + k) % n) for i in range(n)])]
  transfers between devices with their start and end apart: 36 -> 41, of which waited for: 17 -> 20; matrix products, arithmetic and copies ran while one was open for 2% -> 1% of each run, Pallas kernels for 14% -> 16%
where the time goes in v4:
time: 154 us
  waiting for transfers between devices  48.8 us (32%)
  starting transfers between devices  46.1 us (30%)
  Pallas kernels  33 us (21%)
  local copies, waits for them, and re-layouts  23.4 us (15%)
  between operations  2.25 us (1%)
    unnamed x55, local copies, waits for them, and re-layouts  21.8 us
    pallas_call x22, Pallas kernels, call(): pl.pallas_call(run, out_shape=outs, in_specs=[SMEM] * smem + [pl.BlockSpe...  18.5 us
    ppermute x6, waiting for transfers between devices, half_shift(): return lax.ppermute(values, 'fsdp', pairs)  17.9 us
    ppermute x19, starting transfers between devices, plane_shift(): return lax.ppermute(values, PLANE, pairs)  17.2 us
    ppermute x19, waiting for transfers between devices, plane_shift(): return lax.ppermute(values, PLANE, pairs)  13.3 us
    ppermute x12, starting transfers between devices, shift(): return lax.ppermute(values, axis, [(i, (i + k) % n) for i in range(n)])  10.3 us
    ppermute x3, starting transfers between devices, mirror_shift(): lax.ppermute(values, 'fsdp', [(a, (a + half) % n_z) for a in range(n_z)])  9.69 us
    ppermute x3, waiting for transfers between devices, mirror_shift(): lax.ppermute(values, 'fsdp', [(a, (a + half) % n_z) for a in range(n_z)])  9.68 us
  transfers between devices with their start and end apart: 41, of which 20 were waited for; matrix products, arithmetic and copies ran while one was open for 1% of the time, Pallas kernels for 16%

profile of v4, /device:TPU:0, one launch (start us, length us, event | category | flops | bytes accessed | tf_op | source)
XLA Modules:
  0.0 153.7 jit_solution(8328814573445662413)
XLA Ops:
  0.7 1.0 constant_dynamic-slice_fusion.refs_2_
  1.6 4.1 %collective-permute-start.3 = (bf16[128,1024]{1,0:T(8,128)(2,1)S(1)}, bf16[128,1024]{1,0:T(8,128)(2,1)S(1)}, u32[]{:S(2)}, u32[]{:S(2)}) collective-permute-start(bf16[128,1024]{1,0:T(8,128)(2,1)S(1)} %constant_dynamic-slice_fusion.refs_2_), channel_id=1, source_target_pairs={{0,8},{4,12},{8,0},{12,4},{1,9},{5,13},{9,1},{13,5},{2,10},{6,14},... | collective-permute-start | bytes 786440 | tf_op jit(solution)/shard_map/ppermute | solution.py:513
  5.8 1.6 %copy-done = bf16[1024,1024]{1,0:T(8,128)(2,1)S(1)} copy-done((bf16[1024,1024]{1,0:T(8,128)(2,1)S(1)}, bf16[1024,1024]{1,0:T(8,128)(2,1)}, u32[]{:S(2)}) %copy-start) | copy-done | bytes 2097176
  8.0 1.7 %block_u.1 = f32[1,1024]{1,0:T(1,128)S(1)} custom-call(bf16[1024,1024]{1,0:T(8,128)(2,1)S(1)} %copy-done, f32[1,1024]{1,0:T(1,128)S(1)} %bitcast.52, bf16[128,1024]{1,0:T(8,128)(2,1)S(1)} %constant_dynamic-slice_fusion.refs_2_), custom_call_target="tpu_custom_call" | custom-call | bytes 2105344 | tf_op jit(solution)/shard_map/block_u/pallas_call | solution.py:58
  9.8 1.4 collective-permute-start.2
  11.1 1.7 %collective-permute-start.1 = (f32[1,1024]{1,0:T(1,128)S(1)}, f32[1,1024]{1,0:T(1,128)S(1)}, u32[]{:S(2)}, u32[]{:S(2)}) collective-permute-start(f32[1,1024]{1,0:T(1,128)S(1)} %block_u.1), channel_id=1, source_target_pairs={{0,8},{4,12},{8,0},{12,4},{1,9},{5,13},{9,1},{13,5},{2,10},{6,14},... | collective-permute-start | bytes 12296 | tf_op jit(solution)/shard_map/ppermute | solution.py:74
  13.7 4.2 %collective-permute-done.3.refs_6_.refs_0_ = bf16[128,1024]{1,0:T(8,128)(2,1)S(1)} collective-permute-done((bf16[128,1024]{1,0:T(8,128)(2,1)S(1)}, bf16[128,1024]{1,0:T(8,128)(2,1)S(1)}, u32[]{:S(2)}, u32[]{:S(2)}) %collective-permute-start.3) | collective-permute-done | bytes 262176 | tf_op jit(solution)/shard_map/ppermute | solution.py:513
  17.9 2.5 %collective-permute-start.7 = (bf16[128,1024]{1,0:T(8,128)(2,1)S(1)}, bf16[128,1024]{1,0:T(8,128)(2,1)S(1)}, u32[]{:S(2)}, u32[]{:S(2)}) collective-permute-start(bf16[128,1024]{1,0:T(8,128)(2,1)S(1)} %collective-permute-done.3.refs_6_.refs_0_), channel_id=1, source_target_pairs={{0,18},{1,19},{2,16},{3,17},{16,2},{17,3},{18,0},{19,1},{4,22},{5,... | collective-permute-start | bytes 786440 | tf_op jit(solution)/shard_map/ppermute | solution.py:506
  21.4 3.4 %copy-done.6 = bf16[64,16,4096]{2,1,0:T(8,128)(2,1)S(1)} copy-done((bf16[64,16,4096]{2,1,0:T(8,128)(2,1)S(1)}, bf16[64,16,4096]{2,1,0:T(8,128)(2,1)}, u32[]{:S(2)}) %copy-start.6) | copy-done | bytes 8388632
  24.8 8.6 %gate_rows.1 = (bf16[64,2048]{1,0:T(8,128)(2,1)S(1)}, bf16[64,2048]{1,0:T(8,128)(2,1)S(1)}, bf16[1024,4096]{1,0:T(8,128)(2,1)S(1)}, f32[1024,1]{1,0:T(8,128)S(1)...) custom-call(s32[2]{0:T(128)S(1)} %pad_add_fusion.refs_0_.z_ref, ...), custom_call_target="tpu_custom_call" | custom-call | flops 41943040 | bytes 16777216 | tf_op jit(solution)/shard_map/gate_rows/pallas_call | solution.py:174
  33.5 3.3 %copy-done.2 = bf16[1024,4096]{1,0:T(8,128)(2,1)} copy-done((bf16[1024,4096]{1,0:T(8,128)(2,1)}, bf16[1024,4096]{1,0:T(8,128)(2,1)S(1)}, u32[]{:S(2)}) %copy-start.2) | copy-done | bytes 8388632
  37.0 0.8 collective-permute-start.4
  38.0 1.5 collective-permute-start.10
  39.5 1.3 collective-permute-start.11
  41.2 0.7 collective-permute-done.10.refs_4_
  42.4 1.8 %list_counts.1 = (f32[256,1024]{1,0:T(8,128)S(1)}, f32[1,1024]{1,0:T(1,128)S(1)}) custom-call(s32[1]{0:T(128)} %bitcast.46.refs_9_.refs_0_, bf16[1024,1024]{1,0:T(8,128)(2,1)S(1)} %copy-done.9, s32[64,8]{1,0:T(8,128)S(1)} %get-tuple-element.44.refs_2_, s32[64,8]{1,0:T(8,128)S(1)} %collective-permute-done.9.refs_3_, ...), custom_call_target="tpu_custom_call" | custom-call | bytes 3158020 | tf_op jit(solution)/shard_map/list_counts/pallas_call | solution.py:58
  44.3 1.5 collective-permute-done.4.refs_4_
  45.7 1.4 forward.1
  47.2 1.6 %collective-permute-start.13 = (bf16[128,1024]{1,0:T(8,128)(2,1)S(1)}, bf16[128,1024]{1,0:T(8,128)(2,1)S(1)}, u32[]{:S(2)}, u32[]{:S(2)}) collective-permute-start(bf16[128,1024]{1,0:T(8,128)(2,1)S(1)} %get-tuple-element.55.refs_3_), channel_id=1, source_target_pairs={{0,2},{1,3},{2,0},{3,1},{16,18},{17,19},{18,16},{19,17},{4,6},{5,7... | collective-permute-start | bytes 786440 | tf_op jit(solution)/shard_map/ppermute | solution.py:506
  48.8 0.7 collective-permute-start.12
  49.5 4.2 %collective-permute-done.12.refs_1_ = bf16[64,1024]{1,0:T(8,128)(2,1)S(1)} collective-permute-done((bf16[64,1024]{1,0:T(8,128)(2,1)S(1)}, bf16[64,1024]{1,0:T(8,128)(2,1)S(1)}, u32[]{:S(2)}, u32[]{:S(2)}) %collective-permute-start.12) | collective-permute-done | bytes 131104 | tf_op jit(solution)/shard_map/ppermute | solution.py:510
  53.8 1.3 collective-permute-done.13.refs_4_
  55.2 1.6 %collective-permute-start.20 = (bf16[256,1024]{1,0:T(8,128)(2,1)S(1)}, bf16[256,1024]{1,0:T(8,128)(2,1)S(1)}, u32[]{:S(2)}, u32[]{:S(2)}) collective-permute-start(bf16[256,1024]{1,0:T(8,128)(2,1)S(1)} %get-tuple-element.64.refs_2_), channel_id=1, source_target_pairs={{0,16},{1,17},{2,18},{3,19},{16,0},{17,1},{18,2},{19,3},{4,20},{5,... | collective-permute-start | bytes 1572872 | tf_op jit(solution)/shard_map/ppermute | solution.py:506
  56.9 1.5 collective-permute-start.15
  58.6 3.1 %collective-permute-start.23 = (bf16[128,1024]{1,0:T(8,128)(2,1)S(1)}, bf16[128,1024]{1,0:T(8,128)(2,1)S(1)}, u32[]{:S(2)}, u32[]{:S(2)}) collective-permute-start(bf16[128,1024]{1,0:T(8,128)(2,1)S(1)} %get-tuple-element.65), channel_id=1, source_target_pairs={{0,8},{4,12},{8,0},{12,4},{1,9},{5,13},{9,1},{13,5},{2,10},{6,14},... | collective-permute-start | bytes 786440 | tf_op jit(solution)/shard_map/ppermute | solution.py:513
  61.8 1.0 collective-permute-start.21
  62.8 5.1 %collective-permute-done.20.refs_8_.refs_3_ = bf16[256,1024]{1,0:T(8,128)(2,1)S(1)} collective-permute-done((bf16[256,1024]{1,0:T(8,128)(2,1)S(1)}, bf16[256,1024]{1,0:T(8,128)(2,1)S(1)}, u32[]{:S(2)}, u32[]{:S(2)}) %collective-permute-start.20) | collective-permute-done | bytes 524320 | tf_op jit(solution)/shard_map/ppermute | solution.py:506
  67.9 1.4 contrast.1
  69.3 1.7 %collective-permute-start.17 = (bf16[64,1152]{1,0:T(8,128)(2,1)S(1)}, bf16[64,1152]{1,0:T(8,128)(2,1)S(1)}, u32[]{:S(2)}, u32[]{:S(2)}) collective-permute-start(bf16[64,1152]{1,0:T(8,128)(2,1)S(1)} %get-tuple-element.61), channel_id=1, source_target_pairs={{0,3},{1,0},{2,1},{3,2},{4,7},{5,4},{6,5},{7,6},{8,11},{9,8},{10,9... | collective-permute-start | bytes 442376 | tf_op jit(solution)/shard_map/ppermute | solution.py:74
  71.0 3.3 %collective-permute-done.23.refs_11_.refs_5_ = bf16[128,1024]{1,0:T(8,128)(2,1)S(1)} collective-permute-done((bf16[128,1024]{1,0:T(8,128)(2,1)S(1)}, bf16[128,1024]{1,0:T(8,128)(2,1)S(1)}, u32[]{:S(2)}, u32[]{:S(2)}) %collective-permute-start.23) | collective-permute-done | bytes 262176 | tf_op jit(solution)/shard_map/ppermute | solution.py:513
  74.9 0.8 collective-permute-start.18
  75.7 5.9 %collective-permute-done.18.refs_6_ = bf16[64,1152]{1,0:T(8,128)(2,1)S(1)} collective-permute-done((bf16[64,1152]{1,0:T(8,128)(2,1)S(1)}, bf16[64,1152]{1,0:T(8,128)(2,1)S(1)}, u32[]{:S(2)}, u32[]{:S(2)}) %collective-permute-start.18) | collective-permute-done | bytes 147488 | tf_op jit(solution)/shard_map/ppermute | solution.py:74
  83.2 5.0 %collective-permute-done.25.refs_4_ = bf16[64,1024]{1,0:T(8,128)(2,1)S(1)} collective-permute-done((bf16[64,1024]{1,0:T(8,128)(2,1)S(1)}, bf16[64,1024]{1,0:T(8,128)(2,1)S(1)}, u32[]{:S(2)}, u32[]{:S(2)}) %collective-permute-start.25) | collective-permute-done | bytes 131104 | tf_op jit(solution)/shard_map/ppermute | solution.py:510
  88.2 2.2 %backward.1 = (bf16[64,2048]{1,0:T(8,128)(2,1)S(1)}, bf16[64,2048]{1,0:T(8,128)(2,1)S(1)}, bf16[256,1024]{1,0:T(8,128)(2,1)}) custom-call(s32[1]{0:T(128)} %bitcast.9.refs_10_.refs_0_, bf16[1024,1024]{1,0:T(8,128)(2,1)S(1)} %copy-done.1, bf16[1024,1024]{1,0:T(8,128)(2,1)S(1)} %get-tuple-element.49.refs_2_, bf16[64,1024]{1,0:T(8,128)(2,1)S(1)} %get-tuple-element.67.refs_3_, ...), custom_call_target="tpu_custom_call" | custom-call | flops 536870912 | bytes 6029316 | tf_op jit(solution)/shard_map/backward/pallas_call | solution.py:58
  91.1 1.3 collective-permute-start.27
  92.4 5.1 %collective-permute-done.26.rest_1_.refs_1_ = bf16[64,2048]{1,0:T(8,128)(2,1)S(1)} collective-permute-done((bf16[64,2048]{1,0:T(8,128)(2,1)S(1)}, bf16[64,2048]{1,0:T(8,128)(2,1)S(1)}, u32[]{:S(2)}, u32[]{:S(2)}) %collective-permute-start.26) | collective-permute-done | bytes 262176 | tf_op jit(solution)/shard_map/ppermute | solution.py:510
  97.5 0.8 copy-done.10
  98.3 4.1 %all-to-all-start = ((bf16[32,64,128]{2,1,0:T(8,128)(2,1)}), bf16[32,64,128]{2,1,0:T(8,128)(2,1)}, u32[]{:S(2)}, u32[]{:S(2)}) async-start(bf16[32,64,128]{2,1,0:T(8,128)(2,1)} %copy-done.10), calls=%async_computation | async-start | bytes 1048576 | tf_op jit(solution)/shard_map/all_to_all | solution.py:623
  102.6 3.4 %copy-done.3 = bf16[1024,4096]{1,0:T(8,128)(2,1)S(1)} copy-done((bf16[1024,4096]{1,0:T(8,128)(2,1)S(1)}, bf16[1024,4096]{1,0:T(8,128)(2,1)}, u32[]{:S(2)}) %copy-start.3) | copy-done | bytes 8388632
  105.9 1.0 copy-done.12
  107.0 0.9 copy-done.20
  107.9 5.9 %slope_rows.1 = (f32[24,128]{1,0:T(8,128)S(1)}, f32[24,128]{1,0:T(8,128)S(1)}) custom-call(s32[2]{0:T(128)S(1)} %pad_add_fusion.refs_0_.z_ref, bf16[1024,4096]{1,0:T(8,128)(2,1)S(1)} %copy-done.3, f32[1024,1]{1,0:T(8,128)S(1)} %copy-done.12, f32[1,128]{1,0:T(1,128)S(1)} %get-tuple-element.66.loss_ref, bf16[64,2048]{1,0:T(8,128)(2,1)S(1)} %copy-done.20, ...), custom_call_target="tpu_custom_call" | custom-call | flops 16777216 | bytes 8388608 | tf_op jit(solution)/shard_map/slope_rows/pallas_call | solution.py:406
  113.8 1.1 late.1
  115.5 0.8 copy-done.15
  116.2 0.7 collective-permute-done.29.refs_9_
  117.0 0.8 copy-done.17
  117.8 1.0 copy-done.8
  118.9 1.0 copy-done.14
  119.9 1.0 copy-done.16
  121.0 1.0 copy-done.18
  122.0 2.9 %grad_columns.1.refs_1_.refs_0_ = bf16[1024,128]{1,0:T(8,128)(2,1)S(1)} custom-call(s32[32]{0:T(128)S(1)} %stack.186.refs_8_.refs_0_, bf16[32,64,128]{2,1,0:T(8,128)(2,1)} %all-to-all-done.refs_1_, bf16[256,1024]{1,0:T(8,128)(2,1)S(1)} %copy-done.14, bf16[256,1024]{1,0:T(8,128)(2,1)S(1)} %collective-permute-done.20.refs_8_.refs_3_, ...), custom_call_target="tpu_custom_call" | custom-call | flops 536870912 | bytes 4980864 | tf_op jit(solution)/shard_map/grad_columns/pallas_call | solution.py:58
  124.9 2.5 %collective-permute-start.37 = (bf16[1024,128]{1,0:T(8,128)(2,1)S(1)}, bf16[1024,128]{1,0:T(8,128)(2,1)S(1)}, u32[]{:S(2)}, u32[]{:S(2)}) collective-permute-start(bf16[1024,128]{1,0:T(8,128)(2,1)S(1)} %grad_columns.1.refs_1_.refs_0_), channel_id=1, source_target_pairs={{0,18},{1,19},{2,16},{3,17},{16,2},{17,3},{18,0},{19,1},{4,22},{5,... | collective-permute-start | bytes 786440 | tf_op jit(solution)/shard_map/ppermute | solution.py:506
  128.4 1.5 %collective-permute-start.30 = (f32[24,128]{1,0:T(8,128)S(1)}, f32[24,128]{1,0:T(8,128)S(1)}, u32[]{:S(2)}, u32[]{:S(2)}) collective-permute-start(f32[24,128]{1,0:T(8,128)S(1)} %slopes_out.3), channel_id=1, source_target_pairs={{0,4},{4,0},{8,12},{12,8},{1,5},{5,1},{9,13},{13,9},{2,6},{6,2},{1... | collective-permute-start | bytes 36872 | tf_op jit(solution)/shard_map/ppermute | solution.py:510
  130.0 2.2 %collective-permute-done.30.refs_1_ = f32[24,128]{1,0:T(8,128)S(1)} collective-permute-done((f32[24,128]{1,0:T(8,128)S(1)}, f32[24,128]{1,0:T(8,128)S(1)}, u32[]{:S(2)}, u32[]{:S(2)}) %collective-permute-start.30) | collective-permute-done | bytes 12320 | tf_op jit(solution)/shard_map/ppermute | solution.py:510
  132.1 2.4 %collective-permute-start.31 = (f32[24,128]{1,0:T(8,128)S(1)}, f32[24,128]{1,0:T(8,128)S(1)}, u32[]{:S(2)}, u32[]{:S(2)}) collective-permute-start(f32[24,128]{1,0:T(8,128)S(1)} %sum_half.1.refs_0_), channel_id=1, source_target_pairs={{0,8},{4,12},{8,0},{12,4},{1,9},{5,13},{9,1},{13,5},{2,10},{6,14},... | collective-permute-start | bytes 36872 | tf_op jit(solution)/shard_map/ppermute | solution.py:513
  134.6 2.2 %collective-permute-done.31.refs_1_ = f32[24,128]{1,0:T(8,128)S(1)} collective-permute-done((f32[24,128]{1,0:T(8,128)S(1)}, f32[24,128]{1,0:T(8,128)S(1)}, u32[]{:S(2)}, u32[]{:S(2)}) %collective-permute-start.31) | collective-permute-done | bytes 12320 | tf_op jit(solution)/shard_map/ppermute | solution.py:513
  136.7 1.5 collective-permute-start.32
  138.3 2.2 %collective-permute-done.32.refs_1_ = f32[24,128]{1,0:T(8,128)S(1)} collective-permute-done((f32[24,128]{1,0:T(8,128)S(1)}, f32[24,128]{1,0:T(8,128)S(1)}, u32[]{:S(2)}, u32[]{:S(2)}) %collective-permute-start.32) | collective-permute-done | bytes 12320 | tf_op jit(solution)/shard_map/ppermute | solution.py:506
  140.4 1.5 %collective-permute-start.33 = (f32[24,128]{1,0:T(8,128)S(1)}, f32[24,128]{1,0:T(8,128)S(1)}, u32[]{:S(2)}, u32[]{:S(2)}) collective-permute-start(f32[24,128]{1,0:T(8,128)S(1)} %sum_plane.3.refs_0_), channel_id=1, source_target_pairs={{0,2},{1,3},{2,0},{3,1},{16,18},{17,19},{18,16},{19,17},{4,6},{5,7... | collective-permute-start | bytes 36872 | tf_op jit(solution)/shard_map/ppermute | solution.py:506
  142.0 2.2 %collective-permute-done.33.refs_1_ = f32[24,128]{1,0:T(8,128)S(1)} collective-permute-done((f32[24,128]{1,0:T(8,128)S(1)}, f32[24,128]{1,0:T(8,128)S(1)}, u32[]{:S(2)}, u32[]{:S(2)}) %collective-permute-start.33) | collective-permute-done | bytes 12320 | tf_op jit(solution)/shard_map/ppermute | solution.py:506
  144.1 1.2 collective-permute-done.34.refs_1_
  145.7 1.3 slope_sum.1
  146.9 1.6 %collective-permute-start.39 = (f32[1,1024]{1,0:T(1,128)S(1)}, f32[1,1024]{1,0:T(1,128)S(1)}, u32[]{:S(2)}, u32[]{:S(2)}) collective-permute-start(f32[1,1024]{1,0:T(1,128)S(1)} %get-tuple-element.76.refs_0_), channel_id=1, source_target_pairs={{0,4},{4,0},{8,12},{12,8},{1,5},{5,1},{9,13},{13,9},{2,6},{6,2},{1... | collective-permute-start | bytes 12296 | tf_op jit(solution)/shard_map/ppermute | solution.py:510
  148.6 3.4 %finish.1 = (f32[1024,1024]{1,0:T(8,128)}, f32[8,128]{1,0:T(8,128)S(1)}) custom-call(s32[8]{0:T(128)S(1)} %stack.149.refs_7_.refs_1_.refs_0_, f32[1,1024]{1,0:T(1,128)S(1)} %bitcast.53, f32[8,128]{1,0:T(8,128)S(1)} %get-tuple-element.74.refs_2_, bf16[4096,128]{1,0:T(8,128)(2,1)S(1)} %pack_columns.1.refs_3_, bf16[4096,128]{1,0:T(8,128)(2,1)S(1)} %collective-permute-done.38.refs_4_), custom_call_target="tpu_custom_call" | custom-call | bytes 6303776 | tf_op jit(solution)/shard_map/finish/pallas_call | solution.py:58
  (109 shorter events, 9.6 us)
Async XLA Ops:
  0.6 12.3 %copy-start.25 = (bf16[4096]{0:T(1024)(128)(2,1)S(1)}, bf16[4096]{0:T(1024)(128)(2,1)}, u32[]{:S(2)}) copy-start(bf16[4096]{0:T(1024)(128)(2,1)} %param.12) | copy-start | bytes 24580
  0.6 12.3 %copy-start.24 = (s32[64,32]{0,1:T(8,128)S(1)}, s32[64,32]{0,1:T(8,128)}, u32[]{:S(2)}) copy-start(s32[64,32]{0,1:T(8,128)} %param.10) | copy-start | bytes 24580
  0.7 12.4 %copy-start.26 = (s32[64]{0:T(128)S(1)}, s32[64]{0:T(128)}, u32[]{:S(2)}) copy-start(s32[64]{0:T(128)} %param.11) | copy-start | bytes 772
  1.6 16.2 %collective-permute-start.3 = (bf16[128,1024]{1,0:T(8,128)(2,1)S(1)}, bf16[128,1024]{1,0:T(8,128)(2,1)S(1)}, u32[]{:S(2)}, u32[]{:S(2)}) collective-permute-start(bf16[128,1024]{1,0:T(8,128)(2,1)S(1)} %constant_dynamic-slice_fusion.refs_2_), channel_id=1, source_target_pairs={{0,8},{4,12},{8,0},{12,4},{1,9},{5,13},{9,1},{13,5},{2,10},{6,14},... | collective-permute-start | bytes 786440 | tf_op jit(solution)/shard_map/ppermute | solution.py:513
  5.8 1.6 %copy-start = (bf16[1024,1024]{1,0:T(8,128)(2,1)S(1)}, bf16[1024,1024]{1,0:T(8,128)(2,1)}, u32[]{:S(2)}) copy-start(bf16[1024,1024]{1,0:T(8,128)(2,1)} %refs_1_.5) | copy-start | bytes 6291460
  9.8 11.7 %collective-permute-start.2 = (f32[1,1024]{1,0:T(1,128)S(1)}, f32[1,1024]{1,0:T(1,128)S(1)}, u32[]{:S(2)}, u32[]{:S(2)}) collective-permute-start(f32[1,1024]{1,0:T(1,128)S(1)} %block_u.1), channel_id=1, source_target_pairs={{0,12},{4,0},{8,4},{12,8},{1,13},{5,1},{9,5},{13,9},{2,14},{6,2},{... | collective-permute-start | bytes 12296 | tf_op jit(solution)/shard_map/ppermute | solution.py:74
  11.1 10.3 %collective-permute-start.1 = (f32[1,1024]{1,0:T(1,128)S(1)}, f32[1,1024]{1,0:T(1,128)S(1)}, u32[]{:S(2)}, u32[]{:S(2)}) collective-permute-start(f32[1,1024]{1,0:T(1,128)S(1)} %block_u.1), channel_id=1, source_target_pairs={{0,8},{4,12},{8,0},{12,4},{1,9},{5,13},{9,1},{13,5},{2,10},{6,14},... | collective-permute-start | bytes 12296 | tf_op jit(solution)/shard_map/ppermute | solution.py:74
  12.8 8.1 %collective-permute-start = (f32[1,1024]{1,0:T(1,128)S(1)}, f32[1,1024]{1,0:T(1,128)S(1)}, u32[]{:S(2)}, u32[]{:S(2)}) collective-permute-start(f32[1,1024]{1,0:T(1,128)S(1)} %block_u.1), channel_id=1, source_target_pairs={{0,4},{4,8},{8,12},{12,0},{1,5},{5,9},{9,13},{13,1},{2,6},{6,10},{... | collective-permute-start | bytes 12296 | tf_op jit(solution)/shard_map/ppermute | solution.py:74
  17.9 18.9 %collective-permute-start.7 = (bf16[128,1024]{1,0:T(8,128)(2,1)S(1)}, bf16[128,1024]{1,0:T(8,128)(2,1)S(1)}, u32[]{:S(2)}, u32[]{:S(2)}) collective-permute-start(bf16[128,1024]{1,0:T(8,128)(2,1)S(1)} %collective-permute-done.3.refs_6_.refs_0_), channel_id=1, source_target_pairs={{0,18},{1,19},{2,16},{3,17},{16,2},{17,3},{18,0},{19,1},{4,22},{5,... | collective-permute-start | bytes 786440 | tf_op jit(solution)/shard_map/ppermute | solution.py:506
  20.4 16.4 %collective-permute-start.6 = (bf16[128,1024]{1,0:T(8,128)(2,1)S(1)}, bf16[128,1024]{1,0:T(8,128)(2,1)S(1)}, u32[]{:S(2)}, u32[]{:S(2)}) collective-permute-start(bf16[128,1024]{1,0:T(8,128)(2,1)S(1)} %collective-permute-done.3.refs_6_.refs_0_), channel_id=1, source_target_pairs={{0,16},{1,17},{2,18},{3,19},{16,0},{17,1},{18,2},{19,3},{4,20},{5,... | collective-permute-start | bytes 786440 | tf_op jit(solution)/shard_map/ppermute | solution.py:506
  20.9 15.9 %collective-permute-start.5 = (bf16[128,1024]{1,0:T(8,128)(2,1)S(1)}, bf16[128,1024]{1,0:T(8,128)(2,1)S(1)}, u32[]{:S(2)}, u32[]{:S(2)}) collective-permute-start(bf16[128,1024]{1,0:T(8,128)(2,1)S(1)} %collective-permute-done.3.refs_6_.refs_0_), channel_id=1, source_target_pairs={{0,2},{1,3},{2,0},{3,1},{16,18},{17,19},{18,16},{19,17},{4,6},{5,7... | collective-permute-start | bytes 786440 | tf_op jit(solution)/shard_map/ppermute | solution.py:506
  21.4 3.4 %copy-start.6 = (bf16[64,16,4096]{2,1,0:T(8,128)(2,1)S(1)}, bf16[64,16,4096]{2,1,0:T(8,128)(2,1)}, u32[]{:S(2)}) copy-start(bf16[64,16,4096]{2,1,0:T(8,128)(2,1)} %param.8) | copy-start | bytes 25165828
  33.5 3.3 %copy-start.2 = (bf16[1024,4096]{1,0:T(8,128)(2,1)}, bf16[1024,4096]{1,0:T(8,128)(2,1)S(1)}, u32[]{:S(2)}) copy-start(bf16[1024,4096]{1,0:T(8,128)(2,1)S(1)} %get-tuple-element.50.normed_ref) | copy-start | bytes 25165828
  36.8 7.5 %copy-start.11 = (f32[1024,1]{1,0:T(8,128)}, f32[1024,1]{1,0:T(8,128)S(1)}, u32[]{:S(2)}) copy-start(f32[1024,1]{1,0:T(8,128)S(1)} %get-tuple-element.51.curve_ref) | copy-start | bytes 12292
  36.8 5.6 %copy-start.9 = (bf16[1024,1024]{1,0:T(8,128)(2,1)S(1)}, bf16[1024,1024]{1,0:T(8,128)(2,1)}, u32[]{:S(2)}) copy-start(bf16[1024,1024]{1,0:T(8,128)(2,1)} %refs_0_.4) | copy-start | bytes 6291460
  36.8 8.9 %copy-start.1 = (bf16[1024,1024]{1,0:T(8,128)(2,1)S(1)}, bf16[1024,1024]{1,0:T(8,128)(2,1)}, u32[]{:S(2)}) copy-start(bf16[1024,1024]{1,0:T(8,128)(2,1)} %refs_1_.5) | copy-start | bytes 6291460
  36.9 8.8 %collective-permute-start.8 = (bf16[512,1024]{1,0:T(8,128)(2,1)S(1)}, bf16[512,1024]{1,0:T(8,128)(2,1)S(1)}, u32[]{:S(2)}, u32[]{:S(2)}) collective-permute-start(bf16[512,1024]{1,0:T(8,128)(2,1)S(1)} %pack_shares.1.refs_5_), channel_id=1, source_target_pairs={{0,1},{1,0},{2,3},{3,2},{16,17},{17,16},{18,19},{19,18},{4,5},{5,4... | collective-permute-start | bytes 3145736 | tf_op jit(solution)/shard_map/ppermute | solution.py:506
  37.0 8.7 %collective-permute-start.4 = (bf16[64,2048]{1,0:T(8,128)(2,1)S(1)}, bf16[64,2048]{1,0:T(8,128)(2,1)S(1)}, u32[]{:S(2)}, u32[]{:S(2)}) collective-permute-start(bf16[64,2048]{1,0:T(8,128)(2,1)S(1)} %get-tuple-element.42), channel_id=1, source_target_pairs={{0,4},{4,0},{8,12},{12,8},{1,5},{5,1},{9,13},{13,9},{2,6},{6,2},{1... | collective-permute-start | bytes 786440 | tf_op jit(solution)/shard_map/ppermute | solution.py:510
  37.8 3.3 %collective-permute-start.9 = (s32[64,8]{1,0:T(8,128)S(1)}, s32[64,8]{1,0:T(8,128)S(1)}, u32[]{:S(2)}, u32[]{:S(2)}) collective-permute-start(s32[64,8]{1,0:T(8,128)S(1)} %get-tuple-element.45), channel_id=1, source_target_pairs={{0,1},{1,2},{2,3},{3,0},{4,5},{5,6},{6,7},{7,4},{8,9},{9,10},{10,1... | collective-permute-start | bytes 6152 | tf_op jit(solution)/shard_map/ppermute | solution.py:74
  38.0 3.9 %collective-permute-start.10 = (s32[64,8]{1,0:T(8,128)S(1)}, s32[64,8]{1,0:T(8,128)S(1)}, u32[]{:S(2)}, u32[]{:S(2)}) collective-permute-start(s32[64,8]{1,0:T(8,128)S(1)} %get-tuple-element.46), channel_id=1, source_target_pairs={{0,2},{1,3},{2,0},{3,1},{4,6},{5,7},{6,4},{7,5},{8,10},{9,11},{10,... | collective-permute-start | bytes 6152 | tf_op jit(solution)/shard_map/ppermute | solution.py:74
  39.5 2.9 %collective-permute-start.11 = (s32[64,8]{1,0:T(8,128)S(1)}, s32[64,8]{1,0:T(8,128)S(1)}, u32[]{:S(2)}, u32[]{:S(2)}) collective-permute-start(s32[64,8]{1,0:T(8,128)S(1)} %get-tuple-element.47), channel_id=1, source_target_pairs={{0,3},{1,0},{2,1},{3,2},{4,7},{5,4},{6,5},{7,6},{8,11},{9,8},{10,9... | collective-permute-start | bytes 6152 | tf_op jit(solution)/shard_map/ppermute | solution.py:74
  47.1 41.0 %copy-start.4 = (bf16[1024,1024]{1,0:T(8,128)(2,1)}, bf16[1024,1024]{1,0:T(8,128)(2,1)S(1)}, u32[]{:S(2)}) copy-start(bf16[1024,1024]{1,0:T(8,128)(2,1)S(1)} %get-tuple-element.49.refs_2_) | copy-start | bytes 6291460
  47.2 7.9 %collective-permute-start.13 = (bf16[128,1024]{1,0:T(8,128)(2,1)S(1)}, bf16[128,1024]{1,0:T(8,128)(2,1)S(1)}, u32[]{:S(2)}, u32[]{:S(2)}) collective-permute-start(bf16[128,1024]{1,0:T(8,128)(2,1)S(1)} %get-tuple-element.55.refs_3_), channel_id=1, source_target_pairs={{0,2},{1,3},{2,0},{3,1},{16,18},{17,19},{18,16},{19,17},{4,6},{5,7... | collective-permute-start | bytes 786440 | tf_op jit(solution)/shard_map/ppermute | solution.py:506
  48.8 5.0 %collective-permute-start.12 = (bf16[64,1024]{1,0:T(8,128)(2,1)S(1)}, bf16[64,1024]{1,0:T(8,128)(2,1)S(1)}, u32[]{:S(2)}, u32[]{:S(2)}) collective-permute-start(bf16[64,1024]{1,0:T(8,128)(2,1)S(1)} %get-tuple-element.53), channel_id=1, source_target_pairs={{0,4},{4,0},{8,12},{12,8},{1,5},{5,1},{9,13},{13,9},{2,6},{6,2},{1... | collective-permute-start | bytes 393224 | tf_op jit(solution)/shard_map/ppermute | solution.py:510
  55.2 27.4 %copy-start.13 = (bf16[256,1024]{1,0:T(8,128)(2,1)}, bf16[256,1024]{1,0:T(8,128)(2,1)S(1)}, u32[]{:S(2)}) copy-start(bf16[256,1024]{1,0:T(8,128)(2,1)S(1)} %get-tuple-element.64.refs_2_) | copy-start | bytes 1572868
  55.2 27.5 %copy-start.21 = (bf16[64,1024]{1,0:T(8,128)(2,1)S(1)}, bf16[64,1024]{1,0:T(8,128)(2,1)}, u32[]{:S(2)}) copy-start(bf16[64,1024]{1,0:T(8,128)(2,1)} %refs_0_.5) | copy-start | bytes 393220
  55.2 12.7 %collective-permute-start.20 = (bf16[256,1024]{1,0:T(8,128)(2,1)S(1)}, bf16[256,1024]{1,0:T(8,128)(2,1)S(1)}, u32[]{:S(2)}, u32[]{:S(2)}) collective-permute-start(bf16[256,1024]{1,0:T(8,128)(2,1)S(1)} %get-tuple-element.64.refs_2_), channel_id=1, source_target_pairs={{0,16},{1,17},{2,18},{3,19},{16,0},{17,1},{18,2},{19,3},{4,20},{5,... | collective-permute-start | bytes 1572872 | tf_op jit(solution)/shard_map/ppermute | solution.py:506
  56.9 4.9 %collective-permute-start.16 = (bf16[64,1024]{1,0:T(8,128)(2,1)S(1)}, bf16[64,1024]{1,0:T(8,128)(2,1)S(1)}, u32[]{:S(2)}, u32[]{:S(2)}) collective-permute-start(bf16[64,1024]{1,0:T(8,128)(2,1)S(1)} %get-tuple-element.58.refs_3_), channel_id=1, source_target_pairs={{0,3},{1,0},{2,1},{3,2},{4,7},{5,4},{6,5},{7,6},{8,11},{9,8},{10,9... | collective-permute-start | bytes 393224 | tf_op jit(solution)/shard_map/ppermute | solution.py:74
  56.9 11.1 %collective-permute-start.15 = (bf16[64,1024]{1,0:T(8,128)(2,1)S(1)}, bf16[64,1024]{1,0:T(8,128)(2,1)S(1)}, u32[]{:S(2)}, u32[]{:S(2)}) collective-permute-start(bf16[64,1024]{1,0:T(8,128)(2,1)S(1)} %get-tuple-element.58.refs_3_), channel_id=1, source_target_pairs={{0,2},{1,3},{2,0},{3,1},{4,6},{5,7},{6,4},{7,5},{8,10},{9,11},{10,... | collective-permute-start | bytes 393224 | tf_op jit(solution)/shard_map/ppermute | solution.py:74
  58.4 9.5 %collective-permute-start.14 = (bf16[64,1024]{1,0:T(8,128)(2,1)S(1)}, bf16[64,1024]{1,0:T(8,128)(2,1)S(1)}, u32[]{:S(2)}, u32[]{:S(2)}) collective-permute-start(bf16[64,1024]{1,0:T(8,128)(2,1)S(1)} %get-tuple-element.58.refs_3_), channel_id=1, source_target_pairs={{0,1},{1,2},{2,3},{3,0},{4,5},{5,6},{6,7},{7,4},{8,9},{9,10},{10,1... | collective-permute-start | bytes 393224 | tf_op jit(solution)/shard_map/ppermute | solution.py:74
  58.6 15.7 %collective-permute-start.23 = (bf16[128,1024]{1,0:T(8,128)(2,1)S(1)}, bf16[128,1024]{1,0:T(8,128)(2,1)S(1)}, u32[]{:S(2)}, u32[]{:S(2)}) collective-permute-start(bf16[128,1024]{1,0:T(8,128)(2,1)S(1)} %get-tuple-element.65), channel_id=1, source_target_pairs={{0,8},{4,12},{8,0},{12,4},{1,9},{5,13},{9,1},{13,5},{2,10},{6,14},... | collective-permute-start | bytes 786440 | tf_op jit(solution)/shard_map/ppermute | solution.py:513
  61.8 20.9 %collective-permute-start.21 = (bf16[256,1024]{1,0:T(8,128)(2,1)S(1)}, bf16[256,1024]{1,0:T(8,128)(2,1)S(1)}, u32[]{:S(2)}, u32[]{:S(2)}) collective-permute-start(bf16[256,1024]{1,0:T(8,128)(2,1)S(1)} %get-tuple-element.64.refs_2_), channel_id=1, source_target_pairs={{0,1},{1,0},{2,3},{3,2},{16,17},{17,16},{18,19},{19,18},{4,5},{5,4... | collective-permute-start | bytes 1572872 | tf_op jit(solution)/shard_map/ppermute | solution.py:506
  67.9 14.8 %collective-permute-start.22 = (bf16[256,1024]{1,0:T(8,128)(2,1)S(1)}, bf16[256,1024]{1,0:T(8,128)(2,1)S(1)}, u32[]{:S(2)}, u32[]{:S(2)}) collective-permute-start(bf16[256,1024]{1,0:T(8,128)(2,1)S(1)} %collective-permute-done.20.refs_8_.refs_3_), channel_id=1, source_target_pairs={{0,1},{1,0},{2,3},{3,2},{16,17},{17,16},{18,19},{19,18},{4,5},{5,4... | collective-permute-start | bytes 1572872 | tf_op jit(solution)/shard_map/ppermute | solution.py:506
  69.3 6.4 %collective-permute-start.17 = (bf16[64,1152]{1,0:T(8,128)(2,1)S(1)}, bf16[64,1152]{1,0:T(8,128)(2,1)S(1)}, u32[]{:S(2)}, u32[]{:S(2)}) collective-permute-start(bf16[64,1152]{1,0:T(8,128)(2,1)S(1)} %get-tuple-element.61), channel_id=1, source_target_pairs={{0,3},{1,0},{2,1},{3,2},{4,7},{5,4},{6,5},{7,6},{8,11},{9,8},{10,9... | collective-permute-start | bytes 442376 | tf_op jit(solution)/shard_map/ppermute | solution.py:74
  74.3 8.3 %collective-permute-start.24 = (bf16[128,1024]{1,0:T(8,128)(2,1)S(1)}, bf16[128,1024]{1,0:T(8,128)(2,1)S(1)}, u32[]{:S(2)}, u32[]{:S(2)}) collective-permute-start(bf16[128,1024]{1,0:T(8,128)(2,1)S(1)} %collective-permute-done.23.refs_11_.refs_5_), channel_id=1, source_target_pairs={{0,16},{1,17},{2,18},{3,19},{16,0},{17,1},{18,2},{19,3},{4,20},{5,... | collective-permute-start | bytes 786440 | tf_op jit(solution)/shard_map/ppermute | solution.py:506
  74.9 6.7 %collective-permute-start.18 = (bf16[64,1152]{1,0:T(8,128)(2,1)S(1)}, bf16[64,1152]{1,0:T(8,128)(2,1)S(1)}, u32[]{:S(2)}, u32[]{:S(2)}) collective-permute-start(bf16[64,1152]{1,0:T(8,128)(2,1)S(1)} %get-tuple-element.62), channel_id=1, source_target_pairs={{0,2},{1,3},{2,0},{3,1},{4,6},{5,7},{6,4},{7,5},{8,10},{9,11},{10,... | collective-permute-start | bytes 442376 | tf_op jit(solution)/shard_map/ppermute | solution.py:74
  75.7 6.3 %collective-permute-start.19 = (bf16[64,1152]{1,0:T(8,128)(2,1)S(1)}, bf16[64,1152]{1,0:T(8,128)(2,1)S(1)}, u32[]{:S(2)}, u32[]{:S(2)}) collective-permute-start(bf16[64,1152]{1,0:T(8,128)(2,1)S(1)} %get-tuple-element.63), channel_id=1, source_target_pairs={{0,1},{1,2},{2,3},{3,0},{4,5},{5,6},{6,7},{7,4},{8,9},{9,10},{10,1... | collective-permute-start | bytes 442376 | tf_op jit(solution)/shard_map/ppermute | solution.py:74
  82.7 7.7 %copy-start.7 = (bf16[256,1024]{1,0:T(8,128)(2,1)}, bf16[256,1024]{1,0:T(8,128)(2,1)S(1)}, u32[]{:S(2)}) copy-start(bf16[256,1024]{1,0:T(8,128)(2,1)S(1)} %collective-permute-done.22.refs_10_.refs_7_) | copy-start | bytes 1572868
  83.1 5.0 %collective-permute-start.25 = (bf16[64,1024]{1,0:T(8,128)(2,1)S(1)}, bf16[64,1024]{1,0:T(8,128)(2,1)S(1)}, u32[]{:S(2)}, u32[]{:S(2)}) collective-permute-start(bf16[64,1024]{1,0:T(8,128)(2,1)S(1)} %get-tuple-element.67.refs_3_), channel_id=1, source_target_pairs={{0,4},{4,0},{8,12},{12,8},{1,5},{5,1},{9,13},{13,9},{2,6},{6,2},{1... | collective-permute-start | bytes 393224 | tf_op jit(solution)/shard_map/ppermute | solution.py:510
  91.1 6.4 %collective-permute-start.26 = (bf16[64,2048]{1,0:T(8,128)(2,1)S(1)}, bf16[64,2048]{1,0:T(8,128)(2,1)S(1)}, u32[]{:S(2)}, u32[]{:S(2)}) collective-permute-start(bf16[64,2048]{1,0:T(8,128)(2,1)S(1)} %get-tuple-element.69), channel_id=1, source_target_pairs={{0,4},{4,0},{8,12},{12,8},{1,5},{5,1},{9,13},{13,9},{2,6},{6,2},{1... | collective-permute-start | bytes 786440 | tf_op jit(solution)/shard_map/ppermute | solution.py:510
  91.1 22.7 %collective-permute-start.27 = (bf16[256,1024]{1,0:T(8,128)(2,1)}, bf16[256,1024]{1,0:T(8,128)(2,1)}, u32[]{:S(2)}, u32[]{:S(2)}) collective-permute-start(bf16[256,1024]{1,0:T(8,128)(2,1)} %get-tuple-element.72.refs_4_), channel_id=1, source_target_pairs={{0,2},{1,3},{2,0},{3,1},{16,18},{17,19},{18,16},{19,17},{4,6},{5,7... | collective-permute-start | bytes 1572872 | tf_op jit(solution)/shard_map/ppermute | solution.py:506
  98.3 19.5 %all-to-all-start = ((bf16[32,64,128]{2,1,0:T(8,128)(2,1)}), bf16[32,64,128]{2,1,0:T(8,128)(2,1)}, u32[]{:S(2)}, u32[]{:S(2)}) async-start(bf16[32,64,128]{2,1,0:T(8,128)(2,1)} %copy-done.10), calls=%async_computation | async-start | bytes 1048576 | tf_op jit(solution)/shard_map/all_to_all | solution.py:623
  102.5 13.0 %collective-permute-start.28 = (bf16[256,1024]{1,0:T(8,128)(2,1)}, bf16[256,1024]{1,0:T(8,128)(2,1)S(1)}, u32[]{:S(2)}, u32[]{:S(2)}) collective-permute-start(bf16[256,1024]{1,0:T(8,128)(2,1)} %get-tuple-element.72.refs_4_), channel_id=1, source_target_pairs={{0,1},{1,0},{2,3},{3,2},{16,17},{17,16},{18,19},{19,18},{4,5},{5,4... | collective-permute-start | bytes 1572872 | tf_op jit(solution)/shard_map/ppermute | solution.py:506
  102.6 3.4 %copy-start.3 = (bf16[1024,4096]{1,0:T(8,128)(2,1)S(1)}, bf16[1024,4096]{1,0:T(8,128)(2,1)}, u32[]{:S(2)}) copy-start(bf16[1024,4096]{1,0:T(8,128)(2,1)} %copy-done.2) | copy-start | bytes 25165828
  105.9 1.0 copy-start.12
  107.0 0.9 copy-start.20
  114.9 2.1 %collective-permute-start.29 = (bf16[256,1024]{1,0:T(8,128)(2,1)S(1)}, bf16[256,1024]{1,0:T(8,128)(2,1)S(1)}, u32[]{:S(2)}, u32[]{:S(2)}) collective-permute-start(bf16[256,1024]{1,0:T(8,128)(2,1)S(1)} %late.1), channel_id=1, source_target_pairs={{0,1},{1,0},{2,3},{3,2},{16,17},{17,16},{18,19},{19,18},{4,5},{5,4... | collective-permute-start | bytes 1572872 | tf_op jit(solution)/shard_map/ppermute | solution.py:506
  117.0 0.8 copy-start.17
  117.8 1.0 copy-start.8
  118.9 1.0 copy-start.14
  119.9 1.0 copy-start.16
  121.0 1.0 copy-start.18
  124.9 20.8 %copy-start.5 = (bf16[1024,1024]{1,0:T(8,128)(2,1)S(1)}, bf16[1024,1024]{1,0:T(8,128)(2,1)}, u32[]{:S(2)}) copy-start(bf16[1024,1024]{1,0:T(8,128)(2,1)} %copy-done.4) | copy-start | bytes 6291460
  124.9 20.5 %collective-permute-start.37 = (bf16[1024,128]{1,0:T(8,128)(2,1)S(1)}, bf16[1024,128]{1,0:T(8,128)(2,1)S(1)}, u32[]{:S(2)}, u32[]{:S(2)}) collective-permute-start(bf16[1024,128]{1,0:T(8,128)(2,1)S(1)} %grad_columns.1.refs_1_.refs_0_), channel_id=1, source_target_pairs={{0,18},{1,19},{2,16},{3,17},{16,2},{17,3},{18,0},{19,1},{4,22},{5,... | collective-permute-start | bytes 786440 | tf_op jit(solution)/shard_map/ppermute | solution.py:506
  127.4 17.9 %collective-permute-start.36 = (bf16[1024,128]{1,0:T(8,128)(2,1)S(1)}, bf16[1024,128]{1,0:T(8,128)(2,1)S(1)}, u32[]{:S(2)}, u32[]{:S(2)}) collective-permute-start(bf16[1024,128]{1,0:T(8,128)(2,1)S(1)} %grad_columns.1.refs_1_.refs_0_), channel_id=1, source_target_pairs={{0,16},{1,17},{2,18},{3,19},{16,0},{17,1},{18,2},{19,3},{4,20},{5,... | collective-permute-start | bytes 786440 | tf_op jit(solution)/shard_map/ppermute | solution.py:506
  128.0 17.4 %collective-permute-start.35 = (bf16[1024,128]{1,0:T(8,128)(2,1)S(1)}, bf16[1024,128]{1,0:T(8,128)(2,1)S(1)}, u32[]{:S(2)}, u32[]{:S(2)}) collective-permute-start(bf16[1024,128]{1,0:T(8,128)(2,1)S(1)} %grad_columns.1.refs_1_.refs_0_), channel_id=1, source_target_pairs={{0,2},{1,3},{2,0},{3,1},{16,18},{17,19},{18,16},{19,17},{4,6},{5,7... | collective-permute-start | bytes 786440 | tf_op jit(solution)/shard_map/ppermute | solution.py:506
  128.4 3.7 %collective-permute-start.30 = (f32[24,128]{1,0:T(8,128)S(1)}, f32[24,128]{1,0:T(8,128)S(1)}, u32[]{:S(2)}, u32[]{:S(2)}) collective-permute-start(f32[24,128]{1,0:T(8,128)S(1)} %slopes_out.3), channel_id=1, source_target_pairs={{0,4},{4,0},{8,12},{12,8},{1,5},{5,1},{9,13},{13,9},{2,6},{6,2},{1... | collective-permute-start | bytes 36872 | tf_op jit(solution)/shard_map/ppermute | solution.py:510
  132.1 4.6 %collective-permute-start.31 = (f32[24,128]{1,0:T(8,128)S(1)}, f32[24,128]{1,0:T(8,128)S(1)}, u32[]{:S(2)}, u32[]{:S(2)}) collective-permute-start(f32[24,128]{1,0:T(8,128)S(1)} %sum_half.1.refs_0_), channel_id=1, source_target_pairs={{0,8},{4,12},{8,0},{12,4},{1,9},{5,13},{9,1},{13,5},{2,10},{6,14},... | collective-permute-start | bytes 36872 | tf_op jit(solution)/shard_map/ppermute | solution.py:513
  136.7 3.7 %collective-permute-start.32 = (f32[24,128]{1,0:T(8,128)S(1)}, f32[24,128]{1,0:T(8,128)S(1)}, u32[]{:S(2)}, u32[]{:S(2)}) collective-permute-start(f32[24,128]{1,0:T(8,128)S(1)} %sum_mirror.1.refs_0_), channel_id=1, source_target_pairs={{0,16},{1,17},{2,18},{3,19},{16,0},{17,1},{18,2},{19,3},{4,20},{5,... | collective-permute-start | bytes 36872 | tf_op jit(solution)/shard_map/ppermute | solution.py:506
  140.4 3.7 %collective-permute-start.33 = (f32[24,128]{1,0:T(8,128)S(1)}, f32[24,128]{1,0:T(8,128)S(1)}, u32[]{:S(2)}, u32[]{:S(2)}) collective-permute-start(f32[24,128]{1,0:T(8,128)S(1)} %sum_plane.3.refs_0_), channel_id=1, source_target_pairs={{0,2},{1,3},{2,0},{3,1},{16,18},{17,19},{18,16},{19,17},{4,6},{5,7... | collective-permute-start | bytes 36872 | tf_op jit(solution)/shard_map/ppermute | solution.py:506
  144.1 1.2 collective-permute-start.34
  145.4 3.1 %copy-start.23 = (f32[1024]{0:T(1024)S(1)}, f32[1024]{0:T(1024)}, u32[]{:S(2)}) copy-start(f32[1024]{0:T(1024)} %param.14) | copy-start | bytes 12292
  145.4 3.1 %collective-permute-start.38 = (bf16[4096,128]{1,0:T(8,128)(2,1)S(1)}, bf16[4096,128]{1,0:T(8,128)(2,1)S(1)}, u32[]{:S(2)}, u32[]{:S(2)}) collective-permute-start(bf16[4096,128]{1,0:T(8,128)(2,1)S(1)} %pack_columns.1.refs_3_), channel_id=1, source_target_pairs={{0,1},{1,0},{2,3},{3,2},{16,17},{17,16},{18,19},{19,18},{4,5},{5,4... | collective-permute-start | bytes 3145736 | tf_op jit(solution)/shard_map/ppermute | solution.py:506
  146.9 5.0 %collective-permute-start.39 = (f32[1,1024]{1,0:T(1,128)S(1)}, f32[1,1024]{1,0:T(1,128)S(1)}, u32[]{:S(2)}, u32[]{:S(2)}) collective-permute-start(f32[1,1024]{1,0:T(1,128)S(1)} %get-tuple-element.76.refs_0_), channel_id=1, source_target_pairs={{0,4},{4,0},{8,12},{12,8},{1,5},{5,1},{9,13},{13,9},{2,6},{6,2},{1... | collective-permute-start | bytes 12296 | tf_op jit(solution)/shard_map/ppermute | solution.py:510
  (4 other events, 3.0 us)

commit v5 on v4

--- a/solution.py
+++ b/solution.py
@@ -64,7 +64,9 @@
         out_specs=[VMEM] * len(outs),
         scratch_shapes=list(scratch),
         cost_estimate=pl.CostEstimate(flops=flops, bytes_accessed=moved, transcendentals=0),
-        compiler_params=pltpu.CompilerParams(vmem_limit_bytes=2 * (moved + held) + 6 * MIB),
+        compiler_params=pltpu.CompilerParams(
+            vmem_limit_bytes=(4 if copy else 2) * (moved + held) + (12 if copy else 6) * MIB
+        ),
         name=name,
     )(*ins, *after)
 
@@ -190,7 +192,7 @@
         cost_estimate=pl.CostEstimate(
             flops=10 * tokens * width, bytes_accessed=4 * tokens * width, transcendentals=0
         ),
-        compiler_params=pltpu.CompilerParams(vmem_limit_bytes=20 * MIB),
+        compiler_params=pltpu.CompilerParams(vmem_limit_bytes=50 * MIB),
         name="gate_rows",
     )(*inputs, *events)
 
@@ -593,23 +595,24 @@
 
     pieces = [embedded] + [shift(embedded, "item", k) for k in steps_i]
     near_far = [plane_shift(near, dg, 0, 0) for dg in range(1, n_g)]
+    near_cores = [plane_shift(near, 0, 0, dc) for dc in range(1, n_c)]
     wide = (queries, proj_width + LANES)
     parts = call(
         functools.partial(contrast_kernel, n_i),
         [shape(wide, F32)] + [shape(wide, BF16)] * (n_i - 1),
         [slab, slab_scale, counts] + pieces, "contrast",
-        flops=4 * n_i * queries * slab.shape[0] * proj_width,
-    )
+        flops=4 * n_i * queries * slab.shape[0] * proj_width, after=near_cores,
+    )
+    near_far_late = [passed(array, "near_far", parts[0]) for array in near_far]
     parts = [parts[0]] + [shift(parts[k], "item", -k) for k in steps_i]
-    near_cores = [plane_shift(near, 0, 0, dc) for dc in range(1, n_c)]
-    near_far_cores = [[plane_shift(array, 0, 0, dc) for array in near_far] for dc in range(1, n_c)]
+    near_far_cores = [[plane_shift(array, 0, 0, dc) for array in near_far_late] for dc in range(1, n_c)]
+    other = passed(other, "other", parts[1 % n_i])
     others = [other] + [plane_shift(other, dg, 0, 0) for dg in range(1, n_g)]
     cols = proj_width // n_plane
     grad, grad_columns, loss = call(
         functools.partial(grad_kernel, n_i, root),
         [row16, shape((n_all, queries, cols), BF16), shape((1, LANES), F32)],
         [positives, pooled, unit, embedded] + parts, "grad_pooled",
-        after=near_far + near_cores + sum(near_far_cores, []) + others,
     )
 
     pieces = [grad] + [half_shift(grad, k) for k in range(1, half)]
@@ -617,13 +620,17 @@
         functools.partial(back_kernel, half, n_g),
         [shape((queries, 2 * depth), BF16)] * half + [shape((n_g * half * queries, depth), BF16)],
         [side_arr, proj_weight, mirror] + pieces + others, "backward",
-        flops=4 * half * queries * depth * proj_width, smem=1,
+        flops=4 * half * queries * depth * proj_width, smem=1, after=near_cores + sum(near_far_cores, []),
     )
     backs = [backs[0]] + [half_shift(backs[k], -k) for k in range(1, half)]
     all_columns = lax.all_to_all(
         passed(grad_columns, "columns_out", backs[-1]), EVERY, 0, 0, tiled=True
     )
     slopes = slope_rows(both_arr, normed, curve, loss, backs, seq, n_z)
+    def total(parts, name):
+        return call(add_kernel, [shape(parts[0].shape, F32)], parts, name)[0]
+
+    slope = total([slopes[0]] + [half_shift(slopes[k], k) for k in range(1, half)], "sum_half")
     across = [plane_shift(others, 0, dh, 0) for dh in range(1, n_h)]
     late = [pack([array], "late", slopes[0]) for array in across]
     spread = []
@@ -636,14 +643,10 @@
     block_columns = call(
         functools.partial(columns_kernel, len(spread)), [shape((depth, cols), BF16)],
         [ranks, all_columns] + spread, "grad_columns",
-        flops=2 * n_all * queries * depth * cols, scratch=[pltpu.VMEM((n_all * queries, cols), BF16)], smem=1, copy=True,
+        flops=2 * n_all * queries * depth * cols, scratch=[pltpu.VMEM((n_all * queries, cols), BF16)], smem=1, copy=True, after=[slope],
     )[0]
     on_chips = [block_columns if dg == dh == 0 else plane_shift(block_columns, dg, dh, 0) for dg, dh in chips]
-    def total(parts, name):
-        return call(add_kernel, [shape(parts[0].shape, F32)], parts, name)[0]
-
-    slopes = [passed(array, "slopes_out", block_columns) for array in slopes]
-    slope = total([slopes[0]] + [half_shift(slopes[k], k) for k in range(1, half)], "sum_half")
+    slope = passed(slope, "slope_out", block_columns)
     slope = total([slope, mirror_shift(slope)], "sum_mirror")
     for axis, size in ((0, n_g), (1, n_h), (2, n_c)):
         if size > 1:

time: 154 us -> 152 us (0.987)
  local copies, waits for them, and re-layouts: 23.4 us -> 16.7 us
  Pallas kernels: 33 us -> 36.1 us
  waiting for transfers between devices: 48.8 us -> 50.6 us
    unnamed x55 -> x51, local copies, waits for them, and re-layouts: 21.8 us -> 15.1 us
    pallas_call x1, Pallas kernels: 8.63 us -> 11.6 us  [gate_rows(): pl.pallas_call(run, grid=(queries // group,), out_shape=outs, in_specs=[S...]
    ppermute x19, starting transfers between devices: 17.2 us -> 14.5 us  [plane_shift(): return lax.ppermute(values, PLANE, pairs)]
    ppermute x3, waiting for transfers between devices: 9.68 us -> 12.2 us  [mirror_shift(): lax.ppermute(values, 'fsdp', [(a, (a + half) % n_z) for a in range(n_z)])]
    ppermute x6, starting transfers between devices: 4.73 us -> 6.63 us  [half_shift(): return lax.ppermute(values, 'fsdp', pairs)]
    ppermute x12, waiting for transfers between devices: 7.95 us -> 6.27 us  [shift(): return lax.ppermute(values, axis, [(i, (i + k) % n) for i in range(n)])]
    pallas_call x22 -> x23, Pallas kernels: 18.5 us -> 18.6 us  [call(): pl.pallas_call(run, out_shape=outs, in_specs=[SMEM] * smem + [pl.BlockSpe...]
  transfers between devices with their start and end apart: 41 -> 41, of which waited for: 20 -> 20; matrix products, arithmetic and copies ran while one was open for 1% -> 1% of each run, Pallas kernels for 16% -> 19%
where the time goes in v5:
time: 152 us
  waiting for transfers between devices  50.6 us (33%)
  starting transfers between devices  46 us (30%)
  Pallas kernels  36.1 us (24%)
  local copies, waits for them, and re-layouts  16.7 us (11%)
  between operations  2.23 us (1%)
    pallas_call x23, Pallas kernels, call(): pl.pallas_call(run, out_shape=outs, in_specs=[SMEM] * smem + [pl.BlockSpe...  18.6 us
    ppermute x6, waiting for transfers between devices, half_shift(): return lax.ppermute(values, 'fsdp', pairs)  17.8 us
    unnamed x51, local copies, waits for them, and re-layouts  15.1 us
    ppermute x19, starting transfers between devices, plane_shift(): return lax.ppermute(values, PLANE, pairs)  14.5 us
    ppermute x19, waiting for transfers between devices, plane_shift(): return lax.ppermute(values, PLANE, pairs)  14.3 us
    ppermute x3, waiting for transfers between devices, mirror_shift(): lax.ppermute(values, 'fsdp', [(a, (a + half) % n_z) for a in range(n_z)])  12.2 us
    pallas_call x1, Pallas kernels, gate_rows(): pl.pallas_call(run, grid=(queries // group,), out_shape=outs, in_specs=[S...  11.6 us
    ppermute x12, starting transfers between devices, shift(): return lax.ppermute(values, axis, [(i, (i + k) % n) for i in range(n)])  9.97 us
  transfers between devices with their start and end apart: 41, of which 20 were waited for; matrix products, arithmetic and copies ran while one was open for 1% of the time, Pallas kernels for 19%

profile of v5, /device:TPU:0, one launch (start us, length us, event | category | flops | bytes accessed | tf_op | source)
XLA Modules:
  0.0 151.6 jit_solution(873853573694519721)
XLA Ops:
  0.7 1.0 constant_dynamic-slice_fusion.refs_2_
  1.6 4.1 %collective-permute-start.3 = (bf16[128,1024]{1,0:T(8,128)(2,1)S(1)}, bf16[128,1024]{1,0:T(8,128)(2,1)S(1)}, u32[]{:S(2)}, u32[]{:S(2)}) collective-permute-start(bf16[128,1024]{1,0:T(8,128)(2,1)S(1)} %constant_dynamic-slice_fusion.refs_2_), channel_id=1, source_target_pairs={{0,8},{4,12},{8,0},{12,4},{1,9},{5,13},{9,1},{13,5},{2,10},{6,14},... | collective-permute-start | bytes 786440 | tf_op jit(solution)/shard_map/ppermute | solution.py:515
  5.8 1.6 %copy-done = bf16[1024,1024]{1,0:T(8,128)(2,1)S(1)} copy-done((bf16[1024,1024]{1,0:T(8,128)(2,1)S(1)}, bf16[1024,1024]{1,0:T(8,128)(2,1)}, u32[]{:S(2)}) %copy-start) | copy-done | bytes 2097176
  7.3 0.7 copy-done.20
  8.0 1.7 %block_u.1 = f32[1,1024]{1,0:T(1,128)S(1)} custom-call(bf16[1024,1024]{1,0:T(8,128)(2,1)S(1)} %copy-done, f32[1,1024]{1,0:T(1,128)S(1)} %bitcast.51, bf16[128,1024]{1,0:T(8,128)(2,1)S(1)} %constant_dynamic-slice_fusion.refs_2_), custom_call_target="tpu_custom_call" | custom-call | bytes 2105344 | tf_op jit(solution)/shard_map/block_u/pallas_call | solution.py:58
  9.8 1.4 collective-permute-start.2
  11.1 1.7 %collective-permute-start.1 = (f32[1,1024]{1,0:T(1,128)S(1)}, f32[1,1024]{1,0:T(1,128)S(1)}, u32[]{:S(2)}, u32[]{:S(2)}) collective-permute-start(f32[1,1024]{1,0:T(1,128)S(1)} %block_u.1), channel_id=1, source_target_pairs={{0,8},{4,12},{8,0},{12,4},{1,9},{5,13},{9,1},{13,5},{2,10},{6,14},... | collective-permute-start | bytes 12296 | tf_op jit(solution)/shard_map/ppermute | solution.py:76
  13.7 4.2 %collective-permute-done.3.refs_6_.refs_0_ = bf16[128,1024]{1,0:T(8,128)(2,1)S(1)} collective-permute-done((bf16[128,1024]{1,0:T(8,128)(2,1)S(1)}, bf16[128,1024]{1,0:T(8,128)(2,1)S(1)}, u32[]{:S(2)}, u32[]{:S(2)}) %collective-permute-start.3) | collective-permute-done | bytes 262176 | tf_op jit(solution)/shard_map/ppermute | solution.py:515
  17.9 2.5 %collective-permute-start.7 = (bf16[128,1024]{1,0:T(8,128)(2,1)S(1)}, bf16[128,1024]{1,0:T(8,128)(2,1)S(1)}, u32[]{:S(2)}, u32[]{:S(2)}) collective-permute-start(bf16[128,1024]{1,0:T(8,128)(2,1)S(1)} %collective-permute-done.3.refs_6_.refs_0_), channel_id=1, source_target_pairs={{0,18},{1,19},{2,16},{3,17},{16,2},{17,3},{18,0},{19,1},{4,22},{5,... | collective-permute-start | bytes 786440 | tf_op jit(solution)/shard_map/ppermute | solution.py:508
  21.4 11.6 %gate_rows.1 = (bf16[64,2048]{1,0:T(8,128)(2,1)S(1)}, bf16[64,2048]{1,0:T(8,128)(2,1)S(1)}, bf16[1024,4096]{1,0:T(8,128)(2,1)}, f32[1024,1]{1,0:T(8,128)S(1)}, f...) custom-call(s32[2]{0:T(128)S(1)} %pad_add_fusion.refs_0_.z_ref, ...), custom_call_target="tpu_custom_call" | custom-call | flops 41943040 | bytes 16777216 | tf_op jit(solution)/shard_map/gate_rows/pallas_call | solution.py:176
  33.2 0.8 collective-permute-start.4
  34.2 1.5 %collective-permute-start.10 = (s32[64,8]{1,0:T(8,128)S(1)}, s32[64,8]{1,0:T(8,128)S(1)}, u32[]{:S(2)}, u32[]{:S(2)}) collective-permute-start(s32[64,8]{1,0:T(8,128)S(1)} %get-tuple-element.46), channel_id=1, source_target_pairs={{0,2},{1,3},{2,0},{3,1},{4,6},{5,7},{6,4},{7,5},{8,10},{9,11},{10,... | collective-permute-start | bytes 6152 | tf_op jit(solution)/shard_map/ppermute | solution.py:76
  35.7 1.3 collective-permute-start.11
  37.4 0.7 collective-permute-done.10.refs_4_
  38.6 1.8 %list_counts.1 = (f32[256,1024]{1,0:T(8,128)S(1)}, f32[1,1024]{1,0:T(1,128)S(1)}) custom-call(s32[1]{0:T(128)} %bitcast.46.refs_9_.refs_0_, bf16[1024,1024]{1,0:T(8,128)(2,1)S(1)} %copy-done.4, s32[64,8]{1,0:T(8,128)S(1)} %get-tuple-element.44.refs_2_, s32[64,8]{1,0:T(8,128)S(1)} %collective-permute-done.9.refs_3_, ...), custom_call_target="tpu_custom_call" | custom-call | bytes 3158020 | tf_op jit(solution)/shard_map/list_counts/pallas_call | solution.py:58
  40.5 1.5 collective-permute-done.4.refs_4_
  42.0 1.4 forward.1
  43.4 1.6 %collective-permute-start.13 = (bf16[128,1024]{1,0:T(8,128)(2,1)S(1)}, bf16[128,1024]{1,0:T(8,128)(2,1)S(1)}, u32[]{:S(2)}, u32[]{:S(2)}) collective-permute-start(bf16[128,1024]{1,0:T(8,128)(2,1)S(1)} %get-tuple-element.55.refs_3_), channel_id=1, source_target_pairs={{0,2},{1,3},{2,0},{3,1},{16,18},{17,19},{18,16},{19,17},{4,6},{5,7... | collective-permute-start | bytes 786440 | tf_op jit(solution)/shard_map/ppermute | solution.py:508
  45.0 0.7 collective-permute-start.12
  45.7 4.2 %collective-permute-done.12.refs_1_ = bf16[64,1024]{1,0:T(8,128)(2,1)S(1)} collective-permute-done((bf16[64,1024]{1,0:T(8,128)(2,1)S(1)}, bf16[64,1024]{1,0:T(8,128)(2,1)S(1)}, u32[]{:S(2)}, u32[]{:S(2)}) %collective-permute-start.12) | collective-permute-done | bytes 131104 | tf_op jit(solution)/shard_map/ppermute | solution.py:512
  50.0 1.3 collective-permute-done.13.refs_4_
  51.5 1.6 %collective-permute-start.24 = (bf16[256,1024]{1,0:T(8,128)(2,1)S(1)}, bf16[256,1024]{1,0:T(8,128)(2,1)S(1)}, u32[]{:S(2)}, u32[]{:S(2)}) collective-permute-start(bf16[256,1024]{1,0:T(8,128)(2,1)S(1)} %get-tuple-element.60.refs_2_), channel_id=1, source_target_pairs={{0,16},{1,17},{2,18},{3,19},{16,0},{17,1},{18,2},{19,3},{4,20},{5,... | collective-permute-start | bytes 1572872 | tf_op jit(solution)/shard_map/ppermute | solution.py:508
  53.2 1.3 collective-permute-start.16
  55.0 3.4 %collective-permute-done.16.refs_6_ = bf16[64,1024]{1,0:T(8,128)(2,1)S(1)} collective-permute-done((bf16[64,1024]{1,0:T(8,128)(2,1)S(1)}, bf16[64,1024]{1,0:T(8,128)(2,1)S(1)}, u32[]{:S(2)}, u32[]{:S(2)}) %collective-permute-start.16) | collective-permute-done | bytes 131104 | tf_op jit(solution)/shard_map/ppermute | solution.py:76
  58.3 3.2 %collective-permute-start.22 = (bf16[128,1024]{1,0:T(8,128)(2,1)S(1)}, bf16[128,1024]{1,0:T(8,128)(2,1)S(1)}, u32[]{:S(2)}, u32[]{:S(2)}) collective-permute-start(bf16[128,1024]{1,0:T(8,128)(2,1)S(1)} %get-tuple-element.67), channel_id=1, source_target_pairs={{0,8},{4,12},{8,0},{12,4},{1,9},{5,13},{9,1},{13,5},{2,10},{6,14},... | collective-permute-start | bytes 786440 | tf_op jit(solution)/shard_map/ppermute | solution.py:515
  61.9 1.4 contrast.1
  63.3 2.6 %collective-permute-done.24.refs_0_.refs_3_ = bf16[256,1024]{1,0:T(8,128)(2,1)S(1)} collective-permute-done((bf16[256,1024]{1,0:T(8,128)(2,1)S(1)}, bf16[256,1024]{1,0:T(8,128)(2,1)S(1)}, u32[]{:S(2)}, u32[]{:S(2)}) %collective-permute-start.24) | collective-permute-done | bytes 524320 | tf_op jit(solution)/shard_map/ppermute | solution.py:508
  66.0 1.7 %collective-permute-start.18 = (bf16[64,1152]{1,0:T(8,128)(2,1)S(1)}, bf16[64,1152]{1,0:T(8,128)(2,1)S(1)}, u32[]{:S(2)}, u32[]{:S(2)}) collective-permute-start(bf16[64,1152]{1,0:T(8,128)(2,1)S(1)} %get-tuple-element.62), channel_id=1, source_target_pairs={{0,3},{1,0},{2,1},{3,2},{4,7},{5,4},{6,5},{7,6},{8,11},{9,8},{10,9... | collective-permute-start | bytes 442376 | tf_op jit(solution)/shard_map/ppermute | solution.py:76
  68.1 5.8 %collective-permute-done.22.refs_0_ = bf16[128,1024]{1,0:T(8,128)(2,1)S(1)} collective-permute-done((bf16[128,1024]{1,0:T(8,128)(2,1)S(1)}, bf16[128,1024]{1,0:T(8,128)(2,1)S(1)}, u32[]{:S(2)}, u32[]{:S(2)}) %collective-permute-start.22) | collective-permute-done | bytes 262176 | tf_op jit(solution)/shard_map/ppermute | solution.py:515
  74.0 0.6 collective-permute-start.23
  74.6 0.9 collective-permute-done.19.refs_6_
  75.9 1.2 collective-permute-start.21
  77.1 3.9 %collective-permute-done.21.refs_4_ = bf16[64,1024]{1,0:T(8,128)(2,1)S(1)} collective-permute-done((bf16[64,1024]{1,0:T(8,128)(2,1)S(1)}, bf16[64,1024]{1,0:T(8,128)(2,1)S(1)}, u32[]{:S(2)}, u32[]{:S(2)}) %collective-permute-start.21) | collective-permute-done | bytes 131104 | tf_op jit(solution)/shard_map/ppermute | solution.py:512
  81.0 1.4 collective-permute-done.23.refs_6_
  82.4 2.2 %backward.1 = (bf16[64,2048]{1,0:T(8,128)(2,1)S(1)}, bf16[64,2048]{1,0:T(8,128)(2,1)S(1)}, bf16[256,1024]{1,0:T(8,128)(2,1)}) custom-call(s32[1]{0:T(128)} %bitcast.9.refs_10_.refs_0_, bf16[1024,1024]{1,0:T(8,128)(2,1)S(1)} %copy-done.1, bf16[1024,1024]{1,0:T(8,128)(2,1)S(1)} %get-tuple-element.49.refs_2_, bf16[64,1024]{1,0:T(8,128)(2,1)S(1)} %get-tuple-element.66.refs_3_, ...), custom_call_target="tpu_custom_call" | custom-call | flops 536870912 | bytes 6029316 | tf_op jit(solution)/shard_map/backward/pallas_call | solution.py:58
  84.6 0.7 copy-done.17
  85.3 0.9 collective-permute-start.26
  86.7 6.1 %collective-permute-done.26.rest_1_.refs_1_ = bf16[64,2048]{1,0:T(8,128)(2,1)S(1)} collective-permute-done((bf16[64,2048]{1,0:T(8,128)(2,1)S(1)}, bf16[64,2048]{1,0:T(8,128)(2,1)S(1)}, u32[]{:S(2)}, u32[]{:S(2)}) %collective-permute-start.26) | collective-permute-done | bytes 262176 | tf_op jit(solution)/shard_map/ppermute | solution.py:512
  92.9 0.8 copy-done.8
  93.7 5.2 %all-to-all-start = ((bf16[32,64,128]{2,1,0:T(8,128)(2,1)}), bf16[32,64,128]{2,1,0:T(8,128)(2,1)}, u32[]{:S(2)}, u32[]{:S(2)}) async-start(bf16[32,64,128]{2,1,0:T(8,128)(2,1)} %copy-done.8), calls=%async_computation | async-start | bytes 1048576 | tf_op jit(solution)/shard_map/all_to_all | solution.py:626
  99.0 3.4 %copy-done.5 = bf16[1024,4096]{1,0:T(8,128)(2,1)S(1)} copy-done((bf16[1024,4096]{1,0:T(8,128)(2,1)S(1)}, bf16[1024,4096]{1,0:T(8,128)(2,1)}, u32[]{:S(2)}) %copy-start.5) | copy-done | bytes 8388632
  102.4 1.0 copy-done.10
  103.4 0.9 copy-done.18
  104.4 5.9 %slope_rows.1 = (f32[24,128]{1,0:T(8,128)S(1)}, f32[24,128]{1,0:T(8,128)S(1)}) custom-call(s32[2]{0:T(128)S(1)} %pad_add_fusion.refs_0_.z_ref, bf16[1024,4096]{1,0:T(8,128)(2,1)S(1)} %copy-done.5, f32[1024,1]{1,0:T(8,128)S(1)} %copy-done.10, f32[1,128]{1,0:T(1,128)S(1)} %get-tuple-element.65.loss_ref, bf16[64,2048]{1,0:T(8,128)(2,1)S(1)} %copy-done.18, ...), custom_call_target="tpu_custom_call" | custom-call | flops 16777216 | bytes 8388608 | tf_op jit(solution)/shard_map/slope_rows/pallas_call | solution.py:408
  110.2 1.1 late.1
  111.9 1.5 %collective-permute-start.27 = (f32[24,128]{1,0:T(8,128)S(1)}, f32[24,128]{1,0:T(8,128)S(1)}, u32[]{:S(2)}, u32[]{:S(2)}) collective-permute-start(f32[24,128]{1,0:T(8,128)S(1)} %get-tuple-element.71), channel_id=1, source_target_pairs={{0,4},{4,0},{8,12},{12,8},{1,5},{5,1},{9,13},{13,9},{2,6},{6,2},{1... | collective-permute-start | bytes 36872 | tf_op jit(solution)/shard_map/ppermute | solution.py:512
  113.4 2.2 %collective-permute-done.27.refs_1_ = f32[24,128]{1,0:T(8,128)S(1)} collective-permute-done((f32[24,128]{1,0:T(8,128)S(1)}, f32[24,128]{1,0:T(8,128)S(1)}, u32[]{:S(2)}, u32[]{:S(2)}) %collective-permute-start.27) | collective-permute-done | bytes 12320 | tf_op jit(solution)/shard_map/ppermute | solution.py:512
  115.6 0.8 copy-done.13
  116.4 0.8 copy-done.15
  117.2 1.0 copy-done.7
  118.3 1.0 copy-done.12
  119.3 1.0 copy-done.14
  120.3 1.0 copy-done.16
  121.4 2.9 %grad_columns.1.refs_1_.refs_0_ = bf16[1024,128]{1,0:T(8,128)(2,1)S(1)} custom-call(s32[32]{0:T(128)S(1)} %stack.186.refs_8_.refs_0_, bf16[32,64,128]{2,1,0:T(8,128)(2,1)} %all-to-all-done.refs_1_, bf16[256,1024]{1,0:T(8,128)(2,1)S(1)} %copy-done.12, bf16[256,1024]{1,0:T(8,128)(2,1)S(1)} %copy-done.7, bf16[256,1024]{1,0:T(8,128)(2,1)} %get-tuple-element.73.refs_4_, ...), custom_call_target="tpu_custom_call" | custom-call | flops 536870912 | bytes 4980864 | tf_op jit(solution)/shard_map/grad_columns/pallas_call | solution.py:58
  124.3 2.5 %collective-permute-start.37 = (bf16[1024,128]{1,0:T(8,128)(2,1)S(1)}, bf16[1024,128]{1,0:T(8,128)(2,1)S(1)}, u32[]{:S(2)}, u32[]{:S(2)}) collective-permute-start(bf16[1024,128]{1,0:T(8,128)(2,1)S(1)} %grad_columns.1.refs_1_.refs_0_), channel_id=1, source_target_pairs={{0,18},{1,19},{2,16},{3,17},{16,2},{17,3},{18,0},{19,1},{4,22},{5,... | collective-permute-start | bytes 786440 | tf_op jit(solution)/shard_map/ppermute | solution.py:508
  127.8 2.4 %collective-permute-start.31 = (f32[24,128]{1,0:T(8,128)S(1)}, f32[24,128]{1,0:T(8,128)S(1)}, u32[]{:S(2)}, u32[]{:S(2)}) collective-permute-start(f32[24,128]{1,0:T(8,128)S(1)} %slope_out.1.refs_0_), channel_id=1, source_target_pairs={{0,8},{4,12},{8,0},{12,4},{1,9},{5,13},{9,1},{13,5},{2,10},{6,14},... | collective-permute-start | bytes 36872 | tf_op jit(solution)/shard_map/ppermute | solution.py:515
  130.3 2.2 %collective-permute-done.31.refs_1_ = f32[24,128]{1,0:T(8,128)S(1)} collective-permute-done((f32[24,128]{1,0:T(8,128)S(1)}, f32[24,128]{1,0:T(8,128)S(1)}, u32[]{:S(2)}, u32[]{:S(2)}) %collective-permute-start.31) | collective-permute-done | bytes 12320 | tf_op jit(solution)/shard_map/ppermute | solution.py:515
  132.4 1.5 %collective-permute-start.32 = (f32[24,128]{1,0:T(8,128)S(1)}, f32[24,128]{1,0:T(8,128)S(1)}, u32[]{:S(2)}, u32[]{:S(2)}) collective-permute-start(f32[24,128]{1,0:T(8,128)S(1)} %sum_mirror.1.refs_0_), channel_id=1, source_target_pairs={{0,16},{1,17},{2,18},{3,19},{16,0},{17,1},{18,2},{19,3},{4,20},{5,... | collective-permute-start | bytes 36872 | tf_op jit(solution)/shard_map/ppermute | solution.py:508
  133.9 4.5 %collective-permute-done.32.refs_1_ = f32[24,128]{1,0:T(8,128)S(1)} collective-permute-done((f32[24,128]{1,0:T(8,128)S(1)}, f32[24,128]{1,0:T(8,128)S(1)}, u32[]{:S(2)}, u32[]{:S(2)}) %collective-permute-start.32) | collective-permute-done | bytes 12320 | tf_op jit(solution)/shard_map/ppermute | solution.py:508
  138.9 3.3 %collective-permute-done.33.refs_1_ = f32[24,128]{1,0:T(8,128)S(1)} collective-permute-done((f32[24,128]{1,0:T(8,128)S(1)}, f32[24,128]{1,0:T(8,128)S(1)}, u32[]{:S(2)}, u32[]{:S(2)}) %collective-permute-start.33) | collective-permute-done | bytes 12320 | tf_op jit(solution)/shard_map/ppermute | solution.py:508
  142.1 1.2 collective-permute-done.34.refs_1_
  143.7 1.3 slope_sum.1
  144.9 1.5 collective-permute-start.39
  146.5 3.4 %finish.1 = (f32[1024,1024]{1,0:T(8,128)}, f32[8,128]{1,0:T(8,128)S(1)}) custom-call(s32[8]{0:T(128)S(1)} %stack.149.refs_7_.refs_1_.refs_0_, f32[1,1024]{1,0:T(1,128)S(1)} %bitcast.52, f32[8,128]{1,0:T(8,128)S(1)} %get-tuple-element.74.refs_2_, bf16[4096,128]{1,0:T(8,128)(2,1)S(1)} %pack_columns.1.refs_3_, bf16[4096,128]{1,0:T(8,128)(2,1)S(1)} %collective-permute-done.38.refs_4_), custom_call_target="tpu_custom_call" | custom-call | bytes 6303776 | tf_op jit(solution)/shard_map/finish/pallas_call | solution.py:58
  (106 shorter events, 8.9 us)
Async XLA Ops:
  0.6 12.3 %copy-start.23 = (bf16[4096]{0:T(1024)(128)(2,1)S(1)}, bf16[4096]{0:T(1024)(128)(2,1)}, u32[]{:S(2)}) copy-start(bf16[4096]{0:T(1024)(128)(2,1)} %param.12) | copy-start | bytes 24580
  0.6 12.3 %copy-start.22 = (s32[64,32]{0,1:T(8,128)S(1)}, s32[64,32]{0,1:T(8,128)}, u32[]{:S(2)}) copy-start(s32[64,32]{0,1:T(8,128)} %param.10) | copy-start | bytes 24580
  0.7 12.4 %copy-start.24 = (s32[64]{0:T(128)S(1)}, s32[64]{0:T(128)}, u32[]{:S(2)}) copy-start(s32[64]{0:T(128)} %param.11) | copy-start | bytes 772
  1.6 16.2 %collective-permute-start.3 = (bf16[128,1024]{1,0:T(8,128)(2,1)S(1)}, bf16[128,1024]{1,0:T(8,128)(2,1)S(1)}, u32[]{:S(2)}, u32[]{:S(2)}) collective-permute-start(bf16[128,1024]{1,0:T(8,128)(2,1)S(1)} %constant_dynamic-slice_fusion.refs_2_), channel_id=1, source_target_pairs={{0,8},{4,12},{8,0},{12,4},{1,9},{5,13},{9,1},{13,5},{2,10},{6,14},... | collective-permute-start | bytes 786440 | tf_op jit(solution)/shard_map/ppermute | solution.py:515
  5.8 1.6 %copy-start = (bf16[1024,1024]{1,0:T(8,128)(2,1)S(1)}, bf16[1024,1024]{1,0:T(8,128)(2,1)}, u32[]{:S(2)}) copy-start(bf16[1024,1024]{1,0:T(8,128)(2,1)} %refs_1_.5) | copy-start | bytes 6291460
  9.8 11.7 %collective-permute-start.2 = (f32[1,1024]{1,0:T(1,128)S(1)}, f32[1,1024]{1,0:T(1,128)S(1)}, u32[]{:S(2)}, u32[]{:S(2)}) collective-permute-start(f32[1,1024]{1,0:T(1,128)S(1)} %block_u.1), channel_id=1, source_target_pairs={{0,12},{4,0},{8,4},{12,8},{1,13},{5,1},{9,5},{13,9},{2,14},{6,2},{... | collective-permute-start | bytes 12296 | tf_op jit(solution)/shard_map/ppermute | solution.py:76
  11.1 10.3 %collective-permute-start.1 = (f32[1,1024]{1,0:T(1,128)S(1)}, f32[1,1024]{1,0:T(1,128)S(1)}, u32[]{:S(2)}, u32[]{:S(2)}) collective-permute-start(f32[1,1024]{1,0:T(1,128)S(1)} %block_u.1), channel_id=1, source_target_pairs={{0,8},{4,12},{8,0},{12,4},{1,9},{5,13},{9,1},{13,5},{2,10},{6,14},... | collective-permute-start | bytes 12296 | tf_op jit(solution)/shard_map/ppermute | solution.py:76
  12.8 8.1 %collective-permute-start = (f32[1,1024]{1,0:T(1,128)S(1)}, f32[1,1024]{1,0:T(1,128)S(1)}, u32[]{:S(2)}, u32[]{:S(2)}) collective-permute-start(f32[1,1024]{1,0:T(1,128)S(1)} %block_u.1), channel_id=1, source_target_pairs={{0,4},{4,8},{8,12},{12,0},{1,5},{5,9},{9,13},{13,1},{2,6},{6,10},{... | collective-permute-start | bytes 12296 | tf_op jit(solution)/shard_map/ppermute | solution.py:76
  17.9 15.1 %collective-permute-start.7 = (bf16[128,1024]{1,0:T(8,128)(2,1)S(1)}, bf16[128,1024]{1,0:T(8,128)(2,1)S(1)}, u32[]{:S(2)}, u32[]{:S(2)}) collective-permute-start(bf16[128,1024]{1,0:T(8,128)(2,1)S(1)} %collective-permute-done.3.refs_6_.refs_0_), channel_id=1, source_target_pairs={{0,18},{1,19},{2,16},{3,17},{16,2},{17,3},{18,0},{19,1},{4,22},{5,... | collective-permute-start | bytes 786440 | tf_op jit(solution)/shard_map/ppermute | solution.py:508
  20.4 12.6 %collective-permute-start.6 = (bf16[128,1024]{1,0:T(8,128)(2,1)S(1)}, bf16[128,1024]{1,0:T(8,128)(2,1)S(1)}, u32[]{:S(2)}, u32[]{:S(2)}) collective-permute-start(bf16[128,1024]{1,0:T(8,128)(2,1)S(1)} %collective-permute-done.3.refs_6_.refs_0_), channel_id=1, source_target_pairs={{0,16},{1,17},{2,18},{3,19},{16,0},{17,1},{18,2},{19,3},{4,20},{5,... | collective-permute-start | bytes 786440 | tf_op jit(solution)/shard_map/ppermute | solution.py:508
  20.9 12.1 %collective-permute-start.5 = (bf16[128,1024]{1,0:T(8,128)(2,1)S(1)}, bf16[128,1024]{1,0:T(8,128)(2,1)S(1)}, u32[]{:S(2)}, u32[]{:S(2)}) collective-permute-start(bf16[128,1024]{1,0:T(8,128)(2,1)S(1)} %collective-permute-done.3.refs_6_.refs_0_), channel_id=1, source_target_pairs={{0,2},{1,3},{2,0},{3,1},{16,18},{17,19},{18,16},{19,17},{4,6},{5,7... | collective-permute-start | bytes 786440 | tf_op jit(solution)/shard_map/ppermute | solution.py:508
  33.0 7.5 %copy-start.9 = (f32[1024,1]{1,0:T(8,128)}, f32[1024,1]{1,0:T(8,128)S(1)}, u32[]{:S(2)}) copy-start(f32[1024,1]{1,0:T(8,128)S(1)} %get-tuple-element.51.curve_ref) | copy-start | bytes 12292
  33.0 5.6 %copy-start.4 = (bf16[1024,1024]{1,0:T(8,128)(2,1)S(1)}, bf16[1024,1024]{1,0:T(8,128)(2,1)}, u32[]{:S(2)}) copy-start(bf16[1024,1024]{1,0:T(8,128)(2,1)} %refs_0_.4) | copy-start | bytes 6291460
  33.1 8.9 %copy-start.1 = (bf16[1024,1024]{1,0:T(8,128)(2,1)S(1)}, bf16[1024,1024]{1,0:T(8,128)(2,1)}, u32[]{:S(2)}) copy-start(bf16[1024,1024]{1,0:T(8,128)(2,1)} %refs_1_.5) | copy-start | bytes 6291460
  33.1 8.8 %collective-permute-start.8 = (bf16[512,1024]{1,0:T(8,128)(2,1)S(1)}, bf16[512,1024]{1,0:T(8,128)(2,1)S(1)}, u32[]{:S(2)}, u32[]{:S(2)}) collective-permute-start(bf16[512,1024]{1,0:T(8,128)(2,1)S(1)} %pack_shares.1.refs_5_), channel_id=1, source_target_pairs={{0,1},{1,0},{2,3},{3,2},{16,17},{17,16},{18,19},{19,18},{4,5},{5,4... | collective-permute-start | bytes 3145736 | tf_op jit(solution)/shard_map/ppermute | solution.py:508
  33.2 8.7 %collective-permute-start.4 = (bf16[64,2048]{1,0:T(8,128)(2,1)S(1)}, bf16[64,2048]{1,0:T(8,128)(2,1)S(1)}, u32[]{:S(2)}, u32[]{:S(2)}) collective-permute-start(bf16[64,2048]{1,0:T(8,128)(2,1)S(1)} %get-tuple-element.42), channel_id=1, source_target_pairs={{0,4},{4,0},{8,12},{12,8},{1,5},{5,1},{9,13},{13,9},{2,6},{6,2},{1... | collective-permute-start | bytes 786440 | tf_op jit(solution)/shard_map/ppermute | solution.py:512
  34.1 3.3 %collective-permute-start.9 = (s32[64,8]{1,0:T(8,128)S(1)}, s32[64,8]{1,0:T(8,128)S(1)}, u32[]{:S(2)}, u32[]{:S(2)}) collective-permute-start(s32[64,8]{1,0:T(8,128)S(1)} %get-tuple-element.45), channel_id=1, source_target_pairs={{0,1},{1,2},{2,3},{3,0},{4,5},{5,6},{6,7},{7,4},{8,9},{9,10},{10,1... | collective-permute-start | bytes 6152 | tf_op jit(solution)/shard_map/ppermute | solution.py:76
  34.2 3.9 %collective-permute-start.10 = (s32[64,8]{1,0:T(8,128)S(1)}, s32[64,8]{1,0:T(8,128)S(1)}, u32[]{:S(2)}, u32[]{:S(2)}) collective-permute-start(s32[64,8]{1,0:T(8,128)S(1)} %get-tuple-element.46), channel_id=1, source_target_pairs={{0,2},{1,3},{2,0},{3,1},{4,6},{5,7},{6,4},{7,5},{8,10},{9,11},{10,... | collective-permute-start | bytes 6152 | tf_op jit(solution)/shard_map/ppermute | solution.py:76
  35.7 2.9 %collective-permute-start.11 = (s32[64,8]{1,0:T(8,128)S(1)}, s32[64,8]{1,0:T(8,128)S(1)}, u32[]{:S(2)}, u32[]{:S(2)}) collective-permute-start(s32[64,8]{1,0:T(8,128)S(1)} %get-tuple-element.47), channel_id=1, source_target_pairs={{0,3},{1,0},{2,1},{3,2},{4,7},{5,4},{6,5},{7,6},{8,11},{9,8},{10,9... | collective-permute-start | bytes 6152 | tf_op jit(solution)/shard_map/ppermute | solution.py:76
  43.4 39.0 %copy-start.2 = (bf16[1024,1024]{1,0:T(8,128)(2,1)}, bf16[1024,1024]{1,0:T(8,128)(2,1)S(1)}, u32[]{:S(2)}) copy-start(bf16[1024,1024]{1,0:T(8,128)(2,1)S(1)} %get-tuple-element.49.refs_2_) | copy-start | bytes 6291460
  43.4 7.9 %collective-permute-start.13 = (bf16[128,1024]{1,0:T(8,128)(2,1)S(1)}, bf16[128,1024]{1,0:T(8,128)(2,1)S(1)}, u32[]{:S(2)}, u32[]{:S(2)}) collective-permute-start(bf16[128,1024]{1,0:T(8,128)(2,1)S(1)} %get-tuple-element.55.refs_3_), channel_id=1, source_target_pairs={{0,2},{1,3},{2,0},{3,1},{16,18},{17,19},{18,16},{19,17},{4,6},{5,7... | collective-permute-start | bytes 786440 | tf_op jit(solution)/shard_map/ppermute | solution.py:508
  45.0 5.0 %collective-permute-start.12 = (bf16[64,1024]{1,0:T(8,128)(2,1)S(1)}, bf16[64,1024]{1,0:T(8,128)(2,1)S(1)}, u32[]{:S(2)}, u32[]{:S(2)}) collective-permute-start(bf16[64,1024]{1,0:T(8,128)(2,1)S(1)} %get-tuple-element.53), channel_id=1, source_target_pairs={{0,4},{4,0},{8,12},{12,8},{1,5},{5,1},{9,13},{13,9},{2,6},{6,2},{1... | collective-permute-start | bytes 393224 | tf_op jit(solution)/shard_map/ppermute | solution.py:512
  51.5 11.8 %copy-start.11 = (bf16[256,1024]{1,0:T(8,128)(2,1)}, bf16[256,1024]{1,0:T(8,128)(2,1)S(1)}, u32[]{:S(2)}) copy-start(bf16[256,1024]{1,0:T(8,128)(2,1)S(1)} %get-tuple-element.60.refs_2_) | copy-start | bytes 1572868
  51.5 10.4 %collective-permute-start.17 = (bf16[256,1024]{1,0:T(8,128)(2,1)S(1)}, bf16[256,1024]{1,0:T(8,128)(2,1)S(1)}, u32[]{:S(2)}, u32[]{:S(2)}) collective-permute-start(bf16[256,1024]{1,0:T(8,128)(2,1)S(1)} %get-tuple-element.60.refs_2_), channel_id=1, source_target_pairs={{0,1},{1,0},{2,3},{3,2},{16,17},{17,16},{18,19},{19,18},{4,5},{5,4... | collective-permute-start | bytes 1572872 | tf_op jit(solution)/shard_map/ppermute | solution.py:508
  51.5 14.3 %collective-permute-start.24 = (bf16[256,1024]{1,0:T(8,128)(2,1)S(1)}, bf16[256,1024]{1,0:T(8,128)(2,1)S(1)}, u32[]{:S(2)}, u32[]{:S(2)}) collective-permute-start(bf16[256,1024]{1,0:T(8,128)(2,1)S(1)} %get-tuple-element.60.refs_2_), channel_id=1, source_target_pairs={{0,16},{1,17},{2,18},{3,19},{16,0},{17,1},{18,2},{19,3},{4,20},{5,... | collective-permute-start | bytes 1572872 | tf_op jit(solution)/shard_map/ppermute | solution.py:508
  53.2 5.2 %collective-permute-start.16 = (bf16[64,1024]{1,0:T(8,128)(2,1)S(1)}, bf16[64,1024]{1,0:T(8,128)(2,1)S(1)}, u32[]{:S(2)}, u32[]{:S(2)}) collective-permute-start(bf16[64,1024]{1,0:T(8,128)(2,1)S(1)} %get-tuple-element.58.refs_3_), channel_id=1, source_target_pairs={{0,3},{1,0},{2,1},{3,2},{4,7},{5,4},{6,5},{7,6},{8,11},{9,8},{10,9... | collective-permute-start | bytes 393224 | tf_op jit(solution)/shard_map/ppermute | solution.py:76
  54.4 7.4 %collective-permute-start.15 = (bf16[64,1024]{1,0:T(8,128)(2,1)S(1)}, bf16[64,1024]{1,0:T(8,128)(2,1)S(1)}, u32[]{:S(2)}, u32[]{:S(2)}) collective-permute-start(bf16[64,1024]{1,0:T(8,128)(2,1)S(1)} %get-tuple-element.58.refs_3_), channel_id=1, source_target_pairs={{0,2},{1,3},{2,0},{3,1},{4,6},{5,7},{6,4},{7,5},{8,10},{9,11},{10,... | collective-permute-start | bytes 393224 | tf_op jit(solution)/shard_map/ppermute | solution.py:76
  55.0 6.9 %collective-permute-start.14 = (bf16[64,1024]{1,0:T(8,128)(2,1)S(1)}, bf16[64,1024]{1,0:T(8,128)(2,1)S(1)}, u32[]{:S(2)}, u32[]{:S(2)}) collective-permute-start(bf16[64,1024]{1,0:T(8,128)(2,1)S(1)} %get-tuple-element.58.refs_3_), channel_id=1, source_target_pairs={{0,1},{1,2},{2,3},{3,0},{4,5},{5,6},{6,7},{7,4},{8,9},{9,10},{10,1... | collective-permute-start | bytes 393224 | tf_op jit(solution)/shard_map/ppermute | solution.py:76
  58.3 15.6 %collective-permute-start.22 = (bf16[128,1024]{1,0:T(8,128)(2,1)S(1)}, bf16[128,1024]{1,0:T(8,128)(2,1)S(1)}, u32[]{:S(2)}, u32[]{:S(2)}) collective-permute-start(bf16[128,1024]{1,0:T(8,128)(2,1)S(1)} %get-tuple-element.67), channel_id=1, source_target_pairs={{0,8},{4,12},{8,0},{12,4},{1,9},{5,13},{9,1},{13,5},{2,10},{6,14},... | collective-permute-start | bytes 786440 | tf_op jit(solution)/shard_map/ppermute | solution.py:515
  61.9 13.6 %copy-start.19 = (bf16[64,1024]{1,0:T(8,128)(2,1)S(1)}, bf16[64,1024]{1,0:T(8,128)(2,1)}, u32[]{:S(2)}) copy-start(bf16[64,1024]{1,0:T(8,128)(2,1)} %refs_0_.5) | copy-start | bytes 393220
  65.9 18.7 %copy-start.6 = (bf16[256,1024]{1,0:T(8,128)(2,1)}, bf16[256,1024]{1,0:T(8,128)(2,1)S(1)}, u32[]{:S(2)}) copy-start(bf16[256,1024]{1,0:T(8,128)(2,1)S(1)} %collective-permute-done.24.refs_0_.refs_3_) | copy-start | bytes 1572868
  65.9 16.5 %collective-permute-start.25 = (bf16[256,1024]{1,0:T(8,128)(2,1)S(1)}, bf16[256,1024]{1,0:T(8,128)(2,1)S(1)}, u32[]{:S(2)}, u32[]{:S(2)}) collective-permute-start(bf16[256,1024]{1,0:T(8,128)(2,1)S(1)} %near_far.1), channel_id=1, source_target_pairs={{0,1},{1,0},{2,3},{3,2},{16,17},{17,16},{18,19},{19,18},{4,5},{5,4... | collective-permute-start | bytes 1572872 | tf_op jit(solution)/shard_map/ppermute | solution.py:508
  66.0 7.9 %collective-permute-start.18 = (bf16[64,1152]{1,0:T(8,128)(2,1)S(1)}, bf16[64,1152]{1,0:T(8,128)(2,1)S(1)}, u32[]{:S(2)}, u32[]{:S(2)}) collective-permute-start(bf16[64,1152]{1,0:T(8,128)(2,1)S(1)} %get-tuple-element.62), channel_id=1, source_target_pairs={{0,3},{1,0},{2,1},{3,2},{4,7},{5,4},{6,5},{7,6},{8,11},{9,8},{10,9... | collective-permute-start | bytes 442376 | tf_op jit(solution)/shard_map/ppermute | solution.py:76
  67.7 7.8 %collective-permute-start.19 = (bf16[64,1152]{1,0:T(8,128)(2,1)S(1)}, bf16[64,1152]{1,0:T(8,128)(2,1)S(1)}, u32[]{:S(2)}, u32[]{:S(2)}) collective-permute-start(bf16[64,1152]{1,0:T(8,128)(2,1)S(1)} %get-tuple-element.63), channel_id=1, source_target_pairs={{0,2},{1,3},{2,0},{3,1},{4,6},{5,7},{6,4},{7,5},{8,10},{9,11},{10,... | collective-permute-start | bytes 442376 | tf_op jit(solution)/shard_map/ppermute | solution.py:76
  68.1 7.4 %collective-permute-start.20 = (bf16[64,1152]{1,0:T(8,128)(2,1)S(1)}, bf16[64,1152]{1,0:T(8,128)(2,1)S(1)}, u32[]{:S(2)}, u32[]{:S(2)}) collective-permute-start(bf16[64,1152]{1,0:T(8,128)(2,1)S(1)} %get-tuple-element.64), channel_id=1, source_target_pairs={{0,1},{1,2},{2,3},{3,0},{4,5},{5,6},{6,7},{7,4},{8,9},{9,10},{10,1... | collective-permute-start | bytes 442376 | tf_op jit(solution)/shard_map/ppermute | solution.py:76
  74.0 8.4 %collective-permute-start.23 = (bf16[128,1024]{1,0:T(8,128)(2,1)S(1)}, bf16[128,1024]{1,0:T(8,128)(2,1)S(1)}, u32[]{:S(2)}, u32[]{:S(2)}) collective-permute-start(bf16[128,1024]{1,0:T(8,128)(2,1)S(1)} %other.1.refs_5_), channel_id=1, source_target_pairs={{0,16},{1,17},{2,18},{3,19},{16,0},{17,1},{18,2},{19,3},{4,20},{5,... | collective-permute-start | bytes 786440 | tf_op jit(solution)/shard_map/ppermute | solution.py:508
  75.9 5.0 %collective-permute-start.21 = (bf16[64,1024]{1,0:T(8,128)(2,1)S(1)}, bf16[64,1024]{1,0:T(8,128)(2,1)S(1)}, u32[]{:S(2)}, u32[]{:S(2)}) collective-permute-start(bf16[64,1024]{1,0:T(8,128)(2,1)S(1)} %get-tuple-element.66.refs_3_), channel_id=1, source_target_pairs={{0,4},{4,0},{8,12},{12,8},{1,5},{5,1},{9,13},{13,9},{2,6},{6,2},{1... | collective-permute-start | bytes 393224 | tf_op jit(solution)/shard_map/ppermute | solution.py:512
  85.3 7.5 %collective-permute-start.26 = (bf16[64,2048]{1,0:T(8,128)(2,1)S(1)}, bf16[64,2048]{1,0:T(8,128)(2,1)S(1)}, u32[]{:S(2)}, u32[]{:S(2)}) collective-permute-start(bf16[64,2048]{1,0:T(8,128)(2,1)S(1)} %get-tuple-element.69), channel_id=1, source_target_pairs={{0,4},{4,0},{8,12},{12,8},{1,5},{5,1},{9,13},{13,9},{2,6},{6,2},{1... | collective-permute-start | bytes 786440 | tf_op jit(solution)/shard_map/ppermute | solution.py:512
  86.2 24.0 %collective-permute-start.28 = (bf16[256,1024]{1,0:T(8,128)(2,1)}, bf16[256,1024]{1,0:T(8,128)(2,1)}, u32[]{:S(2)}, u32[]{:S(2)}) collective-permute-start(bf16[256,1024]{1,0:T(8,128)(2,1)} %get-tuple-element.73.refs_4_), channel_id=1, source_target_pairs={{0,2},{1,3},{2,0},{3,1},{16,18},{17,19},{18,16},{19,17},{4,6},{5,7... | collective-permute-start | bytes 1572872 | tf_op jit(solution)/shard_map/ppermute | solution.py:508
  92.8 0.8 copy-start.8
  93.7 23.6 %all-to-all-start = ((bf16[32,64,128]{2,1,0:T(8,128)(2,1)}), bf16[32,64,128]{2,1,0:T(8,128)(2,1)}, u32[]{:S(2)}, u32[]{:S(2)}) async-start(bf16[32,64,128]{2,1,0:T(8,128)(2,1)} %copy-done.8), calls=%async_computation | async-start | bytes 1048576 | tf_op jit(solution)/shard_map/all_to_all | solution.py:626
  98.9 16.7 %collective-permute-start.29 = (bf16[256,1024]{1,0:T(8,128)(2,1)}, bf16[256,1024]{1,0:T(8,128)(2,1)S(1)}, u32[]{:S(2)}, u32[]{:S(2)}) collective-permute-start(bf16[256,1024]{1,0:T(8,128)(2,1)} %get-tuple-element.73.refs_4_), channel_id=1, source_target_pairs={{0,1},{1,0},{2,3},{3,2},{16,17},{17,16},{18,19},{19,18},{4,5},{5,4... | collective-permute-start | bytes 1572872 | tf_op jit(solution)/shard_map/ppermute | solution.py:508
  99.0 3.4 %copy-start.5 = (bf16[1024,4096]{1,0:T(8,128)(2,1)S(1)}, bf16[1024,4096]{1,0:T(8,128)(2,1)}, u32[]{:S(2)}) copy-start(bf16[1024,4096]{1,0:T(8,128)(2,1)} %get-tuple-element.50.normed_ref) | copy-start | bytes 25165828
  102.4 1.0 copy-start.10
  103.4 0.9 copy-start.18
  111.3 5.1 %collective-permute-start.30 = (bf16[256,1024]{1,0:T(8,128)(2,1)S(1)}, bf16[256,1024]{1,0:T(8,128)(2,1)S(1)}, u32[]{:S(2)}, u32[]{:S(2)}) collective-permute-start(bf16[256,1024]{1,0:T(8,128)(2,1)S(1)} %late.1), channel_id=1, source_target_pairs={{0,1},{1,0},{2,3},{3,2},{16,17},{17,16},{18,19},{19,18},{4,5},{5,4... | collective-permute-start | bytes 1572872 | tf_op jit(solution)/shard_map/ppermute | solution.py:508
  111.9 3.7 %collective-permute-start.27 = (f32[24,128]{1,0:T(8,128)S(1)}, f32[24,128]{1,0:T(8,128)S(1)}, u32[]{:S(2)}, u32[]{:S(2)}) collective-permute-start(f32[24,128]{1,0:T(8,128)S(1)} %get-tuple-element.71), channel_id=1, source_target_pairs={{0,4},{4,0},{8,12},{12,8},{1,5},{5,1},{9,13},{13,9},{2,6},{6,2},{1... | collective-permute-start | bytes 36872 | tf_op jit(solution)/shard_map/ppermute | solution.py:512
  115.6 0.8 copy-start.13
  116.4 0.8 copy-start.15
  117.2 1.0 copy-start.7
  118.3 1.0 copy-start.12
  119.3 1.0 copy-start.14
  120.3 1.0 copy-start.16
  124.3 19.4 %copy-start.3 = (bf16[1024,1024]{1,0:T(8,128)(2,1)S(1)}, bf16[1024,1024]{1,0:T(8,128)(2,1)}, u32[]{:S(2)}) copy-start(bf16[1024,1024]{1,0:T(8,128)(2,1)} %copy-done.2) | copy-start | bytes 6291460
  124.3 19.1 %collective-permute-start.37 = (bf16[1024,128]{1,0:T(8,128)(2,1)S(1)}, bf16[1024,128]{1,0:T(8,128)(2,1)S(1)}, u32[]{:S(2)}, u32[]{:S(2)}) collective-permute-start(bf16[1024,128]{1,0:T(8,128)(2,1)S(1)} %grad_columns.1.refs_1_.refs_0_), channel_id=1, source_target_pairs={{0,18},{1,19},{2,16},{3,17},{16,2},{17,3},{18,0},{19,1},{4,22},{5,... | collective-permute-start | bytes 786440 | tf_op jit(solution)/shard_map/ppermute | solution.py:508
  126.8 16.6 %collective-permute-start.36 = (bf16[1024,128]{1,0:T(8,128)(2,1)S(1)}, bf16[1024,128]{1,0:T(8,128)(2,1)S(1)}, u32[]{:S(2)}, u32[]{:S(2)}) collective-permute-start(bf16[1024,128]{1,0:T(8,128)(2,1)S(1)} %grad_columns.1.refs_1_.refs_0_), channel_id=1, source_target_pairs={{0,16},{1,17},{2,18},{3,19},{16,0},{17,1},{18,2},{19,3},{4,20},{5,... | collective-permute-start | bytes 786440 | tf_op jit(solution)/shard_map/ppermute | solution.py:508
  127.3 16.0 %collective-permute-start.35 = (bf16[1024,128]{1,0:T(8,128)(2,1)S(1)}, bf16[1024,128]{1,0:T(8,128)(2,1)S(1)}, u32[]{:S(2)}, u32[]{:S(2)}) collective-permute-start(bf16[1024,128]{1,0:T(8,128)(2,1)S(1)} %grad_columns.1.refs_1_.refs_0_), channel_id=1, source_target_pairs={{0,2},{1,3},{2,0},{3,1},{16,18},{17,19},{18,16},{19,17},{4,6},{5,7... | collective-permute-start | bytes 786440 | tf_op jit(solution)/shard_map/ppermute | solution.py:508
  127.8 4.6 %collective-permute-start.31 = (f32[24,128]{1,0:T(8,128)S(1)}, f32[24,128]{1,0:T(8,128)S(1)}, u32[]{:S(2)}, u32[]{:S(2)}) collective-permute-start(f32[24,128]{1,0:T(8,128)S(1)} %slope_out.1.refs_0_), channel_id=1, source_target_pairs={{0,8},{4,12},{8,0},{12,4},{1,9},{5,13},{9,1},{13,5},{2,10},{6,14},... | collective-permute-start | bytes 36872 | tf_op jit(solution)/shard_map/ppermute | solution.py:515
  132.4 6.0 %collective-permute-start.32 = (f32[24,128]{1,0:T(8,128)S(1)}, f32[24,128]{1,0:T(8,128)S(1)}, u32[]{:S(2)}, u32[]{:S(2)}) collective-permute-start(f32[24,128]{1,0:T(8,128)S(1)} %sum_mirror.1.refs_0_), channel_id=1, source_target_pairs={{0,16},{1,17},{2,18},{3,19},{16,0},{17,1},{18,2},{19,3},{4,20},{5,... | collective-permute-start | bytes 36872 | tf_op jit(solution)/shard_map/ppermute | solution.py:508
  138.4 3.7 %collective-permute-start.33 = (f32[24,128]{1,0:T(8,128)S(1)}, f32[24,128]{1,0:T(8,128)S(1)}, u32[]{:S(2)}, u32[]{:S(2)}) collective-permute-start(f32[24,128]{1,0:T(8,128)S(1)} %sum_plane.3.refs_0_), channel_id=1, source_target_pairs={{0,2},{1,3},{2,0},{3,1},{16,18},{17,19},{18,16},{19,17},{4,6},{5,7... | collective-permute-start | bytes 36872 | tf_op jit(solution)/shard_map/ppermute | solution.py:508
  142.1 1.2 collective-permute-start.34
  143.4 3.1 %copy-start.21 = (f32[1024]{0:T(1024)S(1)}, f32[1024]{0:T(1024)}, u32[]{:S(2)}) copy-start(f32[1024]{0:T(1024)} %param.14) | copy-start | bytes 12292
  143.4 3.0 %collective-permute-start.38 = (bf16[4096,128]{1,0:T(8,128)(2,1)S(1)}, bf16[4096,128]{1,0:T(8,128)(2,1)S(1)}, u32[]{:S(2)}, u32[]{:S(2)}) collective-permute-start(bf16[4096,128]{1,0:T(8,128)(2,1)S(1)} %pack_columns.1.refs_3_), channel_id=1, source_target_pairs={{0,1},{1,0},{2,3},{3,2},{16,17},{17,16},{18,19},{19,18},{4,5},{5,4... | collective-permute-start | bytes 3145736 | tf_op jit(solution)/shard_map/ppermute | solution.py:508
  144.9 5.0 %collective-permute-start.39 = (f32[1,1024]{1,0:T(1,128)S(1)}, f32[1,1024]{1,0:T(1,128)S(1)}, u32[]{:S(2)}, u32[]{:S(2)}) collective-permute-start(f32[1,1024]{1,0:T(1,128)S(1)} %get-tuple-element.76.refs_0_), channel_id=1, source_target_pairs={{0,4},{4,0},{8,12},{12,8},{1,5},{5,1},{9,13},{13,9},{2,6},{6,2},{1... | collective-permute-start | bytes 12296 | tf_op jit(solution)/shard_map/ppermute | solution.py:512
  (2 other events, 1.4 us)

commit v6 on v5

--- a/solution.py
+++ b/solution.py
@@ -43,14 +43,14 @@
     return run
 
 
-def call(kernel, outs, ins, name, flops=0, scratch=(), smem=0, after=(), copy=False):
+def call(kernel, outs, ins, name, flops=0, scratch=(), smem=0, after=(), copy=False, streamed=False):
     count = len(ins)
     if copy:
         shapes = [pltpu.VMEM(a.shape, a.dtype) for a in ins[smem:]]
         kernel = copying(kernel, smem, shapes)
         scratch = [*scratch, *shapes, pltpu.SemaphoreType.DMA((len(shapes),))]
     moved = sum(math.prod(a.shape) * a.dtype.itemsize for a in list(ins) + list(outs))
-    held = 0 if copy else sum(math.prod(s.shape) * jnp.dtype(s.dtype).itemsize for s in scratch)
+    held = 0 if copy or streamed else sum(math.prod(s.shape) * jnp.dtype(s.dtype).itemsize for s in scratch)
 
     def run(*refs):
         kernel(*refs[:count], *refs[count + len(after) :])
@@ -61,11 +61,11 @@
         in_specs=[SMEM] * smem
         + [pl.BlockSpec(memory_space=pl.ANY) if copy else VMEM] * (count - smem)
         + [pl.BlockSpec(memory_space=pl.ANY)] * len(after),
-        out_specs=[VMEM] * len(outs),
+        out_specs=([pl.BlockSpec(memory_space=pl.ANY)] if streamed else [VMEM]) + [VMEM] * (len(outs) - 1),
         scratch_shapes=list(scratch),
         cost_estimate=pl.CostEstimate(flops=flops, bytes_accessed=moved, transcendentals=0),
         compiler_params=pltpu.CompilerParams(
-            vmem_limit_bytes=(4 if copy else 2) * (moved + held) + (12 if copy else 6) * MIB
+            vmem_limit_bytes=61 * MIB if copy else 2 * (moved + held) + 6 * MIB
         ),
         name=name,
     )(*ins, *after)
@@ -203,9 +203,34 @@
         refs[-1][k * rows : (k + 1) * rows, :] = ref[...]
 
 
-def pack(pieces, name, event):
+def pack_copies(n, *refs):
+    out_ref, sems = refs[-2], refs[-1]
+    rows = refs[0].shape[0]
+    copies = [
+        pltpu.make_async_copy(refs[k], out_ref.at[pl.ds(k * rows, rows), :], sems.at[k]) for k in range(n)
+    ]
+    for copy in copies:
+        copy.start()
+    for copy in copies:
+        copy.wait()
+
+
+def pack(pieces, name, event, copy=False):
     rows, width = pieces[0].shape
-    out = shape((len(pieces) * rows, width), pieces[0].dtype)
+    n = len(pieces)
+    out = shape((n * rows, width), pieces[0].dtype)
+    if copy:
+        anywhere = pl.BlockSpec(memory_space=pl.ANY)
+        return pl.pallas_call(
+            functools.partial(pack_copies, n),
+            out_shape=out,
+            in_specs=[anywhere] * (n + 1),
+            out_specs=anywhere,
+            scratch_shapes=[pltpu.SemaphoreType.DMA((n,))],
+            cost_estimate=pl.CostEstimate(flops=0, bytes_accessed=4 * n * rows * width, transcendentals=0),
+            compiler_params=pltpu.CompilerParams(vmem_limit_bytes=4 * MIB),
+            name=name,
+        )(*pieces, event)
     return call(pack_kernel, [out], pieces, name, after=[event])[0]
 
 
@@ -463,18 +488,25 @@
 
 
 def finish_kernel(n, place_ref, pool_ref, slope_ref, *refs):
-    pieces, out_ref, token_ref = refs[:n], refs[-2], refs[-1]
+    pieces, result_ref, token_ref, out_ref, sems = refs[:n], *refs[n:]
     token_ref[...] = jnp.zeros_like(token_ref)
     places = place_ref.shape[0]
     rows, cols = out_ref.shape[0], pieces[0].shape[1]
+    copies = []
     for line in range(rows // LANES):
-        part = slice(line * LANES, (line + 1) * LANES)
+        part = pl.ds(line * LANES, LANES)
         slope = jnp.broadcast_to(slope_ref[line : line + 1, :], (LANES, LANES)).T
         for k in range(places):
             base = k % (places // n) * rows + line * LANES
             mine = pieces[k // (places // n)][base : base + LANES, :].astype(F32)
             at = pl.ds(pl.multiple_of(place_ref[k] * cols, LANES), cols)
             out_ref[part, at] = mine + slope * pool_ref[:, at]
+        copies.append(
+            pltpu.make_async_copy(out_ref.at[part, :], result_ref.at[part, :], sems.at[line])
+        )
+        copies[-1].start()
+    for copy in copies:
+        copy.wait()
 
 
 def body(hidden_states, positives, negatives, lengths, norm_gain, proj_weight, pool_query, slab):
@@ -630,7 +662,6 @@
     def total(parts, name):
         return call(add_kernel, [shape(parts[0].shape, F32)], parts, name)[0]
 
-    slope = total([slopes[0]] + [half_shift(slopes[k], k) for k in range(1, half)], "sum_half")
     across = [plane_shift(others, 0, dh, 0) for dh in range(1, n_h)]
     late = [pack([array], "late", slopes[0]) for array in across]
     spread = []
@@ -643,27 +674,34 @@
     block_columns = call(
         functools.partial(columns_kernel, len(spread)), [shape((depth, cols), BF16)],
         [ranks, all_columns] + spread, "grad_columns",
-        flops=2 * n_all * queries * depth * cols, scratch=[pltpu.VMEM((n_all * queries, cols), BF16)], smem=1, copy=True, after=[slope],
+        flops=2 * n_all * queries * depth * cols, scratch=[pltpu.VMEM((n_all * queries, cols), BF16)], smem=1, copy=True,
     )[0]
     on_chips = [block_columns if dg == dh == 0 else plane_shift(block_columns, dg, dh, 0) for dg, dh in chips]
-    slope = passed(slope, "slope_out", block_columns)
-    slope = total([slope, mirror_shift(slope)], "sum_mirror")
-    for axis, size in ((0, n_g), (1, n_h), (2, n_c)):
-        if size > 1:
-            moves = [[k if a == axis else 0 for a in range(3)] for k in range(1, size)]
-            slope = total([slope] + [plane_shift(slope, *move) for move in moves], "sum_plane")
+    slopes = [passed(array, "slope_out", block_columns) for array in slopes]
+    stage = [slopes[0]]
+    for k in range(half):
+        for flip in (0, 1):
+            if k or flip:
+                pairs = [(a, (a // half + flip) % 2 * half + (a % half + k) % half) for a in range(n_z)]
+                stage.append(lax.ppermute(slopes[k], "fsdp", pairs))
+    slope = total(stage, "sum_line")
+    if n_g > 1:
+        slope = total([slope] + [shift(slope, "grp", k) for k in range(1, n_g)], "sum_groups")
+    if n_i > 1:
+        slope = total([slope] + [shift(slope, "item", k) for k in steps_i], "sum_items")
     query_part, my_slope, loss_total = call(
         query_kernel,
         [shape((1, proj_width), F32), shape((depth // LANES, LANES), F32), shape((1, LANES), F32)],
         [side_arr, proj_weight, mirror, slope], "slope_sum", smem=1,
     )
-    finished = [pack(on_chips, "pack_columns", slope)]
+    finished = [pack(on_chips, "pack_columns", slope, True)]
     finished += [plane_shift(finished[0], 0, 0, dc) for dc in range(1, n_c)]
     query_parts = [query_part] + [half_shift(query_part, k) for k in range(1, half)]
     grad_proj, finish_token = call(
         functools.partial(finish_kernel, len(finished)),
         [shape((depth, proj_width), F32), shape((8, LANES), F32)],
-        [share_places, pool_query.reshape(1, -1), my_slope] + finished, "finish", smem=1,
+        [share_places, pool_query.reshape(1, -1), my_slope] + finished, "finish", smem=1, streamed=True,
+        scratch=[pltpu.VMEM((depth, proj_width), F32), pltpu.SemaphoreType.DMA((depth // LANES,))],
     )
     grad_query = call(
         add_kernel, [shape((1, proj_width), F32)], query_parts, "query_sum", after=[finish_token]

time: 152 us -> 148 us (0.974)
  local copies, waits for them, and re-layouts: 16.7 us -> 12 us
  starting transfers between devices: 46 us -> 48.5 us
  waiting for transfers between devices: 50.6 us -> 48.7 us
    ppermute x19 -> x16, waiting for transfers between devices: 14.3 us -> 6.33 us  [plane_shift(): return lax.ppermute(values, PLANE, pairs)]
    ppermute x12 -> x16, waiting for transfers between devices: 6.27 us -> 11.9 us  [shift(): return lax.ppermute(values, axis, [(i, (i + k) % n) for i in range(n)])]
    ppermute x0 -> x3, starting transfers between devices: none -> 4.89 us  [body(): stage.append(lax.ppermute(slopes[k], 'fsdp', pairs))]
    unnamed x51 -> x47, local copies, waits for them, and re-layouts: 15.1 us -> 10.4 us
    ppermute x0 -> x3, waiting for transfers between devices: none -> 3.39 us  [body(): stage.append(lax.ppermute(slopes[k], 'fsdp', pairs))]
    ppermute x12 -> x16, starting transfers between devices: 9.97 us -> 13.3 us  [shift(): return lax.ppermute(values, axis, [(i, (i + k) % n) for i in range(n)])]
    ppermute x3 -> x2, waiting for transfers between devices: 12.2 us -> 9.3 us  [mirror_shift(): lax.ppermute(values, 'fsdp', [(a, (a + half) % n_z) for a in range(n_z)])]
    ppermute x6 -> x5, waiting for transfers between devices: 17.8 us -> 15.1 us  [half_shift(): return lax.ppermute(values, 'fsdp', pairs)]
  transfers between devices with their start and end apart: 41 -> 43, of which waited for: 20 -> 23; matrix products, arithmetic and copies ran while one was open for 1% -> 1% of each run, Pallas kernels for 19% -> 18%
where the time goes in v6:
time: 148 us
  waiting for transfers between devices  48.7 us (33%)
  starting transfers between devices  48.5 us (33%)
  Pallas kernels  36.2 us (24%)
  local copies, waits for them, and re-layouts  12 us (8%)
  between operations  2.32 us (2%)
    pallas_call x21, Pallas kernels, call(): pl.pallas_call(run, out_shape=outs, in_specs=[SMEM] * smem + [pl.BlockSpe...  18.6 us
    ppermute x5, waiting for transfers between devices, half_shift(): return lax.ppermute(values, 'fsdp', pairs)  15.1 us
    ppermute x16, starting transfers between devices, shift(): return lax.ppermute(values, axis, [(i, (i + k) % n) for i in range(n)])  13.3 us
    ppermute x16, starting transfers between devices, plane_shift(): return lax.ppermute(values, PLANE, pairs)  12.8 us
    ppermute x16, waiting for transfers between devices, shift(): return lax.ppermute(values, axis, [(i, (i + k) % n) for i in range(n)])  11.9 us
    pallas_call x1, Pallas kernels, gate_rows(): pl.pallas_call(run, grid=(queries // group,), out_shape=outs, in_specs=[S...  11.6 us
    unnamed x47, local copies, waits for them, and re-layouts  10.4 us
    ppermute x2, waiting for transfers between devices, mirror_shift(): lax.ppermute(values, 'fsdp', [(a, (a + half) % n_z) for a in range(n_z)])  9.3 us
  transfers between devices with their start and end apart: 43, of which 23 were waited for; matrix products, arithmetic and copies ran while one was open for 1% of the time, Pallas kernels for 18%

profile of v6, /device:TPU:0, one launch (start us, length us, event | category | flops | bytes accessed | tf_op | source)
XLA Modules:
  0.0 147.8 jit_solution(15720742783542596964)
XLA Ops:
  0.7 1.0 constant_dynamic-slice_fusion.refs_2_
  1.6 4.1 %collective-permute-start.3 = (bf16[128,1024]{1,0:T(8,128)(2,1)S(1)}, bf16[128,1024]{1,0:T(8,128)(2,1)S(1)}, u32[]{:S(2)}, u32[]{:S(2)}) collective-permute-start(bf16[128,1024]{1,0:T(8,128)(2,1)S(1)} %constant_dynamic-slice_fusion.refs_2_), channel_id=1, source_target_pairs={{0,8},{4,12},{8,0},{12,4},{1,9},{5,13},{9,1},{13,5},{2,10},{6,14},... | collective-permute-start | bytes 786440 | tf_op jit(solution)/shard_map/ppermute | solution.py:547
  5.8 1.6 %copy-done = bf16[1024,1024]{1,0:T(8,128)(2,1)S(1)} copy-done((bf16[1024,1024]{1,0:T(8,128)(2,1)S(1)}, bf16[1024,1024]{1,0:T(8,128)(2,1)}, u32[]{:S(2)}) %copy-start) | copy-done | bytes 2097176
  7.3 0.7 copy-done.17
  8.0 1.7 %block_u.1 = f32[1,1024]{1,0:T(1,128)S(1)} custom-call(bf16[1024,1024]{1,0:T(8,128)(2,1)S(1)} %copy-done, f32[1,1024]{1,0:T(1,128)S(1)} %bitcast.51, bf16[128,1024]{1,0:T(8,128)(2,1)S(1)} %constant_dynamic-slice_fusion.refs_2_), custom_call_target="tpu_custom_call" | custom-call | bytes 2105344 | tf_op jit(solution)/shard_map/block_u/pallas_call | solution.py:58
  9.8 1.4 collective-permute-start.2
  11.1 1.7 %collective-permute-start.1 = (f32[1,1024]{1,0:T(1,128)S(1)}, f32[1,1024]{1,0:T(1,128)S(1)}, u32[]{:S(2)}, u32[]{:S(2)}) collective-permute-start(f32[1,1024]{1,0:T(1,128)S(1)} %block_u.1), channel_id=1, source_target_pairs={{0,8},{4,12},{8,0},{12,4},{1,9},{5,13},{9,1},{13,5},{2,10},{6,14},... | collective-permute-start | bytes 12296 | tf_op jit(solution)/shard_map/ppermute | solution.py:76
  13.7 4.2 %collective-permute-done.3.refs_6_.refs_0_ = bf16[128,1024]{1,0:T(8,128)(2,1)S(1)} collective-permute-done((bf16[128,1024]{1,0:T(8,128)(2,1)S(1)}, bf16[128,1024]{1,0:T(8,128)(2,1)S(1)}, u32[]{:S(2)}, u32[]{:S(2)}) %collective-permute-start.3) | collective-permute-done | bytes 262176 | tf_op jit(solution)/shard_map/ppermute | solution.py:547
  17.9 2.5 %collective-permute-start.7 = (bf16[128,1024]{1,0:T(8,128)(2,1)S(1)}, bf16[128,1024]{1,0:T(8,128)(2,1)S(1)}, u32[]{:S(2)}, u32[]{:S(2)}) collective-permute-start(bf16[128,1024]{1,0:T(8,128)(2,1)S(1)} %collective-permute-done.3.refs_6_.refs_0_), channel_id=1, source_target_pairs={{0,18},{1,19},{2,16},{3,17},{16,2},{17,3},{18,0},{19,1},{4,22},{5,... | collective-permute-start | bytes 786440 | tf_op jit(solution)/shard_map/ppermute | solution.py:540
  21.4 11.6 %gate_rows.1 = (bf16[64,2048]{1,0:T(8,128)(2,1)S(1)}, bf16[64,2048]{1,0:T(8,128)(2,1)S(1)}, bf16[1024,4096]{1,0:T(8,128)(2,1)}, f32[1024,1]{1,0:T(8,128)S(1)}, f...) custom-call(s32[2]{0:T(128)S(1)} %pad_add_fusion.refs_0_.z_ref, ...), custom_call_target="tpu_custom_call" | custom-call | flops 41943040 | bytes 16777216 | tf_op jit(solution)/shard_map/gate_rows/pallas_call | solution.py:176
  33.2 0.8 collective-permute-start.4
  34.2 1.5 %collective-permute-start.10 = (s32[64,8]{1,0:T(8,128)S(1)}, s32[64,8]{1,0:T(8,128)S(1)}, u32[]{:S(2)}, u32[]{:S(2)}) collective-permute-start(s32[64,8]{1,0:T(8,128)S(1)} %get-tuple-element.46), channel_id=1, source_target_pairs={{0,2},{1,3},{2,0},{3,1},{4,6},{5,7},{6,4},{7,5},{8,10},{9,11},{10,... | collective-permute-start | bytes 6152 | tf_op jit(solution)/shard_map/ppermute | solution.py:76
  35.8 1.3 collective-permute-start.11
  37.4 0.7 collective-permute-done.10.refs_4_
  38.7 1.8 %list_counts.1 = (f32[256,1024]{1,0:T(8,128)S(1)}, f32[1,1024]{1,0:T(1,128)S(1)}) custom-call(s32[1]{0:T(128)} %bitcast.46.refs_9_.refs_0_, bf16[1024,1024]{1,0:T(8,128)(2,1)S(1)} %copy-done.4, s32[64,8]{1,0:T(8,128)S(1)} %get-tuple-element.44.refs_2_, s32[64,8]{1,0:T(8,128)S(1)} %collective-permute-done.9.refs_3_, ...), custom_call_target="tpu_custom_call" | custom-call | bytes 3158020 | tf_op jit(solution)/shard_map/list_counts/pallas_call | solution.py:58
  40.5 1.5 collective-permute-done.4.refs_4_
  42.0 1.4 forward.1
  43.4 1.6 %collective-permute-start.13 = (bf16[128,1024]{1,0:T(8,128)(2,1)S(1)}, bf16[128,1024]{1,0:T(8,128)(2,1)S(1)}, u32[]{:S(2)}, u32[]{:S(2)}) collective-permute-start(bf16[128,1024]{1,0:T(8,128)(2,1)S(1)} %get-tuple-element.55.refs_3_), channel_id=1, source_target_pairs={{0,2},{1,3},{2,0},{3,1},{16,18},{17,19},{18,16},{19,17},{4,6},{5,7... | collective-permute-start | bytes 786440 | tf_op jit(solution)/shard_map/ppermute | solution.py:540
  45.0 0.7 collective-permute-start.12
  45.8 4.2 %collective-permute-done.12.refs_1_ = bf16[64,1024]{1,0:T(8,128)(2,1)S(1)} collective-permute-done((bf16[64,1024]{1,0:T(8,128)(2,1)S(1)}, bf16[64,1024]{1,0:T(8,128)(2,1)S(1)}, u32[]{:S(2)}, u32[]{:S(2)}) %collective-permute-start.12) | collective-permute-done | bytes 131104 | tf_op jit(solution)/shard_map/ppermute | solution.py:544
  50.0 1.3 collective-permute-done.13.refs_4_
  51.6 1.6 %collective-permute-start.24 = (bf16[256,1024]{1,0:T(8,128)(2,1)S(1)}, bf16[256,1024]{1,0:T(8,128)(2,1)S(1)}, u32[]{:S(2)}, u32[]{:S(2)}) collective-permute-start(bf16[256,1024]{1,0:T(8,128)(2,1)S(1)} %get-tuple-element.60.refs_2_), channel_id=1, source_target_pairs={{0,16},{1,17},{2,18},{3,19},{16,0},{17,1},{18,2},{19,3},{4,20},{5,... | collective-permute-start | bytes 1572872 | tf_op jit(solution)/shard_map/ppermute | solution.py:540
  53.2 1.3 collective-permute-start.16
  55.0 3.4 %collective-permute-done.16.refs_6_ = bf16[64,1024]{1,0:T(8,128)(2,1)S(1)} collective-permute-done((bf16[64,1024]{1,0:T(8,128)(2,1)S(1)}, bf16[64,1024]{1,0:T(8,128)(2,1)S(1)}, u32[]{:S(2)}, u32[]{:S(2)}) %collective-permute-start.16) | collective-permute-done | bytes 131104 | tf_op jit(solution)/shard_map/ppermute | solution.py:76
  58.3 3.2 %collective-permute-start.22 = (bf16[128,1024]{1,0:T(8,128)(2,1)S(1)}, bf16[128,1024]{1,0:T(8,128)(2,1)S(1)}, u32[]{:S(2)}, u32[]{:S(2)}) collective-permute-start(bf16[128,1024]{1,0:T(8,128)(2,1)S(1)} %get-tuple-element.67), channel_id=1, source_target_pairs={{0,8},{4,12},{8,0},{12,4},{1,9},{5,13},{9,1},{13,5},{2,10},{6,14},... | collective-permute-start | bytes 786440 | tf_op jit(solution)/shard_map/ppermute | solution.py:547
  61.9 1.4 contrast.1
  63.3 2.6 %collective-permute-done.24.refs_0_.refs_3_ = bf16[256,1024]{1,0:T(8,128)(2,1)S(1)} collective-permute-done((bf16[256,1024]{1,0:T(8,128)(2,1)S(1)}, bf16[256,1024]{1,0:T(8,128)(2,1)S(1)}, u32[]{:S(2)}, u32[]{:S(2)}) %collective-permute-start.24) | collective-permute-done | bytes 524320 | tf_op jit(solution)/shard_map/ppermute | solution.py:540
  65.9 0.8 copy-done.11
  66.7 1.7 %collective-permute-start.18 = (bf16[64,1152]{1,0:T(8,128)(2,1)S(1)}, bf16[64,1152]{1,0:T(8,128)(2,1)S(1)}, u32[]{:S(2)}, u32[]{:S(2)}) collective-permute-start(bf16[64,1152]{1,0:T(8,128)(2,1)S(1)} %get-tuple-element.62), channel_id=1, source_target_pairs={{0,3},{1,0},{2,1},{3,2},{4,7},{5,4},{6,5},{7,6},{8,11},{9,8},{10,9... | collective-permute-start | bytes 442376 | tf_op jit(solution)/shard_map/ppermute | solution.py:76
  68.9 5.1 %collective-permute-done.22.refs_0_ = bf16[128,1024]{1,0:T(8,128)(2,1)S(1)} collective-permute-done((bf16[128,1024]{1,0:T(8,128)(2,1)S(1)}, bf16[128,1024]{1,0:T(8,128)(2,1)S(1)}, u32[]{:S(2)}, u32[]{:S(2)}) %collective-permute-start.22) | collective-permute-done | bytes 262176 | tf_op jit(solution)/shard_map/ppermute | solution.py:547
  74.6 1.6 %collective-permute-done.19.refs_6_ = bf16[64,1152]{1,0:T(8,128)(2,1)S(1)} collective-permute-done((bf16[64,1152]{1,0:T(8,128)(2,1)S(1)}, bf16[64,1152]{1,0:T(8,128)(2,1)S(1)}, u32[]{:S(2)}, u32[]{:S(2)}) %collective-permute-start.19) | collective-permute-done | bytes 147488 | tf_op jit(solution)/shard_map/ppermute | solution.py:76
  76.6 1.2 collective-permute-start.21
  77.8 3.9 %collective-permute-done.21.refs_4_ = bf16[64,1024]{1,0:T(8,128)(2,1)S(1)} collective-permute-done((bf16[64,1024]{1,0:T(8,128)(2,1)S(1)}, bf16[64,1024]{1,0:T(8,128)(2,1)S(1)}, u32[]{:S(2)}, u32[]{:S(2)}) %collective-permute-start.21) | collective-permute-done | bytes 131104 | tf_op jit(solution)/shard_map/ppermute | solution.py:544
  81.7 0.7 collective-permute-done.23.refs_6_
  82.4 2.2 %backward.1 = (bf16[64,2048]{1,0:T(8,128)(2,1)S(1)}, bf16[64,2048]{1,0:T(8,128)(2,1)S(1)}, bf16[256,1024]{1,0:T(8,128)(2,1)}) custom-call(s32[1]{0:T(128)} %bitcast.9.refs_10_.refs_0_, bf16[1024,1024]{1,0:T(8,128)(2,1)S(1)} %copy-done.1, bf16[1024,1024]{1,0:T(8,128)(2,1)S(1)} %get-tuple-element.49.refs_2_, bf16[64,1024]{1,0:T(8,128)(2,1)S(1)} %get-tuple-element.66.refs_3_, ...), custom_call_target="tpu_custom_call" | custom-call | flops 536870912 | bytes 6029316 | tf_op jit(solution)/shard_map/backward/pallas_call | solution.py:58
  84.6 0.8 collective-permute-start.26
  85.4 1.1 collective-permute-start.27
  86.6 5.5 %collective-permute-done.26.rest_1_.refs_1_ = bf16[64,2048]{1,0:T(8,128)(2,1)S(1)} collective-permute-done((bf16[64,2048]{1,0:T(8,128)(2,1)S(1)}, bf16[64,2048]{1,0:T(8,128)(2,1)S(1)}, u32[]{:S(2)}, u32[]{:S(2)}) %collective-permute-start.26) | collective-permute-done | bytes 262176 | tf_op jit(solution)/shard_map/ppermute | solution.py:544
  92.2 0.8 copy-done.12
  93.0 5.4 %all-to-all-start = ((bf16[32,64,128]{2,1,0:T(8,128)(2,1)}), bf16[32,64,128]{2,1,0:T(8,128)(2,1)}, u32[]{:S(2)}, u32[]{:S(2)}) async-start(bf16[32,64,128]{2,1,0:T(8,128)(2,1)} %copy-done.12), calls=%async_computation | async-start | bytes 1048576 | tf_op jit(solution)/shard_map/all_to_all | solution.py:658
  98.4 3.4 %copy-done.5 = bf16[1024,4096]{1,0:T(8,128)(2,1)S(1)} copy-done((bf16[1024,4096]{1,0:T(8,128)(2,1)S(1)}, bf16[1024,4096]{1,0:T(8,128)(2,1)}, u32[]{:S(2)}) %copy-start.5) | copy-done | bytes 8388632
  101.8 1.0 copy-done.14
  102.9 5.9 %slope_rows.1 = (f32[24,128]{1,0:T(8,128)S(1)}, f32[24,128]{1,0:T(8,128)S(1)}) custom-call(s32[2]{0:T(128)S(1)} %pad_add_fusion.refs_0_.z_ref, bf16[1024,4096]{1,0:T(8,128)(2,1)S(1)} %copy-done.5, f32[1024,1]{1,0:T(8,128)S(1)} %copy-done.14, f32[1,128]{1,0:T(1,128)S(1)} %get-tuple-element.65.loss_ref, bf16[64,2048]{1,0:T(8,128)(2,1)S(1)} %get-tuple-element.68.rest_0_, ...), custom_call_target="tpu_custom_call" | custom-call | flops 16777216 | bytes 8388608 | tf_op jit(solution)/shard_map/slope_rows/pallas_call | solution.py:433
  109.4 1.7 %collective-permute-done.29.refs_9_ = bf16[256,1024]{1,0:T(8,128)(2,1)} collective-permute-done((bf16[256,1024]{1,0:T(8,128)(2,1)S(1)}, bf16[256,1024]{1,0:T(8,128)(2,1)}, u32[]{:S(2)}, u32[]{:S(2)}) %collective-permute-start.29) | collective-permute-done | bytes 524320 | tf_op jit(solution)/shard_map/ppermute | solution.py:540
  111.0 2.7 %all-to-all-done.refs_1_ = bf16[32,64,128]{2,1,0:T(8,128)(2,1)} async-done(((bf16[32,64,128]{2,1,0:T(8,128)(2,1)}), bf16[32,64,128]{2,1,0:T(8,128)(2,1)}, u32[]{:S(2)}, u32[]{:S(2)}) %all-to-all-start) | async-done | bytes 524320 | tf_op jit(solution)/shard_map/all_to_all | solution.py:658
  113.7 4.6 %grad_columns.1.refs_1_.refs_0_ = bf16[1024,128]{1,0:T(8,128)(2,1)} custom-call(s32[32]{0:T(128)} %copy-done.19, bf16[32,64,128]{2,1,0:T(8,128)(2,1)} %all-to-all-done.refs_1_, bf16[256,1024]{1,0:T(8,128)(2,1)} %copy-done.15, bf16[256,1024]{1,0:T(8,128)(2,1)} %copy-done.11, bf16[256,1024]{1,0:T(8,128)(2,1)} %get-tuple-element.72.refs_4_, ...), custom_call_target="tpu_custom_call" | custom-call | flops 536870912 | bytes 4980864 | tf_op jit(solution)/shard_map/grad_columns/pallas_call | solution.py:58
  118.3 1.9 %collective-permute-start.39 = (bf16[1024,128]{1,0:T(8,128)(2,1)}, bf16[1024,128]{1,0:T(8,128)(2,1)S(1)}, u32[]{:S(2)}, u32[]{:S(2)}) collective-permute-start(bf16[1024,128]{1,0:T(8,128)(2,1)} %grad_columns.1.refs_1_.refs_0_), channel_id=1, source_target_pairs={{0,18},{1,19},{2,16},{3,17},{16,2},{17,3},{18,0},{19,1},{4,22},{5,... | collective-permute-start | bytes 786440 | tf_op jit(solution)/shard_map/ppermute | solution.py:540
  120.8 1.1 collective-permute-start.37
  121.9 1.0 copy-done.7
  123.2 3.2 %collective-permute-start.32 = (f32[24,128]{1,0:T(8,128)S(1)}, f32[24,128]{1,0:T(8,128)S(1)}, u32[]{:S(2)}, u32[]{:S(2)}) collective-permute-start(f32[24,128]{1,0:T(8,128)S(1)} %slope_out.3), channel_id=1, source_target_pairs={{0,12},{4,8},{8,4},{12,0},{1,13},{5,9},{9,5},{13,1},{2,14},{6,10},... | collective-permute-start | bytes 36872 | tf_op jit(solution)/shard_map/ppermute | solution.py:686
  126.5 1.0 collective-permute-done.30.refs_1_
  127.4 1.3 collective-permute-start.31
  128.7 2.4 %collective-permute-done.31.refs_2_ = f32[24,128]{1,0:T(8,128)S(1)} collective-permute-done((f32[24,128]{1,0:T(8,128)S(1)}, f32[24,128]{1,0:T(8,128)S(1)}, u32[]{:S(2)}, u32[]{:S(2)}) %collective-permute-start.31) | collective-permute-done | bytes 12320 | tf_op jit(solution)/shard_map/ppermute | solution.py:686
  131.1 1.2 collective-permute-start.33
  132.4 2.4 %collective-permute-done.33.refs_1_ = f32[24,128]{1,0:T(8,128)S(1)} collective-permute-done((f32[24,128]{1,0:T(8,128)S(1)}, f32[24,128]{1,0:T(8,128)S(1)}, u32[]{:S(2)}, u32[]{:S(2)}) %collective-permute-start.33) | collective-permute-done | bytes 12320 | tf_op jit(solution)/shard_map/ppermute | solution.py:76
  134.8 1.0 collective-permute-start.35
  136.3 1.1 collective-permute-start.34
  137.3 1.2 collective-permute-done.35.refs_2_
  138.5 0.8 collective-permute-done.34.refs_1_
  139.4 0.9 copy-done.8
  140.6 1.3 slope_sum.1
  141.9 1.3 collective-permute-start.41
  143.2 2.8 %finish.1 = (f32[1024,1024]{1,0:T(8,128)}, f32[8,128]{1,0:T(8,128)S(1)}) custom-call(s32[8]{0:T(128)S(1)} %stack.149.refs_7_.refs_1_.refs_0_, f32[1,1024]{1,0:T(1,128)S(1)} %bitcast.52, f32[8,128]{1,0:T(8,128)S(1)} %get-tuple-element.74.refs_2_, bf16[4096,128]{1,0:T(8,128)(2,1)S(1)} %pack_columns.1.refs_3_, bf16[4096,128]{1,0:T(8,128)(2,1)S(1)} %collective-permute-done.40.refs_4_), custom_call_target="tpu_custom_call" | custom-call | bytes 6303776 | tf_op jit(solution)/shard_map/finish/pallas_call | solution.py:58
  146.1 0.6 query_sum.1
  (105 shorter events, 8.1 us)
Async XLA Ops:
  0.6 12.3 %copy-start.21 = (bf16[4096]{0:T(1024)(128)(2,1)S(1)}, bf16[4096]{0:T(1024)(128)(2,1)}, u32[]{:S(2)}) copy-start(bf16[4096]{0:T(1024)(128)(2,1)} %param.12) | copy-start | bytes 24580
  0.6 12.3 %copy-start.20 = (s32[64,32]{0,1:T(8,128)S(1)}, s32[64,32]{0,1:T(8,128)}, u32[]{:S(2)}) copy-start(s32[64,32]{0,1:T(8,128)} %param.10) | copy-start | bytes 24580
  0.7 12.4 %copy-start.22 = (s32[64]{0:T(128)S(1)}, s32[64]{0:T(128)}, u32[]{:S(2)}) copy-start(s32[64]{0:T(128)} %param.11) | copy-start | bytes 772
  1.6 16.2 %collective-permute-start.3 = (bf16[128,1024]{1,0:T(8,128)(2,1)S(1)}, bf16[128,1024]{1,0:T(8,128)(2,1)S(1)}, u32[]{:S(2)}, u32[]{:S(2)}) collective-permute-start(bf16[128,1024]{1,0:T(8,128)(2,1)S(1)} %constant_dynamic-slice_fusion.refs_2_), channel_id=1, source_target_pairs={{0,8},{4,12},{8,0},{12,4},{1,9},{5,13},{9,1},{13,5},{2,10},{6,14},... | collective-permute-start | bytes 786440 | tf_op jit(solution)/shard_map/ppermute | solution.py:547
  5.8 1.6 %copy-start = (bf16[1024,1024]{1,0:T(8,128)(2,1)S(1)}, bf16[1024,1024]{1,0:T(8,128)(2,1)}, u32[]{:S(2)}) copy-start(bf16[1024,1024]{1,0:T(8,128)(2,1)} %refs_1_.5) | copy-start | bytes 6291460
  9.8 11.7 %collective-permute-start.2 = (f32[1,1024]{1,0:T(1,128)S(1)}, f32[1,1024]{1,0:T(1,128)S(1)}, u32[]{:S(2)}, u32[]{:S(2)}) collective-permute-start(f32[1,1024]{1,0:T(1,128)S(1)} %block_u.1), channel_id=1, source_target_pairs={{0,12},{4,0},{8,4},{12,8},{1,13},{5,1},{9,5},{13,9},{2,14},{6,2},{... | collective-permute-start | bytes 12296 | tf_op jit(solution)/shard_map/ppermute | solution.py:76
  11.1 10.3 %collective-permute-start.1 = (f32[1,1024]{1,0:T(1,128)S(1)}, f32[1,1024]{1,0:T(1,128)S(1)}, u32[]{:S(2)}, u32[]{:S(2)}) collective-permute-start(f32[1,1024]{1,0:T(1,128)S(1)} %block_u.1), channel_id=1, source_target_pairs={{0,8},{4,12},{8,0},{12,4},{1,9},{5,13},{9,1},{13,5},{2,10},{6,14},... | collective-permute-start | bytes 12296 | tf_op jit(solution)/shard_map/ppermute | solution.py:76
  12.8 8.1 %collective-permute-start = (f32[1,1024]{1,0:T(1,128)S(1)}, f32[1,1024]{1,0:T(1,128)S(1)}, u32[]{:S(2)}, u32[]{:S(2)}) collective-permute-start(f32[1,1024]{1,0:T(1,128)S(1)} %block_u.1), channel_id=1, source_target_pairs={{0,4},{4,8},{8,12},{12,0},{1,5},{5,9},{9,13},{13,1},{2,6},{6,10},{... | collective-permute-start | bytes 12296 | tf_op jit(solution)/shard_map/ppermute | solution.py:76
  13.7 19.4 %copy-start.19 = (s32[32]{0:T(128)}, s32[32]{0:T(128)S(1)}, u32[]{:S(2)}) copy-start(s32[32]{0:T(128)S(1)} %stack.186.refs_8_.refs_0_) | copy-start | bytes 388
  17.9 15.1 %collective-permute-start.7 = (bf16[128,1024]{1,0:T(8,128)(2,1)S(1)}, bf16[128,1024]{1,0:T(8,128)(2,1)S(1)}, u32[]{:S(2)}, u32[]{:S(2)}) collective-permute-start(bf16[128,1024]{1,0:T(8,128)(2,1)S(1)} %collective-permute-done.3.refs_6_.refs_0_), channel_id=1, source_target_pairs={{0,18},{1,19},{2,16},{3,17},{16,2},{17,3},{18,0},{19,1},{4,22},{5,... | collective-permute-start | bytes 786440 | tf_op jit(solution)/shard_map/ppermute | solution.py:540
  20.4 12.7 %collective-permute-start.6 = (bf16[128,1024]{1,0:T(8,128)(2,1)S(1)}, bf16[128,1024]{1,0:T(8,128)(2,1)S(1)}, u32[]{:S(2)}, u32[]{:S(2)}) collective-permute-start(bf16[128,1024]{1,0:T(8,128)(2,1)S(1)} %collective-permute-done.3.refs_6_.refs_0_), channel_id=1, source_target_pairs={{0,16},{1,17},{2,18},{3,19},{16,0},{17,1},{18,2},{19,3},{4,20},{5,... | collective-permute-start | bytes 786440 | tf_op jit(solution)/shard_map/ppermute | solution.py:540
  20.9 12.1 %collective-permute-start.5 = (bf16[128,1024]{1,0:T(8,128)(2,1)S(1)}, bf16[128,1024]{1,0:T(8,128)(2,1)S(1)}, u32[]{:S(2)}, u32[]{:S(2)}) collective-permute-start(bf16[128,1024]{1,0:T(8,128)(2,1)S(1)} %collective-permute-done.3.refs_6_.refs_0_), channel_id=1, source_target_pairs={{0,2},{1,3},{2,0},{3,1},{16,18},{17,19},{18,16},{19,17},{4,6},{5,7... | collective-permute-start | bytes 786440 | tf_op jit(solution)/shard_map/ppermute | solution.py:540
  33.0 7.5 %copy-start.13 = (f32[1024,1]{1,0:T(8,128)}, f32[1024,1]{1,0:T(8,128)S(1)}, u32[]{:S(2)}) copy-start(f32[1024,1]{1,0:T(8,128)S(1)} %get-tuple-element.51.curve_ref) | copy-start | bytes 12292
  33.0 5.6 %copy-start.4 = (bf16[1024,1024]{1,0:T(8,128)(2,1)S(1)}, bf16[1024,1024]{1,0:T(8,128)(2,1)}, u32[]{:S(2)}) copy-start(bf16[1024,1024]{1,0:T(8,128)(2,1)} %refs_0_.4) | copy-start | bytes 6291460
  33.1 8.9 %copy-start.1 = (bf16[1024,1024]{1,0:T(8,128)(2,1)S(1)}, bf16[1024,1024]{1,0:T(8,128)(2,1)}, u32[]{:S(2)}) copy-start(bf16[1024,1024]{1,0:T(8,128)(2,1)} %refs_1_.5) | copy-start | bytes 6291460
  33.2 8.8 %collective-permute-start.8 = (bf16[512,1024]{1,0:T(8,128)(2,1)S(1)}, bf16[512,1024]{1,0:T(8,128)(2,1)S(1)}, u32[]{:S(2)}, u32[]{:S(2)}) collective-permute-start(bf16[512,1024]{1,0:T(8,128)(2,1)S(1)} %pack_shares.1.refs_5_), channel_id=1, source_target_pairs={{0,1},{1,0},{2,3},{3,2},{16,17},{17,16},{18,19},{19,18},{4,5},{5,4... | collective-permute-start | bytes 3145736 | tf_op jit(solution)/shard_map/ppermute | solution.py:540
  33.2 8.7 %collective-permute-start.4 = (bf16[64,2048]{1,0:T(8,128)(2,1)S(1)}, bf16[64,2048]{1,0:T(8,128)(2,1)S(1)}, u32[]{:S(2)}, u32[]{:S(2)}) collective-permute-start(bf16[64,2048]{1,0:T(8,128)(2,1)S(1)} %get-tuple-element.42), channel_id=1, source_target_pairs={{0,4},{4,0},{8,12},{12,8},{1,5},{5,1},{9,13},{13,9},{2,6},{6,2},{1... | collective-permute-start | bytes 786440 | tf_op jit(solution)/shard_map/ppermute | solution.py:544
  34.1 3.3 %collective-permute-start.9 = (s32[64,8]{1,0:T(8,128)S(1)}, s32[64,8]{1,0:T(8,128)S(1)}, u32[]{:S(2)}, u32[]{:S(2)}) collective-permute-start(s32[64,8]{1,0:T(8,128)S(1)} %get-tuple-element.45), channel_id=1, source_target_pairs={{0,1},{1,2},{2,3},{3,0},{4,5},{5,6},{6,7},{7,4},{8,9},{9,10},{10,1... | collective-permute-start | bytes 6152 | tf_op jit(solution)/shard_map/ppermute | solution.py:76
  34.2 3.9 %collective-permute-start.10 = (s32[64,8]{1,0:T(8,128)S(1)}, s32[64,8]{1,0:T(8,128)S(1)}, u32[]{:S(2)}, u32[]{:S(2)}) collective-permute-start(s32[64,8]{1,0:T(8,128)S(1)} %get-tuple-element.46), channel_id=1, source_target_pairs={{0,2},{1,3},{2,0},{3,1},{4,6},{5,7},{6,4},{7,5},{8,10},{9,11},{10,... | collective-permute-start | bytes 6152 | tf_op jit(solution)/shard_map/ppermute | solution.py:76
  35.8 2.9 %collective-permute-start.11 = (s32[64,8]{1,0:T(8,128)S(1)}, s32[64,8]{1,0:T(8,128)S(1)}, u32[]{:S(2)}, u32[]{:S(2)}) collective-permute-start(s32[64,8]{1,0:T(8,128)S(1)} %get-tuple-element.47), channel_id=1, source_target_pairs={{0,3},{1,0},{2,1},{3,2},{4,7},{5,4},{6,5},{7,6},{8,11},{9,8},{10,9... | collective-permute-start | bytes 6152 | tf_op jit(solution)/shard_map/ppermute | solution.py:76
  43.4 39.0 %copy-start.2 = (bf16[1024,1024]{1,0:T(8,128)(2,1)}, bf16[1024,1024]{1,0:T(8,128)(2,1)S(1)}, u32[]{:S(2)}) copy-start(bf16[1024,1024]{1,0:T(8,128)(2,1)S(1)} %get-tuple-element.49.refs_2_) | copy-start | bytes 6291460
  43.4 7.9 %collective-permute-start.13 = (bf16[128,1024]{1,0:T(8,128)(2,1)S(1)}, bf16[128,1024]{1,0:T(8,128)(2,1)S(1)}, u32[]{:S(2)}, u32[]{:S(2)}) collective-permute-start(bf16[128,1024]{1,0:T(8,128)(2,1)S(1)} %get-tuple-element.55.refs_3_), channel_id=1, source_target_pairs={{0,2},{1,3},{2,0},{3,1},{16,18},{17,19},{18,16},{19,17},{4,6},{5,7... | collective-permute-start | bytes 786440 | tf_op jit(solution)/shard_map/ppermute | solution.py:540
  45.0 5.0 %collective-permute-start.12 = (bf16[64,1024]{1,0:T(8,128)(2,1)S(1)}, bf16[64,1024]{1,0:T(8,128)(2,1)S(1)}, u32[]{:S(2)}, u32[]{:S(2)}) collective-permute-start(bf16[64,1024]{1,0:T(8,128)(2,1)S(1)} %get-tuple-element.53), channel_id=1, source_target_pairs={{0,4},{4,0},{8,12},{12,8},{1,5},{5,1},{9,13},{13,9},{2,6},{6,2},{1... | collective-permute-start | bytes 393224 | tf_op jit(solution)/shard_map/ppermute | solution.py:544
  51.5 11.8 %copy-start.15 = (bf16[256,1024]{1,0:T(8,128)(2,1)}, bf16[256,1024]{1,0:T(8,128)(2,1)S(1)}, u32[]{:S(2)}) copy-start(bf16[256,1024]{1,0:T(8,128)(2,1)S(1)} %get-tuple-element.60.refs_2_) | copy-start | bytes 1572868
  51.5 10.4 %collective-permute-start.17 = (bf16[256,1024]{1,0:T(8,128)(2,1)S(1)}, bf16[256,1024]{1,0:T(8,128)(2,1)S(1)}, u32[]{:S(2)}, u32[]{:S(2)}) collective-permute-start(bf16[256,1024]{1,0:T(8,128)(2,1)S(1)} %get-tuple-element.60.refs_2_), channel_id=1, source_target_pairs={{0,1},{1,0},{2,3},{3,2},{16,17},{17,16},{18,19},{19,18},{4,5},{5,4... | collective-permute-start | bytes 1572872 | tf_op jit(solution)/shard_map/ppermute | solution.py:540
  51.6 14.3 %collective-permute-start.24 = (bf16[256,1024]{1,0:T(8,128)(2,1)S(1)}, bf16[256,1024]{1,0:T(8,128)(2,1)S(1)}, u32[]{:S(2)}, u32[]{:S(2)}) collective-permute-start(bf16[256,1024]{1,0:T(8,128)(2,1)S(1)} %get-tuple-element.60.refs_2_), channel_id=1, source_target_pairs={{0,16},{1,17},{2,18},{3,19},{16,0},{17,1},{18,2},{19,3},{4,20},{5,... | collective-permute-start | bytes 1572872 | tf_op jit(solution)/shard_map/ppermute | solution.py:540
  53.2 5.2 %collective-permute-start.16 = (bf16[64,1024]{1,0:T(8,128)(2,1)S(1)}, bf16[64,1024]{1,0:T(8,128)(2,1)S(1)}, u32[]{:S(2)}, u32[]{:S(2)}) collective-permute-start(bf16[64,1024]{1,0:T(8,128)(2,1)S(1)} %get-tuple-element.58.refs_3_), channel_id=1, source_target_pairs={{0,3},{1,0},{2,1},{3,2},{4,7},{5,4},{6,5},{7,6},{8,11},{9,8},{10,9... | collective-permute-start | bytes 393224 | tf_op jit(solution)/shard_map/ppermute | solution.py:76
  54.4 7.4 %collective-permute-start.15 = (bf16[64,1024]{1,0:T(8,128)(2,1)S(1)}, bf16[64,1024]{1,0:T(8,128)(2,1)S(1)}, u32[]{:S(2)}, u32[]{:S(2)}) collective-permute-start(bf16[64,1024]{1,0:T(8,128)(2,1)S(1)} %get-tuple-element.58.refs_3_), channel_id=1, source_target_pairs={{0,2},{1,3},{2,0},{3,1},{4,6},{5,7},{6,4},{7,5},{8,10},{9,11},{10,... | collective-permute-start | bytes 393224 | tf_op jit(solution)/shard_map/ppermute | solution.py:76
  55.0 6.9 %collective-permute-start.14 = (bf16[64,1024]{1,0:T(8,128)(2,1)S(1)}, bf16[64,1024]{1,0:T(8,128)(2,1)S(1)}, u32[]{:S(2)}, u32[]{:S(2)}) collective-permute-start(bf16[64,1024]{1,0:T(8,128)(2,1)S(1)} %get-tuple-element.58.refs_3_), channel_id=1, source_target_pairs={{0,1},{1,2},{2,3},{3,0},{4,5},{5,6},{6,7},{7,4},{8,9},{9,10},{10,1... | collective-permute-start | bytes 393224 | tf_op jit(solution)/shard_map/ppermute | solution.py:76
  58.3 15.6 %collective-permute-start.22 = (bf16[128,1024]{1,0:T(8,128)(2,1)S(1)}, bf16[128,1024]{1,0:T(8,128)(2,1)S(1)}, u32[]{:S(2)}, u32[]{:S(2)}) collective-permute-start(bf16[128,1024]{1,0:T(8,128)(2,1)S(1)} %get-tuple-element.67), channel_id=1, source_target_pairs={{0,8},{4,12},{8,0},{12,4},{1,9},{5,13},{9,1},{13,5},{2,10},{6,14},... | collective-permute-start | bytes 786440 | tf_op jit(solution)/shard_map/ppermute | solution.py:547
  61.9 20.5 %copy-start.6 = (bf16[256,1024]{1,0:T(8,128)(2,1)}, bf16[256,1024]{1,0:T(8,128)(2,1)S(1)}, u32[]{:S(2)}) copy-start(bf16[256,1024]{1,0:T(8,128)(2,1)S(1)} %collective-permute-done.17.refs_7_.refs_6_) | copy-start | bytes 1572868
  61.9 14.3 %copy-start.16 = (bf16[64,1024]{1,0:T(8,128)(2,1)S(1)}, bf16[64,1024]{1,0:T(8,128)(2,1)}, u32[]{:S(2)}) copy-start(bf16[64,1024]{1,0:T(8,128)(2,1)} %refs_0_.5) | copy-start | bytes 393220
  65.9 0.8 copy-start.11
  66.7 15.7 %collective-permute-start.25 = (bf16[256,1024]{1,0:T(8,128)(2,1)S(1)}, bf16[256,1024]{1,0:T(8,128)(2,1)S(1)}, u32[]{:S(2)}, u32[]{:S(2)}) collective-permute-start(bf16[256,1024]{1,0:T(8,128)(2,1)S(1)} %near_far.1), channel_id=1, source_target_pairs={{0,1},{1,0},{2,3},{3,2},{16,17},{17,16},{18,19},{19,18},{4,5},{5,4... | collective-permute-start | bytes 1572872 | tf_op jit(solution)/shard_map/ppermute | solution.py:540
  66.7 7.2 %collective-permute-start.18 = (bf16[64,1152]{1,0:T(8,128)(2,1)S(1)}, bf16[64,1152]{1,0:T(8,128)(2,1)S(1)}, u32[]{:S(2)}, u32[]{:S(2)}) collective-permute-start(bf16[64,1152]{1,0:T(8,128)(2,1)S(1)} %get-tuple-element.62), channel_id=1, source_target_pairs={{0,3},{1,0},{2,1},{3,2},{4,7},{5,4},{6,5},{7,6},{8,11},{9,8},{10,9... | collective-permute-start | bytes 442376 | tf_op jit(solution)/shard_map/ppermute | solution.py:76
  68.4 7.8 %collective-permute-start.19 = (bf16[64,1152]{1,0:T(8,128)(2,1)S(1)}, bf16[64,1152]{1,0:T(8,128)(2,1)S(1)}, u32[]{:S(2)}, u32[]{:S(2)}) collective-permute-start(bf16[64,1152]{1,0:T(8,128)(2,1)S(1)} %get-tuple-element.63), channel_id=1, source_target_pairs={{0,2},{1,3},{2,0},{3,1},{4,6},{5,7},{6,4},{7,5},{8,10},{9,11},{10,... | collective-permute-start | bytes 442376 | tf_op jit(solution)/shard_map/ppermute | solution.py:76
  68.9 7.3 %collective-permute-start.20 = (bf16[64,1152]{1,0:T(8,128)(2,1)S(1)}, bf16[64,1152]{1,0:T(8,128)(2,1)S(1)}, u32[]{:S(2)}, u32[]{:S(2)}) collective-permute-start(bf16[64,1152]{1,0:T(8,128)(2,1)S(1)} %get-tuple-element.64), channel_id=1, source_target_pairs={{0,1},{1,2},{2,3},{3,0},{4,5},{5,6},{6,7},{7,4},{8,9},{9,10},{10,1... | collective-permute-start | bytes 442376 | tf_op jit(solution)/shard_map/ppermute | solution.py:76
  74.0 8.4 %collective-permute-start.23 = (bf16[128,1024]{1,0:T(8,128)(2,1)S(1)}, bf16[128,1024]{1,0:T(8,128)(2,1)S(1)}, u32[]{:S(2)}, u32[]{:S(2)}) collective-permute-start(bf16[128,1024]{1,0:T(8,128)(2,1)S(1)} %other.1.refs_5_), channel_id=1, source_target_pairs={{0,16},{1,17},{2,18},{3,19},{16,0},{17,1},{18,2},{19,3},{4,20},{5,... | collective-permute-start | bytes 786440 | tf_op jit(solution)/shard_map/ppermute | solution.py:540
  76.6 5.0 %collective-permute-start.21 = (bf16[64,1024]{1,0:T(8,128)(2,1)S(1)}, bf16[64,1024]{1,0:T(8,128)(2,1)S(1)}, u32[]{:S(2)}, u32[]{:S(2)}) collective-permute-start(bf16[64,1024]{1,0:T(8,128)(2,1)S(1)} %get-tuple-element.66.refs_3_), channel_id=1, source_target_pairs={{0,4},{4,0},{8,12},{12,8},{1,5},{5,1},{9,13},{13,9},{2,6},{6,2},{1... | collective-permute-start | bytes 393224 | tf_op jit(solution)/shard_map/ppermute | solution.py:544
  82.4 2.2 %copy-start.9 = (bf16[256,1024]{1,0:T(8,128)(2,1)}, bf16[256,1024]{1,0:T(8,128)(2,1)S(1)}, u32[]{:S(2)}) copy-start(bf16[256,1024]{1,0:T(8,128)(2,1)S(1)} %collective-permute-done.25.refs_8_.refs_7_) | copy-start | bytes 1572868
  84.6 7.5 %collective-permute-start.26 = (bf16[64,2048]{1,0:T(8,128)(2,1)S(1)}, bf16[64,2048]{1,0:T(8,128)(2,1)S(1)}, u32[]{:S(2)}, u32[]{:S(2)}) collective-permute-start(bf16[64,2048]{1,0:T(8,128)(2,1)S(1)} %get-tuple-element.69), channel_id=1, source_target_pairs={{0,4},{4,0},{8,12},{12,8},{1,5},{5,1},{9,13},{13,9},{2,6},{6,2},{1... | collective-permute-start | bytes 786440 | tf_op jit(solution)/shard_map/ppermute | solution.py:544
  85.4 23.3 %collective-permute-start.27 = (bf16[256,1024]{1,0:T(8,128)(2,1)}, bf16[256,1024]{1,0:T(8,128)(2,1)S(1)}, u32[]{:S(2)}, u32[]{:S(2)}) collective-permute-start(bf16[256,1024]{1,0:T(8,128)(2,1)} %get-tuple-element.72.refs_4_), channel_id=1, source_target_pairs={{0,2},{1,3},{2,0},{3,1},{16,18},{17,19},{18,16},{19,17},{4,6},{5,7... | collective-permute-start | bytes 1572872 | tf_op jit(solution)/shard_map/ppermute | solution.py:540
  93.0 20.7 %all-to-all-start = ((bf16[32,64,128]{2,1,0:T(8,128)(2,1)}), bf16[32,64,128]{2,1,0:T(8,128)(2,1)}, u32[]{:S(2)}, u32[]{:S(2)}) async-start(bf16[32,64,128]{2,1,0:T(8,128)(2,1)} %copy-done.12), calls=%async_computation | async-start | bytes 1048576 | tf_op jit(solution)/shard_map/all_to_all | solution.py:658
  98.4 11.0 %collective-permute-start.28 = (bf16[256,1024]{1,0:T(8,128)(2,1)}, bf16[256,1024]{1,0:T(8,128)(2,1)}, u32[]{:S(2)}, u32[]{:S(2)}) collective-permute-start(bf16[256,1024]{1,0:T(8,128)(2,1)} %get-tuple-element.72.refs_4_), channel_id=1, source_target_pairs={{0,1},{1,0},{2,3},{3,2},{16,17},{17,16},{18,19},{19,18},{4,5},{5,4... | collective-permute-start | bytes 1572872 | tf_op jit(solution)/shard_map/ppermute | solution.py:540
  98.4 3.4 %copy-start.5 = (bf16[1024,4096]{1,0:T(8,128)(2,1)S(1)}, bf16[1024,4096]{1,0:T(8,128)(2,1)}, u32[]{:S(2)}) copy-start(bf16[1024,4096]{1,0:T(8,128)(2,1)} %get-tuple-element.50.normed_ref) | copy-start | bytes 25165828
  101.8 1.0 copy-start.14
  108.7 5.0 %copy-start.10 = (bf16[256,1024]{1,0:T(8,128)(2,1)}, bf16[256,1024]{1,0:T(8,128)(2,1)S(1)}, u32[]{:S(2)}) copy-start(bf16[256,1024]{1,0:T(8,128)(2,1)S(1)} %collective-permute-done.27.refs_0_.refs_5_) | copy-start | bytes 1572868
  108.8 2.2 %collective-permute-start.29 = (bf16[256,1024]{1,0:T(8,128)(2,1)S(1)}, bf16[256,1024]{1,0:T(8,128)(2,1)}, u32[]{:S(2)}, u32[]{:S(2)}) collective-permute-start(bf16[256,1024]{1,0:T(8,128)(2,1)S(1)} %late.1), channel_id=1, source_target_pairs={{0,1},{1,0},{2,3},{3,2},{16,17},{17,16},{18,19},{19,18},{4,5},{5,4... | collective-permute-start | bytes 1572872 | tf_op jit(solution)/shard_map/ppermute | solution.py:540
  118.3 22.3 %copy-start.3 = (bf16[1024,1024]{1,0:T(8,128)(2,1)S(1)}, bf16[1024,1024]{1,0:T(8,128)(2,1)}, u32[]{:S(2)}) copy-start(bf16[1024,1024]{1,0:T(8,128)(2,1)} %copy-done.2) | copy-start | bytes 6291460
  118.3 21.1 %collective-permute-start.39 = (bf16[1024,128]{1,0:T(8,128)(2,1)}, bf16[1024,128]{1,0:T(8,128)(2,1)S(1)}, u32[]{:S(2)}, u32[]{:S(2)}) collective-permute-start(bf16[1024,128]{1,0:T(8,128)(2,1)} %grad_columns.1.refs_1_.refs_0_), channel_id=1, source_target_pairs={{0,18},{1,19},{2,16},{3,17},{16,2},{17,3},{18,0},{19,1},{4,22},{5,... | collective-permute-start | bytes 786440 | tf_op jit(solution)/shard_map/ppermute | solution.py:540
  120.2 19.2 %collective-permute-start.38 = (bf16[1024,128]{1,0:T(8,128)(2,1)}, bf16[1024,128]{1,0:T(8,128)(2,1)S(1)}, u32[]{:S(2)}, u32[]{:S(2)}) collective-permute-start(bf16[1024,128]{1,0:T(8,128)(2,1)} %grad_columns.1.refs_1_.refs_0_), channel_id=1, source_target_pairs={{0,16},{1,17},{2,18},{3,19},{16,0},{17,1},{18,2},{19,3},{4,20},{5,... | collective-permute-start | bytes 786440 | tf_op jit(solution)/shard_map/ppermute | solution.py:540
  120.8 18.6 %collective-permute-start.37 = (bf16[1024,128]{1,0:T(8,128)(2,1)}, bf16[1024,128]{1,0:T(8,128)(2,1)S(1)}, u32[]{:S(2)}, u32[]{:S(2)}) collective-permute-start(bf16[1024,128]{1,0:T(8,128)(2,1)} %grad_columns.1.refs_1_.refs_0_), channel_id=1, source_target_pairs={{0,2},{1,3},{2,0},{3,1},{16,18},{17,19},{18,16},{19,17},{4,6},{5,7... | collective-permute-start | bytes 786440 | tf_op jit(solution)/shard_map/ppermute | solution.py:540
  121.9 1.0 copy-start.7
  122.8 4.6 %collective-permute-start.30 = (f32[24,128]{1,0:T(8,128)S(1)}, f32[24,128]{1,0:T(8,128)S(1)}, u32[]{:S(2)}, u32[]{:S(2)}) collective-permute-start(f32[24,128]{1,0:T(8,128)S(1)} %slope_out.2.refs_0_), channel_id=1, source_target_pairs={{0,8},{4,12},{8,0},{12,4},{1,9},{5,13},{9,1},{13,5},{2,10},{6,14},... | collective-permute-start | bytes 36872 | tf_op jit(solution)/shard_map/ppermute | solution.py:686
  123.2 5.5 %collective-permute-start.32 = (f32[24,128]{1,0:T(8,128)S(1)}, f32[24,128]{1,0:T(8,128)S(1)}, u32[]{:S(2)}, u32[]{:S(2)}) collective-permute-start(f32[24,128]{1,0:T(8,128)S(1)} %slope_out.3), channel_id=1, source_target_pairs={{0,12},{4,8},{8,4},{12,0},{1,13},{5,9},{9,5},{13,1},{2,14},{6,10},... | collective-permute-start | bytes 36872 | tf_op jit(solution)/shard_map/ppermute | solution.py:686
  127.4 3.7 %collective-permute-start.31 = (f32[24,128]{1,0:T(8,128)S(1)}, f32[24,128]{1,0:T(8,128)S(1)}, u32[]{:S(2)}, u32[]{:S(2)}) collective-permute-start(f32[24,128]{1,0:T(8,128)S(1)} %slope_out.3), channel_id=1, source_target_pairs={{0,4},{4,0},{8,12},{12,8},{1,5},{5,1},{9,13},{13,9},{2,6},{6,2},{1... | collective-permute-start | bytes 36872 | tf_op jit(solution)/shard_map/ppermute | solution.py:686
  131.1 3.7 %collective-permute-start.33 = (f32[24,128]{1,0:T(8,128)S(1)}, f32[24,128]{1,0:T(8,128)S(1)}, u32[]{:S(2)}, u32[]{:S(2)}) collective-permute-start(f32[24,128]{1,0:T(8,128)S(1)} %sum_line.1.refs_0_), channel_id=1, source_target_pairs={{0,16},{16,0},{1,17},{17,1},{2,18},{18,2},{3,19},{19,3},{4,20},{20... | collective-permute-start | bytes 36872 | tf_op jit(solution)/shard_map/ppermute | solution.py:76
  134.8 1.4 collective-permute-start.36
  134.8 3.7 %collective-permute-start.35 = (f32[24,128]{1,0:T(8,128)S(1)}, f32[24,128]{1,0:T(8,128)S(1)}, u32[]{:S(2)}, u32[]{:S(2)}) collective-permute-start(f32[24,128]{1,0:T(8,128)S(1)} %sum_groups.1.refs_0_), channel_id=1, source_target_pairs={{0,2},{1,3},{2,0},{3,1},{4,6},{5,7},{6,4},{7,5},{8,10},{9,11},{10,... | collective-permute-start | bytes 36872 | tf_op jit(solution)/shard_map/ppermute | solution.py:76
  136.3 3.1 %collective-permute-start.34 = (f32[24,128]{1,0:T(8,128)S(1)}, f32[24,128]{1,0:T(8,128)S(1)}, u32[]{:S(2)}, u32[]{:S(2)}) collective-permute-start(f32[24,128]{1,0:T(8,128)S(1)} %sum_groups.1.refs_0_), channel_id=1, source_target_pairs={{0,1},{1,2},{2,3},{3,0},{4,5},{5,6},{6,7},{7,4},{8,9},{9,10},{10,1... | collective-permute-start | bytes 36872 | tf_op jit(solution)/shard_map/ppermute | solution.py:76
  139.4 1.0 copy-start.8
  140.5 2.7 %copy-start.18 = (f32[1024]{0:T(1024)S(1)}, f32[1024]{0:T(1024)}, u32[]{:S(2)}) copy-start(f32[1024]{0:T(1024)} %param.14) | copy-start | bytes 12292
  140.5 2.7 %collective-permute-start.40 = (bf16[4096,128]{1,0:T(8,128)(2,1)S(1)}, bf16[4096,128]{1,0:T(8,128)(2,1)S(1)}, u32[]{:S(2)}, u32[]{:S(2)}) collective-permute-start(bf16[4096,128]{1,0:T(8,128)(2,1)S(1)} %pack_columns.1.refs_3_), channel_id=1, source_target_pairs={{0,1},{1,0},{2,3},{3,2},{16,17},{17,16},{18,19},{19,18},{4,5},{5,4... | collective-permute-start | bytes 3145736 | tf_op jit(solution)/shard_map/ppermute | solution.py:540
  141.9 4.2 %collective-permute-start.41 = (f32[1,1024]{1,0:T(1,128)S(1)}, f32[1,1024]{1,0:T(1,128)S(1)}, u32[]{:S(2)}, u32[]{:S(2)}) collective-permute-start(f32[1,1024]{1,0:T(1,128)S(1)} %get-tuple-element.76.refs_0_), channel_id=1, source_target_pairs={{0,4},{4,0},{8,12},{12,8},{1,5},{5,1},{9,13},{13,9},{2,6},{6,2},{1... | collective-permute-start | bytes 12296 | tf_op jit(solution)/shard_map/ppermute | solution.py:544
  (2 other events, 1.5 us)

commit v7 on v6

--- a/solution.py
+++ b/solution.py
@@ -662,6 +662,7 @@
     def total(parts, name):
         return call(add_kernel, [shape(parts[0].shape, F32)], parts, name)[0]
 
+    slope = total([slopes[0]] + [half_shift(slopes[k], k) for k in range(1, half)], "sum_half")
     across = [plane_shift(others, 0, dh, 0) for dh in range(1, n_h)]
     late = [pack([array], "late", slopes[0]) for array in across]
     spread = []
@@ -674,17 +675,11 @@
     block_columns = call(
         functools.partial(columns_kernel, len(spread)), [shape((depth, cols), BF16)],
         [ranks, all_columns] + spread, "grad_columns",
-        flops=2 * n_all * queries * depth * cols, scratch=[pltpu.VMEM((n_all * queries, cols), BF16)], smem=1, copy=True,
+        flops=2 * n_all * queries * depth * cols, scratch=[pltpu.VMEM((n_all * queries, cols), BF16)], smem=1, copy=True, after=[slope],
     )[0]
     on_chips = [block_columns if dg == dh == 0 else plane_shift(block_columns, dg, dh, 0) for dg, dh in chips]
-    slopes = [passed(array, "slope_out", block_columns) for array in slopes]
-    stage = [slopes[0]]
-    for k in range(half):
-        for flip in (0, 1):
-            if k or flip:
-                pairs = [(a, (a // half + flip) % 2 * half + (a % half + k) % half) for a in range(n_z)]
-                stage.append(lax.ppermute(slopes[k], "fsdp", pairs))
-    slope = total(stage, "sum_line")
+    slope = passed(slope, "slope_out", block_columns)
+    slope = total([slope, mirror_shift(slope)], "sum_mirror")
     if n_g > 1:
         slope = total([slope] + [shift(slope, "grp", k) for k in range(1, n_g)], "sum_groups")
     if n_i > 1:

time: 148 us -> 147 us (level)
  starting transfers between devices: 48.5 us -> 46.6 us
    ppermute x3 -> x0, starting transfers between devices: 4.89 us -> none  [body(): stage.append(lax.ppermute(slopes[k], 'fsdp', pairs))]
    ppermute x3 -> x0, waiting for transfers between devices: 3.39 us -> none  [body(): stage.append(lax.ppermute(slopes[k], 'fsdp', pairs))]
    ppermute x16, waiting for transfers between devices: 11.9 us -> 14.7 us  [shift(): return lax.ppermute(values, axis, [(i, (i + k) % n) for i in range(n)])]
    all_to_all x1, waiting for transfers between devices: 2.67 us -> 0.01 us  [body(): lax.all_to_all(passed(grad_columns, 'columns_out', backs[-1]), EVERY, 0,...]
    ppermute x2 -> x3, starting transfers between devices: 7.26 us -> 9.55 us  [mirror_shift(): lax.ppermute(values, 'fsdp', [(a, (a + half) % n_z) for a in range(n_z)])]
    ppermute x5 -> x6, waiting for transfers between devices: 15.1 us -> 17.4 us  [half_shift(): return lax.ppermute(values, 'fsdp', pairs)]
    ppermute x2 -> x3, waiting for transfers between devices: 9.3 us -> 11.6 us  [mirror_shift(): lax.ppermute(values, 'fsdp', [(a, (a + half) % n_z) for a in range(n_z)])]
    ppermute x5 -> x6, starting transfers between devices: 4.86 us -> 6.1 us  [half_shift(): return lax.ppermute(values, 'fsdp', pairs)]
  transfers between devices with their start and end apart: 43 -> 42, of which waited for: 23 -> 22; matrix products, arithmetic and copies ran while one was open for 1% -> 1% of each run, Pallas kernels for 18% -> 18%
where the time goes in v7:
time: 147 us; the launch traced here: 146 us
  waiting for transfers between devices  48.6 us (33%)
  starting transfers between devices  46.6 us (32%)
  Pallas kernels  36.2 us (25%)
  local copies, waits for them, and re-layouts  12.6 us (9%)
  between operations  2.32 us (2%)
    pallas_call x21, Pallas kernels, call(): pl.pallas_call(run, out_shape=outs, in_specs=[SMEM] * smem + [pl.BlockSpe...  18.6 us
    ppermute x6, waiting for transfers between devices, half_shift(): return lax.ppermute(values, 'fsdp', pairs)  17.4 us
    ppermute x16, waiting for transfers between devices, shift(): return lax.ppermute(values, axis, [(i, (i + k) % n) for i in range(n)])  14.7 us
    ppermute x16, starting transfers between devices, plane_shift(): return lax.ppermute(values, PLANE, pairs)  12.9 us
    ppermute x16, starting transfers between devices, shift(): return lax.ppermute(values, axis, [(i, (i + k) % n) for i in range(n)])  12.7 us
    pallas_call x1, Pallas kernels, gate_rows(): pl.pallas_call(run, grid=(queries // group,), out_shape=outs, in_specs=[S...  11.6 us
    ppermute x3, waiting for transfers between devices, mirror_shift(): lax.ppermute(values, 'fsdp', [(a, (a + half) % n_z) for a in range(n_z)])  11.6 us
    unnamed x51, local copies, waits for them, and re-layouts  11 us
  transfers between devices with their start and end apart: 42, of which 22 were waited for; matrix products, arithmetic and copies ran while one was open for 1% of the time, Pallas kernels for 18%

profile of v7, /device:TPU:0, one launch (start us, length us, event | category | flops | bytes accessed | tf_op | source)
XLA Modules:
  0.0 146.5 jit_solution(15041306262351857702)
XLA Ops:
  0.7 1.0 constant_dynamic-slice_fusion.refs_2_
  1.6 4.1 %collective-permute-start.3 = (bf16[128,1024]{1,0:T(8,128)(2,1)S(1)}, bf16[128,1024]{1,0:T(8,128)(2,1)S(1)}, u32[]{:S(2)}, u32[]{:S(2)}) collective-permute-start(bf16[128,1024]{1,0:T(8,128)(2,1)S(1)} %constant_dynamic-slice_fusion.refs_2_), channel_id=1, source_target_pairs={{0,8},{4,12},{8,0},{12,4},{1,9},{5,13},{9,1},{13,5},{2,10},{6,14},... | collective-permute-start | bytes 786440 | tf_op jit(solution)/shard_map/ppermute | solution.py:547
  5.8 1.6 %copy-done = bf16[1024,1024]{1,0:T(8,128)(2,1)S(1)} copy-done((bf16[1024,1024]{1,0:T(8,128)(2,1)S(1)}, bf16[1024,1024]{1,0:T(8,128)(2,1)}, u32[]{:S(2)}) %copy-start) | copy-done | bytes 2097176
  7.3 0.7 copy-done.19
  8.0 1.7 %block_u.1 = f32[1,1024]{1,0:T(1,128)S(1)} custom-call(bf16[1024,1024]{1,0:T(8,128)(2,1)S(1)} %copy-done, f32[1,1024]{1,0:T(1,128)S(1)} %bitcast.51, bf16[128,1024]{1,0:T(8,128)(2,1)S(1)} %constant_dynamic-slice_fusion.refs_2_), custom_call_target="tpu_custom_call" | custom-call | bytes 2105344 | tf_op jit(solution)/shard_map/block_u/pallas_call | solution.py:58
  9.8 1.4 collective-permute-start.2
  11.1 1.7 %collective-permute-start.1 = (f32[1,1024]{1,0:T(1,128)S(1)}, f32[1,1024]{1,0:T(1,128)S(1)}, u32[]{:S(2)}, u32[]{:S(2)}) collective-permute-start(f32[1,1024]{1,0:T(1,128)S(1)} %block_u.1), channel_id=1, source_target_pairs={{0,8},{4,12},{8,0},{12,4},{1,9},{5,13},{9,1},{13,5},{2,10},{6,14},... | collective-permute-start | bytes 12296 | tf_op jit(solution)/shard_map/ppermute | solution.py:76
  13.7 4.2 %collective-permute-done.3.refs_6_.refs_0_ = bf16[128,1024]{1,0:T(8,128)(2,1)S(1)} collective-permute-done((bf16[128,1024]{1,0:T(8,128)(2,1)S(1)}, bf16[128,1024]{1,0:T(8,128)(2,1)S(1)}, u32[]{:S(2)}, u32[]{:S(2)}) %collective-permute-start.3) | collective-permute-done | bytes 262176 | tf_op jit(solution)/shard_map/ppermute | solution.py:547
  17.9 2.5 %collective-permute-start.7 = (bf16[128,1024]{1,0:T(8,128)(2,1)S(1)}, bf16[128,1024]{1,0:T(8,128)(2,1)S(1)}, u32[]{:S(2)}, u32[]{:S(2)}) collective-permute-start(bf16[128,1024]{1,0:T(8,128)(2,1)S(1)} %collective-permute-done.3.refs_6_.refs_0_), channel_id=1, source_target_pairs={{0,18},{1,19},{2,16},{3,17},{16,2},{17,3},{18,0},{19,1},{4,22},{5,... | collective-permute-start | bytes 786440 | tf_op jit(solution)/shard_map/ppermute | solution.py:540
  21.4 11.6 %gate_rows.1 = (bf16[64,2048]{1,0:T(8,128)(2,1)S(1)}, bf16[64,2048]{1,0:T(8,128)(2,1)S(1)}, bf16[1024,4096]{1,0:T(8,128)(2,1)}, f32[1024,1]{1,0:T(8,128)S(1)}, f...) custom-call(s32[2]{0:T(128)S(1)} %pad_add_fusion.refs_0_.z_ref, ...), custom_call_target="tpu_custom_call" | custom-call | flops 41943040 | bytes 16777216 | tf_op jit(solution)/shard_map/gate_rows/pallas_call | solution.py:176
  33.2 0.8 collective-permute-start.4
  34.2 1.5 %collective-permute-start.10 = (s32[64,8]{1,0:T(8,128)S(1)}, s32[64,8]{1,0:T(8,128)S(1)}, u32[]{:S(2)}, u32[]{:S(2)}) collective-permute-start(s32[64,8]{1,0:T(8,128)S(1)} %get-tuple-element.46), channel_id=1, source_target_pairs={{0,2},{1,3},{2,0},{3,1},{4,6},{5,7},{6,4},{7,5},{8,10},{9,11},{10,... | collective-permute-start | bytes 6152 | tf_op jit(solution)/shard_map/ppermute | solution.py:76
  35.8 1.3 collective-permute-start.11
  37.4 0.7 collective-permute-done.10.refs_4_
  38.7 1.8 %list_counts.1 = (f32[256,1024]{1,0:T(8,128)S(1)}, f32[1,1024]{1,0:T(1,128)S(1)}) custom-call(s32[1]{0:T(128)} %bitcast.46.refs_9_.refs_0_, bf16[1024,1024]{1,0:T(8,128)(2,1)S(1)} %copy-done.4, s32[64,8]{1,0:T(8,128)S(1)} %get-tuple-element.44.refs_2_, s32[64,8]{1,0:T(8,128)S(1)} %collective-permute-done.9.refs_3_, ...), custom_call_target="tpu_custom_call" | custom-call | bytes 3158020 | tf_op jit(solution)/shard_map/list_counts/pallas_call | solution.py:58
  40.5 1.5 collective-permute-done.4.refs_4_
  42.0 1.4 forward.1
  43.4 1.6 %collective-permute-start.13 = (bf16[128,1024]{1,0:T(8,128)(2,1)S(1)}, bf16[128,1024]{1,0:T(8,128)(2,1)S(1)}, u32[]{:S(2)}, u32[]{:S(2)}) collective-permute-start(bf16[128,1024]{1,0:T(8,128)(2,1)S(1)} %get-tuple-element.55.refs_3_), channel_id=1, source_target_pairs={{0,2},{1,3},{2,0},{3,1},{16,18},{17,19},{18,16},{19,17},{4,6},{5,7... | collective-permute-start | bytes 786440 | tf_op jit(solution)/shard_map/ppermute | solution.py:540
  45.0 0.7 collective-permute-start.12
  45.8 4.2 %collective-permute-done.12.refs_1_ = bf16[64,1024]{1,0:T(8,128)(2,1)S(1)} collective-permute-done((bf16[64,1024]{1,0:T(8,128)(2,1)S(1)}, bf16[64,1024]{1,0:T(8,128)(2,1)S(1)}, u32[]{:S(2)}, u32[]{:S(2)}) %collective-permute-start.12) | collective-permute-done | bytes 131104 | tf_op jit(solution)/shard_map/ppermute | solution.py:544
  50.0 1.3 collective-permute-done.13.refs_4_
  51.6 1.6 %collective-permute-start.24 = (bf16[256,1024]{1,0:T(8,128)(2,1)S(1)}, bf16[256,1024]{1,0:T(8,128)(2,1)S(1)}, u32[]{:S(2)}, u32[]{:S(2)}) collective-permute-start(bf16[256,1024]{1,0:T(8,128)(2,1)S(1)} %get-tuple-element.60.refs_2_), channel_id=1, source_target_pairs={{0,16},{1,17},{2,18},{3,19},{16,0},{17,1},{18,2},{19,3},{4,20},{5,... | collective-permute-start | bytes 1572872 | tf_op jit(solution)/shard_map/ppermute | solution.py:540
  53.2 1.3 collective-permute-start.16
  55.0 3.4 %collective-permute-done.16.refs_6_ = bf16[64,1024]{1,0:T(8,128)(2,1)S(1)} collective-permute-done((bf16[64,1024]{1,0:T(8,128)(2,1)S(1)}, bf16[64,1024]{1,0:T(8,128)(2,1)S(1)}, u32[]{:S(2)}, u32[]{:S(2)}) %collective-permute-start.16) | collective-permute-done | bytes 131104 | tf_op jit(solution)/shard_map/ppermute | solution.py:76
  58.4 3.1 %collective-permute-start.22 = (bf16[128,1024]{1,0:T(8,128)(2,1)S(1)}, bf16[128,1024]{1,0:T(8,128)(2,1)S(1)}, u32[]{:S(2)}, u32[]{:S(2)}) collective-permute-start(bf16[128,1024]{1,0:T(8,128)(2,1)S(1)} %get-tuple-element.67), channel_id=1, source_target_pairs={{0,8},{4,12},{8,0},{12,4},{1,9},{5,13},{9,1},{13,5},{2,10},{6,14},... | collective-permute-start | bytes 786440 | tf_op jit(solution)/shard_map/ppermute | solution.py:547
  61.9 1.4 contrast.1
  63.3 2.6 %collective-permute-done.24.refs_0_.refs_3_ = bf16[256,1024]{1,0:T(8,128)(2,1)S(1)} collective-permute-done((bf16[256,1024]{1,0:T(8,128)(2,1)S(1)}, bf16[256,1024]{1,0:T(8,128)(2,1)S(1)}, u32[]{:S(2)}, u32[]{:S(2)}) %collective-permute-start.24) | collective-permute-done | bytes 524320 | tf_op jit(solution)/shard_map/ppermute | solution.py:540
  66.0 0.8 copy-done.11
  66.8 1.7 %collective-permute-start.18 = (bf16[64,1152]{1,0:T(8,128)(2,1)S(1)}, bf16[64,1152]{1,0:T(8,128)(2,1)S(1)}, u32[]{:S(2)}, u32[]{:S(2)}) collective-permute-start(bf16[64,1152]{1,0:T(8,128)(2,1)S(1)} %get-tuple-element.62), channel_id=1, source_target_pairs={{0,3},{1,0},{2,1},{3,2},{4,7},{5,4},{6,5},{7,6},{8,11},{9,8},{10,9... | collective-permute-start | bytes 442376 | tf_op jit(solution)/shard_map/ppermute | solution.py:76
  68.9 5.1 %collective-permute-done.22.refs_0_ = bf16[128,1024]{1,0:T(8,128)(2,1)S(1)} collective-permute-done((bf16[128,1024]{1,0:T(8,128)(2,1)S(1)}, bf16[128,1024]{1,0:T(8,128)(2,1)S(1)}, u32[]{:S(2)}, u32[]{:S(2)}) %collective-permute-start.22) | collective-permute-done | bytes 262176 | tf_op jit(solution)/shard_map/ppermute | solution.py:547
  74.0 0.6 collective-permute-start.23
  74.6 1.6 %collective-permute-done.19.refs_6_ = bf16[64,1152]{1,0:T(8,128)(2,1)S(1)} collective-permute-done((bf16[64,1152]{1,0:T(8,128)(2,1)S(1)}, bf16[64,1152]{1,0:T(8,128)(2,1)S(1)}, u32[]{:S(2)}, u32[]{:S(2)}) %collective-permute-start.19) | collective-permute-done | bytes 147488 | tf_op jit(solution)/shard_map/ppermute | solution.py:76
  76.7 1.2 collective-permute-start.21
  77.8 3.9 %collective-permute-done.21.refs_4_ = bf16[64,1024]{1,0:T(8,128)(2,1)S(1)} collective-permute-done((bf16[64,1024]{1,0:T(8,128)(2,1)S(1)}, bf16[64,1024]{1,0:T(8,128)(2,1)S(1)}, u32[]{:S(2)}, u32[]{:S(2)}) %collective-permute-start.21) | collective-permute-done | bytes 131104 | tf_op jit(solution)/shard_map/ppermute | solution.py:544
  81.7 0.7 collective-permute-done.23.refs_6_
  82.4 2.2 %backward.1 = (bf16[64,2048]{1,0:T(8,128)(2,1)S(1)}, bf16[64,2048]{1,0:T(8,128)(2,1)S(1)}, bf16[256,1024]{1,0:T(8,128)(2,1)}) custom-call(s32[1]{0:T(128)} %bitcast.9.refs_10_.refs_0_, bf16[1024,1024]{1,0:T(8,128)(2,1)S(1)} %copy-done.1, bf16[1024,1024]{1,0:T(8,128)(2,1)S(1)} %get-tuple-element.49.refs_2_, bf16[64,1024]{1,0:T(8,128)(2,1)S(1)} %get-tuple-element.66.refs_3_, ...), custom_call_target="tpu_custom_call" | custom-call | flops 536870912 | bytes 6029316 | tf_op jit(solution)/shard_map/backward/pallas_call | solution.py:58
  84.6 0.8 collective-permute-start.26
  85.4 1.1 collective-permute-start.28
  86.6 5.5 %collective-permute-done.26.rest_1_.refs_1_ = bf16[64,2048]{1,0:T(8,128)(2,1)S(1)} collective-permute-done((bf16[64,2048]{1,0:T(8,128)(2,1)S(1)}, bf16[64,2048]{1,0:T(8,128)(2,1)S(1)}, u32[]{:S(2)}, u32[]{:S(2)}) %collective-permute-start.26) | collective-permute-done | bytes 262176 | tf_op jit(solution)/shard_map/ppermute | solution.py:544
  92.2 0.8 copy-done.12
  93.0 5.4 %all-to-all-start = ((bf16[32,64,128]{2,1,0:T(8,128)(2,1)}), bf16[32,64,128]{2,1,0:T(8,128)(2,1)}, u32[]{:S(2)}, u32[]{:S(2)}) async-start(bf16[32,64,128]{2,1,0:T(8,128)(2,1)} %copy-done.12), calls=%async_computation | async-start | bytes 1048576 | tf_op jit(solution)/shard_map/all_to_all | solution.py:658
  98.5 3.4 %copy-done.5 = bf16[1024,4096]{1,0:T(8,128)(2,1)S(1)} copy-done((bf16[1024,4096]{1,0:T(8,128)(2,1)S(1)}, bf16[1024,4096]{1,0:T(8,128)(2,1)}, u32[]{:S(2)}) %copy-start.5) | copy-done | bytes 8388632
  101.8 1.0 copy-done.14
  102.9 5.9 %slope_rows.1 = (f32[24,128]{1,0:T(8,128)S(1)}, f32[24,128]{1,0:T(8,128)S(1)}) custom-call(s32[2]{0:T(128)S(1)} %pad_add_fusion.refs_0_.z_ref, bf16[1024,4096]{1,0:T(8,128)(2,1)S(1)} %copy-done.5, f32[1024,1]{1,0:T(8,128)S(1)} %copy-done.14, f32[1,128]{1,0:T(1,128)S(1)} %get-tuple-element.65.loss_ref, bf16[64,2048]{1,0:T(8,128)(2,1)S(1)} %get-tuple-element.68.rest_0_, ...), custom_call_target="tpu_custom_call" | custom-call | flops 16777216 | bytes 8388608 | tf_op jit(solution)/shard_map/slope_rows/pallas_call | solution.py:433
  109.4 1.5 %collective-permute-start.27 = (f32[24,128]{1,0:T(8,128)S(1)}, f32[24,128]{1,0:T(8,128)S(1)}, u32[]{:S(2)}, u32[]{:S(2)}) collective-permute-start(f32[24,128]{1,0:T(8,128)S(1)} %get-tuple-element.71), channel_id=1, source_target_pairs={{0,4},{4,0},{8,12},{12,8},{1,5},{5,1},{9,13},{13,9},{2,6},{6,2},{1... | collective-permute-start | bytes 36872 | tf_op jit(solution)/shard_map/ppermute | solution.py:544
  110.9 2.3 %collective-permute-done.27.refs_1_ = f32[24,128]{1,0:T(8,128)S(1)} collective-permute-done((f32[24,128]{1,0:T(8,128)S(1)}, f32[24,128]{1,0:T(8,128)S(1)}, u32[]{:S(2)}, u32[]{:S(2)}) %collective-permute-start.27) | collective-permute-done | bytes 12320 | tf_op jit(solution)/shard_map/ppermute | solution.py:544
  113.2 0.6 copy-done.17
  113.8 4.6 %grad_columns.1.refs_1_.refs_0_ = bf16[1024,128]{1,0:T(8,128)(2,1)} custom-call(s32[32]{0:T(128)} %copy-done.21, bf16[32,64,128]{2,1,0:T(8,128)(2,1)} %all-to-all-done.refs_1_, bf16[256,1024]{1,0:T(8,128)(2,1)} %copy-done.15, bf16[256,1024]{1,0:T(8,128)(2,1)} %copy-done.11, bf16[256,1024]{1,0:T(8,128)(2,1)} %get-tuple-element.73.refs_4_, ...), custom_call_target="tpu_custom_call" | custom-call | flops 536870912 | bytes 4980864 | tf_op jit(solution)/shard_map/grad_columns/pallas_call | solution.py:58
  118.5 2.5 %collective-permute-start.38 = (bf16[1024,128]{1,0:T(8,128)(2,1)}, bf16[1024,128]{1,0:T(8,128)(2,1)S(1)}, u32[]{:S(2)}, u32[]{:S(2)}) collective-permute-start(bf16[1024,128]{1,0:T(8,128)(2,1)} %grad_columns.1.refs_1_.refs_0_), channel_id=1, source_target_pairs={{0,18},{1,19},{2,16},{3,17},{16,2},{17,3},{18,0},{19,1},{4,22},{5,... | collective-permute-start | bytes 786440 | tf_op jit(solution)/shard_map/ppermute | solution.py:540
  122.0 1.0 copy-done.7
  123.0 2.3 %collective-permute-start.31 = (f32[24,128]{1,0:T(8,128)S(1)}, f32[24,128]{1,0:T(8,128)S(1)}, u32[]{:S(2)}, u32[]{:S(2)}) collective-permute-start(f32[24,128]{1,0:T(8,128)S(1)} %slope_out.1.refs_0_), channel_id=1, source_target_pairs={{0,8},{4,12},{8,0},{12,4},{1,9},{5,13},{9,1},{13,5},{2,10},{6,14},... | collective-permute-start | bytes 36872 | tf_op jit(solution)/shard_map/ppermute | solution.py:547
  125.3 2.3 %collective-permute-done.31.refs_1_ = f32[24,128]{1,0:T(8,128)S(1)} collective-permute-done((f32[24,128]{1,0:T(8,128)S(1)}, f32[24,128]{1,0:T(8,128)S(1)}, u32[]{:S(2)}, u32[]{:S(2)}) %collective-permute-start.31) | collective-permute-done | bytes 12320 | tf_op jit(solution)/shard_map/ppermute | solution.py:547
  127.6 1.5 collective-permute-start.32
  129.1 4.4 %collective-permute-done.32.refs_1_ = f32[24,128]{1,0:T(8,128)S(1)} collective-permute-done((f32[24,128]{1,0:T(8,128)S(1)}, f32[24,128]{1,0:T(8,128)S(1)}, u32[]{:S(2)}, u32[]{:S(2)}) %collective-permute-start.32) | collective-permute-done | bytes 12320 | tf_op jit(solution)/shard_map/ppermute | solution.py:76
  133.5 0.6 collective-permute-start.34
  134.1 0.8 collective-permute-done.35.refs_3_
  134.9 0.7 collective-permute-start.33
  135.6 1.6 %collective-permute-done.34.refs_2_ = f32[24,128]{1,0:T(8,128)S(1)} collective-permute-done((f32[24,128]{1,0:T(8,128)S(1)}, f32[24,128]{1,0:T(8,128)S(1)}, u32[]{:S(2)}, u32[]{:S(2)}) %collective-permute-start.34) | collective-permute-done | bytes 12320 | tf_op jit(solution)/shard_map/ppermute | solution.py:76
  137.2 0.8 collective-permute-done.33.refs_1_
  138.1 0.9 copy-done.8
  139.2 1.3 slope_sum.1
  140.5 1.0 collective-permute-start.40
  141.9 2.8 %finish.1 = (f32[1024,1024]{1,0:T(8,128)}, f32[8,128]{1,0:T(8,128)S(1)}) custom-call(s32[8]{0:T(128)S(1)} %stack.149.refs_7_.refs_1_.refs_0_, f32[1,1024]{1,0:T(1,128)S(1)} %bitcast.52, f32[8,128]{1,0:T(8,128)S(1)} %get-tuple-element.74.refs_2_, bf16[4096,128]{1,0:T(8,128)(2,1)S(1)} %pack_columns.1.refs_3_, bf16[4096,128]{1,0:T(8,128)(2,1)S(1)} %collective-permute-done.39.refs_4_), custom_call_target="tpu_custom_call" | custom-call | bytes 6303776 | tf_op jit(solution)/shard_map/finish/pallas_call | solution.py:58
  144.7 0.6 query_sum.1
  (107 shorter events, 7.5 us)
Async XLA Ops:
  0.6 12.3 %copy-start.23 = (bf16[4096]{0:T(1024)(128)(2,1)S(1)}, bf16[4096]{0:T(1024)(128)(2,1)}, u32[]{:S(2)}) copy-start(bf16[4096]{0:T(1024)(128)(2,1)} %param.12) | copy-start | bytes 24580
  0.6 12.3 %copy-start.22 = (s32[64,32]{0,1:T(8,128)S(1)}, s32[64,32]{0,1:T(8,128)}, u32[]{:S(2)}) copy-start(s32[64,32]{0,1:T(8,128)} %param.10) | copy-start | bytes 24580
  0.7 12.4 %copy-start.24 = (s32[64]{0:T(128)S(1)}, s32[64]{0:T(128)}, u32[]{:S(2)}) copy-start(s32[64]{0:T(128)} %param.11) | copy-start | bytes 772
  1.6 16.2 %collective-permute-start.3 = (bf16[128,1024]{1,0:T(8,128)(2,1)S(1)}, bf16[128,1024]{1,0:T(8,128)(2,1)S(1)}, u32[]{:S(2)}, u32[]{:S(2)}) collective-permute-start(bf16[128,1024]{1,0:T(8,128)(2,1)S(1)} %constant_dynamic-slice_fusion.refs_2_), channel_id=1, source_target_pairs={{0,8},{4,12},{8,0},{12,4},{1,9},{5,13},{9,1},{13,5},{2,10},{6,14},... | collective-permute-start | bytes 786440 | tf_op jit(solution)/shard_map/ppermute | solution.py:547
  5.8 1.6 %copy-start = (bf16[1024,1024]{1,0:T(8,128)(2,1)S(1)}, bf16[1024,1024]{1,0:T(8,128)(2,1)}, u32[]{:S(2)}) copy-start(bf16[1024,1024]{1,0:T(8,128)(2,1)} %refs_1_.5) | copy-start | bytes 6291460
  9.8 11.7 %collective-permute-start.2 = (f32[1,1024]{1,0:T(1,128)S(1)}, f32[1,1024]{1,0:T(1,128)S(1)}, u32[]{:S(2)}, u32[]{:S(2)}) collective-permute-start(f32[1,1024]{1,0:T(1,128)S(1)} %block_u.1), channel_id=1, source_target_pairs={{0,12},{4,0},{8,4},{12,8},{1,13},{5,1},{9,5},{13,9},{2,14},{6,2},{... | collective-permute-start | bytes 12296 | tf_op jit(solution)/shard_map/ppermute | solution.py:76
  11.1 10.3 %collective-permute-start.1 = (f32[1,1024]{1,0:T(1,128)S(1)}, f32[1,1024]{1,0:T(1,128)S(1)}, u32[]{:S(2)}, u32[]{:S(2)}) collective-permute-start(f32[1,1024]{1,0:T(1,128)S(1)} %block_u.1), channel_id=1, source_target_pairs={{0,8},{4,12},{8,0},{12,4},{1,9},{5,13},{9,1},{13,5},{2,10},{6,14},... | collective-permute-start | bytes 12296 | tf_op jit(solution)/shard_map/ppermute | solution.py:76
  12.8 8.1 %collective-permute-start = (f32[1,1024]{1,0:T(1,128)S(1)}, f32[1,1024]{1,0:T(1,128)S(1)}, u32[]{:S(2)}, u32[]{:S(2)}) collective-permute-start(f32[1,1024]{1,0:T(1,128)S(1)} %block_u.1), channel_id=1, source_target_pairs={{0,4},{4,8},{8,12},{12,0},{1,5},{5,9},{9,13},{13,1},{2,6},{6,10},{... | collective-permute-start | bytes 12296 | tf_op jit(solution)/shard_map/ppermute | solution.py:76
  13.7 19.4 %copy-start.21 = (s32[32]{0:T(128)}, s32[32]{0:T(128)S(1)}, u32[]{:S(2)}) copy-start(s32[32]{0:T(128)S(1)} %stack.186.refs_8_.refs_0_) | copy-start | bytes 388
  17.9 15.2 %collective-permute-start.7 = (bf16[128,1024]{1,0:T(8,128)(2,1)S(1)}, bf16[128,1024]{1,0:T(8,128)(2,1)S(1)}, u32[]{:S(2)}, u32[]{:S(2)}) collective-permute-start(bf16[128,1024]{1,0:T(8,128)(2,1)S(1)} %collective-permute-done.3.refs_6_.refs_0_), channel_id=1, source_target_pairs={{0,18},{1,19},{2,16},{3,17},{16,2},{17,3},{18,0},{19,1},{4,22},{5,... | collective-permute-start | bytes 786440 | tf_op jit(solution)/shard_map/ppermute | solution.py:540
  20.4 12.7 %collective-permute-start.6 = (bf16[128,1024]{1,0:T(8,128)(2,1)S(1)}, bf16[128,1024]{1,0:T(8,128)(2,1)S(1)}, u32[]{:S(2)}, u32[]{:S(2)}) collective-permute-start(bf16[128,1024]{1,0:T(8,128)(2,1)S(1)} %collective-permute-done.3.refs_6_.refs_0_), channel_id=1, source_target_pairs={{0,16},{1,17},{2,18},{3,19},{16,0},{17,1},{18,2},{19,3},{4,20},{5,... | collective-permute-start | bytes 786440 | tf_op jit(solution)/shard_map/ppermute | solution.py:540
  20.9 12.1 %collective-permute-start.5 = (bf16[128,1024]{1,0:T(8,128)(2,1)S(1)}, bf16[128,1024]{1,0:T(8,128)(2,1)S(1)}, u32[]{:S(2)}, u32[]{:S(2)}) collective-permute-start(bf16[128,1024]{1,0:T(8,128)(2,1)S(1)} %collective-permute-done.3.refs_6_.refs_0_), channel_id=1, source_target_pairs={{0,2},{1,3},{2,0},{3,1},{16,18},{17,19},{18,16},{19,17},{4,6},{5,7... | collective-permute-start | bytes 786440 | tf_op jit(solution)/shard_map/ppermute | solution.py:540
  33.0 7.5 %copy-start.13 = (f32[1024,1]{1,0:T(8,128)}, f32[1024,1]{1,0:T(8,128)S(1)}, u32[]{:S(2)}) copy-start(f32[1024,1]{1,0:T(8,128)S(1)} %get-tuple-element.51.curve_ref) | copy-start | bytes 12292
  33.0 5.6 %copy-start.4 = (bf16[1024,1024]{1,0:T(8,128)(2,1)S(1)}, bf16[1024,1024]{1,0:T(8,128)(2,1)}, u32[]{:S(2)}) copy-start(bf16[1024,1024]{1,0:T(8,128)(2,1)} %refs_0_.4) | copy-start | bytes 6291460
  33.1 8.9 %copy-start.1 = (bf16[1024,1024]{1,0:T(8,128)(2,1)S(1)}, bf16[1024,1024]{1,0:T(8,128)(2,1)}, u32[]{:S(2)}) copy-start(bf16[1024,1024]{1,0:T(8,128)(2,1)} %refs_1_.5) | copy-start | bytes 6291460
  33.2 8.8 %collective-permute-start.8 = (bf16[512,1024]{1,0:T(8,128)(2,1)S(1)}, bf16[512,1024]{1,0:T(8,128)(2,1)S(1)}, u32[]{:S(2)}, u32[]{:S(2)}) collective-permute-start(bf16[512,1024]{1,0:T(8,128)(2,1)S(1)} %pack_shares.1.refs_5_), channel_id=1, source_target_pairs={{0,1},{1,0},{2,3},{3,2},{16,17},{17,16},{18,19},{19,18},{4,5},{5,4... | collective-permute-start | bytes 3145736 | tf_op jit(solution)/shard_map/ppermute | solution.py:540
  33.2 8.7 %collective-permute-start.4 = (bf16[64,2048]{1,0:T(8,128)(2,1)S(1)}, bf16[64,2048]{1,0:T(8,128)(2,1)S(1)}, u32[]{:S(2)}, u32[]{:S(2)}) collective-permute-start(bf16[64,2048]{1,0:T(8,128)(2,1)S(1)} %get-tuple-element.42), channel_id=1, source_target_pairs={{0,4},{4,0},{8,12},{12,8},{1,5},{5,1},{9,13},{13,9},{2,6},{6,2},{1... | collective-permute-start | bytes 786440 | tf_op jit(solution)/shard_map/ppermute | solution.py:544
  34.1 3.3 %collective-permute-start.9 = (s32[64,8]{1,0:T(8,128)S(1)}, s32[64,8]{1,0:T(8,128)S(1)}, u32[]{:S(2)}, u32[]{:S(2)}) collective-permute-start(s32[64,8]{1,0:T(8,128)S(1)} %get-tuple-element.45), channel_id=1, source_target_pairs={{0,1},{1,2},{2,3},{3,0},{4,5},{5,6},{6,7},{7,4},{8,9},{9,10},{10,1... | collective-permute-start | bytes 6152 | tf_op jit(solution)/shard_map/ppermute | solution.py:76
  34.2 3.9 %collective-permute-start.10 = (s32[64,8]{1,0:T(8,128)S(1)}, s32[64,8]{1,0:T(8,128)S(1)}, u32[]{:S(2)}, u32[]{:S(2)}) collective-permute-start(s32[64,8]{1,0:T(8,128)S(1)} %get-tuple-element.46), channel_id=1, source_target_pairs={{0,2},{1,3},{2,0},{3,1},{4,6},{5,7},{6,4},{7,5},{8,10},{9,11},{10,... | collective-permute-start | bytes 6152 | tf_op jit(solution)/shard_map/ppermute | solution.py:76
  35.8 2.9 %collective-permute-start.11 = (s32[64,8]{1,0:T(8,128)S(1)}, s32[64,8]{1,0:T(8,128)S(1)}, u32[]{:S(2)}, u32[]{:S(2)}) collective-permute-start(s32[64,8]{1,0:T(8,128)S(1)} %get-tuple-element.47), channel_id=1, source_target_pairs={{0,3},{1,0},{2,1},{3,2},{4,7},{5,4},{6,5},{7,6},{8,11},{9,8},{10,9... | collective-permute-start | bytes 6152 | tf_op jit(solution)/shard_map/ppermute | solution.py:76
  43.4 39.0 %copy-start.2 = (bf16[1024,1024]{1,0:T(8,128)(2,1)}, bf16[1024,1024]{1,0:T(8,128)(2,1)S(1)}, u32[]{:S(2)}) copy-start(bf16[1024,1024]{1,0:T(8,128)(2,1)S(1)} %get-tuple-element.49.refs_2_) | copy-start | bytes 6291460
  43.4 7.9 %collective-permute-start.13 = (bf16[128,1024]{1,0:T(8,128)(2,1)S(1)}, bf16[128,1024]{1,0:T(8,128)(2,1)S(1)}, u32[]{:S(2)}, u32[]{:S(2)}) collective-permute-start(bf16[128,1024]{1,0:T(8,128)(2,1)S(1)} %get-tuple-element.55.refs_3_), channel_id=1, source_target_pairs={{0,2},{1,3},{2,0},{3,1},{16,18},{17,19},{18,16},{19,17},{4,6},{5,7... | collective-permute-start | bytes 786440 | tf_op jit(solution)/shard_map/ppermute | solution.py:540
  45.0 5.0 %collective-permute-start.12 = (bf16[64,1024]{1,0:T(8,128)(2,1)S(1)}, bf16[64,1024]{1,0:T(8,128)(2,1)S(1)}, u32[]{:S(2)}, u32[]{:S(2)}) collective-permute-start(bf16[64,1024]{1,0:T(8,128)(2,1)S(1)} %get-tuple-element.53), channel_id=1, source_target_pairs={{0,4},{4,0},{8,12},{12,8},{1,5},{5,1},{9,13},{13,9},{2,6},{6,2},{1... | collective-permute-start | bytes 393224 | tf_op jit(solution)/shard_map/ppermute | solution.py:544
  51.5 11.8 %copy-start.15 = (bf16[256,1024]{1,0:T(8,128)(2,1)}, bf16[256,1024]{1,0:T(8,128)(2,1)S(1)}, u32[]{:S(2)}) copy-start(bf16[256,1024]{1,0:T(8,128)(2,1)S(1)} %get-tuple-element.60.refs_2_) | copy-start | bytes 1572868
  51.5 10.4 %collective-permute-start.17 = (bf16[256,1024]{1,0:T(8,128)(2,1)S(1)}, bf16[256,1024]{1,0:T(8,128)(2,1)S(1)}, u32[]{:S(2)}, u32[]{:S(2)}) collective-permute-start(bf16[256,1024]{1,0:T(8,128)(2,1)S(1)} %get-tuple-element.60.refs_2_), channel_id=1, source_target_pairs={{0,1},{1,0},{2,3},{3,2},{16,17},{17,16},{18,19},{19,18},{4,5},{5,4... | collective-permute-start | bytes 1572872 | tf_op jit(solution)/shard_map/ppermute | solution.py:540
  51.6 14.3 %collective-permute-start.24 = (bf16[256,1024]{1,0:T(8,128)(2,1)S(1)}, bf16[256,1024]{1,0:T(8,128)(2,1)S(1)}, u32[]{:S(2)}, u32[]{:S(2)}) collective-permute-start(bf16[256,1024]{1,0:T(8,128)(2,1)S(1)} %get-tuple-element.60.refs_2_), channel_id=1, source_target_pairs={{0,16},{1,17},{2,18},{3,19},{16,0},{17,1},{18,2},{19,3},{4,20},{5,... | collective-permute-start | bytes 1572872 | tf_op jit(solution)/shard_map/ppermute | solution.py:540
  53.2 5.2 %collective-permute-start.16 = (bf16[64,1024]{1,0:T(8,128)(2,1)S(1)}, bf16[64,1024]{1,0:T(8,128)(2,1)S(1)}, u32[]{:S(2)}, u32[]{:S(2)}) collective-permute-start(bf16[64,1024]{1,0:T(8,128)(2,1)S(1)} %get-tuple-element.58.refs_3_), channel_id=1, source_target_pairs={{0,3},{1,0},{2,1},{3,2},{4,7},{5,4},{6,5},{7,6},{8,11},{9,8},{10,9... | collective-permute-start | bytes 393224 | tf_op jit(solution)/shard_map/ppermute | solution.py:76
  54.5 7.4 %collective-permute-start.15 = (bf16[64,1024]{1,0:T(8,128)(2,1)S(1)}, bf16[64,1024]{1,0:T(8,128)(2,1)S(1)}, u32[]{:S(2)}, u32[]{:S(2)}) collective-permute-start(bf16[64,1024]{1,0:T(8,128)(2,1)S(1)} %get-tuple-element.58.refs_3_), channel_id=1, source_target_pairs={{0,2},{1,3},{2,0},{3,1},{4,6},{5,7},{6,4},{7,5},{8,10},{9,11},{10,... | collective-permute-start | bytes 393224 | tf_op jit(solution)/shard_map/ppermute | solution.py:76
  55.0 6.9 %collective-permute-start.14 = (bf16[64,1024]{1,0:T(8,128)(2,1)S(1)}, bf16[64,1024]{1,0:T(8,128)(2,1)S(1)}, u32[]{:S(2)}, u32[]{:S(2)}) collective-permute-start(bf16[64,1024]{1,0:T(8,128)(2,1)S(1)} %get-tuple-element.58.refs_3_), channel_id=1, source_target_pairs={{0,1},{1,2},{2,3},{3,0},{4,5},{5,6},{6,7},{7,4},{8,9},{9,10},{10,1... | collective-permute-start | bytes 393224 | tf_op jit(solution)/shard_map/ppermute | solution.py:76
  58.4 15.6 %collective-permute-start.22 = (bf16[128,1024]{1,0:T(8,128)(2,1)S(1)}, bf16[128,1024]{1,0:T(8,128)(2,1)S(1)}, u32[]{:S(2)}, u32[]{:S(2)}) collective-permute-start(bf16[128,1024]{1,0:T(8,128)(2,1)S(1)} %get-tuple-element.67), channel_id=1, source_target_pairs={{0,8},{4,12},{8,0},{12,4},{1,9},{5,13},{9,1},{13,5},{2,10},{6,14},... | collective-permute-start | bytes 786440 | tf_op jit(solution)/shard_map/ppermute | solution.py:547
  61.9 20.5 %copy-start.6 = (bf16[256,1024]{1,0:T(8,128)(2,1)}, bf16[256,1024]{1,0:T(8,128)(2,1)S(1)}, u32[]{:S(2)}) copy-start(bf16[256,1024]{1,0:T(8,128)(2,1)S(1)} %collective-permute-done.17.refs_7_.refs_6_) | copy-start | bytes 1572868
  61.9 14.3 %copy-start.16 = (bf16[64,1024]{1,0:T(8,128)(2,1)S(1)}, bf16[64,1024]{1,0:T(8,128)(2,1)}, u32[]{:S(2)}) copy-start(bf16[64,1024]{1,0:T(8,128)(2,1)} %refs_0_.5) | copy-start | bytes 393220
  66.8 15.6 %collective-permute-start.25 = (bf16[256,1024]{1,0:T(8,128)(2,1)S(1)}, bf16[256,1024]{1,0:T(8,128)(2,1)S(1)}, u32[]{:S(2)}, u32[]{:S(2)}) collective-permute-start(bf16[256,1024]{1,0:T(8,128)(2,1)S(1)} %near_far.1), channel_id=1, source_target_pairs={{0,1},{1,0},{2,3},{3,2},{16,17},{17,16},{18,19},{19,18},{4,5},{5,4... | collective-permute-start | bytes 1572872 | tf_op jit(solution)/shard_map/ppermute | solution.py:540
  66.8 7.2 %collective-permute-start.18 = (bf16[64,1152]{1,0:T(8,128)(2,1)S(1)}, bf16[64,1152]{1,0:T(8,128)(2,1)S(1)}, u32[]{:S(2)}, u32[]{:S(2)}) collective-permute-start(bf16[64,1152]{1,0:T(8,128)(2,1)S(1)} %get-tuple-element.62), channel_id=1, source_target_pairs={{0,3},{1,0},{2,1},{3,2},{4,7},{5,4},{6,5},{7,6},{8,11},{9,8},{10,9... | collective-permute-start | bytes 442376 | tf_op jit(solution)/shard_map/ppermute | solution.py:76
  68.4 7.8 %collective-permute-start.19 = (bf16[64,1152]{1,0:T(8,128)(2,1)S(1)}, bf16[64,1152]{1,0:T(8,128)(2,1)S(1)}, u32[]{:S(2)}, u32[]{:S(2)}) collective-permute-start(bf16[64,1152]{1,0:T(8,128)(2,1)S(1)} %get-tuple-element.63), channel_id=1, source_target_pairs={{0,2},{1,3},{2,0},{3,1},{4,6},{5,7},{6,4},{7,5},{8,10},{9,11},{10,... | collective-permute-start | bytes 442376 | tf_op jit(solution)/shard_map/ppermute | solution.py:76
  68.9 7.3 %collective-permute-start.20 = (bf16[64,1152]{1,0:T(8,128)(2,1)S(1)}, bf16[64,1152]{1,0:T(8,128)(2,1)S(1)}, u32[]{:S(2)}, u32[]{:S(2)}) collective-permute-start(bf16[64,1152]{1,0:T(8,128)(2,1)S(1)} %get-tuple-element.64), channel_id=1, source_target_pairs={{0,1},{1,2},{2,3},{3,0},{4,5},{5,6},{6,7},{7,4},{8,9},{9,10},{10,1... | collective-permute-start | bytes 442376 | tf_op jit(solution)/shard_map/ppermute | solution.py:76
  74.0 8.4 %collective-permute-start.23 = (bf16[128,1024]{1,0:T(8,128)(2,1)S(1)}, bf16[128,1024]{1,0:T(8,128)(2,1)S(1)}, u32[]{:S(2)}, u32[]{:S(2)}) collective-permute-start(bf16[128,1024]{1,0:T(8,128)(2,1)S(1)} %other.1.refs_5_), channel_id=1, source_target_pairs={{0,16},{1,17},{2,18},{3,19},{16,0},{17,1},{18,2},{19,3},{4,20},{5,... | collective-permute-start | bytes 786440 | tf_op jit(solution)/shard_map/ppermute | solution.py:540
  76.7 5.0 %collective-permute-start.21 = (bf16[64,1024]{1,0:T(8,128)(2,1)S(1)}, bf16[64,1024]{1,0:T(8,128)(2,1)S(1)}, u32[]{:S(2)}, u32[]{:S(2)}) collective-permute-start(bf16[64,1024]{1,0:T(8,128)(2,1)S(1)} %get-tuple-element.66.refs_3_), channel_id=1, source_target_pairs={{0,4},{4,0},{8,12},{12,8},{1,5},{5,1},{9,13},{13,9},{2,6},{6,2},{1... | collective-permute-start | bytes 393224 | tf_op jit(solution)/shard_map/ppermute | solution.py:544
  82.4 2.2 %copy-start.9 = (bf16[256,1024]{1,0:T(8,128)(2,1)}, bf16[256,1024]{1,0:T(8,128)(2,1)S(1)}, u32[]{:S(2)}) copy-start(bf16[256,1024]{1,0:T(8,128)(2,1)S(1)} %collective-permute-done.25.refs_8_.refs_7_) | copy-start | bytes 1572868
  84.6 7.5 %collective-permute-start.26 = (bf16[64,2048]{1,0:T(8,128)(2,1)S(1)}, bf16[64,2048]{1,0:T(8,128)(2,1)S(1)}, u32[]{:S(2)}, u32[]{:S(2)}) collective-permute-start(bf16[64,2048]{1,0:T(8,128)(2,1)S(1)} %get-tuple-element.69), channel_id=1, source_target_pairs={{0,4},{4,0},{8,12},{12,8},{1,5},{5,1},{9,13},{13,9},{2,6},{6,2},{1... | collective-permute-start | bytes 786440 | tf_op jit(solution)/shard_map/ppermute | solution.py:544
  85.4 23.3 %collective-permute-start.28 = (bf16[256,1024]{1,0:T(8,128)(2,1)}, bf16[256,1024]{1,0:T(8,128)(2,1)S(1)}, u32[]{:S(2)}, u32[]{:S(2)}) collective-permute-start(bf16[256,1024]{1,0:T(8,128)(2,1)} %get-tuple-element.73.refs_4_), channel_id=1, source_target_pairs={{0,2},{1,3},{2,0},{3,1},{16,18},{17,19},{18,16},{19,17},{4,6},{5,7... | collective-permute-start | bytes 1572872 | tf_op jit(solution)/shard_map/ppermute | solution.py:540
  92.1 0.8 copy-start.12
  93.0 20.8 %all-to-all-start = ((bf16[32,64,128]{2,1,0:T(8,128)(2,1)}), bf16[32,64,128]{2,1,0:T(8,128)(2,1)}, u32[]{:S(2)}, u32[]{:S(2)}) async-start(bf16[32,64,128]{2,1,0:T(8,128)(2,1)} %copy-done.12), calls=%async_computation | async-start | bytes 1048576 | tf_op jit(solution)/shard_map/all_to_all | solution.py:658
  98.4 15.4 %collective-permute-start.29 = (bf16[256,1024]{1,0:T(8,128)(2,1)}, bf16[256,1024]{1,0:T(8,128)(2,1)}, u32[]{:S(2)}, u32[]{:S(2)}) collective-permute-start(bf16[256,1024]{1,0:T(8,128)(2,1)} %get-tuple-element.73.refs_4_), channel_id=1, source_target_pairs={{0,1},{1,0},{2,3},{3,2},{16,17},{17,16},{18,19},{19,18},{4,5},{5,4... | collective-permute-start | bytes 1572872 | tf_op jit(solution)/shard_map/ppermute | solution.py:540
  98.4 3.4 %copy-start.5 = (bf16[1024,4096]{1,0:T(8,128)(2,1)S(1)}, bf16[1024,4096]{1,0:T(8,128)(2,1)}, u32[]{:S(2)}) copy-start(bf16[1024,4096]{1,0:T(8,128)(2,1)} %get-tuple-element.50.normed_ref) | copy-start | bytes 25165828
  101.8 1.0 copy-start.14
  108.8 5.1 %copy-start.10 = (bf16[256,1024]{1,0:T(8,128)(2,1)}, bf16[256,1024]{1,0:T(8,128)(2,1)S(1)}, u32[]{:S(2)}) copy-start(bf16[256,1024]{1,0:T(8,128)(2,1)S(1)} %collective-permute-done.28.refs_0_.refs_5_) | copy-start | bytes 1572868
  108.8 5.0 %collective-permute-start.30 = (bf16[256,1024]{1,0:T(8,128)(2,1)S(1)}, bf16[256,1024]{1,0:T(8,128)(2,1)}, u32[]{:S(2)}, u32[]{:S(2)}) collective-permute-start(bf16[256,1024]{1,0:T(8,128)(2,1)S(1)} %late.1), channel_id=1, source_target_pairs={{0,1},{1,0},{2,3},{3,2},{16,17},{17,16},{18,19},{19,18},{4,5},{5,4... | collective-permute-start | bytes 1572872 | tf_op jit(solution)/shard_map/ppermute | solution.py:540
  109.4 3.8 %collective-permute-start.27 = (f32[24,128]{1,0:T(8,128)S(1)}, f32[24,128]{1,0:T(8,128)S(1)}, u32[]{:S(2)}, u32[]{:S(2)}) collective-permute-start(f32[24,128]{1,0:T(8,128)S(1)} %get-tuple-element.71), channel_id=1, source_target_pairs={{0,4},{4,0},{8,12},{12,8},{1,5},{5,1},{9,13},{13,9},{2,6},{6,2},{1... | collective-permute-start | bytes 36872 | tf_op jit(solution)/shard_map/ppermute | solution.py:544
  113.8 8.2 %copy-start.18 = (f32[24,128]{1,0:T(8,128)S(1)}, f32[24,128]{1,0:T(8,128)}, u32[]{:S(2)}) copy-start(f32[24,128]{1,0:T(8,128)} %copy-done.17) | copy-start | bytes 36868
  118.4 20.8 %copy-start.3 = (bf16[1024,1024]{1,0:T(8,128)(2,1)S(1)}, bf16[1024,1024]{1,0:T(8,128)(2,1)}, u32[]{:S(2)}) copy-start(bf16[1024,1024]{1,0:T(8,128)(2,1)} %copy-done.2) | copy-start | bytes 6291460
  118.5 19.6 %collective-permute-start.38 = (bf16[1024,128]{1,0:T(8,128)(2,1)}, bf16[1024,128]{1,0:T(8,128)(2,1)S(1)}, u32[]{:S(2)}, u32[]{:S(2)}) collective-permute-start(bf16[1024,128]{1,0:T(8,128)(2,1)} %grad_columns.1.refs_1_.refs_0_), channel_id=1, source_target_pairs={{0,18},{1,19},{2,16},{3,17},{16,2},{17,3},{18,0},{19,1},{4,22},{5,... | collective-permute-start | bytes 786440 | tf_op jit(solution)/shard_map/ppermute | solution.py:540
  120.9 17.1 %collective-permute-start.37 = (bf16[1024,128]{1,0:T(8,128)(2,1)}, bf16[1024,128]{1,0:T(8,128)(2,1)S(1)}, u32[]{:S(2)}, u32[]{:S(2)}) collective-permute-start(bf16[1024,128]{1,0:T(8,128)(2,1)} %grad_columns.1.refs_1_.refs_0_), channel_id=1, source_target_pairs={{0,16},{1,17},{2,18},{3,19},{16,0},{17,1},{18,2},{19,3},{4,20},{5,... | collective-permute-start | bytes 786440 | tf_op jit(solution)/shard_map/ppermute | solution.py:540
  121.5 16.6 %collective-permute-start.36 = (bf16[1024,128]{1,0:T(8,128)(2,1)}, bf16[1024,128]{1,0:T(8,128)(2,1)S(1)}, u32[]{:S(2)}, u32[]{:S(2)}) collective-permute-start(bf16[1024,128]{1,0:T(8,128)(2,1)} %grad_columns.1.refs_1_.refs_0_), channel_id=1, source_target_pairs={{0,2},{1,3},{2,0},{3,1},{16,18},{17,19},{18,16},{19,17},{4,6},{5,7... | collective-permute-start | bytes 786440 | tf_op jit(solution)/shard_map/ppermute | solution.py:540
  122.0 1.0 copy-start.7
  123.0 4.6 %collective-permute-start.31 = (f32[24,128]{1,0:T(8,128)S(1)}, f32[24,128]{1,0:T(8,128)S(1)}, u32[]{:S(2)}, u32[]{:S(2)}) collective-permute-start(f32[24,128]{1,0:T(8,128)S(1)} %slope_out.1.refs_0_), channel_id=1, source_target_pairs={{0,8},{4,12},{8,0},{12,4},{1,9},{5,13},{9,1},{13,5},{2,10},{6,14},... | collective-permute-start | bytes 36872 | tf_op jit(solution)/shard_map/ppermute | solution.py:547
  127.6 5.9 %collective-permute-start.32 = (f32[24,128]{1,0:T(8,128)S(1)}, f32[24,128]{1,0:T(8,128)S(1)}, u32[]{:S(2)}, u32[]{:S(2)}) collective-permute-start(f32[24,128]{1,0:T(8,128)S(1)} %sum_mirror.1.refs_0_), channel_id=1, source_target_pairs={{0,16},{16,0},{1,17},{17,1},{2,18},{18,2},{3,19},{19,3},{4,20},{20... | collective-permute-start | bytes 36872 | tf_op jit(solution)/shard_map/ppermute | solution.py:76
  133.5 1.4 collective-permute-start.35
  133.5 3.7 %collective-permute-start.34 = (f32[24,128]{1,0:T(8,128)S(1)}, f32[24,128]{1,0:T(8,128)S(1)}, u32[]{:S(2)}, u32[]{:S(2)}) collective-permute-start(f32[24,128]{1,0:T(8,128)S(1)} %sum_groups.1.refs_0_), channel_id=1, source_target_pairs={{0,2},{1,3},{2,0},{3,1},{4,6},{5,7},{6,4},{7,5},{8,10},{9,11},{10,... | collective-permute-start | bytes 36872 | tf_op jit(solution)/shard_map/ppermute | solution.py:76
  134.9 3.1 %collective-permute-start.33 = (f32[24,128]{1,0:T(8,128)S(1)}, f32[24,128]{1,0:T(8,128)S(1)}, u32[]{:S(2)}, u32[]{:S(2)}) collective-permute-start(f32[24,128]{1,0:T(8,128)S(1)} %sum_groups.1.refs_0_), channel_id=1, source_target_pairs={{0,1},{1,2},{2,3},{3,0},{4,5},{5,6},{6,7},{7,4},{8,9},{9,10},{10,1... | collective-permute-start | bytes 36872 | tf_op jit(solution)/shard_map/ppermute | solution.py:76
  138.1 1.0 copy-start.8
  139.1 2.7 %copy-start.20 = (f32[1024]{0:T(1024)S(1)}, f32[1024]{0:T(1024)}, u32[]{:S(2)}) copy-start(f32[1024]{0:T(1024)} %param.14) | copy-start | bytes 12292
  139.2 2.7 %collective-permute-start.39 = (bf16[4096,128]{1,0:T(8,128)(2,1)S(1)}, bf16[4096,128]{1,0:T(8,128)(2,1)S(1)}, u32[]{:S(2)}, u32[]{:S(2)}) collective-permute-start(bf16[4096,128]{1,0:T(8,128)(2,1)S(1)} %pack_columns.1.refs_3_), channel_id=1, source_target_pairs={{0,1},{1,0},{2,3},{3,2},{16,17},{17,16},{18,19},{19,18},{4,5},{5,4... | collective-permute-start | bytes 3145736 | tf_op jit(solution)/shard_map/ppermute | solution.py:540
  140.5 4.2 %collective-permute-start.40 = (f32[1,1024]{1,0:T(1,128)S(1)}, f32[1,1024]{1,0:T(1,128)S(1)}, u32[]{:S(2)}, u32[]{:S(2)}) collective-permute-start(f32[1,1024]{1,0:T(1,128)S(1)} %get-tuple-element.76.refs_0_), channel_id=1, source_target_pairs={{0,4},{4,0},{8,12},{12,8},{1,5},{5,1},{9,13},{13,9},{2,6},{6,2},{1... | collective-permute-start | bytes 12296 | tf_op jit(solution)/shard_map/ppermute | solution.py:544
  (3 other events, 2.1 us)

commit v8 on v7

--- a/solution.py
+++ b/solution.py
@@ -36,9 +36,7 @@
         ]
         for copy in copies:
             copy.start()
-        for copy in copies:
-            copy.wait()
-        kernel(*refs[:smem], *buffers, *refs[smem + n : -n - 1])
+        kernel(copies, *refs[:smem], *buffers, *refs[smem + n : -n - 1])
 
     return run
 
@@ -451,15 +449,18 @@
     )(z, normed, curve, loss, *backs)
 
 
-def columns_kernel(n, order_ref, grads_ref, *refs):
+def columns_kernel(n, copies, order_ref, grads_ref, *refs):
     pieces, (out_ref, sorted_ref) = refs[:n], refs[n:]
     chunk = grads_ref.shape[1]
+    copies[0].wait()
     for j in range(sorted_ref.shape[0] // chunk):
         sorted_ref[j * chunk : (j + 1) * chunk, :] = grads_ref[order_ref[j]]
     at = pieces[0].shape[0]
+    copies[1].wait()
     total = tn(sorted_ref[0:at, :], pieces[0][...])
-    for piece in pieces[1:]:
+    for k, piece in enumerate(pieces[1:]):
         rows = piece.shape[0]
+        copies[k + 2].wait()
         total = total + tn(sorted_ref[at : at + rows, :], piece[...])
         at += rows
     out_ref[...] = total.T.astype(BF16)
@@ -662,9 +663,11 @@
     def total(parts, name):
         return call(add_kernel, [shape(parts[0].shape, F32)], parts, name)[0]
 
-    slope = total([slopes[0]] + [half_shift(slopes[k], k) for k in range(1, half)], "sum_half")
+    own_slope = slopes[0]
+    if n_g > 1:
+        slopes = [total([a] + [shift(a, "grp", k) for k in range(1, n_g)], "sum_groups") for a in slopes]
     across = [plane_shift(others, 0, dh, 0) for dh in range(1, n_h)]
-    late = [pack([array], "late", slopes[0]) for array in across]
+    late = [pack([array], "late", own_slope) for array in across]
     spread = []
     for dc in range(n_c):
         if dc == 0:
@@ -675,13 +678,12 @@
     block_columns = call(
         functools.partial(columns_kernel, len(spread)), [shape((depth, cols), BF16)],
         [ranks, all_columns] + spread, "grad_columns",
-        flops=2 * n_all * queries * depth * cols, scratch=[pltpu.VMEM((n_all * queries, cols), BF16)], smem=1, copy=True, after=[slope],
+        flops=2 * n_all * queries * depth * cols, scratch=[pltpu.VMEM((n_all * queries, cols), BF16)], smem=1, copy=True, after=slopes,
     )[0]
     on_chips = [block_columns if dg == dh == 0 else plane_shift(block_columns, dg, dh, 0) for dg, dh in chips]
-    slope = passed(slope, "slope_out", block_columns)
+    slopes = [passed(array, "slope_out", block_columns) for array in slopes]
+    slope = total([slopes[0]] + [half_shift(slopes[k], k) for k in range(1, half)], "sum_half")
     slope = total([slope, mirror_shift(slope)], "sum_mirror")
-    if n_g > 1:
-        slope = total([slope] + [shift(slope, "grp", k) for k in range(1, n_g)], "sum_groups")
     if n_i > 1:
         slope = total([slope] + [shift(slope, "item", k) for k in steps_i], "sum_items")
     query_part, my_slope, loss_total = call(

time: 147 us -> 146 us (level)
  waiting for transfers between devices: 48.6 us -> 44.6 us
  starting transfers between devices: 46.6 us -> 49.4 us
    ppermute x16 -> x17, waiting for transfers between devices: 14.7 us -> 11.2 us  [shift(): return lax.ppermute(values, axis, [(i, (i + k) % n) for i in range(n)])]
    ppermute x16 -> x17, starting transfers between devices: 12.7 us -> 15 us  [shift(): return lax.ppermute(values, axis, [(i, (i + k) % n) for i in range(n)])]
    unnamed x51 -> x55, local copies, waits for them, and re-layouts: 11 us -> 11.6 us
    pallas_call x21 -> x23, Pallas kernels: 18.6 us -> 18.1 us  [call(): pl.pallas_call(run, out_shape=outs, in_specs=[SMEM] * smem + [pl.BlockSpe...]
  transfers between devices with their start and end apart: 42 -> 43, of which waited for: 22 -> 21; matrix products, arithmetic and copies ran while one was open for 1% -> 1% of each run, Pallas kernels for 18% -> 19%
where the time goes in v8:
time: 146 us; the launch traced here: 145 us
  starting transfers between devices  49.4 us (34%)
  waiting for transfers between devices  44.6 us (31%)
  Pallas kernels  35.7 us (24%)
  local copies, waits for them, and re-layouts  13.2 us (9%)
  between operations  2.34 us (2%)
    pallas_call x23, Pallas kernels, call(): pl.pallas_call(run, out_shape=outs, in_specs=[SMEM] * smem + [pl.BlockSpe...  18.1 us
    ppermute x6, waiting for transfers between devices, half_shift(): return lax.ppermute(values, 'fsdp', pairs)  17.3 us
    ppermute x17, starting transfers between devices, shift(): return lax.ppermute(values, axis, [(i, (i + k) % n) for i in range(n)])  15 us
    ppermute x16, starting transfers between devices, plane_shift(): return lax.ppermute(values, PLANE, pairs)  12.8 us
    pallas_call x1, Pallas kernels, gate_rows(): pl.pallas_call(run, grid=(queries // group,), out_shape=outs, in_specs=[S...  11.6 us
    unnamed x55, local copies, waits for them, and re-layouts  11.6 us
    ppermute x3, waiting for transfers between devices, mirror_shift(): lax.ppermute(values, 'fsdp', [(a, (a + half) % n_z) for a in range(n_z)])  11.5 us
    ppermute x17, waiting for transfers between devices, shift(): return lax.ppermute(values, axis, [(i, (i + k) % n) for i in range(n)])  11.2 us
  transfers between devices with their start and end apart: 43, of which 21 were waited for; matrix products, arithmetic and copies ran while one was open for 1% of the time, Pallas kernels for 19%

profile of v8, /device:TPU:0, one launch (start us, length us, event | category | flops | bytes accessed | tf_op | source)
XLA Modules:
  0.0 145.3 jit_solution(12447983757613038554)
XLA Ops:
  0.7 1.0 constant_dynamic-slice_fusion.refs_2_
  1.6 4.1 %collective-permute-start.3 = (bf16[128,1024]{1,0:T(8,128)(2,1)S(1)}, bf16[128,1024]{1,0:T(8,128)(2,1)S(1)}, u32[]{:S(2)}, u32[]{:S(2)}) collective-permute-start(bf16[128,1024]{1,0:T(8,128)(2,1)S(1)} %constant_dynamic-slice_fusion.refs_2_), channel_id=1, source_target_pairs={{0,8},{4,12},{8,0},{12,4},{1,9},{5,13},{9,1},{13,5},{2,10},{6,14},... | collective-permute-start | bytes 786440 | tf_op jit(solution)/shard_map/ppermute | solution.py:548
  5.8 1.6 %copy-done = bf16[1024,1024]{1,0:T(8,128)(2,1)S(1)} copy-done((bf16[1024,1024]{1,0:T(8,128)(2,1)S(1)}, bf16[1024,1024]{1,0:T(8,128)(2,1)}, u32[]{:S(2)}) %copy-start) | copy-done | bytes 2097176
  7.3 0.7 copy-done.21
  8.0 1.7 %block_u.1 = f32[1,1024]{1,0:T(1,128)S(1)} custom-call(bf16[1024,1024]{1,0:T(8,128)(2,1)S(1)} %copy-done, f32[1,1024]{1,0:T(1,128)S(1)} %bitcast.51, bf16[128,1024]{1,0:T(8,128)(2,1)S(1)} %constant_dynamic-slice_fusion.refs_2_), custom_call_target="tpu_custom_call" | custom-call | bytes 2105344 | tf_op jit(solution)/shard_map/block_u/pallas_call | solution.py:56
  9.8 1.4 collective-permute-start.2
  11.1 1.7 %collective-permute-start.1 = (f32[1,1024]{1,0:T(1,128)S(1)}, f32[1,1024]{1,0:T(1,128)S(1)}, u32[]{:S(2)}, u32[]{:S(2)}) collective-permute-start(f32[1,1024]{1,0:T(1,128)S(1)} %block_u.1), channel_id=1, source_target_pairs={{0,8},{4,12},{8,0},{12,4},{1,9},{5,13},{9,1},{13,5},{2,10},{6,14},... | collective-permute-start | bytes 12296 | tf_op jit(solution)/shard_map/ppermute | solution.py:74
  13.7 4.2 %collective-permute-done.3.refs_6_.refs_0_ = bf16[128,1024]{1,0:T(8,128)(2,1)S(1)} collective-permute-done((bf16[128,1024]{1,0:T(8,128)(2,1)S(1)}, bf16[128,1024]{1,0:T(8,128)(2,1)S(1)}, u32[]{:S(2)}, u32[]{:S(2)}) %collective-permute-start.3) | collective-permute-done | bytes 262176 | tf_op jit(solution)/shard_map/ppermute | solution.py:548
  17.9 2.5 %collective-permute-start.7 = (bf16[128,1024]{1,0:T(8,128)(2,1)S(1)}, bf16[128,1024]{1,0:T(8,128)(2,1)S(1)}, u32[]{:S(2)}, u32[]{:S(2)}) collective-permute-start(bf16[128,1024]{1,0:T(8,128)(2,1)S(1)} %collective-permute-done.3.refs_6_.refs_0_), channel_id=1, source_target_pairs={{0,18},{1,19},{2,16},{3,17},{16,2},{17,3},{18,0},{19,1},{4,22},{5,... | collective-permute-start | bytes 786440 | tf_op jit(solution)/shard_map/ppermute | solution.py:541
  21.4 11.6 %gate_rows.1 = (bf16[64,2048]{1,0:T(8,128)(2,1)S(1)}, bf16[64,2048]{1,0:T(8,128)(2,1)S(1)}, bf16[1024,4096]{1,0:T(8,128)(2,1)}, f32[1024,1]{1,0:T(8,128)S(1)}, f...) custom-call(s32[2]{0:T(128)S(1)} %pad_add_fusion.refs_0_.z_ref, ...), custom_call_target="tpu_custom_call" | custom-call | flops 41943040 | bytes 16777216 | tf_op jit(solution)/shard_map/gate_rows/pallas_call | solution.py:174
  33.2 0.8 collective-permute-start.4
  34.2 1.5 %collective-permute-start.10 = (s32[64,8]{1,0:T(8,128)S(1)}, s32[64,8]{1,0:T(8,128)S(1)}, u32[]{:S(2)}, u32[]{:S(2)}) collective-permute-start(s32[64,8]{1,0:T(8,128)S(1)} %get-tuple-element.46), channel_id=1, source_target_pairs={{0,2},{1,3},{2,0},{3,1},{4,6},{5,7},{6,4},{7,5},{8,10},{9,11},{10,... | collective-permute-start | bytes 6152 | tf_op jit(solution)/shard_map/ppermute | solution.py:74
  35.8 1.3 collective-permute-start.11
  37.4 0.7 collective-permute-done.10.refs_4_
  38.7 1.8 %list_counts.1 = (f32[256,1024]{1,0:T(8,128)S(1)}, f32[1,1024]{1,0:T(1,128)S(1)}) custom-call(s32[1]{0:T(128)} %bitcast.46.refs_9_.refs_0_, bf16[1024,1024]{1,0:T(8,128)(2,1)S(1)} %copy-done.4, s32[64,8]{1,0:T(8,128)S(1)} %get-tuple-element.44.refs_2_, s32[64,8]{1,0:T(8,128)S(1)} %collective-permute-done.9.refs_3_, ...), custom_call_target="tpu_custom_call" | custom-call | bytes 3158020 | tf_op jit(solution)/shard_map/list_counts/pallas_call | solution.py:56
  40.5 1.5 %collective-permute-done.4.refs_4_ = bf16[64,2048]{1,0:T(8,128)(2,1)S(1)} collective-permute-done((bf16[64,2048]{1,0:T(8,128)(2,1)S(1)}, bf16[64,2048]{1,0:T(8,128)(2,1)S(1)}, u32[]{:S(2)}, u32[]{:S(2)}) %collective-permute-start.4) | collective-permute-done | bytes 262176 | tf_op jit(solution)/shard_map/ppermute | solution.py:545
  42.0 1.4 forward.1
  43.4 1.6 %collective-permute-start.13 = (bf16[128,1024]{1,0:T(8,128)(2,1)S(1)}, bf16[128,1024]{1,0:T(8,128)(2,1)S(1)}, u32[]{:S(2)}, u32[]{:S(2)}) collective-permute-start(bf16[128,1024]{1,0:T(8,128)(2,1)S(1)} %get-tuple-element.55.refs_3_), channel_id=1, source_target_pairs={{0,2},{1,3},{2,0},{3,1},{16,18},{17,19},{18,16},{19,17},{4,6},{5,7... | collective-permute-start | bytes 786440 | tf_op jit(solution)/shard_map/ppermute | solution.py:541
  45.0 0.7 collective-permute-start.12
  45.7 4.2 %collective-permute-done.12.refs_1_ = bf16[64,1024]{1,0:T(8,128)(2,1)S(1)} collective-permute-done((bf16[64,1024]{1,0:T(8,128)(2,1)S(1)}, bf16[64,1024]{1,0:T(8,128)(2,1)S(1)}, u32[]{:S(2)}, u32[]{:S(2)}) %collective-permute-start.12) | collective-permute-done | bytes 131104 | tf_op jit(solution)/shard_map/ppermute | solution.py:545
  50.0 1.3 collective-permute-done.13.refs_4_
  51.6 1.6 %collective-permute-start.24 = (bf16[256,1024]{1,0:T(8,128)(2,1)S(1)}, bf16[256,1024]{1,0:T(8,128)(2,1)S(1)}, u32[]{:S(2)}, u32[]{:S(2)}) collective-permute-start(bf16[256,1024]{1,0:T(8,128)(2,1)S(1)} %get-tuple-element.60.refs_2_), channel_id=1, source_target_pairs={{0,16},{1,17},{2,18},{3,19},{16,0},{17,1},{18,2},{19,3},{4,20},{5,... | collective-permute-start | bytes 1572872 | tf_op jit(solution)/shard_map/ppermute | solution.py:541
  53.2 1.3 collective-permute-start.16
  55.0 3.4 %collective-permute-done.16.refs_6_ = bf16[64,1024]{1,0:T(8,128)(2,1)S(1)} collective-permute-done((bf16[64,1024]{1,0:T(8,128)(2,1)S(1)}, bf16[64,1024]{1,0:T(8,128)(2,1)S(1)}, u32[]{:S(2)}, u32[]{:S(2)}) %collective-permute-start.16) | collective-permute-done | bytes 131104 | tf_op jit(solution)/shard_map/ppermute | solution.py:74
  58.3 3.2 %collective-permute-start.22 = (bf16[128,1024]{1,0:T(8,128)(2,1)S(1)}, bf16[128,1024]{1,0:T(8,128)(2,1)S(1)}, u32[]{:S(2)}, u32[]{:S(2)}) collective-permute-start(bf16[128,1024]{1,0:T(8,128)(2,1)S(1)} %get-tuple-element.67), channel_id=1, source_target_pairs={{0,8},{4,12},{8,0},{12,4},{1,9},{5,13},{9,1},{13,5},{2,10},{6,14},... | collective-permute-start | bytes 786440 | tf_op jit(solution)/shard_map/ppermute | solution.py:548
  61.9 1.4 contrast.1
  63.3 2.6 %collective-permute-done.24.refs_0_.refs_3_ = bf16[256,1024]{1,0:T(8,128)(2,1)S(1)} collective-permute-done((bf16[256,1024]{1,0:T(8,128)(2,1)S(1)}, bf16[256,1024]{1,0:T(8,128)(2,1)S(1)}, u32[]{:S(2)}, u32[]{:S(2)}) %collective-permute-start.24) | collective-permute-done | bytes 524320 | tf_op jit(solution)/shard_map/ppermute | solution.py:541
  66.0 0.8 copy-done.11
  66.7 1.7 %collective-permute-start.18 = (bf16[64,1152]{1,0:T(8,128)(2,1)S(1)}, bf16[64,1152]{1,0:T(8,128)(2,1)S(1)}, u32[]{:S(2)}, u32[]{:S(2)}) collective-permute-start(bf16[64,1152]{1,0:T(8,128)(2,1)S(1)} %get-tuple-element.62), channel_id=1, source_target_pairs={{0,3},{1,0},{2,1},{3,2},{4,7},{5,4},{6,5},{7,6},{8,11},{9,8},{10,9... | collective-permute-start | bytes 442376 | tf_op jit(solution)/shard_map/ppermute | solution.py:74
  68.9 5.1 %collective-permute-done.22.refs_0_ = bf16[128,1024]{1,0:T(8,128)(2,1)S(1)} collective-permute-done((bf16[128,1024]{1,0:T(8,128)(2,1)S(1)}, bf16[128,1024]{1,0:T(8,128)(2,1)S(1)}, u32[]{:S(2)}, u32[]{:S(2)}) %collective-permute-start.22) | collective-permute-done | bytes 262176 | tf_op jit(solution)/shard_map/ppermute | solution.py:548
  74.0 0.6 collective-permute-start.23
  74.6 1.6 %collective-permute-done.19.refs_6_ = bf16[64,1152]{1,0:T(8,128)(2,1)S(1)} collective-permute-done((bf16[64,1152]{1,0:T(8,128)(2,1)S(1)}, bf16[64,1152]{1,0:T(8,128)(2,1)S(1)}, u32[]{:S(2)}, u32[]{:S(2)}) %collective-permute-start.19) | collective-permute-done | bytes 147488 | tf_op jit(solution)/shard_map/ppermute | solution.py:74
  76.6 1.2 collective-permute-start.21
  77.8 3.9 %collective-permute-done.21.refs_4_ = bf16[64,1024]{1,0:T(8,128)(2,1)S(1)} collective-permute-done((bf16[64,1024]{1,0:T(8,128)(2,1)S(1)}, bf16[64,1024]{1,0:T(8,128)(2,1)S(1)}, u32[]{:S(2)}, u32[]{:S(2)}) %collective-permute-start.21) | collective-permute-done | bytes 131104 | tf_op jit(solution)/shard_map/ppermute | solution.py:545
  81.7 0.7 collective-permute-done.23.refs_6_
  82.4 2.2 %backward.1 = (bf16[64,2048]{1,0:T(8,128)(2,1)S(1)}, bf16[64,2048]{1,0:T(8,128)(2,1)S(1)}, bf16[256,1024]{1,0:T(8,128)(2,1)}) custom-call(s32[1]{0:T(128)} %bitcast.9.refs_10_.refs_0_, bf16[1024,1024]{1,0:T(8,128)(2,1)S(1)} %copy-done.1, bf16[1024,1024]{1,0:T(8,128)(2,1)S(1)} %get-tuple-element.49.refs_2_, bf16[64,1024]{1,0:T(8,128)(2,1)S(1)} %get-tuple-element.66.refs_3_, ...), custom_call_target="tpu_custom_call" | custom-call | flops 536870912 | bytes 6029316 | tf_op jit(solution)/shard_map/backward/pallas_call | solution.py:56
  84.6 0.9 collective-permute-start.26
  85.5 1.1 collective-permute-start.28
  86.6 5.5 %collective-permute-done.26.rest_1_.refs_1_ = bf16[64,2048]{1,0:T(8,128)(2,1)S(1)} collective-permute-done((bf16[64,2048]{1,0:T(8,128)(2,1)S(1)}, bf16[64,2048]{1,0:T(8,128)(2,1)S(1)}, u32[]{:S(2)}, u32[]{:S(2)}) %collective-permute-start.26) | collective-permute-done | bytes 262176 | tf_op jit(solution)/shard_map/ppermute | solution.py:545
  92.2 0.8 copy-done.12
  92.9 5.4 %all-to-all-start = ((bf16[32,64,128]{2,1,0:T(8,128)(2,1)}), bf16[32,64,128]{2,1,0:T(8,128)(2,1)}, u32[]{:S(2)}, u32[]{:S(2)}) async-start(bf16[32,64,128]{2,1,0:T(8,128)(2,1)} %copy-done.12), calls=%async_computation | async-start | bytes 1048576 | tf_op jit(solution)/shard_map/all_to_all | solution.py:659
  98.4 3.4 %copy-done.5 = bf16[1024,4096]{1,0:T(8,128)(2,1)S(1)} copy-done((bf16[1024,4096]{1,0:T(8,128)(2,1)S(1)}, bf16[1024,4096]{1,0:T(8,128)(2,1)}, u32[]{:S(2)}) %copy-start.5) | copy-done | bytes 8388632
  101.8 1.0 copy-done.14
  102.8 5.9 %slope_rows.1 = (f32[24,128]{1,0:T(8,128)S(1)}, f32[24,128]{1,0:T(8,128)S(1)}) custom-call(s32[2]{0:T(128)S(1)} %pad_add_fusion.refs_0_.z_ref, bf16[1024,4096]{1,0:T(8,128)(2,1)S(1)} %copy-done.5, f32[1024,1]{1,0:T(8,128)S(1)} %copy-done.14, f32[1,128]{1,0:T(1,128)S(1)} %get-tuple-element.65.loss_ref, bf16[64,2048]{1,0:T(8,128)(2,1)S(1)} %get-tuple-element.68.rest_0_, ...), custom_call_target="tpu_custom_call" | custom-call | flops 16777216 | bytes 8388608 | tf_op jit(solution)/shard_map/slope_rows/pallas_call | solution.py:431
  109.3 1.5 %collective-permute-start.31 = (f32[24,128]{1,0:T(8,128)S(1)}, f32[24,128]{1,0:T(8,128)S(1)}, u32[]{:S(2)}, u32[]{:S(2)}) collective-permute-start(f32[24,128]{1,0:T(8,128)S(1)} %get-tuple-element.73.refs_0_), channel_id=1, source_target_pairs={{0,16},{16,0},{1,17},{17,1},{2,18},{18,2},{3,19},{19,3},{4,20},{20... | collective-permute-start | bytes 36872 | tf_op jit(solution)/shard_map/ppermute | solution.py:74
  111.3 1.7 %collective-permute-done.31.refs_1_ = f32[24,128]{1,0:T(8,128)S(1)} collective-permute-done((f32[24,128]{1,0:T(8,128)S(1)}, f32[24,128]{1,0:T(8,128)S(1)}, u32[]{:S(2)}, u32[]{:S(2)}) %collective-permute-start.31) | collective-permute-done | bytes 12320 | tf_op jit(solution)/shard_map/ppermute | solution.py:74
  113.6 0.9 collective-permute-done.27.refs_1_
  115.2 4.1 %grad_columns.1.refs_1_.refs_0_ = bf16[1024,128]{1,0:T(8,128)(2,1)} custom-call(s32[32]{0:T(128)} %copy-done.23, bf16[32,64,128]{2,1,0:T(8,128)(2,1)} %all-to-all-done.refs_1_, bf16[256,1024]{1,0:T(8,128)(2,1)} %copy-done.15, bf16[256,1024]{1,0:T(8,128)(2,1)} %copy-done.11, bf16[256,1024]{1,0:T(8,128)(2,1)} %get-tuple-element.72.refs_4_, ...), custom_call_target="tpu_custom_call" | custom-call | flops 536870912 | bytes 4980864 | tf_op jit(solution)/shard_map/grad_columns/pallas_call | solution.py:56
  119.3 1.6 %collective-permute-start.39 = (bf16[1024,128]{1,0:T(8,128)(2,1)}, bf16[1024,128]{1,0:T(8,128)(2,1)S(1)}, u32[]{:S(2)}, u32[]{:S(2)}) collective-permute-start(bf16[1024,128]{1,0:T(8,128)(2,1)} %grad_columns.1.refs_1_.refs_0_), channel_id=1, source_target_pairs={{0,18},{1,19},{2,16},{3,17},{16,2},{17,3},{18,0},{19,1},{4,22},{5,... | collective-permute-start | bytes 786440 | tf_op jit(solution)/shard_map/ppermute | solution.py:541
  120.9 1.4 collective-permute-start.38
  122.8 1.0 copy-done.7
  123.8 1.5 %collective-permute-start.32 = (f32[24,128]{1,0:T(8,128)S(1)}, f32[24,128]{1,0:T(8,128)S(1)}, u32[]{:S(2)}, u32[]{:S(2)}) collective-permute-start(f32[24,128]{1,0:T(8,128)S(1)} %slope_out.3), channel_id=1, source_target_pairs={{0,4},{4,0},{8,12},{12,8},{1,5},{5,1},{9,13},{13,9},{2,6},{6,2},{1... | collective-permute-start | bytes 36872 | tf_op jit(solution)/shard_map/ppermute | solution.py:545
  125.3 2.2 %collective-permute-done.32.refs_1_ = f32[24,128]{1,0:T(8,128)S(1)} collective-permute-done((f32[24,128]{1,0:T(8,128)S(1)}, f32[24,128]{1,0:T(8,128)S(1)}, u32[]{:S(2)}, u32[]{:S(2)}) %collective-permute-start.32) | collective-permute-done | bytes 12320 | tf_op jit(solution)/shard_map/ppermute | solution.py:545
  127.5 2.4 %collective-permute-start.33 = (f32[24,128]{1,0:T(8,128)S(1)}, f32[24,128]{1,0:T(8,128)S(1)}, u32[]{:S(2)}, u32[]{:S(2)}) collective-permute-start(f32[24,128]{1,0:T(8,128)S(1)} %sum_half.1.refs_0_), channel_id=1, source_target_pairs={{0,8},{4,12},{8,0},{12,4},{1,9},{5,13},{9,1},{13,5},{2,10},{6,14},... | collective-permute-start | bytes 36872 | tf_op jit(solution)/shard_map/ppermute | solution.py:548
  130.0 2.2 %collective-permute-done.33.refs_1_ = f32[24,128]{1,0:T(8,128)S(1)} collective-permute-done((f32[24,128]{1,0:T(8,128)S(1)}, f32[24,128]{1,0:T(8,128)S(1)}, u32[]{:S(2)}, u32[]{:S(2)}) %collective-permute-start.33) | collective-permute-done | bytes 12320 | tf_op jit(solution)/shard_map/ppermute | solution.py:548
  132.1 1.5 %collective-permute-start.35 = (f32[24,128]{1,0:T(8,128)S(1)}, f32[24,128]{1,0:T(8,128)S(1)}, u32[]{:S(2)}, u32[]{:S(2)}) collective-permute-start(f32[24,128]{1,0:T(8,128)S(1)} %sum_mirror.1.refs_0_), channel_id=1, source_target_pairs={{0,2},{1,3},{2,0},{3,1},{4,6},{5,7},{6,4},{7,5},{8,10},{9,11},{10,... | collective-permute-start | bytes 36872 | tf_op jit(solution)/shard_map/ppermute | solution.py:74
  133.6 1.5 %collective-permute-start.34 = (f32[24,128]{1,0:T(8,128)S(1)}, f32[24,128]{1,0:T(8,128)S(1)}, u32[]{:S(2)}, u32[]{:S(2)}) collective-permute-start(f32[24,128]{1,0:T(8,128)S(1)} %sum_mirror.1.refs_0_), channel_id=1, source_target_pairs={{0,1},{1,2},{2,3},{3,0},{4,5},{5,6},{6,7},{7,4},{8,9},{9,10},{10,1... | collective-permute-start | bytes 36872 | tf_op jit(solution)/shard_map/ppermute | solution.py:74
  135.1 0.7 collective-permute-done.35.refs_2_
  135.8 0.9 collective-permute-done.34.refs_1_
  136.8 0.9 copy-done.8
  137.9 1.3 slope_sum.1
  139.2 1.5 %collective-permute-start.41 = (f32[1,1024]{1,0:T(1,128)S(1)}, f32[1,1024]{1,0:T(1,128)S(1)}, u32[]{:S(2)}, u32[]{:S(2)}) collective-permute-start(f32[1,1024]{1,0:T(1,128)S(1)} %get-tuple-element.76.refs_0_), channel_id=1, source_target_pairs={{0,4},{4,0},{8,12},{12,8},{1,5},{5,1},{9,13},{13,9},{2,6},{6,2},{1... | collective-permute-start | bytes 12296 | tf_op jit(solution)/shard_map/ppermute | solution.py:545
  140.8 2.8 %finish.1 = (f32[1024,1024]{1,0:T(8,128)}, f32[8,128]{1,0:T(8,128)S(1)}) custom-call(s32[8]{0:T(128)S(1)} %stack.149.refs_7_.refs_1_.refs_0_, f32[1,1024]{1,0:T(1,128)S(1)} %bitcast.52, f32[8,128]{1,0:T(8,128)S(1)} %get-tuple-element.74.refs_2_, bf16[4096,128]{1,0:T(8,128)(2,1)S(1)} %pack_columns.1.refs_3_, bf16[4096,128]{1,0:T(8,128)(2,1)S(1)} %collective-permute-done.40.refs_4_), custom_call_target="tpu_custom_call" | custom-call | bytes 6303776 | tf_op jit(solution)/shard_map/finish/pallas_call | solution.py:56
  143.6 0.6 query_sum.1
  (115 shorter events, 8.3 us)
Async XLA Ops:
  0.6 12.3 %copy-start.25 = (bf16[4096]{0:T(1024)(128)(2,1)S(1)}, bf16[4096]{0:T(1024)(128)(2,1)}, u32[]{:S(2)}) copy-start(bf16[4096]{0:T(1024)(128)(2,1)} %param.12) | copy-start | bytes 24580
  0.6 12.3 %copy-start.24 = (s32[64,32]{0,1:T(8,128)S(1)}, s32[64,32]{0,1:T(8,128)}, u32[]{:S(2)}) copy-start(s32[64,32]{0,1:T(8,128)} %param.10) | copy-start | bytes 24580
  0.7 12.4 %copy-start.26 = (s32[64]{0:T(128)S(1)}, s32[64]{0:T(128)}, u32[]{:S(2)}) copy-start(s32[64]{0:T(128)} %param.11) | copy-start | bytes 772
  1.6 16.2 %collective-permute-start.3 = (bf16[128,1024]{1,0:T(8,128)(2,1)S(1)}, bf16[128,1024]{1,0:T(8,128)(2,1)S(1)}, u32[]{:S(2)}, u32[]{:S(2)}) collective-permute-start(bf16[128,1024]{1,0:T(8,128)(2,1)S(1)} %constant_dynamic-slice_fusion.refs_2_), channel_id=1, source_target_pairs={{0,8},{4,12},{8,0},{12,4},{1,9},{5,13},{9,1},{13,5},{2,10},{6,14},... | collective-permute-start | bytes 786440 | tf_op jit(solution)/shard_map/ppermute | solution.py:548
  5.8 1.6 %copy-start = (bf16[1024,1024]{1,0:T(8,128)(2,1)S(1)}, bf16[1024,1024]{1,0:T(8,128)(2,1)}, u32[]{:S(2)}) copy-start(bf16[1024,1024]{1,0:T(8,128)(2,1)} %refs_1_.5) | copy-start | bytes 6291460
  9.8 11.7 %collective-permute-start.2 = (f32[1,1024]{1,0:T(1,128)S(1)}, f32[1,1024]{1,0:T(1,128)S(1)}, u32[]{:S(2)}, u32[]{:S(2)}) collective-permute-start(f32[1,1024]{1,0:T(1,128)S(1)} %block_u.1), channel_id=1, source_target_pairs={{0,12},{4,0},{8,4},{12,8},{1,13},{5,1},{9,5},{13,9},{2,14},{6,2},{... | collective-permute-start | bytes 12296 | tf_op jit(solution)/shard_map/ppermute | solution.py:74
  11.1 10.3 %collective-permute-start.1 = (f32[1,1024]{1,0:T(1,128)S(1)}, f32[1,1024]{1,0:T(1,128)S(1)}, u32[]{:S(2)}, u32[]{:S(2)}) collective-permute-start(f32[1,1024]{1,0:T(1,128)S(1)} %block_u.1), channel_id=1, source_target_pairs={{0,8},{4,12},{8,0},{12,4},{1,9},{5,13},{9,1},{13,5},{2,10},{6,14},... | collective-permute-start | bytes 12296 | tf_op jit(solution)/shard_map/ppermute | solution.py:74
  12.8 8.1 %collective-permute-start = (f32[1,1024]{1,0:T(1,128)S(1)}, f32[1,1024]{1,0:T(1,128)S(1)}, u32[]{:S(2)}, u32[]{:S(2)}) collective-permute-start(f32[1,1024]{1,0:T(1,128)S(1)} %block_u.1), channel_id=1, source_target_pairs={{0,4},{4,8},{8,12},{12,0},{1,5},{5,9},{9,13},{13,1},{2,6},{6,10},{... | collective-permute-start | bytes 12296 | tf_op jit(solution)/shard_map/ppermute | solution.py:74
  13.7 19.4 %copy-start.23 = (s32[32]{0:T(128)}, s32[32]{0:T(128)S(1)}, u32[]{:S(2)}) copy-start(s32[32]{0:T(128)S(1)} %stack.186.refs_8_.refs_0_) | copy-start | bytes 388
  17.9 15.1 %collective-permute-start.7 = (bf16[128,1024]{1,0:T(8,128)(2,1)S(1)}, bf16[128,1024]{1,0:T(8,128)(2,1)S(1)}, u32[]{:S(2)}, u32[]{:S(2)}) collective-permute-start(bf16[128,1024]{1,0:T(8,128)(2,1)S(1)} %collective-permute-done.3.refs_6_.refs_0_), channel_id=1, source_target_pairs={{0,18},{1,19},{2,16},{3,17},{16,2},{17,3},{18,0},{19,1},{4,22},{5,... | collective-permute-start | bytes 786440 | tf_op jit(solution)/shard_map/ppermute | solution.py:541
  20.4 12.7 %collective-permute-start.6 = (bf16[128,1024]{1,0:T(8,128)(2,1)S(1)}, bf16[128,1024]{1,0:T(8,128)(2,1)S(1)}, u32[]{:S(2)}, u32[]{:S(2)}) collective-permute-start(bf16[128,1024]{1,0:T(8,128)(2,1)S(1)} %collective-permute-done.3.refs_6_.refs_0_), channel_id=1, source_target_pairs={{0,16},{1,17},{2,18},{3,19},{16,0},{17,1},{18,2},{19,3},{4,20},{5,... | collective-permute-start | bytes 786440 | tf_op jit(solution)/shard_map/ppermute | solution.py:541
  20.9 12.1 %collective-permute-start.5 = (bf16[128,1024]{1,0:T(8,128)(2,1)S(1)}, bf16[128,1024]{1,0:T(8,128)(2,1)S(1)}, u32[]{:S(2)}, u32[]{:S(2)}) collective-permute-start(bf16[128,1024]{1,0:T(8,128)(2,1)S(1)} %collective-permute-done.3.refs_6_.refs_0_), channel_id=1, source_target_pairs={{0,2},{1,3},{2,0},{3,1},{16,18},{17,19},{18,16},{19,17},{4,6},{5,7... | collective-permute-start | bytes 786440 | tf_op jit(solution)/shard_map/ppermute | solution.py:541
  33.0 7.5 %copy-start.13 = (f32[1024,1]{1,0:T(8,128)}, f32[1024,1]{1,0:T(8,128)S(1)}, u32[]{:S(2)}) copy-start(f32[1024,1]{1,0:T(8,128)S(1)} %get-tuple-element.51.curve_ref) | copy-start | bytes 12292
  33.0 5.6 %copy-start.4 = (bf16[1024,1024]{1,0:T(8,128)(2,1)S(1)}, bf16[1024,1024]{1,0:T(8,128)(2,1)}, u32[]{:S(2)}) copy-start(bf16[1024,1024]{1,0:T(8,128)(2,1)} %refs_0_.4) | copy-start | bytes 6291460
  33.1 8.9 %copy-start.1 = (bf16[1024,1024]{1,0:T(8,128)(2,1)S(1)}, bf16[1024,1024]{1,0:T(8,128)(2,1)}, u32[]{:S(2)}) copy-start(bf16[1024,1024]{1,0:T(8,128)(2,1)} %refs_1_.5) | copy-start | bytes 6291460
  33.2 8.8 %collective-permute-start.8 = (bf16[512,1024]{1,0:T(8,128)(2,1)S(1)}, bf16[512,1024]{1,0:T(8,128)(2,1)S(1)}, u32[]{:S(2)}, u32[]{:S(2)}) collective-permute-start(bf16[512,1024]{1,0:T(8,128)(2,1)S(1)} %pack_shares.1.refs_5_), channel_id=1, source_target_pairs={{0,1},{1,0},{2,3},{3,2},{16,17},{17,16},{18,19},{19,18},{4,5},{5,4... | collective-permute-start | bytes 3145736 | tf_op jit(solution)/shard_map/ppermute | solution.py:541
  33.2 8.7 %collective-permute-start.4 = (bf16[64,2048]{1,0:T(8,128)(2,1)S(1)}, bf16[64,2048]{1,0:T(8,128)(2,1)S(1)}, u32[]{:S(2)}, u32[]{:S(2)}) collective-permute-start(bf16[64,2048]{1,0:T(8,128)(2,1)S(1)} %get-tuple-element.42), channel_id=1, source_target_pairs={{0,4},{4,0},{8,12},{12,8},{1,5},{5,1},{9,13},{13,9},{2,6},{6,2},{1... | collective-permute-start | bytes 786440 | tf_op jit(solution)/shard_map/ppermute | solution.py:545
  34.1 3.3 %collective-permute-start.9 = (s32[64,8]{1,0:T(8,128)S(1)}, s32[64,8]{1,0:T(8,128)S(1)}, u32[]{:S(2)}, u32[]{:S(2)}) collective-permute-start(s32[64,8]{1,0:T(8,128)S(1)} %get-tuple-element.45), channel_id=1, source_target_pairs={{0,1},{1,2},{2,3},{3,0},{4,5},{5,6},{6,7},{7,4},{8,9},{9,10},{10,1... | collective-permute-start | bytes 6152 | tf_op jit(solution)/shard_map/ppermute | solution.py:74
  34.2 3.9 %collective-permute-start.10 = (s32[64,8]{1,0:T(8,128)S(1)}, s32[64,8]{1,0:T(8,128)S(1)}, u32[]{:S(2)}, u32[]{:S(2)}) collective-permute-start(s32[64,8]{1,0:T(8,128)S(1)} %get-tuple-element.46), channel_id=1, source_target_pairs={{0,2},{1,3},{2,0},{3,1},{4,6},{5,7},{6,4},{7,5},{8,10},{9,11},{10,... | collective-permute-start | bytes 6152 | tf_op jit(solution)/shard_map/ppermute | solution.py:74
  35.8 2.9 %collective-permute-start.11 = (s32[64,8]{1,0:T(8,128)S(1)}, s32[64,8]{1,0:T(8,128)S(1)}, u32[]{:S(2)}, u32[]{:S(2)}) collective-permute-start(s32[64,8]{1,0:T(8,128)S(1)} %get-tuple-element.47), channel_id=1, source_target_pairs={{0,3},{1,0},{2,1},{3,2},{4,7},{5,4},{6,5},{7,6},{8,11},{9,8},{10,9... | collective-permute-start | bytes 6152 | tf_op jit(solution)/shard_map/ppermute | solution.py:74
  43.4 39.0 %copy-start.2 = (bf16[1024,1024]{1,0:T(8,128)(2,1)}, bf16[1024,1024]{1,0:T(8,128)(2,1)S(1)}, u32[]{:S(2)}) copy-start(bf16[1024,1024]{1,0:T(8,128)(2,1)S(1)} %get-tuple-element.49.refs_2_) | copy-start | bytes 6291460
  43.4 7.9 %collective-permute-start.13 = (bf16[128,1024]{1,0:T(8,128)(2,1)S(1)}, bf16[128,1024]{1,0:T(8,128)(2,1)S(1)}, u32[]{:S(2)}, u32[]{:S(2)}) collective-permute-start(bf16[128,1024]{1,0:T(8,128)(2,1)S(1)} %get-tuple-element.55.refs_3_), channel_id=1, source_target_pairs={{0,2},{1,3},{2,0},{3,1},{16,18},{17,19},{18,16},{19,17},{4,6},{5,7... | collective-permute-start | bytes 786440 | tf_op jit(solution)/shard_map/ppermute | solution.py:541
  45.0 5.0 %collective-permute-start.12 = (bf16[64,1024]{1,0:T(8,128)(2,1)S(1)}, bf16[64,1024]{1,0:T(8,128)(2,1)S(1)}, u32[]{:S(2)}, u32[]{:S(2)}) collective-permute-start(bf16[64,1024]{1,0:T(8,128)(2,1)S(1)} %get-tuple-element.53), channel_id=1, source_target_pairs={{0,4},{4,0},{8,12},{12,8},{1,5},{5,1},{9,13},{13,9},{2,6},{6,2},{1... | collective-permute-start | bytes 393224 | tf_op jit(solution)/shard_map/ppermute | solution.py:545
  51.5 11.8 %copy-start.15 = (bf16[256,1024]{1,0:T(8,128)(2,1)}, bf16[256,1024]{1,0:T(8,128)(2,1)S(1)}, u32[]{:S(2)}) copy-start(bf16[256,1024]{1,0:T(8,128)(2,1)S(1)} %get-tuple-element.60.refs_2_) | copy-start | bytes 1572868
  51.5 10.4 %collective-permute-start.17 = (bf16[256,1024]{1,0:T(8,128)(2,1)S(1)}, bf16[256,1024]{1,0:T(8,128)(2,1)S(1)}, u32[]{:S(2)}, u32[]{:S(2)}) collective-permute-start(bf16[256,1024]{1,0:T(8,128)(2,1)S(1)} %get-tuple-element.60.refs_2_), channel_id=1, source_target_pairs={{0,1},{1,0},{2,3},{3,2},{16,17},{17,16},{18,19},{19,18},{4,5},{5,4... | collective-permute-start | bytes 1572872 | tf_op jit(solution)/shard_map/ppermute | solution.py:541
  51.6 14.3 %collective-permute-start.24 = (bf16[256,1024]{1,0:T(8,128)(2,1)S(1)}, bf16[256,1024]{1,0:T(8,128)(2,1)S(1)}, u32[]{:S(2)}, u32[]{:S(2)}) collective-permute-start(bf16[256,1024]{1,0:T(8,128)(2,1)S(1)} %get-tuple-element.60.refs_2_), channel_id=1, source_target_pairs={{0,16},{1,17},{2,18},{3,19},{16,0},{17,1},{18,2},{19,3},{4,20},{5,... | collective-permute-start | bytes 1572872 | tf_op jit(solution)/shard_map/ppermute | solution.py:541
  53.2 5.2 %collective-permute-start.16 = (bf16[64,1024]{1,0:T(8,128)(2,1)S(1)}, bf16[64,1024]{1,0:T(8,128)(2,1)S(1)}, u32[]{:S(2)}, u32[]{:S(2)}) collective-permute-start(bf16[64,1024]{1,0:T(8,128)(2,1)S(1)} %get-tuple-element.58.refs_3_), channel_id=1, source_target_pairs={{0,3},{1,0},{2,1},{3,2},{4,7},{5,4},{6,5},{7,6},{8,11},{9,8},{10,9... | collective-permute-start | bytes 393224 | tf_op jit(solution)/shard_map/ppermute | solution.py:74
  54.4 7.4 %collective-permute-start.15 = (bf16[64,1024]{1,0:T(8,128)(2,1)S(1)}, bf16[64,1024]{1,0:T(8,128)(2,1)S(1)}, u32[]{:S(2)}, u32[]{:S(2)}) collective-permute-start(bf16[64,1024]{1,0:T(8,128)(2,1)S(1)} %get-tuple-element.58.refs_3_), channel_id=1, source_target_pairs={{0,2},{1,3},{2,0},{3,1},{4,6},{5,7},{6,4},{7,5},{8,10},{9,11},{10,... | collective-permute-start | bytes 393224 | tf_op jit(solution)/shard_map/ppermute | solution.py:74
  55.0 6.9 %collective-permute-start.14 = (bf16[64,1024]{1,0:T(8,128)(2,1)S(1)}, bf16[64,1024]{1,0:T(8,128)(2,1)S(1)}, u32[]{:S(2)}, u32[]{:S(2)}) collective-permute-start(bf16[64,1024]{1,0:T(8,128)(2,1)S(1)} %get-tuple-element.58.refs_3_), channel_id=1, source_target_pairs={{0,1},{1,2},{2,3},{3,0},{4,5},{5,6},{6,7},{7,4},{8,9},{9,10},{10,1... | collective-permute-start | bytes 393224 | tf_op jit(solution)/shard_map/ppermute | solution.py:74
  58.3 15.6 %collective-permute-start.22 = (bf16[128,1024]{1,0:T(8,128)(2,1)S(1)}, bf16[128,1024]{1,0:T(8,128)(2,1)S(1)}, u32[]{:S(2)}, u32[]{:S(2)}) collective-permute-start(bf16[128,1024]{1,0:T(8,128)(2,1)S(1)} %get-tuple-element.67), channel_id=1, source_target_pairs={{0,8},{4,12},{8,0},{12,4},{1,9},{5,13},{9,1},{13,5},{2,10},{6,14},... | collective-permute-start | bytes 786440 | tf_op jit(solution)/shard_map/ppermute | solution.py:548
  61.9 20.5 %copy-start.6 = (bf16[256,1024]{1,0:T(8,128)(2,1)}, bf16[256,1024]{1,0:T(8,128)(2,1)S(1)}, u32[]{:S(2)}) copy-start(bf16[256,1024]{1,0:T(8,128)(2,1)S(1)} %collective-permute-done.17.refs_7_.refs_6_) | copy-start | bytes 1572868
  61.9 14.3 %copy-start.16 = (bf16[64,1024]{1,0:T(8,128)(2,1)S(1)}, bf16[64,1024]{1,0:T(8,128)(2,1)}, u32[]{:S(2)}) copy-start(bf16[64,1024]{1,0:T(8,128)(2,1)} %refs_0_.5) | copy-start | bytes 393220
  66.7 15.7 %collective-permute-start.25 = (bf16[256,1024]{1,0:T(8,128)(2,1)S(1)}, bf16[256,1024]{1,0:T(8,128)(2,1)S(1)}, u32[]{:S(2)}, u32[]{:S(2)}) collective-permute-start(bf16[256,1024]{1,0:T(8,128)(2,1)S(1)} %near_far.1), channel_id=1, source_target_pairs={{0,1},{1,0},{2,3},{3,2},{16,17},{17,16},{18,19},{19,18},{4,5},{5,4... | collective-permute-start | bytes 1572872 | tf_op jit(solution)/shard_map/ppermute | solution.py:541
  66.7 7.2 %collective-permute-start.18 = (bf16[64,1152]{1,0:T(8,128)(2,1)S(1)}, bf16[64,1152]{1,0:T(8,128)(2,1)S(1)}, u32[]{:S(2)}, u32[]{:S(2)}) collective-permute-start(bf16[64,1152]{1,0:T(8,128)(2,1)S(1)} %get-tuple-element.62), channel_id=1, source_target_pairs={{0,3},{1,0},{2,1},{3,2},{4,7},{5,4},{6,5},{7,6},{8,11},{9,8},{10,9... | collective-permute-start | bytes 442376 | tf_op jit(solution)/shard_map/ppermute | solution.py:74
  68.4 7.8 %collective-permute-start.19 = (bf16[64,1152]{1,0:T(8,128)(2,1)S(1)}, bf16[64,1152]{1,0:T(8,128)(2,1)S(1)}, u32[]{:S(2)}, u32[]{:S(2)}) collective-permute-start(bf16[64,1152]{1,0:T(8,128)(2,1)S(1)} %get-tuple-element.63), channel_id=1, source_target_pairs={{0,2},{1,3},{2,0},{3,1},{4,6},{5,7},{6,4},{7,5},{8,10},{9,11},{10,... | collective-permute-start | bytes 442376 | tf_op jit(solution)/shard_map/ppermute | solution.py:74
  68.9 7.3 %collective-permute-start.20 = (bf16[64,1152]{1,0:T(8,128)(2,1)S(1)}, bf16[64,1152]{1,0:T(8,128)(2,1)S(1)}, u32[]{:S(2)}, u32[]{:S(2)}) collective-permute-start(bf16[64,1152]{1,0:T(8,128)(2,1)S(1)} %get-tuple-element.64), channel_id=1, source_target_pairs={{0,1},{1,2},{2,3},{3,0},{4,5},{5,6},{6,7},{7,4},{8,9},{9,10},{10,1... | collective-permute-start | bytes 442376 | tf_op jit(solution)/shard_map/ppermute | solution.py:74
  74.0 8.4 %collective-permute-start.23 = (bf16[128,1024]{1,0:T(8,128)(2,1)S(1)}, bf16[128,1024]{1,0:T(8,128)(2,1)S(1)}, u32[]{:S(2)}, u32[]{:S(2)}) collective-permute-start(bf16[128,1024]{1,0:T(8,128)(2,1)S(1)} %other.1.refs_5_), channel_id=1, source_target_pairs={{0,16},{1,17},{2,18},{3,19},{16,0},{17,1},{18,2},{19,3},{4,20},{5,... | collective-permute-start | bytes 786440 | tf_op jit(solution)/shard_map/ppermute | solution.py:541
  76.6 5.0 %collective-permute-start.21 = (bf16[64,1024]{1,0:T(8,128)(2,1)S(1)}, bf16[64,1024]{1,0:T(8,128)(2,1)S(1)}, u32[]{:S(2)}, u32[]{:S(2)}) collective-permute-start(bf16[64,1024]{1,0:T(8,128)(2,1)S(1)} %get-tuple-element.66.refs_3_), channel_id=1, source_target_pairs={{0,4},{4,0},{8,12},{12,8},{1,5},{5,1},{9,13},{13,9},{2,6},{6,2},{1... | collective-permute-start | bytes 393224 | tf_op jit(solution)/shard_map/ppermute | solution.py:545
  82.4 2.2 %copy-start.9 = (bf16[256,1024]{1,0:T(8,128)(2,1)}, bf16[256,1024]{1,0:T(8,128)(2,1)S(1)}, u32[]{:S(2)}) copy-start(bf16[256,1024]{1,0:T(8,128)(2,1)S(1)} %collective-permute-done.25.refs_8_.refs_7_) | copy-start | bytes 1572868
  84.6 7.5 %collective-permute-start.26 = (bf16[64,2048]{1,0:T(8,128)(2,1)S(1)}, bf16[64,2048]{1,0:T(8,128)(2,1)S(1)}, u32[]{:S(2)}, u32[]{:S(2)}) collective-permute-start(bf16[64,2048]{1,0:T(8,128)(2,1)S(1)} %get-tuple-element.69), channel_id=1, source_target_pairs={{0,4},{4,0},{8,12},{12,8},{1,5},{5,1},{9,13},{13,9},{2,6},{6,2},{1... | collective-permute-start | bytes 786440 | tf_op jit(solution)/shard_map/ppermute | solution.py:545
  85.5 23.2 %collective-permute-start.28 = (bf16[256,1024]{1,0:T(8,128)(2,1)}, bf16[256,1024]{1,0:T(8,128)(2,1)S(1)}, u32[]{:S(2)}, u32[]{:S(2)}) collective-permute-start(bf16[256,1024]{1,0:T(8,128)(2,1)} %get-tuple-element.72.refs_4_), channel_id=1, source_target_pairs={{0,2},{1,3},{2,0},{3,1},{16,18},{17,19},{18,16},{19,17},{4,6},{5,7... | collective-permute-start | bytes 1572872 | tf_op jit(solution)/shard_map/ppermute | solution.py:541
  92.9 22.2 %all-to-all-start = ((bf16[32,64,128]{2,1,0:T(8,128)(2,1)}), bf16[32,64,128]{2,1,0:T(8,128)(2,1)}, u32[]{:S(2)}, u32[]{:S(2)}) async-start(bf16[32,64,128]{2,1,0:T(8,128)(2,1)} %copy-done.12), calls=%async_computation | async-start | bytes 1048576 | tf_op jit(solution)/shard_map/all_to_all | solution.py:659
  98.3 16.8 %collective-permute-start.29 = (bf16[256,1024]{1,0:T(8,128)(2,1)}, bf16[256,1024]{1,0:T(8,128)(2,1)}, u32[]{:S(2)}, u32[]{:S(2)}) collective-permute-start(bf16[256,1024]{1,0:T(8,128)(2,1)} %get-tuple-element.72.refs_4_), channel_id=1, source_target_pairs={{0,1},{1,0},{2,3},{3,2},{16,17},{17,16},{18,19},{19,18},{4,5},{5,4... | collective-permute-start | bytes 1572872 | tf_op jit(solution)/shard_map/ppermute | solution.py:541
  98.4 3.4 %copy-start.5 = (bf16[1024,4096]{1,0:T(8,128)(2,1)S(1)}, bf16[1024,4096]{1,0:T(8,128)(2,1)}, u32[]{:S(2)}) copy-start(bf16[1024,4096]{1,0:T(8,128)(2,1)} %get-tuple-element.50.normed_ref) | copy-start | bytes 25165828
  101.8 1.0 copy-start.14
  108.7 6.5 %copy-start.10 = (bf16[256,1024]{1,0:T(8,128)(2,1)}, bf16[256,1024]{1,0:T(8,128)(2,1)S(1)}, u32[]{:S(2)}) copy-start(bf16[256,1024]{1,0:T(8,128)(2,1)S(1)} %collective-permute-done.28.refs_0_.refs_5_) | copy-start | bytes 1572868
  108.8 6.4 %collective-permute-start.30 = (bf16[256,1024]{1,0:T(8,128)(2,1)S(1)}, bf16[256,1024]{1,0:T(8,128)(2,1)}, u32[]{:S(2)}, u32[]{:S(2)}) collective-permute-start(bf16[256,1024]{1,0:T(8,128)(2,1)S(1)} %late.1), channel_id=1, source_target_pairs={{0,1},{1,0},{2,3},{3,2},{16,17},{17,16},{18,19},{19,18},{4,5},{5,4... | collective-permute-start | bytes 1572872 | tf_op jit(solution)/shard_map/ppermute | solution.py:541
  109.3 3.7 %collective-permute-start.31 = (f32[24,128]{1,0:T(8,128)S(1)}, f32[24,128]{1,0:T(8,128)S(1)}, u32[]{:S(2)}, u32[]{:S(2)}) collective-permute-start(f32[24,128]{1,0:T(8,128)S(1)} %get-tuple-element.73.refs_0_), channel_id=1, source_target_pairs={{0,16},{16,0},{1,17},{17,1},{2,18},{18,2},{3,19},{19,3},{4,20},{20... | collective-permute-start | bytes 36872 | tf_op jit(solution)/shard_map/ppermute | solution.py:74
  110.8 3.7 %collective-permute-start.27 = (f32[24,128]{1,0:T(8,128)S(1)}, f32[24,128]{1,0:T(8,128)S(1)}, u32[]{:S(2)}, u32[]{:S(2)}) collective-permute-start(f32[24,128]{1,0:T(8,128)S(1)} %get-tuple-element.70.refs_0_.refs_1_), channel_id=1, source_target_pairs={{0,16},{16,0},{1,17},{17,1},{2,18},{18,2},{3,19},{19,3},{4,20},{20... | collective-permute-start | bytes 36872 | tf_op jit(solution)/shard_map/ppermute | solution.py:74
  115.1 7.7 %copy-start.18 = (f32[24,128]{1,0:T(8,128)S(1)}, f32[24,128]{1,0:T(8,128)}, u32[]{:S(2)}) copy-start(f32[24,128]{1,0:T(8,128)} %copy-done.17) | copy-start | bytes 36868
  115.2 10.2 %copy-start.20 = (f32[24,128]{1,0:T(8,128)S(1)}, f32[24,128]{1,0:T(8,128)}, u32[]{:S(2)}) copy-start(f32[24,128]{1,0:T(8,128)} %copy-done.19) | copy-start | bytes 36868
  119.3 18.6 %copy-start.3 = (bf16[1024,1024]{1,0:T(8,128)(2,1)S(1)}, bf16[1024,1024]{1,0:T(8,128)(2,1)}, u32[]{:S(2)}) copy-start(bf16[1024,1024]{1,0:T(8,128)(2,1)} %copy-done.2) | copy-start | bytes 6291460
  119.3 17.4 %collective-permute-start.39 = (bf16[1024,128]{1,0:T(8,128)(2,1)}, bf16[1024,128]{1,0:T(8,128)(2,1)S(1)}, u32[]{:S(2)}, u32[]{:S(2)}) collective-permute-start(bf16[1024,128]{1,0:T(8,128)(2,1)} %grad_columns.1.refs_1_.refs_0_), channel_id=1, source_target_pairs={{0,18},{1,19},{2,16},{3,17},{16,2},{17,3},{18,0},{19,1},{4,22},{5,... | collective-permute-start | bytes 786440 | tf_op jit(solution)/shard_map/ppermute | solution.py:541
  120.9 15.9 %collective-permute-start.38 = (bf16[1024,128]{1,0:T(8,128)(2,1)}, bf16[1024,128]{1,0:T(8,128)(2,1)S(1)}, u32[]{:S(2)}, u32[]{:S(2)}) collective-permute-start(bf16[1024,128]{1,0:T(8,128)(2,1)} %grad_columns.1.refs_1_.refs_0_), channel_id=1, source_target_pairs={{0,16},{1,17},{2,18},{3,19},{16,0},{17,1},{18,2},{19,3},{4,20},{5,... | collective-permute-start | bytes 786440 | tf_op jit(solution)/shard_map/ppermute | solution.py:541
  122.3 14.5 %collective-permute-start.37 = (bf16[1024,128]{1,0:T(8,128)(2,1)}, bf16[1024,128]{1,0:T(8,128)(2,1)S(1)}, u32[]{:S(2)}, u32[]{:S(2)}) collective-permute-start(bf16[1024,128]{1,0:T(8,128)(2,1)} %grad_columns.1.refs_1_.refs_0_), channel_id=1, source_target_pairs={{0,2},{1,3},{2,0},{3,1},{16,18},{17,19},{18,16},{19,17},{4,6},{5,7... | collective-permute-start | bytes 786440 | tf_op jit(solution)/shard_map/ppermute | solution.py:541
  122.8 1.0 copy-start.7
  123.8 3.7 %collective-permute-start.32 = (f32[24,128]{1,0:T(8,128)S(1)}, f32[24,128]{1,0:T(8,128)S(1)}, u32[]{:S(2)}, u32[]{:S(2)}) collective-permute-start(f32[24,128]{1,0:T(8,128)S(1)} %slope_out.3), channel_id=1, source_target_pairs={{0,4},{4,0},{8,12},{12,8},{1,5},{5,1},{9,13},{13,9},{2,6},{6,2},{1... | collective-permute-start | bytes 36872 | tf_op jit(solution)/shard_map/ppermute | solution.py:545
  127.5 4.6 %collective-permute-start.33 = (f32[24,128]{1,0:T(8,128)S(1)}, f32[24,128]{1,0:T(8,128)S(1)}, u32[]{:S(2)}, u32[]{:S(2)}) collective-permute-start(f32[24,128]{1,0:T(8,128)S(1)} %sum_half.1.refs_0_), channel_id=1, source_target_pairs={{0,8},{4,12},{8,0},{12,4},{1,9},{5,13},{9,1},{13,5},{2,10},{6,14},... | collective-permute-start | bytes 36872 | tf_op jit(solution)/shard_map/ppermute | solution.py:548
  132.1 1.5 %collective-permute-start.36 = (f32[24,128]{1,0:T(8,128)S(1)}, f32[24,128]{1,0:T(8,128)S(1)}, u32[]{:S(2)}, u32[]{:S(2)}) collective-permute-start(f32[24,128]{1,0:T(8,128)S(1)} %sum_mirror.1.refs_0_), channel_id=1, source_target_pairs={{0,3},{1,0},{2,1},{3,2},{4,7},{5,4},{6,5},{7,6},{8,11},{9,8},{10,9... | collective-permute-start | bytes 36872 | tf_op jit(solution)/shard_map/ppermute | solution.py:74
  132.1 3.7 %collective-permute-start.35 = (f32[24,128]{1,0:T(8,128)S(1)}, f32[24,128]{1,0:T(8,128)S(1)}, u32[]{:S(2)}, u32[]{:S(2)}) collective-permute-start(f32[24,128]{1,0:T(8,128)S(1)} %sum_mirror.1.refs_0_), channel_id=1, source_target_pairs={{0,2},{1,3},{2,0},{3,1},{4,6},{5,7},{6,4},{7,5},{8,10},{9,11},{10,... | collective-permute-start | bytes 36872 | tf_op jit(solution)/shard_map/ppermute | solution.py:74
  133.6 3.1 %collective-permute-start.34 = (f32[24,128]{1,0:T(8,128)S(1)}, f32[24,128]{1,0:T(8,128)S(1)}, u32[]{:S(2)}, u32[]{:S(2)}) collective-permute-start(f32[24,128]{1,0:T(8,128)S(1)} %sum_mirror.1.refs_0_), channel_id=1, source_target_pairs={{0,1},{1,2},{2,3},{3,0},{4,5},{5,6},{6,7},{7,4},{8,9},{9,10},{10,1... | collective-permute-start | bytes 36872 | tf_op jit(solution)/shard_map/ppermute | solution.py:74
  137.8 2.9 %copy-start.22 = (f32[1024]{0:T(1024)S(1)}, f32[1024]{0:T(1024)}, u32[]{:S(2)}) copy-start(f32[1024]{0:T(1024)} %param.14) | copy-start | bytes 12292
  137.8 2.9 %collective-permute-start.40 = (bf16[4096,128]{1,0:T(8,128)(2,1)S(1)}, bf16[4096,128]{1,0:T(8,128)(2,1)S(1)}, u32[]{:S(2)}, u32[]{:S(2)}) collective-permute-start(bf16[4096,128]{1,0:T(8,128)(2,1)S(1)} %pack_columns.1.refs_3_), channel_id=1, source_target_pairs={{0,1},{1,0},{2,3},{3,2},{16,17},{17,16},{18,19},{19,18},{4,5},{5,4... | collective-permute-start | bytes 3145736 | tf_op jit(solution)/shard_map/ppermute | solution.py:541
  139.2 4.4 %collective-permute-start.41 = (f32[1,1024]{1,0:T(1,128)S(1)}, f32[1,1024]{1,0:T(1,128)S(1)}, u32[]{:S(2)}, u32[]{:S(2)}) collective-permute-start(f32[1,1024]{1,0:T(1,128)S(1)} %get-tuple-element.76.refs_0_), channel_id=1, source_target_pairs={{0,4},{4,0},{8,12},{12,8},{1,5},{5,1},{9,13},{13,9},{2,6},{6,2},{1... | collective-permute-start | bytes 12296 | tf_op jit(solution)/shard_map/ppermute | solution.py:545
  (6 other events, 4.4 us)

commit v9 on v8

--- a/solution.py
+++ b/solution.py
@@ -157,7 +157,7 @@
 def gate_rows(z, states, gain, u, token_lengths, lists, events, seq, root, blocks, owners):
     tokens, width = states.shape
     queries = tokens // seq
-    group = 16 if queries % 16 == 0 else queries
+    group = 8 if queries % 8 == 0 else queries
     step_tokens = group * seq
     half = blocks // 2
     outs = [shape((queries, width // half), BF16)] * half

time: 146 us -> 148 us (1.014)
  Pallas kernels: 35.7 us -> 37.5 us
    pallas_call x1, Pallas kernels: 11.6 us -> 13.4 us  [gate_rows(): pl.pallas_call(run, grid=(queries // group,), out_shape=outs, in_specs=[S...]
  transfers between devices with their start and end apart: 43 -> 43, of which waited for: 21 -> 21; matrix products, arithmetic and copies ran while one was open for 1% -> 1% of each run, Pallas kernels for 19% -> 20%
where the time goes in v9:
time: 148 us; the launch traced here: 147 us
  starting transfers between devices  49.4 us (33%)
  waiting for transfers between devices  44.7 us (30%)
  Pallas kernels  37.5 us (25%)
  local copies, waits for them, and re-layouts  13.2 us (9%)
  between operations  2.34 us (2%)
    pallas_call x23, Pallas kernels, call(): pl.pallas_call(run, out_shape=outs, in_specs=[SMEM] * smem + [pl.BlockSpe...  18.1 us
    ppermute x6, waiting for transfers between devices, half_shift(): return lax.ppermute(values, 'fsdp', pairs)  17.4 us
    ppermute x17, starting transfers between devices, shift(): return lax.ppermute(values, axis, [(i, (i + k) % n) for i in range(n)])  15 us
    pallas_call x1, Pallas kernels, gate_rows(): pl.pallas_call(run, grid=(queries // group,), out_shape=outs, in_specs=[S...  13.4 us
    ppermute x16, starting transfers between devices, plane_shift(): return lax.ppermute(values, PLANE, pairs)  12.8 us
    unnamed x55, local copies, waits for them, and re-layouts  11.6 us
    ppermute x3, waiting for transfers between devices, mirror_shift(): lax.ppermute(values, 'fsdp', [(a, (a + half) % n_z) for a in range(n_z)])  11.5 us
    ppermute x17, waiting for transfers between devices, shift(): return lax.ppermute(values, axis, [(i, (i + k) % n) for i in range(n)])  11.2 us
  transfers between devices with their start and end apart: 43, of which 21 were waited for; matrix products, arithmetic and copies ran while one was open for 1% of the time, Pallas kernels for 20%

profile of v9, /device:TPU:0, one launch (start us, length us, event | category | flops | bytes accessed | tf_op | source)
XLA Modules:
  0.0 147.1 jit_solution(9692264210153230577)
XLA Ops:
  0.7 1.0 constant_dynamic-slice_fusion.refs_2_
  1.6 4.1 %collective-permute-start.3 = (bf16[128,1024]{1,0:T(8,128)(2,1)S(1)}, bf16[128,1024]{1,0:T(8,128)(2,1)S(1)}, u32[]{:S(2)}, u32[]{:S(2)}) collective-permute-start(bf16[128,1024]{1,0:T(8,128)(2,1)S(1)} %constant_dynamic-slice_fusion.refs_2_), channel_id=1, source_target_pairs={{0,8},{4,12},{8,0},{12,4},{1,9},{5,13},{9,1},{13,5},{2,10},{6,14},... | collective-permute-start | bytes 786440 | tf_op jit(solution)/shard_map/ppermute | solution.py:548
  5.8 1.6 %copy-done = bf16[1024,1024]{1,0:T(8,128)(2,1)S(1)} copy-done((bf16[1024,1024]{1,0:T(8,128)(2,1)S(1)}, bf16[1024,1024]{1,0:T(8,128)(2,1)}, u32[]{:S(2)}) %copy-start) | copy-done | bytes 2097176
  7.3 0.7 copy-done.21
  8.0 1.7 %block_u.1 = f32[1,1024]{1,0:T(1,128)S(1)} custom-call(bf16[1024,1024]{1,0:T(8,128)(2,1)S(1)} %copy-done, f32[1,1024]{1,0:T(1,128)S(1)} %bitcast.51, bf16[128,1024]{1,0:T(8,128)(2,1)S(1)} %constant_dynamic-slice_fusion.refs_2_), custom_call_target="tpu_custom_call" | custom-call | bytes 2105344 | tf_op jit(solution)/shard_map/block_u/pallas_call | solution.py:56
  9.8 1.4 collective-permute-start.2
  11.1 1.7 %collective-permute-start.1 = (f32[1,1024]{1,0:T(1,128)S(1)}, f32[1,1024]{1,0:T(1,128)S(1)}, u32[]{:S(2)}, u32[]{:S(2)}) collective-permute-start(f32[1,1024]{1,0:T(1,128)S(1)} %block_u.1), channel_id=1, source_target_pairs={{0,8},{4,12},{8,0},{12,4},{1,9},{5,13},{9,1},{13,5},{2,10},{6,14},... | collective-permute-start | bytes 12296 | tf_op jit(solution)/shard_map/ppermute | solution.py:74
  13.7 4.2 %collective-permute-done.3.refs_6_.refs_0_ = bf16[128,1024]{1,0:T(8,128)(2,1)S(1)} collective-permute-done((bf16[128,1024]{1,0:T(8,128)(2,1)S(1)}, bf16[128,1024]{1,0:T(8,128)(2,1)S(1)}, u32[]{:S(2)}, u32[]{:S(2)}) %collective-permute-start.3) | collective-permute-done | bytes 262176 | tf_op jit(solution)/shard_map/ppermute | solution.py:548
  17.9 2.5 %collective-permute-start.7 = (bf16[128,1024]{1,0:T(8,128)(2,1)S(1)}, bf16[128,1024]{1,0:T(8,128)(2,1)S(1)}, u32[]{:S(2)}, u32[]{:S(2)}) collective-permute-start(bf16[128,1024]{1,0:T(8,128)(2,1)S(1)} %collective-permute-done.3.refs_6_.refs_0_), channel_id=1, source_target_pairs={{0,18},{1,19},{2,16},{3,17},{16,2},{17,3},{18,0},{19,1},{4,22},{5,... | collective-permute-start | bytes 786440 | tf_op jit(solution)/shard_map/ppermute | solution.py:541
  21.4 13.4 %gate_rows.1 = (bf16[64,2048]{1,0:T(8,128)(2,1)S(1)}, bf16[64,2048]{1,0:T(8,128)(2,1)S(1)}, bf16[1024,4096]{1,0:T(8,128)(2,1)}, f32[1024,1]{1,0:T(8,128)S(1)}, f...) custom-call(s32[2]{0:T(128)S(1)} %pad_add_fusion.refs_0_.z_ref, ...), custom_call_target="tpu_custom_call" | custom-call | flops 41943040 | bytes 16777216 | tf_op jit(solution)/shard_map/gate_rows/pallas_call | solution.py:174
  35.0 0.8 collective-permute-start.4
  36.0 1.5 %collective-permute-start.10 = (s32[64,8]{1,0:T(8,128)S(1)}, s32[64,8]{1,0:T(8,128)S(1)}, u32[]{:S(2)}, u32[]{:S(2)}) collective-permute-start(s32[64,8]{1,0:T(8,128)S(1)} %get-tuple-element.46), channel_id=1, source_target_pairs={{0,2},{1,3},{2,0},{3,1},{4,6},{5,7},{6,4},{7,5},{8,10},{9,11},{10,... | collective-permute-start | bytes 6152 | tf_op jit(solution)/shard_map/ppermute | solution.py:74
  37.5 1.3 collective-permute-start.11
  39.2 0.7 collective-permute-done.10.refs_4_
  40.4 1.8 %list_counts.1 = (f32[256,1024]{1,0:T(8,128)S(1)}, f32[1,1024]{1,0:T(1,128)S(1)}) custom-call(s32[1]{0:T(128)} %bitcast.46.refs_9_.refs_0_, bf16[1024,1024]{1,0:T(8,128)(2,1)S(1)} %copy-done.4, s32[64,8]{1,0:T(8,128)S(1)} %get-tuple-element.44.refs_2_, s32[64,8]{1,0:T(8,128)S(1)} %collective-permute-done.9.refs_3_, ...), custom_call_target="tpu_custom_call" | custom-call | bytes 3158020 | tf_op jit(solution)/shard_map/list_counts/pallas_call | solution.py:56
  42.3 1.5 collective-permute-done.4.refs_4_
  43.7 1.4 forward.1
  45.2 1.6 %collective-permute-start.13 = (bf16[128,1024]{1,0:T(8,128)(2,1)S(1)}, bf16[128,1024]{1,0:T(8,128)(2,1)S(1)}, u32[]{:S(2)}, u32[]{:S(2)}) collective-permute-start(bf16[128,1024]{1,0:T(8,128)(2,1)S(1)} %get-tuple-element.55.refs_3_), channel_id=1, source_target_pairs={{0,2},{1,3},{2,0},{3,1},{16,18},{17,19},{18,16},{19,17},{4,6},{5,7... | collective-permute-start | bytes 786440 | tf_op jit(solution)/shard_map/ppermute | solution.py:541
  46.8 0.7 collective-permute-start.12
  47.5 4.3 %collective-permute-done.12.refs_1_ = bf16[64,1024]{1,0:T(8,128)(2,1)S(1)} collective-permute-done((bf16[64,1024]{1,0:T(8,128)(2,1)S(1)}, bf16[64,1024]{1,0:T(8,128)(2,1)S(1)}, u32[]{:S(2)}, u32[]{:S(2)}) %collective-permute-start.12) | collective-permute-done | bytes 131104 | tf_op jit(solution)/shard_map/ppermute | solution.py:545
  51.8 1.3 collective-permute-done.13.refs_4_
  53.3 1.6 %collective-permute-start.24 = (bf16[256,1024]{1,0:T(8,128)(2,1)S(1)}, bf16[256,1024]{1,0:T(8,128)(2,1)S(1)}, u32[]{:S(2)}, u32[]{:S(2)}) collective-permute-start(bf16[256,1024]{1,0:T(8,128)(2,1)S(1)} %get-tuple-element.60.refs_2_), channel_id=1, source_target_pairs={{0,16},{1,17},{2,18},{3,19},{16,0},{17,1},{18,2},{19,3},{4,20},{5,... | collective-permute-start | bytes 1572872 | tf_op jit(solution)/shard_map/ppermute | solution.py:541
  54.9 1.3 collective-permute-start.16
  56.7 3.4 %collective-permute-done.16.refs_6_ = bf16[64,1024]{1,0:T(8,128)(2,1)S(1)} collective-permute-done((bf16[64,1024]{1,0:T(8,128)(2,1)S(1)}, bf16[64,1024]{1,0:T(8,128)(2,1)S(1)}, u32[]{:S(2)}, u32[]{:S(2)}) %collective-permute-start.16) | collective-permute-done | bytes 131104 | tf_op jit(solution)/shard_map/ppermute | solution.py:74
  60.1 3.2 %collective-permute-start.22 = (bf16[128,1024]{1,0:T(8,128)(2,1)S(1)}, bf16[128,1024]{1,0:T(8,128)(2,1)S(1)}, u32[]{:S(2)}, u32[]{:S(2)}) collective-permute-start(bf16[128,1024]{1,0:T(8,128)(2,1)S(1)} %get-tuple-element.67), channel_id=1, source_target_pairs={{0,8},{4,12},{8,0},{12,4},{1,9},{5,13},{9,1},{13,5},{2,10},{6,14},... | collective-permute-start | bytes 786440 | tf_op jit(solution)/shard_map/ppermute | solution.py:548
  63.7 1.4 contrast.1
  65.1 2.6 %collective-permute-done.24.refs_0_.refs_3_ = bf16[256,1024]{1,0:T(8,128)(2,1)S(1)} collective-permute-done((bf16[256,1024]{1,0:T(8,128)(2,1)S(1)}, bf16[256,1024]{1,0:T(8,128)(2,1)S(1)}, u32[]{:S(2)}, u32[]{:S(2)}) %collective-permute-start.24) | collective-permute-done | bytes 524320 | tf_op jit(solution)/shard_map/ppermute | solution.py:541
  67.7 0.8 copy-done.11
  68.5 1.7 %collective-permute-start.18 = (bf16[64,1152]{1,0:T(8,128)(2,1)S(1)}, bf16[64,1152]{1,0:T(8,128)(2,1)S(1)}, u32[]{:S(2)}, u32[]{:S(2)}) collective-permute-start(bf16[64,1152]{1,0:T(8,128)(2,1)S(1)} %get-tuple-element.62), channel_id=1, source_target_pairs={{0,3},{1,0},{2,1},{3,2},{4,7},{5,4},{6,5},{7,6},{8,11},{9,8},{10,9... | collective-permute-start | bytes 442376 | tf_op jit(solution)/shard_map/ppermute | solution.py:74
  70.7 5.1 %collective-permute-done.22.refs_0_ = bf16[128,1024]{1,0:T(8,128)(2,1)S(1)} collective-permute-done((bf16[128,1024]{1,0:T(8,128)(2,1)S(1)}, bf16[128,1024]{1,0:T(8,128)(2,1)S(1)}, u32[]{:S(2)}, u32[]{:S(2)}) %collective-permute-start.22) | collective-permute-done | bytes 262176 | tf_op jit(solution)/shard_map/ppermute | solution.py:548
  76.4 1.6 %collective-permute-done.19.refs_6_ = bf16[64,1152]{1,0:T(8,128)(2,1)S(1)} collective-permute-done((bf16[64,1152]{1,0:T(8,128)(2,1)S(1)}, bf16[64,1152]{1,0:T(8,128)(2,1)S(1)}, u32[]{:S(2)}, u32[]{:S(2)}) %collective-permute-start.19) | collective-permute-done | bytes 147488 | tf_op jit(solution)/shard_map/ppermute | solution.py:74
  78.4 1.2 collective-permute-start.21
  79.6 3.9 %collective-permute-done.21.refs_4_ = bf16[64,1024]{1,0:T(8,128)(2,1)S(1)} collective-permute-done((bf16[64,1024]{1,0:T(8,128)(2,1)S(1)}, bf16[64,1024]{1,0:T(8,128)(2,1)S(1)}, u32[]{:S(2)}, u32[]{:S(2)}) %collective-permute-start.21) | collective-permute-done | bytes 131104 | tf_op jit(solution)/shard_map/ppermute | solution.py:545
  83.5 0.7 collective-permute-done.23.refs_6_
  84.2 2.2 %backward.1 = (bf16[64,2048]{1,0:T(8,128)(2,1)S(1)}, bf16[64,2048]{1,0:T(8,128)(2,1)S(1)}, bf16[256,1024]{1,0:T(8,128)(2,1)}) custom-call(s32[1]{0:T(128)} %bitcast.9.refs_10_.refs_0_, bf16[1024,1024]{1,0:T(8,128)(2,1)S(1)} %copy-done.1, bf16[1024,1024]{1,0:T(8,128)(2,1)S(1)} %get-tuple-element.49.refs_2_, bf16[64,1024]{1,0:T(8,128)(2,1)S(1)} %get-tuple-element.66.refs_3_, ...), custom_call_target="tpu_custom_call" | custom-call | flops 536870912 | bytes 6029316 | tf_op jit(solution)/shard_map/backward/pallas_call | solution.py:56
  86.4 0.9 collective-permute-start.26
  87.3 1.1 collective-permute-start.28
  88.3 5.5 %collective-permute-done.26.rest_1_.refs_1_ = bf16[64,2048]{1,0:T(8,128)(2,1)S(1)} collective-permute-done((bf16[64,2048]{1,0:T(8,128)(2,1)S(1)}, bf16[64,2048]{1,0:T(8,128)(2,1)S(1)}, u32[]{:S(2)}, u32[]{:S(2)}) %collective-permute-start.26) | collective-permute-done | bytes 262176 | tf_op jit(solution)/shard_map/ppermute | solution.py:545
  93.9 0.8 copy-done.12
  94.7 5.4 %all-to-all-start = ((bf16[32,64,128]{2,1,0:T(8,128)(2,1)}), bf16[32,64,128]{2,1,0:T(8,128)(2,1)}, u32[]{:S(2)}, u32[]{:S(2)}) async-start(bf16[32,64,128]{2,1,0:T(8,128)(2,1)} %copy-done.12), calls=%async_computation | async-start | bytes 1048576 | tf_op jit(solution)/shard_map/all_to_all | solution.py:659
  100.2 3.4 %copy-done.5 = bf16[1024,4096]{1,0:T(8,128)(2,1)S(1)} copy-done((bf16[1024,4096]{1,0:T(8,128)(2,1)S(1)}, bf16[1024,4096]{1,0:T(8,128)(2,1)}, u32[]{:S(2)}) %copy-start.5) | copy-done | bytes 8388632
  103.6 1.0 copy-done.14
  104.6 5.9 %slope_rows.1 = (f32[24,128]{1,0:T(8,128)S(1)}, f32[24,128]{1,0:T(8,128)S(1)}) custom-call(s32[2]{0:T(128)S(1)} %pad_add_fusion.refs_0_.z_ref, bf16[1024,4096]{1,0:T(8,128)(2,1)S(1)} %copy-done.5, f32[1024,1]{1,0:T(8,128)S(1)} %copy-done.14, f32[1,128]{1,0:T(1,128)S(1)} %get-tuple-element.65.loss_ref, bf16[64,2048]{1,0:T(8,128)(2,1)S(1)} %get-tuple-element.68.rest_0_, ...), custom_call_target="tpu_custom_call" | custom-call | flops 16777216 | bytes 8388608 | tf_op jit(solution)/shard_map/slope_rows/pallas_call | solution.py:431
  111.1 1.5 %collective-permute-start.31 = (f32[24,128]{1,0:T(8,128)S(1)}, f32[24,128]{1,0:T(8,128)S(1)}, u32[]{:S(2)}, u32[]{:S(2)}) collective-permute-start(f32[24,128]{1,0:T(8,128)S(1)} %get-tuple-element.73.refs_0_), channel_id=1, source_target_pairs={{0,16},{16,0},{1,17},{17,1},{2,18},{18,2},{3,19},{19,3},{4,20},{20... | collective-permute-start | bytes 36872 | tf_op jit(solution)/shard_map/ppermute | solution.py:74
  113.1 1.7 %collective-permute-done.31.refs_1_ = f32[24,128]{1,0:T(8,128)S(1)} collective-permute-done((f32[24,128]{1,0:T(8,128)S(1)}, f32[24,128]{1,0:T(8,128)S(1)}, u32[]{:S(2)}, u32[]{:S(2)}) %collective-permute-start.31) | collective-permute-done | bytes 12320 | tf_op jit(solution)/shard_map/ppermute | solution.py:74
  114.8 0.6 copy-done.17
  115.4 0.9 collective-permute-done.27.refs_1_
  117.0 4.1 %grad_columns.1.refs_1_.refs_0_ = bf16[1024,128]{1,0:T(8,128)(2,1)} custom-call(s32[32]{0:T(128)} %copy-done.23, bf16[32,64,128]{2,1,0:T(8,128)(2,1)} %all-to-all-done.refs_1_, bf16[256,1024]{1,0:T(8,128)(2,1)} %copy-done.15, bf16[256,1024]{1,0:T(8,128)(2,1)} %copy-done.11, bf16[256,1024]{1,0:T(8,128)(2,1)} %get-tuple-element.72.refs_4_, ...), custom_call_target="tpu_custom_call" | custom-call | flops 536870912 | bytes 4980864 | tf_op jit(solution)/shard_map/grad_columns/pallas_call | solution.py:56
  121.1 1.6 %collective-permute-start.39 = (bf16[1024,128]{1,0:T(8,128)(2,1)}, bf16[1024,128]{1,0:T(8,128)(2,1)S(1)}, u32[]{:S(2)}, u32[]{:S(2)}) collective-permute-start(bf16[1024,128]{1,0:T(8,128)(2,1)} %grad_columns.1.refs_1_.refs_0_), channel_id=1, source_target_pairs={{0,18},{1,19},{2,16},{3,17},{16,2},{17,3},{18,0},{19,1},{4,22},{5,... | collective-permute-start | bytes 786440 | tf_op jit(solution)/shard_map/ppermute | solution.py:541
  122.7 1.4 collective-permute-start.38
  124.6 1.0 copy-done.7
  125.6 1.5 collective-permute-start.32
  127.1 2.2 %collective-permute-done.32.refs_1_ = f32[24,128]{1,0:T(8,128)S(1)} collective-permute-done((f32[24,128]{1,0:T(8,128)S(1)}, f32[24,128]{1,0:T(8,128)S(1)}, u32[]{:S(2)}, u32[]{:S(2)}) %collective-permute-start.32) | collective-permute-done | bytes 12320 | tf_op jit(solution)/shard_map/ppermute | solution.py:545
  129.3 2.4 %collective-permute-start.33 = (f32[24,128]{1,0:T(8,128)S(1)}, f32[24,128]{1,0:T(8,128)S(1)}, u32[]{:S(2)}, u32[]{:S(2)}) collective-permute-start(f32[24,128]{1,0:T(8,128)S(1)} %sum_half.1.refs_0_), channel_id=1, source_target_pairs={{0,8},{4,12},{8,0},{12,4},{1,9},{5,13},{9,1},{13,5},{2,10},{6,14},... | collective-permute-start | bytes 36872 | tf_op jit(solution)/shard_map/ppermute | solution.py:548
  131.8 2.2 %collective-permute-done.33.refs_1_ = f32[24,128]{1,0:T(8,128)S(1)} collective-permute-done((f32[24,128]{1,0:T(8,128)S(1)}, f32[24,128]{1,0:T(8,128)S(1)}, u32[]{:S(2)}, u32[]{:S(2)}) %collective-permute-start.33) | collective-permute-done | bytes 12320 | tf_op jit(solution)/shard_map/ppermute | solution.py:548
  133.9 1.5 collective-permute-start.35
  135.4 1.5 %collective-permute-start.34 = (f32[24,128]{1,0:T(8,128)S(1)}, f32[24,128]{1,0:T(8,128)S(1)}, u32[]{:S(2)}, u32[]{:S(2)}) collective-permute-start(f32[24,128]{1,0:T(8,128)S(1)} %sum_mirror.1.refs_0_), channel_id=1, source_target_pairs={{0,1},{1,2},{2,3},{3,0},{4,5},{5,6},{6,7},{7,4},{8,9},{9,10},{10,1... | collective-permute-start | bytes 36872 | tf_op jit(solution)/shard_map/ppermute | solution.py:74
  136.9 0.7 collective-permute-done.35.refs_2_
  137.6 0.9 collective-permute-done.34.refs_1_
  138.6 0.9 copy-done.8
  139.7 1.3 slope_sum.1
  141.0 1.5 %collective-permute-start.41 = (f32[1,1024]{1,0:T(1,128)S(1)}, f32[1,1024]{1,0:T(1,128)S(1)}, u32[]{:S(2)}, u32[]{:S(2)}) collective-permute-start(f32[1,1024]{1,0:T(1,128)S(1)} %get-tuple-element.76.refs_0_), channel_id=1, source_target_pairs={{0,4},{4,0},{8,12},{12,8},{1,5},{5,1},{9,13},{13,9},{2,6},{6,2},{1... | collective-permute-start | bytes 12296 | tf_op jit(solution)/shard_map/ppermute | solution.py:545
  142.6 2.8 %finish.1 = (f32[1024,1024]{1,0:T(8,128)}, f32[8,128]{1,0:T(8,128)S(1)}) custom-call(s32[8]{0:T(128)S(1)} %stack.149.refs_7_.refs_1_.refs_0_, f32[1,1024]{1,0:T(1,128)S(1)} %bitcast.52, f32[8,128]{1,0:T(8,128)S(1)} %get-tuple-element.74.refs_2_, bf16[4096,128]{1,0:T(8,128)(2,1)S(1)} %pack_columns.1.refs_3_, bf16[4096,128]{1,0:T(8,128)(2,1)S(1)} %collective-permute-done.40.refs_4_), custom_call_target="tpu_custom_call" | custom-call | bytes 6303776 | tf_op jit(solution)/shard_map/finish/pallas_call | solution.py:56
  145.4 0.6 query_sum.1
  (115 shorter events, 8.3 us)
Async XLA Ops:
  0.6 12.3 %copy-start.25 = (bf16[4096]{0:T(1024)(128)(2,1)S(1)}, bf16[4096]{0:T(1024)(128)(2,1)}, u32[]{:S(2)}) copy-start(bf16[4096]{0:T(1024)(128)(2,1)} %param.12) | copy-start | bytes 24580
  0.6 12.3 %copy-start.24 = (s32[64,32]{0,1:T(8,128)S(1)}, s32[64,32]{0,1:T(8,128)}, u32[]{:S(2)}) copy-start(s32[64,32]{0,1:T(8,128)} %param.10) | copy-start | bytes 24580
  0.7 12.4 %copy-start.26 = (s32[64]{0:T(128)S(1)}, s32[64]{0:T(128)}, u32[]{:S(2)}) copy-start(s32[64]{0:T(128)} %param.11) | copy-start | bytes 772
  1.6 16.2 %collective-permute-start.3 = (bf16[128,1024]{1,0:T(8,128)(2,1)S(1)}, bf16[128,1024]{1,0:T(8,128)(2,1)S(1)}, u32[]{:S(2)}, u32[]{:S(2)}) collective-permute-start(bf16[128,1024]{1,0:T(8,128)(2,1)S(1)} %constant_dynamic-slice_fusion.refs_2_), channel_id=1, source_target_pairs={{0,8},{4,12},{8,0},{12,4},{1,9},{5,13},{9,1},{13,5},{2,10},{6,14},... | collective-permute-start | bytes 786440 | tf_op jit(solution)/shard_map/ppermute | solution.py:548
  5.8 1.6 %copy-start = (bf16[1024,1024]{1,0:T(8,128)(2,1)S(1)}, bf16[1024,1024]{1,0:T(8,128)(2,1)}, u32[]{:S(2)}) copy-start(bf16[1024,1024]{1,0:T(8,128)(2,1)} %refs_1_.5) | copy-start | bytes 6291460
  9.8 11.7 %collective-permute-start.2 = (f32[1,1024]{1,0:T(1,128)S(1)}, f32[1,1024]{1,0:T(1,128)S(1)}, u32[]{:S(2)}, u32[]{:S(2)}) collective-permute-start(f32[1,1024]{1,0:T(1,128)S(1)} %block_u.1), channel_id=1, source_target_pairs={{0,12},{4,0},{8,4},{12,8},{1,13},{5,1},{9,5},{13,9},{2,14},{6,2},{... | collective-permute-start | bytes 12296 | tf_op jit(solution)/shard_map/ppermute | solution.py:74
  11.1 10.3 %collective-permute-start.1 = (f32[1,1024]{1,0:T(1,128)S(1)}, f32[1,1024]{1,0:T(1,128)S(1)}, u32[]{:S(2)}, u32[]{:S(2)}) collective-permute-start(f32[1,1024]{1,0:T(1,128)S(1)} %block_u.1), channel_id=1, source_target_pairs={{0,8},{4,12},{8,0},{12,4},{1,9},{5,13},{9,1},{13,5},{2,10},{6,14},... | collective-permute-start | bytes 12296 | tf_op jit(solution)/shard_map/ppermute | solution.py:74
  12.8 8.1 %collective-permute-start = (f32[1,1024]{1,0:T(1,128)S(1)}, f32[1,1024]{1,0:T(1,128)S(1)}, u32[]{:S(2)}, u32[]{:S(2)}) collective-permute-start(f32[1,1024]{1,0:T(1,128)S(1)} %block_u.1), channel_id=1, source_target_pairs={{0,4},{4,8},{8,12},{12,0},{1,5},{5,9},{9,13},{13,1},{2,6},{6,10},{... | collective-permute-start | bytes 12296 | tf_op jit(solution)/shard_map/ppermute | solution.py:74
  13.7 21.1 %copy-start.23 = (s32[32]{0:T(128)}, s32[32]{0:T(128)S(1)}, u32[]{:S(2)}) copy-start(s32[32]{0:T(128)S(1)} %stack.186.refs_8_.refs_0_) | copy-start | bytes 388
  17.9 16.9 %collective-permute-start.7 = (bf16[128,1024]{1,0:T(8,128)(2,1)S(1)}, bf16[128,1024]{1,0:T(8,128)(2,1)S(1)}, u32[]{:S(2)}, u32[]{:S(2)}) collective-permute-start(bf16[128,1024]{1,0:T(8,128)(2,1)S(1)} %collective-permute-done.3.refs_6_.refs_0_), channel_id=1, source_target_pairs={{0,18},{1,19},{2,16},{3,17},{16,2},{17,3},{18,0},{19,1},{4,22},{5,... | collective-permute-start | bytes 786440 | tf_op jit(solution)/shard_map/ppermute | solution.py:541
  20.4 14.4 %collective-permute-start.6 = (bf16[128,1024]{1,0:T(8,128)(2,1)S(1)}, bf16[128,1024]{1,0:T(8,128)(2,1)S(1)}, u32[]{:S(2)}, u32[]{:S(2)}) collective-permute-start(bf16[128,1024]{1,0:T(8,128)(2,1)S(1)} %collective-permute-done.3.refs_6_.refs_0_), channel_id=1, source_target_pairs={{0,16},{1,17},{2,18},{3,19},{16,0},{17,1},{18,2},{19,3},{4,20},{5,... | collective-permute-start | bytes 786440 | tf_op jit(solution)/shard_map/ppermute | solution.py:541
  20.9 13.9 %collective-permute-start.5 = (bf16[128,1024]{1,0:T(8,128)(2,1)S(1)}, bf16[128,1024]{1,0:T(8,128)(2,1)S(1)}, u32[]{:S(2)}, u32[]{:S(2)}) collective-permute-start(bf16[128,1024]{1,0:T(8,128)(2,1)S(1)} %collective-permute-done.3.refs_6_.refs_0_), channel_id=1, source_target_pairs={{0,2},{1,3},{2,0},{3,1},{16,18},{17,19},{18,16},{19,17},{4,6},{5,7... | collective-permute-start | bytes 786440 | tf_op jit(solution)/shard_map/ppermute | solution.py:541
  34.8 7.5 %copy-start.13 = (f32[1024,1]{1,0:T(8,128)}, f32[1024,1]{1,0:T(8,128)S(1)}, u32[]{:S(2)}) copy-start(f32[1024,1]{1,0:T(8,128)S(1)} %get-tuple-element.51.curve_ref) | copy-start | bytes 12292
  34.8 5.6 %copy-start.4 = (bf16[1024,1024]{1,0:T(8,128)(2,1)S(1)}, bf16[1024,1024]{1,0:T(8,128)(2,1)}, u32[]{:S(2)}) copy-start(bf16[1024,1024]{1,0:T(8,128)(2,1)} %refs_0_.4) | copy-start | bytes 6291460
  34.8 8.9 %copy-start.1 = (bf16[1024,1024]{1,0:T(8,128)(2,1)S(1)}, bf16[1024,1024]{1,0:T(8,128)(2,1)}, u32[]{:S(2)}) copy-start(bf16[1024,1024]{1,0:T(8,128)(2,1)} %refs_1_.5) | copy-start | bytes 6291460
  34.9 8.8 %collective-permute-start.8 = (bf16[512,1024]{1,0:T(8,128)(2,1)S(1)}, bf16[512,1024]{1,0:T(8,128)(2,1)S(1)}, u32[]{:S(2)}, u32[]{:S(2)}) collective-permute-start(bf16[512,1024]{1,0:T(8,128)(2,1)S(1)} %pack_shares.1.refs_5_), channel_id=1, source_target_pairs={{0,1},{1,0},{2,3},{3,2},{16,17},{17,16},{18,19},{19,18},{4,5},{5,4... | collective-permute-start | bytes 3145736 | tf_op jit(solution)/shard_map/ppermute | solution.py:541
  35.0 8.7 %collective-permute-start.4 = (bf16[64,2048]{1,0:T(8,128)(2,1)S(1)}, bf16[64,2048]{1,0:T(8,128)(2,1)S(1)}, u32[]{:S(2)}, u32[]{:S(2)}) collective-permute-start(bf16[64,2048]{1,0:T(8,128)(2,1)S(1)} %get-tuple-element.42), channel_id=1, source_target_pairs={{0,4},{4,0},{8,12},{12,8},{1,5},{5,1},{9,13},{13,9},{2,6},{6,2},{1... | collective-permute-start | bytes 786440 | tf_op jit(solution)/shard_map/ppermute | solution.py:545
  35.8 3.3 %collective-permute-start.9 = (s32[64,8]{1,0:T(8,128)S(1)}, s32[64,8]{1,0:T(8,128)S(1)}, u32[]{:S(2)}, u32[]{:S(2)}) collective-permute-start(s32[64,8]{1,0:T(8,128)S(1)} %get-tuple-element.45), channel_id=1, source_target_pairs={{0,1},{1,2},{2,3},{3,0},{4,5},{5,6},{6,7},{7,4},{8,9},{9,10},{10,1... | collective-permute-start | bytes 6152 | tf_op jit(solution)/shard_map/ppermute | solution.py:74
  36.0 3.9 %collective-permute-start.10 = (s32[64,8]{1,0:T(8,128)S(1)}, s32[64,8]{1,0:T(8,128)S(1)}, u32[]{:S(2)}, u32[]{:S(2)}) collective-permute-start(s32[64,8]{1,0:T(8,128)S(1)} %get-tuple-element.46), channel_id=1, source_target_pairs={{0,2},{1,3},{2,0},{3,1},{4,6},{5,7},{6,4},{7,5},{8,10},{9,11},{10,... | collective-permute-start | bytes 6152 | tf_op jit(solution)/shard_map/ppermute | solution.py:74
  37.5 2.9 %collective-permute-start.11 = (s32[64,8]{1,0:T(8,128)S(1)}, s32[64,8]{1,0:T(8,128)S(1)}, u32[]{:S(2)}, u32[]{:S(2)}) collective-permute-start(s32[64,8]{1,0:T(8,128)S(1)} %get-tuple-element.47), channel_id=1, source_target_pairs={{0,3},{1,0},{2,1},{3,2},{4,7},{5,4},{6,5},{7,6},{8,11},{9,8},{10,9... | collective-permute-start | bytes 6152 | tf_op jit(solution)/shard_map/ppermute | solution.py:74
  45.2 39.0 %copy-start.2 = (bf16[1024,1024]{1,0:T(8,128)(2,1)}, bf16[1024,1024]{1,0:T(8,128)(2,1)S(1)}, u32[]{:S(2)}) copy-start(bf16[1024,1024]{1,0:T(8,128)(2,1)S(1)} %get-tuple-element.49.refs_2_) | copy-start | bytes 6291460
  45.2 7.9 %collective-permute-start.13 = (bf16[128,1024]{1,0:T(8,128)(2,1)S(1)}, bf16[128,1024]{1,0:T(8,128)(2,1)S(1)}, u32[]{:S(2)}, u32[]{:S(2)}) collective-permute-start(bf16[128,1024]{1,0:T(8,128)(2,1)S(1)} %get-tuple-element.55.refs_3_), channel_id=1, source_target_pairs={{0,2},{1,3},{2,0},{3,1},{16,18},{17,19},{18,16},{19,17},{4,6},{5,7... | collective-permute-start | bytes 786440 | tf_op jit(solution)/shard_map/ppermute | solution.py:541
  46.8 5.0 %collective-permute-start.12 = (bf16[64,1024]{1,0:T(8,128)(2,1)S(1)}, bf16[64,1024]{1,0:T(8,128)(2,1)S(1)}, u32[]{:S(2)}, u32[]{:S(2)}) collective-permute-start(bf16[64,1024]{1,0:T(8,128)(2,1)S(1)} %get-tuple-element.53), channel_id=1, source_target_pairs={{0,4},{4,0},{8,12},{12,8},{1,5},{5,1},{9,13},{13,9},{2,6},{6,2},{1... | collective-permute-start | bytes 393224 | tf_op jit(solution)/shard_map/ppermute | solution.py:545
  53.2 11.8 %copy-start.15 = (bf16[256,1024]{1,0:T(8,128)(2,1)}, bf16[256,1024]{1,0:T(8,128)(2,1)S(1)}, u32[]{:S(2)}) copy-start(bf16[256,1024]{1,0:T(8,128)(2,1)S(1)} %get-tuple-element.60.refs_2_) | copy-start | bytes 1572868
  53.3 10.4 %collective-permute-start.17 = (bf16[256,1024]{1,0:T(8,128)(2,1)S(1)}, bf16[256,1024]{1,0:T(8,128)(2,1)S(1)}, u32[]{:S(2)}, u32[]{:S(2)}) collective-permute-start(bf16[256,1024]{1,0:T(8,128)(2,1)S(1)} %get-tuple-element.60.refs_2_), channel_id=1, source_target_pairs={{0,1},{1,0},{2,3},{3,2},{16,17},{17,16},{18,19},{19,18},{4,5},{5,4... | collective-permute-start | bytes 1572872 | tf_op jit(solution)/shard_map/ppermute | solution.py:541
  53.3 14.3 %collective-permute-start.24 = (bf16[256,1024]{1,0:T(8,128)(2,1)S(1)}, bf16[256,1024]{1,0:T(8,128)(2,1)S(1)}, u32[]{:S(2)}, u32[]{:S(2)}) collective-permute-start(bf16[256,1024]{1,0:T(8,128)(2,1)S(1)} %get-tuple-element.60.refs_2_), channel_id=1, source_target_pairs={{0,16},{1,17},{2,18},{3,19},{16,0},{17,1},{18,2},{19,3},{4,20},{5,... | collective-permute-start | bytes 1572872 | tf_op jit(solution)/shard_map/ppermute | solution.py:541
  54.9 5.2 %collective-permute-start.16 = (bf16[64,1024]{1,0:T(8,128)(2,1)S(1)}, bf16[64,1024]{1,0:T(8,128)(2,1)S(1)}, u32[]{:S(2)}, u32[]{:S(2)}) collective-permute-start(bf16[64,1024]{1,0:T(8,128)(2,1)S(1)} %get-tuple-element.58.refs_3_), channel_id=1, source_target_pairs={{0,3},{1,0},{2,1},{3,2},{4,7},{5,4},{6,5},{7,6},{8,11},{9,8},{10,9... | collective-permute-start | bytes 393224 | tf_op jit(solution)/shard_map/ppermute | solution.py:74
  56.2 7.4 %collective-permute-start.15 = (bf16[64,1024]{1,0:T(8,128)(2,1)S(1)}, bf16[64,1024]{1,0:T(8,128)(2,1)S(1)}, u32[]{:S(2)}, u32[]{:S(2)}) collective-permute-start(bf16[64,1024]{1,0:T(8,128)(2,1)S(1)} %get-tuple-element.58.refs_3_), channel_id=1, source_target_pairs={{0,2},{1,3},{2,0},{3,1},{4,6},{5,7},{6,4},{7,5},{8,10},{9,11},{10,... | collective-permute-start | bytes 393224 | tf_op jit(solution)/shard_map/ppermute | solution.py:74
  56.7 6.9 %collective-permute-start.14 = (bf16[64,1024]{1,0:T(8,128)(2,1)S(1)}, bf16[64,1024]{1,0:T(8,128)(2,1)S(1)}, u32[]{:S(2)}, u32[]{:S(2)}) collective-permute-start(bf16[64,1024]{1,0:T(8,128)(2,1)S(1)} %get-tuple-element.58.refs_3_), channel_id=1, source_target_pairs={{0,1},{1,2},{2,3},{3,0},{4,5},{5,6},{6,7},{7,4},{8,9},{9,10},{10,1... | collective-permute-start | bytes 393224 | tf_op jit(solution)/shard_map/ppermute | solution.py:74
  60.1 15.6 %collective-permute-start.22 = (bf16[128,1024]{1,0:T(8,128)(2,1)S(1)}, bf16[128,1024]{1,0:T(8,128)(2,1)S(1)}, u32[]{:S(2)}, u32[]{:S(2)}) collective-permute-start(bf16[128,1024]{1,0:T(8,128)(2,1)S(1)} %get-tuple-element.67), channel_id=1, source_target_pairs={{0,8},{4,12},{8,0},{12,4},{1,9},{5,13},{9,1},{13,5},{2,10},{6,14},... | collective-permute-start | bytes 786440 | tf_op jit(solution)/shard_map/ppermute | solution.py:548
  63.7 20.5 %copy-start.6 = (bf16[256,1024]{1,0:T(8,128)(2,1)}, bf16[256,1024]{1,0:T(8,128)(2,1)S(1)}, u32[]{:S(2)}) copy-start(bf16[256,1024]{1,0:T(8,128)(2,1)S(1)} %collective-permute-done.17.refs_7_.refs_6_) | copy-start | bytes 1572868
  63.7 14.3 %copy-start.16 = (bf16[64,1024]{1,0:T(8,128)(2,1)S(1)}, bf16[64,1024]{1,0:T(8,128)(2,1)}, u32[]{:S(2)}) copy-start(bf16[64,1024]{1,0:T(8,128)(2,1)} %refs_0_.5) | copy-start | bytes 393220
  68.5 15.7 %collective-permute-start.25 = (bf16[256,1024]{1,0:T(8,128)(2,1)S(1)}, bf16[256,1024]{1,0:T(8,128)(2,1)S(1)}, u32[]{:S(2)}, u32[]{:S(2)}) collective-permute-start(bf16[256,1024]{1,0:T(8,128)(2,1)S(1)} %near_far.1), channel_id=1, source_target_pairs={{0,1},{1,0},{2,3},{3,2},{16,17},{17,16},{18,19},{19,18},{4,5},{5,4... | collective-permute-start | bytes 1572872 | tf_op jit(solution)/shard_map/ppermute | solution.py:541
  68.5 7.2 %collective-permute-start.18 = (bf16[64,1152]{1,0:T(8,128)(2,1)S(1)}, bf16[64,1152]{1,0:T(8,128)(2,1)S(1)}, u32[]{:S(2)}, u32[]{:S(2)}) collective-permute-start(bf16[64,1152]{1,0:T(8,128)(2,1)S(1)} %get-tuple-element.62), channel_id=1, source_target_pairs={{0,3},{1,0},{2,1},{3,2},{4,7},{5,4},{6,5},{7,6},{8,11},{9,8},{10,9... | collective-permute-start | bytes 442376 | tf_op jit(solution)/shard_map/ppermute | solution.py:74
  70.2 7.8 %collective-permute-start.19 = (bf16[64,1152]{1,0:T(8,128)(2,1)S(1)}, bf16[64,1152]{1,0:T(8,128)(2,1)S(1)}, u32[]{:S(2)}, u32[]{:S(2)}) collective-permute-start(bf16[64,1152]{1,0:T(8,128)(2,1)S(1)} %get-tuple-element.63), channel_id=1, source_target_pairs={{0,2},{1,3},{2,0},{3,1},{4,6},{5,7},{6,4},{7,5},{8,10},{9,11},{10,... | collective-permute-start | bytes 442376 | tf_op jit(solution)/shard_map/ppermute | solution.py:74
  70.7 7.3 %collective-permute-start.20 = (bf16[64,1152]{1,0:T(8,128)(2,1)S(1)}, bf16[64,1152]{1,0:T(8,128)(2,1)S(1)}, u32[]{:S(2)}, u32[]{:S(2)}) collective-permute-start(bf16[64,1152]{1,0:T(8,128)(2,1)S(1)} %get-tuple-element.64), channel_id=1, source_target_pairs={{0,1},{1,2},{2,3},{3,0},{4,5},{5,6},{6,7},{7,4},{8,9},{9,10},{10,1... | collective-permute-start | bytes 442376 | tf_op jit(solution)/shard_map/ppermute | solution.py:74
  75.8 8.4 %collective-permute-start.23 = (bf16[128,1024]{1,0:T(8,128)(2,1)S(1)}, bf16[128,1024]{1,0:T(8,128)(2,1)S(1)}, u32[]{:S(2)}, u32[]{:S(2)}) collective-permute-start(bf16[128,1024]{1,0:T(8,128)(2,1)S(1)} %other.1.refs_5_), channel_id=1, source_target_pairs={{0,16},{1,17},{2,18},{3,19},{16,0},{17,1},{18,2},{19,3},{4,20},{5,... | collective-permute-start | bytes 786440 | tf_op jit(solution)/shard_map/ppermute | solution.py:541
  78.4 5.0 %collective-permute-start.21 = (bf16[64,1024]{1,0:T(8,128)(2,1)S(1)}, bf16[64,1024]{1,0:T(8,128)(2,1)S(1)}, u32[]{:S(2)}, u32[]{:S(2)}) collective-permute-start(bf16[64,1024]{1,0:T(8,128)(2,1)S(1)} %get-tuple-element.66.refs_3_), channel_id=1, source_target_pairs={{0,4},{4,0},{8,12},{12,8},{1,5},{5,1},{9,13},{13,9},{2,6},{6,2},{1... | collective-permute-start | bytes 393224 | tf_op jit(solution)/shard_map/ppermute | solution.py:545
  84.2 2.2 %copy-start.9 = (bf16[256,1024]{1,0:T(8,128)(2,1)}, bf16[256,1024]{1,0:T(8,128)(2,1)S(1)}, u32[]{:S(2)}) copy-start(bf16[256,1024]{1,0:T(8,128)(2,1)S(1)} %collective-permute-done.25.refs_8_.refs_7_) | copy-start | bytes 1572868
  86.4 7.5 %collective-permute-start.26 = (bf16[64,2048]{1,0:T(8,128)(2,1)S(1)}, bf16[64,2048]{1,0:T(8,128)(2,1)S(1)}, u32[]{:S(2)}, u32[]{:S(2)}) collective-permute-start(bf16[64,2048]{1,0:T(8,128)(2,1)S(1)} %get-tuple-element.69), channel_id=1, source_target_pairs={{0,4},{4,0},{8,12},{12,8},{1,5},{5,1},{9,13},{13,9},{2,6},{6,2},{1... | collective-permute-start | bytes 786440 | tf_op jit(solution)/shard_map/ppermute | solution.py:545
  87.3 23.2 %collective-permute-start.28 = (bf16[256,1024]{1,0:T(8,128)(2,1)}, bf16[256,1024]{1,0:T(8,128)(2,1)S(1)}, u32[]{:S(2)}, u32[]{:S(2)}) collective-permute-start(bf16[256,1024]{1,0:T(8,128)(2,1)} %get-tuple-element.72.refs_4_), channel_id=1, source_target_pairs={{0,2},{1,3},{2,0},{3,1},{16,18},{17,19},{18,16},{19,17},{4,6},{5,7... | collective-permute-start | bytes 1572872 | tf_op jit(solution)/shard_map/ppermute | solution.py:541
  94.7 22.2 %all-to-all-start = ((bf16[32,64,128]{2,1,0:T(8,128)(2,1)}), bf16[32,64,128]{2,1,0:T(8,128)(2,1)}, u32[]{:S(2)}, u32[]{:S(2)}) async-start(bf16[32,64,128]{2,1,0:T(8,128)(2,1)} %copy-done.12), calls=%async_computation | async-start | bytes 1048576 | tf_op jit(solution)/shard_map/all_to_all | solution.py:659
  100.1 16.8 %collective-permute-start.29 = (bf16[256,1024]{1,0:T(8,128)(2,1)}, bf16[256,1024]{1,0:T(8,128)(2,1)}, u32[]{:S(2)}, u32[]{:S(2)}) collective-permute-start(bf16[256,1024]{1,0:T(8,128)(2,1)} %get-tuple-element.72.refs_4_), channel_id=1, source_target_pairs={{0,1},{1,0},{2,3},{3,2},{16,17},{17,16},{18,19},{19,18},{4,5},{5,4... | collective-permute-start | bytes 1572872 | tf_op jit(solution)/shard_map/ppermute | solution.py:541
  100.2 3.4 %copy-start.5 = (bf16[1024,4096]{1,0:T(8,128)(2,1)S(1)}, bf16[1024,4096]{1,0:T(8,128)(2,1)}, u32[]{:S(2)}) copy-start(bf16[1024,4096]{1,0:T(8,128)(2,1)} %get-tuple-element.50.normed_ref) | copy-start | bytes 25165828
  103.6 1.0 copy-start.14
  110.5 6.5 %copy-start.10 = (bf16[256,1024]{1,0:T(8,128)(2,1)}, bf16[256,1024]{1,0:T(8,128)(2,1)S(1)}, u32[]{:S(2)}) copy-start(bf16[256,1024]{1,0:T(8,128)(2,1)S(1)} %collective-permute-done.28.refs_0_.refs_5_) | copy-start | bytes 1572868
  110.6 6.4 %collective-permute-start.30 = (bf16[256,1024]{1,0:T(8,128)(2,1)S(1)}, bf16[256,1024]{1,0:T(8,128)(2,1)}, u32[]{:S(2)}, u32[]{:S(2)}) collective-permute-start(bf16[256,1024]{1,0:T(8,128)(2,1)S(1)} %late.1), channel_id=1, source_target_pairs={{0,1},{1,0},{2,3},{3,2},{16,17},{17,16},{18,19},{19,18},{4,5},{5,4... | collective-permute-start | bytes 1572872 | tf_op jit(solution)/shard_map/ppermute | solution.py:541
  111.1 3.7 %collective-permute-start.31 = (f32[24,128]{1,0:T(8,128)S(1)}, f32[24,128]{1,0:T(8,128)S(1)}, u32[]{:S(2)}, u32[]{:S(2)}) collective-permute-start(f32[24,128]{1,0:T(8,128)S(1)} %get-tuple-element.73.refs_0_), channel_id=1, source_target_pairs={{0,16},{16,0},{1,17},{17,1},{2,18},{18,2},{3,19},{19,3},{4,20},{20... | collective-permute-start | bytes 36872 | tf_op jit(solution)/shard_map/ppermute | solution.py:74
  112.6 3.7 %collective-permute-start.27 = (f32[24,128]{1,0:T(8,128)S(1)}, f32[24,128]{1,0:T(8,128)S(1)}, u32[]{:S(2)}, u32[]{:S(2)}) collective-permute-start(f32[24,128]{1,0:T(8,128)S(1)} %get-tuple-element.70.refs_0_.refs_1_), channel_id=1, source_target_pairs={{0,16},{16,0},{1,17},{17,1},{2,18},{18,2},{3,19},{19,3},{4,20},{20... | collective-permute-start | bytes 36872 | tf_op jit(solution)/shard_map/ppermute | solution.py:74
  116.9 7.7 %copy-start.18 = (f32[24,128]{1,0:T(8,128)S(1)}, f32[24,128]{1,0:T(8,128)}, u32[]{:S(2)}) copy-start(f32[24,128]{1,0:T(8,128)} %copy-done.17) | copy-start | bytes 36868
  116.9 10.2 %copy-start.20 = (f32[24,128]{1,0:T(8,128)S(1)}, f32[24,128]{1,0:T(8,128)}, u32[]{:S(2)}) copy-start(f32[24,128]{1,0:T(8,128)} %copy-done.19) | copy-start | bytes 36868
  121.1 18.6 %copy-start.3 = (bf16[1024,1024]{1,0:T(8,128)(2,1)S(1)}, bf16[1024,1024]{1,0:T(8,128)(2,1)}, u32[]{:S(2)}) copy-start(bf16[1024,1024]{1,0:T(8,128)(2,1)} %copy-done.2) | copy-start | bytes 6291460
  121.1 17.4 %collective-permute-start.39 = (bf16[1024,128]{1,0:T(8,128)(2,1)}, bf16[1024,128]{1,0:T(8,128)(2,1)S(1)}, u32[]{:S(2)}, u32[]{:S(2)}) collective-permute-start(bf16[1024,128]{1,0:T(8,128)(2,1)} %grad_columns.1.refs_1_.refs_0_), channel_id=1, source_target_pairs={{0,18},{1,19},{2,16},{3,17},{16,2},{17,3},{18,0},{19,1},{4,22},{5,... | collective-permute-start | bytes 786440 | tf_op jit(solution)/shard_map/ppermute | solution.py:541
  122.7 15.9 %collective-permute-start.38 = (bf16[1024,128]{1,0:T(8,128)(2,1)}, bf16[1024,128]{1,0:T(8,128)(2,1)S(1)}, u32[]{:S(2)}, u32[]{:S(2)}) collective-permute-start(bf16[1024,128]{1,0:T(8,128)(2,1)} %grad_columns.1.refs_1_.refs_0_), channel_id=1, source_target_pairs={{0,16},{1,17},{2,18},{3,19},{16,0},{17,1},{18,2},{19,3},{4,20},{5,... | collective-permute-start | bytes 786440 | tf_op jit(solution)/shard_map/ppermute | solution.py:541
  124.1 14.5 %collective-permute-start.37 = (bf16[1024,128]{1,0:T(8,128)(2,1)}, bf16[1024,128]{1,0:T(8,128)(2,1)S(1)}, u32[]{:S(2)}, u32[]{:S(2)}) collective-permute-start(bf16[1024,128]{1,0:T(8,128)(2,1)} %grad_columns.1.refs_1_.refs_0_), channel_id=1, source_target_pairs={{0,2},{1,3},{2,0},{3,1},{16,18},{17,19},{18,16},{19,17},{4,6},{5,7... | collective-permute-start | bytes 786440 | tf_op jit(solution)/shard_map/ppermute | solution.py:541
  124.6 1.0 copy-start.7
  125.6 3.7 %collective-permute-start.32 = (f32[24,128]{1,0:T(8,128)S(1)}, f32[24,128]{1,0:T(8,128)S(1)}, u32[]{:S(2)}, u32[]{:S(2)}) collective-permute-start(f32[24,128]{1,0:T(8,128)S(1)} %slope_out.3), channel_id=1, source_target_pairs={{0,4},{4,0},{8,12},{12,8},{1,5},{5,1},{9,13},{13,9},{2,6},{6,2},{1... | collective-permute-start | bytes 36872 | tf_op jit(solution)/shard_map/ppermute | solution.py:545
  129.3 4.6 %collective-permute-start.33 = (f32[24,128]{1,0:T(8,128)S(1)}, f32[24,128]{1,0:T(8,128)S(1)}, u32[]{:S(2)}, u32[]{:S(2)}) collective-permute-start(f32[24,128]{1,0:T(8,128)S(1)} %sum_half.1.refs_0_), channel_id=1, source_target_pairs={{0,8},{4,12},{8,0},{12,4},{1,9},{5,13},{9,1},{13,5},{2,10},{6,14},... | collective-permute-start | bytes 36872 | tf_op jit(solution)/shard_map/ppermute | solution.py:548
  133.9 1.5 %collective-permute-start.36 = (f32[24,128]{1,0:T(8,128)S(1)}, f32[24,128]{1,0:T(8,128)S(1)}, u32[]{:S(2)}, u32[]{:S(2)}) collective-permute-start(f32[24,128]{1,0:T(8,128)S(1)} %sum_mirror.1.refs_0_), channel_id=1, source_target_pairs={{0,3},{1,0},{2,1},{3,2},{4,7},{5,4},{6,5},{7,6},{8,11},{9,8},{10,9... | collective-permute-start | bytes 36872 | tf_op jit(solution)/shard_map/ppermute | solution.py:74
  133.9 3.7 %collective-permute-start.35 = (f32[24,128]{1,0:T(8,128)S(1)}, f32[24,128]{1,0:T(8,128)S(1)}, u32[]{:S(2)}, u32[]{:S(2)}) collective-permute-start(f32[24,128]{1,0:T(8,128)S(1)} %sum_mirror.1.refs_0_), channel_id=1, source_target_pairs={{0,2},{1,3},{2,0},{3,1},{4,6},{5,7},{6,4},{7,5},{8,10},{9,11},{10,... | collective-permute-start | bytes 36872 | tf_op jit(solution)/shard_map/ppermute | solution.py:74
  135.4 3.1 %collective-permute-start.34 = (f32[24,128]{1,0:T(8,128)S(1)}, f32[24,128]{1,0:T(8,128)S(1)}, u32[]{:S(2)}, u32[]{:S(2)}) collective-permute-start(f32[24,128]{1,0:T(8,128)S(1)} %sum_mirror.1.refs_0_), channel_id=1, source_target_pairs={{0,1},{1,2},{2,3},{3,0},{4,5},{5,6},{6,7},{7,4},{8,9},{9,10},{10,1... | collective-permute-start | bytes 36872 | tf_op jit(solution)/shard_map/ppermute | solution.py:74
  139.6 2.9 %copy-start.22 = (f32[1024]{0:T(1024)S(1)}, f32[1024]{0:T(1024)}, u32[]{:S(2)}) copy-start(f32[1024]{0:T(1024)} %param.14) | copy-start | bytes 12292
  139.6 2.9 %collective-permute-start.40 = (bf16[4096,128]{1,0:T(8,128)(2,1)S(1)}, bf16[4096,128]{1,0:T(8,128)(2,1)S(1)}, u32[]{:S(2)}, u32[]{:S(2)}) collective-permute-start(bf16[4096,128]{1,0:T(8,128)(2,1)S(1)} %pack_columns.1.refs_3_), channel_id=1, source_target_pairs={{0,1},{1,0},{2,3},{3,2},{16,17},{17,16},{18,19},{19,18},{4,5},{5,4... | collective-permute-start | bytes 3145736 | tf_op jit(solution)/shard_map/ppermute | solution.py:541
  141.0 4.4 %collective-permute-start.41 = (f32[1,1024]{1,0:T(1,128)S(1)}, f32[1,1024]{1,0:T(1,128)S(1)}, u32[]{:S(2)}, u32[]{:S(2)}) collective-permute-start(f32[1,1024]{1,0:T(1,128)S(1)} %get-tuple-element.76.refs_0_), channel_id=1, source_target_pairs={{0,4},{4,0},{8,12},{12,8},{1,5},{5,1},{9,13},{13,9},{2,6},{6,2},{1... | collective-permute-start | bytes 12296 | tf_op jit(solution)/shard_map/ppermute | solution.py:545
  (6 other events, 4.4 us)

commit v10 on v8

--- a/solution.py
+++ b/solution.py
@@ -425,7 +425,7 @@
     half = blocks // 2
     height = 2 * (width // blocks // LANES) // 8 * 8 + 8
     queries = tokens // seq
-    group = 8 if queries % 8 == 0 else queries
+    group = 16 if queries % 16 == 0 else queries
     step_tokens = group * seq
     whole = lambda dims: pl.BlockSpec(dims, lambda i: (0, 0))
     return pl.pallas_call(
@@ -444,7 +444,7 @@
         cost_estimate=pl.CostEstimate(
             flops=4 * tokens * width, bytes_accessed=2 * tokens * width, transcendentals=0
         ),
-        compiler_params=pltpu.CompilerParams(vmem_limit_bytes=20 * MIB),
+        compiler_params=pltpu.CompilerParams(vmem_limit_bytes=32 * MIB),
         name="slope_rows",
     )(z, normed, curve, loss, *backs)
 

time: 146 us -> 145 us (level)
  transfers between devices with their start and end apart: 43 -> 43, of which waited for: 21 -> 21; matrix products, arithmetic and copies ran while one was open for 1% -> 1% of each run, Pallas kernels for 19% -> 18%
where the time goes in v10:
time: 145 us
  starting transfers between devices  49.3 us (34%)
  waiting for transfers between devices  44.7 us (31%)
  Pallas kernels  35.3 us (24%)
  local copies, waits for them, and re-layouts  13.2 us (9%)
  between operations  2.34 us (2%)
    pallas_call x23, Pallas kernels, call(): pl.pallas_call(run, out_shape=outs, in_specs=[SMEM] * smem + [pl.BlockSpe...  18.1 us
    ppermute x6, waiting for transfers between devices, half_shift(): return lax.ppermute(values, 'fsdp', pairs)  17.3 us
    ppermute x17, starting transfers between devices, shift(): return lax.ppermute(values, axis, [(i, (i + k) % n) for i in range(n)])  15 us
    ppermute x16, starting transfers between devices, plane_shift(): return lax.ppermute(values, PLANE, pairs)  12.8 us
    pallas_call x1, Pallas kernels, gate_rows(): pl.pallas_call(run, grid=(queries // group,), out_shape=outs, in_specs=[S...  11.6 us
    unnamed x55, local copies, waits for them, and re-layouts  11.6 us
    ppermute x3, waiting for transfers between devices, mirror_shift(): lax.ppermute(values, 'fsdp', [(a, (a + half) % n_z) for a in range(n_z)])  11.5 us
    ppermute x17, waiting for transfers between devices, shift(): return lax.ppermute(values, axis, [(i, (i + k) % n) for i in range(n)])  11.2 us
  transfers between devices with their start and end apart: 43, of which 21 were waited for; matrix products, arithmetic and copies ran while one was open for 1% of the time, Pallas kernels for 18%

profile of v10, /device:TPU:0, one launch (start us, length us, event | category | flops | bytes accessed | tf_op | source)
XLA Modules:
  0.0 144.9 jit_solution(8788046916482681387)
XLA Ops:
  0.7 1.0 constant_dynamic-slice_fusion.refs_2_
  1.6 4.1 %collective-permute-start.3 = (bf16[128,1024]{1,0:T(8,128)(2,1)S(1)}, bf16[128,1024]{1,0:T(8,128)(2,1)S(1)}, u32[]{:S(2)}, u32[]{:S(2)}) collective-permute-start(bf16[128,1024]{1,0:T(8,128)(2,1)S(1)} %constant_dynamic-slice_fusion.refs_2_), channel_id=1, source_target_pairs={{0,8},{4,12},{8,0},{12,4},{1,9},{5,13},{9,1},{13,5},{2,10},{6,14},... | collective-permute-start | bytes 786440 | tf_op jit(solution)/shard_map/ppermute | solution.py:548
  5.8 1.6 %copy-done = bf16[1024,1024]{1,0:T(8,128)(2,1)S(1)} copy-done((bf16[1024,1024]{1,0:T(8,128)(2,1)S(1)}, bf16[1024,1024]{1,0:T(8,128)(2,1)}, u32[]{:S(2)}) %copy-start) | copy-done | bytes 2097176
  7.3 0.7 copy-done.21
  8.0 1.7 %block_u.1 = f32[1,1024]{1,0:T(1,128)S(1)} custom-call(bf16[1024,1024]{1,0:T(8,128)(2,1)S(1)} %copy-done, f32[1,1024]{1,0:T(1,128)S(1)} %bitcast.51, bf16[128,1024]{1,0:T(8,128)(2,1)S(1)} %constant_dynamic-slice_fusion.refs_2_), custom_call_target="tpu_custom_call" | custom-call | bytes 2105344 | tf_op jit(solution)/shard_map/block_u/pallas_call | solution.py:56
  9.8 1.4 collective-permute-start.2
  11.1 1.7 %collective-permute-start.1 = (f32[1,1024]{1,0:T(1,128)S(1)}, f32[1,1024]{1,0:T(1,128)S(1)}, u32[]{:S(2)}, u32[]{:S(2)}) collective-permute-start(f32[1,1024]{1,0:T(1,128)S(1)} %block_u.1), channel_id=1, source_target_pairs={{0,8},{4,12},{8,0},{12,4},{1,9},{5,13},{9,1},{13,5},{2,10},{6,14},... | collective-permute-start | bytes 12296 | tf_op jit(solution)/shard_map/ppermute | solution.py:74
  13.7 4.2 %collective-permute-done.3.refs_6_.refs_0_ = bf16[128,1024]{1,0:T(8,128)(2,1)S(1)} collective-permute-done((bf16[128,1024]{1,0:T(8,128)(2,1)S(1)}, bf16[128,1024]{1,0:T(8,128)(2,1)S(1)}, u32[]{:S(2)}, u32[]{:S(2)}) %collective-permute-start.3) | collective-permute-done | bytes 262176 | tf_op jit(solution)/shard_map/ppermute | solution.py:548
  17.9 2.5 %collective-permute-start.7 = (bf16[128,1024]{1,0:T(8,128)(2,1)S(1)}, bf16[128,1024]{1,0:T(8,128)(2,1)S(1)}, u32[]{:S(2)}, u32[]{:S(2)}) collective-permute-start(bf16[128,1024]{1,0:T(8,128)(2,1)S(1)} %collective-permute-done.3.refs_6_.refs_0_), channel_id=1, source_target_pairs={{0,18},{1,19},{2,16},{3,17},{16,2},{17,3},{18,0},{19,1},{4,22},{5,... | collective-permute-start | bytes 786440 | tf_op jit(solution)/shard_map/ppermute | solution.py:541
  21.4 11.6 %gate_rows.1 = (bf16[64,2048]{1,0:T(8,128)(2,1)S(1)}, bf16[64,2048]{1,0:T(8,128)(2,1)S(1)}, bf16[1024,4096]{1,0:T(8,128)(2,1)}, f32[1024,1]{1,0:T(8,128)S(1)}, f...) custom-call(s32[2]{0:T(128)S(1)} %pad_add_fusion.refs_0_.z_ref, ...), custom_call_target="tpu_custom_call" | custom-call | flops 41943040 | bytes 16777216 | tf_op jit(solution)/shard_map/gate_rows/pallas_call | solution.py:174
  33.2 0.8 collective-permute-start.4
  34.2 1.5 %collective-permute-start.10 = (s32[64,8]{1,0:T(8,128)S(1)}, s32[64,8]{1,0:T(8,128)S(1)}, u32[]{:S(2)}, u32[]{:S(2)}) collective-permute-start(s32[64,8]{1,0:T(8,128)S(1)} %get-tuple-element.46), channel_id=1, source_target_pairs={{0,2},{1,3},{2,0},{3,1},{4,6},{5,7},{6,4},{7,5},{8,10},{9,11},{10,... | collective-permute-start | bytes 6152 | tf_op jit(solution)/shard_map/ppermute | solution.py:74
  35.8 1.3 collective-permute-start.11
  37.4 0.7 collective-permute-done.10.refs_4_
  38.7 1.8 %list_counts.1 = (f32[256,1024]{1,0:T(8,128)S(1)}, f32[1,1024]{1,0:T(1,128)S(1)}) custom-call(s32[1]{0:T(128)} %bitcast.46.refs_9_.refs_0_, bf16[1024,1024]{1,0:T(8,128)(2,1)S(1)} %copy-done.4, s32[64,8]{1,0:T(8,128)S(1)} %get-tuple-element.44.refs_2_, s32[64,8]{1,0:T(8,128)S(1)} %collective-permute-done.9.refs_3_, ...), custom_call_target="tpu_custom_call" | custom-call | bytes 3158020 | tf_op jit(solution)/shard_map/list_counts/pallas_call | solution.py:56
  40.5 1.5 %collective-permute-done.4.refs_4_ = bf16[64,2048]{1,0:T(8,128)(2,1)S(1)} collective-permute-done((bf16[64,2048]{1,0:T(8,128)(2,1)S(1)}, bf16[64,2048]{1,0:T(8,128)(2,1)S(1)}, u32[]{:S(2)}, u32[]{:S(2)}) %collective-permute-start.4) | collective-permute-done | bytes 262176 | tf_op jit(solution)/shard_map/ppermute | solution.py:545
  42.0 1.4 forward.1
  43.4 1.6 %collective-permute-start.13 = (bf16[128,1024]{1,0:T(8,128)(2,1)S(1)}, bf16[128,1024]{1,0:T(8,128)(2,1)S(1)}, u32[]{:S(2)}, u32[]{:S(2)}) collective-permute-start(bf16[128,1024]{1,0:T(8,128)(2,1)S(1)} %get-tuple-element.55.refs_3_), channel_id=1, source_target_pairs={{0,2},{1,3},{2,0},{3,1},{16,18},{17,19},{18,16},{19,17},{4,6},{5,7... | collective-permute-start | bytes 786440 | tf_op jit(solution)/shard_map/ppermute | solution.py:541
  45.0 0.7 collective-permute-start.12
  45.7 4.2 %collective-permute-done.12.refs_1_ = bf16[64,1024]{1,0:T(8,128)(2,1)S(1)} collective-permute-done((bf16[64,1024]{1,0:T(8,128)(2,1)S(1)}, bf16[64,1024]{1,0:T(8,128)(2,1)S(1)}, u32[]{:S(2)}, u32[]{:S(2)}) %collective-permute-start.12) | collective-permute-done | bytes 131104 | tf_op jit(solution)/shard_map/ppermute | solution.py:545
  50.0 1.3 collective-permute-done.13.refs_4_
  51.6 1.6 %collective-permute-start.24 = (bf16[256,1024]{1,0:T(8,128)(2,1)S(1)}, bf16[256,1024]{1,0:T(8,128)(2,1)S(1)}, u32[]{:S(2)}, u32[]{:S(2)}) collective-permute-start(bf16[256,1024]{1,0:T(8,128)(2,1)S(1)} %get-tuple-element.60.refs_2_), channel_id=1, source_target_pairs={{0,16},{1,17},{2,18},{3,19},{16,0},{17,1},{18,2},{19,3},{4,20},{5,... | collective-permute-start | bytes 1572872 | tf_op jit(solution)/shard_map/ppermute | solution.py:541
  53.2 1.3 collective-permute-start.16
  55.0 3.4 %collective-permute-done.16.refs_6_ = bf16[64,1024]{1,0:T(8,128)(2,1)S(1)} collective-permute-done((bf16[64,1024]{1,0:T(8,128)(2,1)S(1)}, bf16[64,1024]{1,0:T(8,128)(2,1)S(1)}, u32[]{:S(2)}, u32[]{:S(2)}) %collective-permute-start.16) | collective-permute-done | bytes 131104 | tf_op jit(solution)/shard_map/ppermute | solution.py:74
  58.3 3.2 %collective-permute-start.22 = (bf16[128,1024]{1,0:T(8,128)(2,1)S(1)}, bf16[128,1024]{1,0:T(8,128)(2,1)S(1)}, u32[]{:S(2)}, u32[]{:S(2)}) collective-permute-start(bf16[128,1024]{1,0:T(8,128)(2,1)S(1)} %get-tuple-element.67), channel_id=1, source_target_pairs={{0,8},{4,12},{8,0},{12,4},{1,9},{5,13},{9,1},{13,5},{2,10},{6,14},... | collective-permute-start | bytes 786440 | tf_op jit(solution)/shard_map/ppermute | solution.py:548
  61.9 1.4 contrast.1
  63.3 2.6 %collective-permute-done.24.refs_0_.refs_3_ = bf16[256,1024]{1,0:T(8,128)(2,1)S(1)} collective-permute-done((bf16[256,1024]{1,0:T(8,128)(2,1)S(1)}, bf16[256,1024]{1,0:T(8,128)(2,1)S(1)}, u32[]{:S(2)}, u32[]{:S(2)}) %collective-permute-start.24) | collective-permute-done | bytes 524320 | tf_op jit(solution)/shard_map/ppermute | solution.py:541
  66.0 0.8 copy-done.11
  66.7 1.7 %collective-permute-start.18 = (bf16[64,1152]{1,0:T(8,128)(2,1)S(1)}, bf16[64,1152]{1,0:T(8,128)(2,1)S(1)}, u32[]{:S(2)}, u32[]{:S(2)}) collective-permute-start(bf16[64,1152]{1,0:T(8,128)(2,1)S(1)} %get-tuple-element.62), channel_id=1, source_target_pairs={{0,3},{1,0},{2,1},{3,2},{4,7},{5,4},{6,5},{7,6},{8,11},{9,8},{10,9... | collective-permute-start | bytes 442376 | tf_op jit(solution)/shard_map/ppermute | solution.py:74
  68.9 5.1 %collective-permute-done.22.refs_0_ = bf16[128,1024]{1,0:T(8,128)(2,1)S(1)} collective-permute-done((bf16[128,1024]{1,0:T(8,128)(2,1)S(1)}, bf16[128,1024]{1,0:T(8,128)(2,1)S(1)}, u32[]{:S(2)}, u32[]{:S(2)}) %collective-permute-start.22) | collective-permute-done | bytes 262176 | tf_op jit(solution)/shard_map/ppermute | solution.py:548
  74.0 0.6 collective-permute-start.23
  74.6 1.6 %collective-permute-done.19.refs_6_ = bf16[64,1152]{1,0:T(8,128)(2,1)S(1)} collective-permute-done((bf16[64,1152]{1,0:T(8,128)(2,1)S(1)}, bf16[64,1152]{1,0:T(8,128)(2,1)S(1)}, u32[]{:S(2)}, u32[]{:S(2)}) %collective-permute-start.19) | collective-permute-done | bytes 147488 | tf_op jit(solution)/shard_map/ppermute | solution.py:74
  76.6 1.2 collective-permute-start.21
  77.8 3.9 %collective-permute-done.21.refs_4_ = bf16[64,1024]{1,0:T(8,128)(2,1)S(1)} collective-permute-done((bf16[64,1024]{1,0:T(8,128)(2,1)S(1)}, bf16[64,1024]{1,0:T(8,128)(2,1)S(1)}, u32[]{:S(2)}, u32[]{:S(2)}) %collective-permute-start.21) | collective-permute-done | bytes 131104 | tf_op jit(solution)/shard_map/ppermute | solution.py:545
  81.7 0.7 collective-permute-done.23.refs_6_
  82.4 2.2 %backward.1 = (bf16[64,2048]{1,0:T(8,128)(2,1)S(1)}, bf16[64,2048]{1,0:T(8,128)(2,1)S(1)}, bf16[256,1024]{1,0:T(8,128)(2,1)}) custom-call(s32[1]{0:T(128)} %bitcast.9.refs_10_.refs_0_, bf16[1024,1024]{1,0:T(8,128)(2,1)S(1)} %copy-done.1, bf16[1024,1024]{1,0:T(8,128)(2,1)S(1)} %get-tuple-element.49.refs_2_, bf16[64,1024]{1,0:T(8,128)(2,1)S(1)} %get-tuple-element.66.refs_3_, ...), custom_call_target="tpu_custom_call" | custom-call | flops 536870912 | bytes 6029316 | tf_op jit(solution)/shard_map/backward/pallas_call | solution.py:56
  84.6 0.9 collective-permute-start.26
  85.5 1.1 collective-permute-start.28
  86.6 5.5 %collective-permute-done.26.rest_1_.refs_1_ = bf16[64,2048]{1,0:T(8,128)(2,1)S(1)} collective-permute-done((bf16[64,2048]{1,0:T(8,128)(2,1)S(1)}, bf16[64,2048]{1,0:T(8,128)(2,1)S(1)}, u32[]{:S(2)}, u32[]{:S(2)}) %collective-permute-start.26) | collective-permute-done | bytes 262176 | tf_op jit(solution)/shard_map/ppermute | solution.py:545
  92.2 0.8 copy-done.12
  92.9 5.4 %all-to-all-start = ((bf16[32,64,128]{2,1,0:T(8,128)(2,1)}), bf16[32,64,128]{2,1,0:T(8,128)(2,1)}, u32[]{:S(2)}, u32[]{:S(2)}) async-start(bf16[32,64,128]{2,1,0:T(8,128)(2,1)} %copy-done.12), calls=%async_computation | async-start | bytes 1048576 | tf_op jit(solution)/shard_map/all_to_all | solution.py:659
  98.4 3.4 %copy-done.5 = bf16[1024,4096]{1,0:T(8,128)(2,1)S(1)} copy-done((bf16[1024,4096]{1,0:T(8,128)(2,1)S(1)}, bf16[1024,4096]{1,0:T(8,128)(2,1)}, u32[]{:S(2)}) %copy-start.5) | copy-done | bytes 8388632
  101.8 1.0 copy-done.14
  102.8 5.4 %slope_rows.1 = (f32[24,128]{1,0:T(8,128)S(1)}, f32[24,128]{1,0:T(8,128)S(1)}) custom-call(s32[2]{0:T(128)S(1)} %pad_add_fusion.refs_0_.z_ref, bf16[1024,4096]{1,0:T(8,128)(2,1)S(1)} %copy-done.5, f32[1024,1]{1,0:T(8,128)S(1)} %copy-done.14, f32[1,128]{1,0:T(1,128)S(1)} %get-tuple-element.65.loss_ref, bf16[64,2048]{1,0:T(8,128)(2,1)S(1)} %get-tuple-element.68.rest_0_, ...), custom_call_target="tpu_custom_call" | custom-call | flops 16777216 | bytes 8388608 | tf_op jit(solution)/shard_map/slope_rows/pallas_call | solution.py:431
  108.9 1.5 %collective-permute-start.31 = (f32[24,128]{1,0:T(8,128)S(1)}, f32[24,128]{1,0:T(8,128)S(1)}, u32[]{:S(2)}, u32[]{:S(2)}) collective-permute-start(f32[24,128]{1,0:T(8,128)S(1)} %get-tuple-element.73.refs_0_), channel_id=1, source_target_pairs={{0,16},{16,0},{1,17},{17,1},{2,18},{18,2},{3,19},{19,3},{4,20},{20... | collective-permute-start | bytes 36872 | tf_op jit(solution)/shard_map/ppermute | solution.py:74
  110.9 1.7 %collective-permute-done.31.refs_1_ = f32[24,128]{1,0:T(8,128)S(1)} collective-permute-done((f32[24,128]{1,0:T(8,128)S(1)}, f32[24,128]{1,0:T(8,128)S(1)}, u32[]{:S(2)}, u32[]{:S(2)}) %collective-permute-start.31) | collective-permute-done | bytes 12320 | tf_op jit(solution)/shard_map/ppermute | solution.py:74
  113.2 0.9 collective-permute-done.27.refs_1_
  114.7 4.1 %grad_columns.1.refs_1_.refs_0_ = bf16[1024,128]{1,0:T(8,128)(2,1)} custom-call(s32[32]{0:T(128)} %copy-done.23, bf16[32,64,128]{2,1,0:T(8,128)(2,1)} %all-to-all-done.refs_1_, bf16[256,1024]{1,0:T(8,128)(2,1)} %copy-done.15, bf16[256,1024]{1,0:T(8,128)(2,1)} %copy-done.11, bf16[256,1024]{1,0:T(8,128)(2,1)} %get-tuple-element.72.refs_4_, ...), custom_call_target="tpu_custom_call" | custom-call | flops 536870912 | bytes 4980864 | tf_op jit(solution)/shard_map/grad_columns/pallas_call | solution.py:56
  118.8 1.6 %collective-permute-start.39 = (bf16[1024,128]{1,0:T(8,128)(2,1)}, bf16[1024,128]{1,0:T(8,128)(2,1)S(1)}, u32[]{:S(2)}, u32[]{:S(2)}) collective-permute-start(bf16[1024,128]{1,0:T(8,128)(2,1)} %grad_columns.1.refs_1_.refs_0_), channel_id=1, source_target_pairs={{0,18},{1,19},{2,16},{3,17},{16,2},{17,3},{18,0},{19,1},{4,22},{5,... | collective-permute-start | bytes 786440 | tf_op jit(solution)/shard_map/ppermute | solution.py:541
  120.4 1.4 collective-permute-start.38
  122.4 1.0 copy-done.7
  123.4 1.5 %collective-permute-start.32 = (f32[24,128]{1,0:T(8,128)S(1)}, f32[24,128]{1,0:T(8,128)S(1)}, u32[]{:S(2)}, u32[]{:S(2)}) collective-permute-start(f32[24,128]{1,0:T(8,128)S(1)} %slope_out.3), channel_id=1, source_target_pairs={{0,4},{4,0},{8,12},{12,8},{1,5},{5,1},{9,13},{13,9},{2,6},{6,2},{1... | collective-permute-start | bytes 36872 | tf_op jit(solution)/shard_map/ppermute | solution.py:545
  124.9 2.2 %collective-permute-done.32.refs_1_ = f32[24,128]{1,0:T(8,128)S(1)} collective-permute-done((f32[24,128]{1,0:T(8,128)S(1)}, f32[24,128]{1,0:T(8,128)S(1)}, u32[]{:S(2)}, u32[]{:S(2)}) %collective-permute-start.32) | collective-permute-done | bytes 12320 | tf_op jit(solution)/shard_map/ppermute | solution.py:545
  127.1 2.4 %collective-permute-start.33 = (f32[24,128]{1,0:T(8,128)S(1)}, f32[24,128]{1,0:T(8,128)S(1)}, u32[]{:S(2)}, u32[]{:S(2)}) collective-permute-start(f32[24,128]{1,0:T(8,128)S(1)} %sum_half.1.refs_0_), channel_id=1, source_target_pairs={{0,8},{4,12},{8,0},{12,4},{1,9},{5,13},{9,1},{13,5},{2,10},{6,14},... | collective-permute-start | bytes 36872 | tf_op jit(solution)/shard_map/ppermute | solution.py:548
  129.5 2.2 %collective-permute-done.33.refs_1_ = f32[24,128]{1,0:T(8,128)S(1)} collective-permute-done((f32[24,128]{1,0:T(8,128)S(1)}, f32[24,128]{1,0:T(8,128)S(1)}, u32[]{:S(2)}, u32[]{:S(2)}) %collective-permute-start.33) | collective-permute-done | bytes 12320 | tf_op jit(solution)/shard_map/ppermute | solution.py:548
  131.7 1.5 %collective-permute-start.35 = (f32[24,128]{1,0:T(8,128)S(1)}, f32[24,128]{1,0:T(8,128)S(1)}, u32[]{:S(2)}, u32[]{:S(2)}) collective-permute-start(f32[24,128]{1,0:T(8,128)S(1)} %sum_mirror.1.refs_0_), channel_id=1, source_target_pairs={{0,2},{1,3},{2,0},{3,1},{4,6},{5,7},{6,4},{7,5},{8,10},{9,11},{10,... | collective-permute-start | bytes 36872 | tf_op jit(solution)/shard_map/ppermute | solution.py:74
  133.2 1.5 %collective-permute-start.34 = (f32[24,128]{1,0:T(8,128)S(1)}, f32[24,128]{1,0:T(8,128)S(1)}, u32[]{:S(2)}, u32[]{:S(2)}) collective-permute-start(f32[24,128]{1,0:T(8,128)S(1)} %sum_mirror.1.refs_0_), channel_id=1, source_target_pairs={{0,1},{1,2},{2,3},{3,0},{4,5},{5,6},{6,7},{7,4},{8,9},{9,10},{10,1... | collective-permute-start | bytes 36872 | tf_op jit(solution)/shard_map/ppermute | solution.py:74
  134.7 0.7 collective-permute-done.35.refs_2_
  135.4 0.9 collective-permute-done.34.refs_1_
  136.3 0.9 copy-done.8
  137.5 1.3 slope_sum.1
  138.8 1.5 %collective-permute-start.41 = (f32[1,1024]{1,0:T(1,128)S(1)}, f32[1,1024]{1,0:T(1,128)S(1)}, u32[]{:S(2)}, u32[]{:S(2)}) collective-permute-start(f32[1,1024]{1,0:T(1,128)S(1)} %get-tuple-element.76.refs_0_), channel_id=1, source_target_pairs={{0,4},{4,0},{8,12},{12,8},{1,5},{5,1},{9,13},{13,9},{2,6},{6,2},{1... | collective-permute-start | bytes 12296 | tf_op jit(solution)/shard_map/ppermute | solution.py:545
  140.3 2.8 %finish.1 = (f32[1024,1024]{1,0:T(8,128)}, f32[8,128]{1,0:T(8,128)S(1)}) custom-call(s32[8]{0:T(128)S(1)} %stack.149.refs_7_.refs_1_.refs_0_, f32[1,1024]{1,0:T(1,128)S(1)} %bitcast.52, f32[8,128]{1,0:T(8,128)S(1)} %get-tuple-element.74.refs_2_, bf16[4096,128]{1,0:T(8,128)(2,1)S(1)} %pack_columns.1.refs_3_, bf16[4096,128]{1,0:T(8,128)(2,1)S(1)} %collective-permute-done.40.refs_4_), custom_call_target="tpu_custom_call" | custom-call | bytes 6303776 | tf_op jit(solution)/shard_map/finish/pallas_call | solution.py:56
  143.2 0.6 query_sum.1
  (115 shorter events, 8.3 us)
Async XLA Ops:
  0.6 12.3 %copy-start.25 = (bf16[4096]{0:T(1024)(128)(2,1)S(1)}, bf16[4096]{0:T(1024)(128)(2,1)}, u32[]{:S(2)}) copy-start(bf16[4096]{0:T(1024)(128)(2,1)} %param.12) | copy-start | bytes 24580
  0.6 12.3 %copy-start.24 = (s32[64,32]{0,1:T(8,128)S(1)}, s32[64,32]{0,1:T(8,128)}, u32[]{:S(2)}) copy-start(s32[64,32]{0,1:T(8,128)} %param.10) | copy-start | bytes 24580
  0.7 12.4 %copy-start.26 = (s32[64]{0:T(128)S(1)}, s32[64]{0:T(128)}, u32[]{:S(2)}) copy-start(s32[64]{0:T(128)} %param.11) | copy-start | bytes 772
  1.6 16.2 %collective-permute-start.3 = (bf16[128,1024]{1,0:T(8,128)(2,1)S(1)}, bf16[128,1024]{1,0:T(8,128)(2,1)S(1)}, u32[]{:S(2)}, u32[]{:S(2)}) collective-permute-start(bf16[128,1024]{1,0:T(8,128)(2,1)S(1)} %constant_dynamic-slice_fusion.refs_2_), channel_id=1, source_target_pairs={{0,8},{4,12},{8,0},{12,4},{1,9},{5,13},{9,1},{13,5},{2,10},{6,14},... | collective-permute-start | bytes 786440 | tf_op jit(solution)/shard_map/ppermute | solution.py:548
  5.8 1.6 %copy-start = (bf16[1024,1024]{1,0:T(8,128)(2,1)S(1)}, bf16[1024,1024]{1,0:T(8,128)(2,1)}, u32[]{:S(2)}) copy-start(bf16[1024,1024]{1,0:T(8,128)(2,1)} %refs_1_.5) | copy-start | bytes 6291460
  9.8 11.7 %collective-permute-start.2 = (f32[1,1024]{1,0:T(1,128)S(1)}, f32[1,1024]{1,0:T(1,128)S(1)}, u32[]{:S(2)}, u32[]{:S(2)}) collective-permute-start(f32[1,1024]{1,0:T(1,128)S(1)} %block_u.1), channel_id=1, source_target_pairs={{0,12},{4,0},{8,4},{12,8},{1,13},{5,1},{9,5},{13,9},{2,14},{6,2},{... | collective-permute-start | bytes 12296 | tf_op jit(solution)/shard_map/ppermute | solution.py:74
  11.1 10.3 %collective-permute-start.1 = (f32[1,1024]{1,0:T(1,128)S(1)}, f32[1,1024]{1,0:T(1,128)S(1)}, u32[]{:S(2)}, u32[]{:S(2)}) collective-permute-start(f32[1,1024]{1,0:T(1,128)S(1)} %block_u.1), channel_id=1, source_target_pairs={{0,8},{4,12},{8,0},{12,4},{1,9},{5,13},{9,1},{13,5},{2,10},{6,14},... | collective-permute-start | bytes 12296 | tf_op jit(solution)/shard_map/ppermute | solution.py:74
  12.8 8.1 %collective-permute-start = (f32[1,1024]{1,0:T(1,128)S(1)}, f32[1,1024]{1,0:T(1,128)S(1)}, u32[]{:S(2)}, u32[]{:S(2)}) collective-permute-start(f32[1,1024]{1,0:T(1,128)S(1)} %block_u.1), channel_id=1, source_target_pairs={{0,4},{4,8},{8,12},{12,0},{1,5},{5,9},{9,13},{13,1},{2,6},{6,10},{... | collective-permute-start | bytes 12296 | tf_op jit(solution)/shard_map/ppermute | solution.py:74
  13.7 19.4 %copy-start.23 = (s32[32]{0:T(128)}, s32[32]{0:T(128)S(1)}, u32[]{:S(2)}) copy-start(s32[32]{0:T(128)S(1)} %stack.186.refs_8_.refs_0_) | copy-start | bytes 388
  17.9 15.1 %collective-permute-start.7 = (bf16[128,1024]{1,0:T(8,128)(2,1)S(1)}, bf16[128,1024]{1,0:T(8,128)(2,1)S(1)}, u32[]{:S(2)}, u32[]{:S(2)}) collective-permute-start(bf16[128,1024]{1,0:T(8,128)(2,1)S(1)} %collective-permute-done.3.refs_6_.refs_0_), channel_id=1, source_target_pairs={{0,18},{1,19},{2,16},{3,17},{16,2},{17,3},{18,0},{19,1},{4,22},{5,... | collective-permute-start | bytes 786440 | tf_op jit(solution)/shard_map/ppermute | solution.py:541
  20.4 12.7 %collective-permute-start.6 = (bf16[128,1024]{1,0:T(8,128)(2,1)S(1)}, bf16[128,1024]{1,0:T(8,128)(2,1)S(1)}, u32[]{:S(2)}, u32[]{:S(2)}) collective-permute-start(bf16[128,1024]{1,0:T(8,128)(2,1)S(1)} %collective-permute-done.3.refs_6_.refs_0_), channel_id=1, source_target_pairs={{0,16},{1,17},{2,18},{3,19},{16,0},{17,1},{18,2},{19,3},{4,20},{5,... | collective-permute-start | bytes 786440 | tf_op jit(solution)/shard_map/ppermute | solution.py:541
  20.9 12.1 %collective-permute-start.5 = (bf16[128,1024]{1,0:T(8,128)(2,1)S(1)}, bf16[128,1024]{1,0:T(8,128)(2,1)S(1)}, u32[]{:S(2)}, u32[]{:S(2)}) collective-permute-start(bf16[128,1024]{1,0:T(8,128)(2,1)S(1)} %collective-permute-done.3.refs_6_.refs_0_), channel_id=1, source_target_pairs={{0,2},{1,3},{2,0},{3,1},{16,18},{17,19},{18,16},{19,17},{4,6},{5,7... | collective-permute-start | bytes 786440 | tf_op jit(solution)/shard_map/ppermute | solution.py:541
  33.0 7.5 %copy-start.13 = (f32[1024,1]{1,0:T(8,128)}, f32[1024,1]{1,0:T(8,128)S(1)}, u32[]{:S(2)}) copy-start(f32[1024,1]{1,0:T(8,128)S(1)} %get-tuple-element.51.curve_ref) | copy-start | bytes 12292
  33.0 5.6 %copy-start.4 = (bf16[1024,1024]{1,0:T(8,128)(2,1)S(1)}, bf16[1024,1024]{1,0:T(8,128)(2,1)}, u32[]{:S(2)}) copy-start(bf16[1024,1024]{1,0:T(8,128)(2,1)} %refs_0_.4) | copy-start | bytes 6291460
  33.1 8.9 %copy-start.1 = (bf16[1024,1024]{1,0:T(8,128)(2,1)S(1)}, bf16[1024,1024]{1,0:T(8,128)(2,1)}, u32[]{:S(2)}) copy-start(bf16[1024,1024]{1,0:T(8,128)(2,1)} %refs_1_.5) | copy-start | bytes 6291460
  33.2 8.8 %collective-permute-start.8 = (bf16[512,1024]{1,0:T(8,128)(2,1)S(1)}, bf16[512,1024]{1,0:T(8,128)(2,1)S(1)}, u32[]{:S(2)}, u32[]{:S(2)}) collective-permute-start(bf16[512,1024]{1,0:T(8,128)(2,1)S(1)} %pack_shares.1.refs_5_), channel_id=1, source_target_pairs={{0,1},{1,0},{2,3},{3,2},{16,17},{17,16},{18,19},{19,18},{4,5},{5,4... | collective-permute-start | bytes 3145736 | tf_op jit(solution)/shard_map/ppermute | solution.py:541
  33.2 8.7 %collective-permute-start.4 = (bf16[64,2048]{1,0:T(8,128)(2,1)S(1)}, bf16[64,2048]{1,0:T(8,128)(2,1)S(1)}, u32[]{:S(2)}, u32[]{:S(2)}) collective-permute-start(bf16[64,2048]{1,0:T(8,128)(2,1)S(1)} %get-tuple-element.42), channel_id=1, source_target_pairs={{0,4},{4,0},{8,12},{12,8},{1,5},{5,1},{9,13},{13,9},{2,6},{6,2},{1... | collective-permute-start | bytes 786440 | tf_op jit(solution)/shard_map/ppermute | solution.py:545
  34.1 3.3 %collective-permute-start.9 = (s32[64,8]{1,0:T(8,128)S(1)}, s32[64,8]{1,0:T(8,128)S(1)}, u32[]{:S(2)}, u32[]{:S(2)}) collective-permute-start(s32[64,8]{1,0:T(8,128)S(1)} %get-tuple-element.45), channel_id=1, source_target_pairs={{0,1},{1,2},{2,3},{3,0},{4,5},{5,6},{6,7},{7,4},{8,9},{9,10},{10,1... | collective-permute-start | bytes 6152 | tf_op jit(solution)/shard_map/ppermute | solution.py:74
  34.2 3.9 %collective-permute-start.10 = (s32[64,8]{1,0:T(8,128)S(1)}, s32[64,8]{1,0:T(8,128)S(1)}, u32[]{:S(2)}, u32[]{:S(2)}) collective-permute-start(s32[64,8]{1,0:T(8,128)S(1)} %get-tuple-element.46), channel_id=1, source_target_pairs={{0,2},{1,3},{2,0},{3,1},{4,6},{5,7},{6,4},{7,5},{8,10},{9,11},{10,... | collective-permute-start | bytes 6152 | tf_op jit(solution)/shard_map/ppermute | solution.py:74
  35.8 2.9 %collective-permute-start.11 = (s32[64,8]{1,0:T(8,128)S(1)}, s32[64,8]{1,0:T(8,128)S(1)}, u32[]{:S(2)}, u32[]{:S(2)}) collective-permute-start(s32[64,8]{1,0:T(8,128)S(1)} %get-tuple-element.47), channel_id=1, source_target_pairs={{0,3},{1,0},{2,1},{3,2},{4,7},{5,4},{6,5},{7,6},{8,11},{9,8},{10,9... | collective-permute-start | bytes 6152 | tf_op jit(solution)/shard_map/ppermute | solution.py:74
  43.4 39.0 %copy-start.2 = (bf16[1024,1024]{1,0:T(8,128)(2,1)}, bf16[1024,1024]{1,0:T(8,128)(2,1)S(1)}, u32[]{:S(2)}) copy-start(bf16[1024,1024]{1,0:T(8,128)(2,1)S(1)} %get-tuple-element.49.refs_2_) | copy-start | bytes 6291460
  43.4 7.9 %collective-permute-start.13 = (bf16[128,1024]{1,0:T(8,128)(2,1)S(1)}, bf16[128,1024]{1,0:T(8,128)(2,1)S(1)}, u32[]{:S(2)}, u32[]{:S(2)}) collective-permute-start(bf16[128,1024]{1,0:T(8,128)(2,1)S(1)} %get-tuple-element.55.refs_3_), channel_id=1, source_target_pairs={{0,2},{1,3},{2,0},{3,1},{16,18},{17,19},{18,16},{19,17},{4,6},{5,7... | collective-permute-start | bytes 786440 | tf_op jit(solution)/shard_map/ppermute | solution.py:541
  45.0 5.0 %collective-permute-start.12 = (bf16[64,1024]{1,0:T(8,128)(2,1)S(1)}, bf16[64,1024]{1,0:T(8,128)(2,1)S(1)}, u32[]{:S(2)}, u32[]{:S(2)}) collective-permute-start(bf16[64,1024]{1,0:T(8,128)(2,1)S(1)} %get-tuple-element.53), channel_id=1, source_target_pairs={{0,4},{4,0},{8,12},{12,8},{1,5},{5,1},{9,13},{13,9},{2,6},{6,2},{1... | collective-permute-start | bytes 393224 | tf_op jit(solution)/shard_map/ppermute | solution.py:545
  51.5 11.8 %copy-start.15 = (bf16[256,1024]{1,0:T(8,128)(2,1)}, bf16[256,1024]{1,0:T(8,128)(2,1)S(1)}, u32[]{:S(2)}) copy-start(bf16[256,1024]{1,0:T(8,128)(2,1)S(1)} %get-tuple-element.60.refs_2_) | copy-start | bytes 1572868
  51.5 10.4 %collective-permute-start.17 = (bf16[256,1024]{1,0:T(8,128)(2,1)S(1)}, bf16[256,1024]{1,0:T(8,128)(2,1)S(1)}, u32[]{:S(2)}, u32[]{:S(2)}) collective-permute-start(bf16[256,1024]{1,0:T(8,128)(2,1)S(1)} %get-tuple-element.60.refs_2_), channel_id=1, source_target_pairs={{0,1},{1,0},{2,3},{3,2},{16,17},{17,16},{18,19},{19,18},{4,5},{5,4... | collective-permute-start | bytes 1572872 | tf_op jit(solution)/shard_map/ppermute | solution.py:541
  51.6 14.3 %collective-permute-start.24 = (bf16[256,1024]{1,0:T(8,128)(2,1)S(1)}, bf16[256,1024]{1,0:T(8,128)(2,1)S(1)}, u32[]{:S(2)}, u32[]{:S(2)}) collective-permute-start(bf16[256,1024]{1,0:T(8,128)(2,1)S(1)} %get-tuple-element.60.refs_2_), channel_id=1, source_target_pairs={{0,16},{1,17},{2,18},{3,19},{16,0},{17,1},{18,2},{19,3},{4,20},{5,... | collective-permute-start | bytes 1572872 | tf_op jit(solution)/shard_map/ppermute | solution.py:541
  53.2 5.2 %collective-permute-start.16 = (bf16[64,1024]{1,0:T(8,128)(2,1)S(1)}, bf16[64,1024]{1,0:T(8,128)(2,1)S(1)}, u32[]{:S(2)}, u32[]{:S(2)}) collective-permute-start(bf16[64,1024]{1,0:T(8,128)(2,1)S(1)} %get-tuple-element.58.refs_3_), channel_id=1, source_target_pairs={{0,3},{1,0},{2,1},{3,2},{4,7},{5,4},{6,5},{7,6},{8,11},{9,8},{10,9... | collective-permute-start | bytes 393224 | tf_op jit(solution)/shard_map/ppermute | solution.py:74
  54.4 7.4 %collective-permute-start.15 = (bf16[64,1024]{1,0:T(8,128)(2,1)S(1)}, bf16[64,1024]{1,0:T(8,128)(2,1)S(1)}, u32[]{:S(2)}, u32[]{:S(2)}) collective-permute-start(bf16[64,1024]{1,0:T(8,128)(2,1)S(1)} %get-tuple-element.58.refs_3_), channel_id=1, source_target_pairs={{0,2},{1,3},{2,0},{3,1},{4,6},{5,7},{6,4},{7,5},{8,10},{9,11},{10,... | collective-permute-start | bytes 393224 | tf_op jit(solution)/shard_map/ppermute | solution.py:74
  55.0 6.9 %collective-permute-start.14 = (bf16[64,1024]{1,0:T(8,128)(2,1)S(1)}, bf16[64,1024]{1,0:T(8,128)(2,1)S(1)}, u32[]{:S(2)}, u32[]{:S(2)}) collective-permute-start(bf16[64,1024]{1,0:T(8,128)(2,1)S(1)} %get-tuple-element.58.refs_3_), channel_id=1, source_target_pairs={{0,1},{1,2},{2,3},{3,0},{4,5},{5,6},{6,7},{7,4},{8,9},{9,10},{10,1... | collective-permute-start | bytes 393224 | tf_op jit(solution)/shard_map/ppermute | solution.py:74
  58.3 15.6 %collective-permute-start.22 = (bf16[128,1024]{1,0:T(8,128)(2,1)S(1)}, bf16[128,1024]{1,0:T(8,128)(2,1)S(1)}, u32[]{:S(2)}, u32[]{:S(2)}) collective-permute-start(bf16[128,1024]{1,0:T(8,128)(2,1)S(1)} %get-tuple-element.67), channel_id=1, source_target_pairs={{0,8},{4,12},{8,0},{12,4},{1,9},{5,13},{9,1},{13,5},{2,10},{6,14},... | collective-permute-start | bytes 786440 | tf_op jit(solution)/shard_map/ppermute | solution.py:548
  61.9 20.5 %copy-start.6 = (bf16[256,1024]{1,0:T(8,128)(2,1)}, bf16[256,1024]{1,0:T(8,128)(2,1)S(1)}, u32[]{:S(2)}) copy-start(bf16[256,1024]{1,0:T(8,128)(2,1)S(1)} %collective-permute-done.17.refs_7_.refs_6_) | copy-start | bytes 1572868
  61.9 14.3 %copy-start.16 = (bf16[64,1024]{1,0:T(8,128)(2,1)S(1)}, bf16[64,1024]{1,0:T(8,128)(2,1)}, u32[]{:S(2)}) copy-start(bf16[64,1024]{1,0:T(8,128)(2,1)} %refs_0_.5) | copy-start | bytes 393220
  66.7 15.7 %collective-permute-start.25 = (bf16[256,1024]{1,0:T(8,128)(2,1)S(1)}, bf16[256,1024]{1,0:T(8,128)(2,1)S(1)}, u32[]{:S(2)}, u32[]{:S(2)}) collective-permute-start(bf16[256,1024]{1,0:T(8,128)(2,1)S(1)} %near_far.1), channel_id=1, source_target_pairs={{0,1},{1,0},{2,3},{3,2},{16,17},{17,16},{18,19},{19,18},{4,5},{5,4... | collective-permute-start | bytes 1572872 | tf_op jit(solution)/shard_map/ppermute | solution.py:541
  66.7 7.2 %collective-permute-start.18 = (bf16[64,1152]{1,0:T(8,128)(2,1)S(1)}, bf16[64,1152]{1,0:T(8,128)(2,1)S(1)}, u32[]{:S(2)}, u32[]{:S(2)}) collective-permute-start(bf16[64,1152]{1,0:T(8,128)(2,1)S(1)} %get-tuple-element.62), channel_id=1, source_target_pairs={{0,3},{1,0},{2,1},{3,2},{4,7},{5,4},{6,5},{7,6},{8,11},{9,8},{10,9... | collective-permute-start | bytes 442376 | tf_op jit(solution)/shard_map/ppermute | solution.py:74
  68.4 7.8 %collective-permute-start.19 = (bf16[64,1152]{1,0:T(8,128)(2,1)S(1)}, bf16[64,1152]{1,0:T(8,128)(2,1)S(1)}, u32[]{:S(2)}, u32[]{:S(2)}) collective-permute-start(bf16[64,1152]{1,0:T(8,128)(2,1)S(1)} %get-tuple-element.63), channel_id=1, source_target_pairs={{0,2},{1,3},{2,0},{3,1},{4,6},{5,7},{6,4},{7,5},{8,10},{9,11},{10,... | collective-permute-start | bytes 442376 | tf_op jit(solution)/shard_map/ppermute | solution.py:74
  68.9 7.3 %collective-permute-start.20 = (bf16[64,1152]{1,0:T(8,128)(2,1)S(1)}, bf16[64,1152]{1,0:T(8,128)(2,1)S(1)}, u32[]{:S(2)}, u32[]{:S(2)}) collective-permute-start(bf16[64,1152]{1,0:T(8,128)(2,1)S(1)} %get-tuple-element.64), channel_id=1, source_target_pairs={{0,1},{1,2},{2,3},{3,0},{4,5},{5,6},{6,7},{7,4},{8,9},{9,10},{10,1... | collective-permute-start | bytes 442376 | tf_op jit(solution)/shard_map/ppermute | solution.py:74
  74.0 8.4 %collective-permute-start.23 = (bf16[128,1024]{1,0:T(8,128)(2,1)S(1)}, bf16[128,1024]{1,0:T(8,128)(2,1)S(1)}, u32[]{:S(2)}, u32[]{:S(2)}) collective-permute-start(bf16[128,1024]{1,0:T(8,128)(2,1)S(1)} %other.1.refs_5_), channel_id=1, source_target_pairs={{0,16},{1,17},{2,18},{3,19},{16,0},{17,1},{18,2},{19,3},{4,20},{5,... | collective-permute-start | bytes 786440 | tf_op jit(solution)/shard_map/ppermute | solution.py:541
  76.6 5.0 %collective-permute-start.21 = (bf16[64,1024]{1,0:T(8,128)(2,1)S(1)}, bf16[64,1024]{1,0:T(8,128)(2,1)S(1)}, u32[]{:S(2)}, u32[]{:S(2)}) collective-permute-start(bf16[64,1024]{1,0:T(8,128)(2,1)S(1)} %get-tuple-element.66.refs_3_), channel_id=1, source_target_pairs={{0,4},{4,0},{8,12},{12,8},{1,5},{5,1},{9,13},{13,9},{2,6},{6,2},{1... | collective-permute-start | bytes 393224 | tf_op jit(solution)/shard_map/ppermute | solution.py:545
  82.4 2.2 %copy-start.9 = (bf16[256,1024]{1,0:T(8,128)(2,1)}, bf16[256,1024]{1,0:T(8,128)(2,1)S(1)}, u32[]{:S(2)}) copy-start(bf16[256,1024]{1,0:T(8,128)(2,1)S(1)} %collective-permute-done.25.refs_8_.refs_7_) | copy-start | bytes 1572868
  84.6 7.5 %collective-permute-start.26 = (bf16[64,2048]{1,0:T(8,128)(2,1)S(1)}, bf16[64,2048]{1,0:T(8,128)(2,1)S(1)}, u32[]{:S(2)}, u32[]{:S(2)}) collective-permute-start(bf16[64,2048]{1,0:T(8,128)(2,1)S(1)} %get-tuple-element.69), channel_id=1, source_target_pairs={{0,4},{4,0},{8,12},{12,8},{1,5},{5,1},{9,13},{13,9},{2,6},{6,2},{1... | collective-permute-start | bytes 786440 | tf_op jit(solution)/shard_map/ppermute | solution.py:545
  85.5 22.7 %collective-permute-start.28 = (bf16[256,1024]{1,0:T(8,128)(2,1)}, bf16[256,1024]{1,0:T(8,128)(2,1)S(1)}, u32[]{:S(2)}, u32[]{:S(2)}) collective-permute-start(bf16[256,1024]{1,0:T(8,128)(2,1)} %get-tuple-element.72.refs_4_), channel_id=1, source_target_pairs={{0,2},{1,3},{2,0},{3,1},{16,18},{17,19},{18,16},{19,17},{4,6},{5,7... | collective-permute-start | bytes 1572872 | tf_op jit(solution)/shard_map/ppermute | solution.py:541
  92.9 21.8 %all-to-all-start = ((bf16[32,64,128]{2,1,0:T(8,128)(2,1)}), bf16[32,64,128]{2,1,0:T(8,128)(2,1)}, u32[]{:S(2)}, u32[]{:S(2)}) async-start(bf16[32,64,128]{2,1,0:T(8,128)(2,1)} %copy-done.12), calls=%async_computation | async-start | bytes 1048576 | tf_op jit(solution)/shard_map/all_to_all | solution.py:659
  98.3 16.4 %collective-permute-start.29 = (bf16[256,1024]{1,0:T(8,128)(2,1)}, bf16[256,1024]{1,0:T(8,128)(2,1)}, u32[]{:S(2)}, u32[]{:S(2)}) collective-permute-start(bf16[256,1024]{1,0:T(8,128)(2,1)} %get-tuple-element.72.refs_4_), channel_id=1, source_target_pairs={{0,1},{1,0},{2,3},{3,2},{16,17},{17,16},{18,19},{19,18},{4,5},{5,4... | collective-permute-start | bytes 1572872 | tf_op jit(solution)/shard_map/ppermute | solution.py:541
  98.4 3.4 %copy-start.5 = (bf16[1024,4096]{1,0:T(8,128)(2,1)S(1)}, bf16[1024,4096]{1,0:T(8,128)(2,1)}, u32[]{:S(2)}) copy-start(bf16[1024,4096]{1,0:T(8,128)(2,1)} %get-tuple-element.50.normed_ref) | copy-start | bytes 25165828
  101.8 1.0 copy-start.14
  108.3 6.5 %copy-start.10 = (bf16[256,1024]{1,0:T(8,128)(2,1)}, bf16[256,1024]{1,0:T(8,128)(2,1)S(1)}, u32[]{:S(2)}) copy-start(bf16[256,1024]{1,0:T(8,128)(2,1)S(1)} %collective-permute-done.28.refs_0_.refs_5_) | copy-start | bytes 1572868
  108.3 6.4 %collective-permute-start.30 = (bf16[256,1024]{1,0:T(8,128)(2,1)S(1)}, bf16[256,1024]{1,0:T(8,128)(2,1)}, u32[]{:S(2)}, u32[]{:S(2)}) collective-permute-start(bf16[256,1024]{1,0:T(8,128)(2,1)S(1)} %late.1), channel_id=1, source_target_pairs={{0,1},{1,0},{2,3},{3,2},{16,17},{17,16},{18,19},{19,18},{4,5},{5,4... | collective-permute-start | bytes 1572872 | tf_op jit(solution)/shard_map/ppermute | solution.py:541
  108.9 3.7 %collective-permute-start.31 = (f32[24,128]{1,0:T(8,128)S(1)}, f32[24,128]{1,0:T(8,128)S(1)}, u32[]{:S(2)}, u32[]{:S(2)}) collective-permute-start(f32[24,128]{1,0:T(8,128)S(1)} %get-tuple-element.73.refs_0_), channel_id=1, source_target_pairs={{0,16},{16,0},{1,17},{17,1},{2,18},{18,2},{3,19},{19,3},{4,20},{20... | collective-permute-start | bytes 36872 | tf_op jit(solution)/shard_map/ppermute | solution.py:74
  110.4 3.7 %collective-permute-start.27 = (f32[24,128]{1,0:T(8,128)S(1)}, f32[24,128]{1,0:T(8,128)S(1)}, u32[]{:S(2)}, u32[]{:S(2)}) collective-permute-start(f32[24,128]{1,0:T(8,128)S(1)} %get-tuple-element.70.refs_0_.refs_1_), channel_id=1, source_target_pairs={{0,16},{16,0},{1,17},{17,1},{2,18},{18,2},{3,19},{19,3},{4,20},{20... | collective-permute-start | bytes 36872 | tf_op jit(solution)/shard_map/ppermute | solution.py:74
  114.7 7.7 %copy-start.18 = (f32[24,128]{1,0:T(8,128)S(1)}, f32[24,128]{1,0:T(8,128)}, u32[]{:S(2)}) copy-start(f32[24,128]{1,0:T(8,128)} %copy-done.17) | copy-start | bytes 36868
  114.7 10.2 %copy-start.20 = (f32[24,128]{1,0:T(8,128)S(1)}, f32[24,128]{1,0:T(8,128)}, u32[]{:S(2)}) copy-start(f32[24,128]{1,0:T(8,128)} %copy-done.19) | copy-start | bytes 36868
  118.8 18.6 %copy-start.3 = (bf16[1024,1024]{1,0:T(8,128)(2,1)S(1)}, bf16[1024,1024]{1,0:T(8,128)(2,1)}, u32[]{:S(2)}) copy-start(bf16[1024,1024]{1,0:T(8,128)(2,1)} %copy-done.2) | copy-start | bytes 6291460
  118.8 17.4 %collective-permute-start.39 = (bf16[1024,128]{1,0:T(8,128)(2,1)}, bf16[1024,128]{1,0:T(8,128)(2,1)S(1)}, u32[]{:S(2)}, u32[]{:S(2)}) collective-permute-start(bf16[1024,128]{1,0:T(8,128)(2,1)} %grad_columns.1.refs_1_.refs_0_), channel_id=1, source_target_pairs={{0,18},{1,19},{2,16},{3,17},{16,2},{17,3},{18,0},{19,1},{4,22},{5,... | collective-permute-start | bytes 786440 | tf_op jit(solution)/shard_map/ppermute | solution.py:541
  120.4 15.9 %collective-permute-start.38 = (bf16[1024,128]{1,0:T(8,128)(2,1)}, bf16[1024,128]{1,0:T(8,128)(2,1)S(1)}, u32[]{:S(2)}, u32[]{:S(2)}) collective-permute-start(bf16[1024,128]{1,0:T(8,128)(2,1)} %grad_columns.1.refs_1_.refs_0_), channel_id=1, source_target_pairs={{0,16},{1,17},{2,18},{3,19},{16,0},{17,1},{18,2},{19,3},{4,20},{5,... | collective-permute-start | bytes 786440 | tf_op jit(solution)/shard_map/ppermute | solution.py:541
  121.8 14.5 %collective-permute-start.37 = (bf16[1024,128]{1,0:T(8,128)(2,1)}, bf16[1024,128]{1,0:T(8,128)(2,1)S(1)}, u32[]{:S(2)}, u32[]{:S(2)}) collective-permute-start(bf16[1024,128]{1,0:T(8,128)(2,1)} %grad_columns.1.refs_1_.refs_0_), channel_id=1, source_target_pairs={{0,2},{1,3},{2,0},{3,1},{16,18},{17,19},{18,16},{19,17},{4,6},{5,7... | collective-permute-start | bytes 786440 | tf_op jit(solution)/shard_map/ppermute | solution.py:541
  122.4 1.0 copy-start.7
  123.4 3.7 %collective-permute-start.32 = (f32[24,128]{1,0:T(8,128)S(1)}, f32[24,128]{1,0:T(8,128)S(1)}, u32[]{:S(2)}, u32[]{:S(2)}) collective-permute-start(f32[24,128]{1,0:T(8,128)S(1)} %slope_out.3), channel_id=1, source_target_pairs={{0,4},{4,0},{8,12},{12,8},{1,5},{5,1},{9,13},{13,9},{2,6},{6,2},{1... | collective-permute-start | bytes 36872 | tf_op jit(solution)/shard_map/ppermute | solution.py:545
  127.1 4.6 %collective-permute-start.33 = (f32[24,128]{1,0:T(8,128)S(1)}, f32[24,128]{1,0:T(8,128)S(1)}, u32[]{:S(2)}, u32[]{:S(2)}) collective-permute-start(f32[24,128]{1,0:T(8,128)S(1)} %sum_half.1.refs_0_), channel_id=1, source_target_pairs={{0,8},{4,12},{8,0},{12,4},{1,9},{5,13},{9,1},{13,5},{2,10},{6,14},... | collective-permute-start | bytes 36872 | tf_op jit(solution)/shard_map/ppermute | solution.py:548
  131.7 1.5 %collective-permute-start.36 = (f32[24,128]{1,0:T(8,128)S(1)}, f32[24,128]{1,0:T(8,128)S(1)}, u32[]{:S(2)}, u32[]{:S(2)}) collective-permute-start(f32[24,128]{1,0:T(8,128)S(1)} %sum_mirror.1.refs_0_), channel_id=1, source_target_pairs={{0,3},{1,0},{2,1},{3,2},{4,7},{5,4},{6,5},{7,6},{8,11},{9,8},{10,9... | collective-permute-start | bytes 36872 | tf_op jit(solution)/shard_map/ppermute | solution.py:74
  131.7 3.7 %collective-permute-start.35 = (f32[24,128]{1,0:T(8,128)S(1)}, f32[24,128]{1,0:T(8,128)S(1)}, u32[]{:S(2)}, u32[]{:S(2)}) collective-permute-start(f32[24,128]{1,0:T(8,128)S(1)} %sum_mirror.1.refs_0_), channel_id=1, source_target_pairs={{0,2},{1,3},{2,0},{3,1},{4,6},{5,7},{6,4},{7,5},{8,10},{9,11},{10,... | collective-permute-start | bytes 36872 | tf_op jit(solution)/shard_map/ppermute | solution.py:74
  133.2 3.1 %collective-permute-start.34 = (f32[24,128]{1,0:T(8,128)S(1)}, f32[24,128]{1,0:T(8,128)S(1)}, u32[]{:S(2)}, u32[]{:S(2)}) collective-permute-start(f32[24,128]{1,0:T(8,128)S(1)} %sum_mirror.1.refs_0_), channel_id=1, source_target_pairs={{0,1},{1,2},{2,3},{3,0},{4,5},{5,6},{6,7},{7,4},{8,9},{9,10},{10,1... | collective-permute-start | bytes 36872 | tf_op jit(solution)/shard_map/ppermute | solution.py:74
  137.4 2.9 %copy-start.22 = (f32[1024]{0:T(1024)S(1)}, f32[1024]{0:T(1024)}, u32[]{:S(2)}) copy-start(f32[1024]{0:T(1024)} %param.14) | copy-start | bytes 12292
  137.4 2.9 %collective-permute-start.40 = (bf16[4096,128]{1,0:T(8,128)(2,1)S(1)}, bf16[4096,128]{1,0:T(8,128)(2,1)S(1)}, u32[]{:S(2)}, u32[]{:S(2)}) collective-permute-start(bf16[4096,128]{1,0:T(8,128)(2,1)S(1)} %pack_columns.1.refs_3_), channel_id=1, source_target_pairs={{0,1},{1,0},{2,3},{3,2},{16,17},{17,16},{18,19},{19,18},{4,5},{5,4... | collective-permute-start | bytes 3145736 | tf_op jit(solution)/shard_map/ppermute | solution.py:541
  138.8 4.4 %collective-permute-start.41 = (f32[1,1024]{1,0:T(1,128)S(1)}, f32[1,1024]{1,0:T(1,128)S(1)}, u32[]{:S(2)}, u32[]{:S(2)}) collective-permute-start(f32[1,1024]{1,0:T(1,128)S(1)} %get-tuple-element.76.refs_0_), channel_id=1, source_target_pairs={{0,4},{4,0},{8,12},{12,8},{1,5},{5,1},{9,13},{13,9},{2,6},{6,2},{1... | collective-permute-start | bytes 12296 | tf_op jit(solution)/shard_map/ppermute | solution.py:545
  (6 other events, 4.4 us)
